TPU v7x, 32 devices: a whole 2x2x4 slice. The times are simulated.
32 devices in a mesh: groups: 1, dp: 1, expert: 16 (over z, y, core), tensor: 2 (over x).
Axes of the slice: x: 2, y: 2, z: 4, core: 2. Of those that a mesh axis runs over, the one named last changes fastest.
Arguments:
- tokens: bfloat16 [2048, 4096], P(('groups', 'dp', 'expert')), may hold values from -6 to 6
- expert_ids: int32 [2048, 2], P(('groups', 'dp', 'expert')), may hold values from 0 to 15, all different within a row; in each aligned block of 128 rows (0 to 127, 128 to 255, ...) at most 24 rows name the same one
- gate_probs: float32 [2048, 2], P(('groups', 'dp', 'expert')), may hold values from 0.2 to 1
- w_gate: bfloat16 [16, 4096, 3584], P('expert', 'dp', 'tensor'), may hold values from -0.09375 to 0.09375
- w_up: bfloat16 [16, 4096, 3584], P('expert', 'dp', 'tensor'), may hold values from -0.09375 to 0.09375
- w_down: bfloat16 [16, 3584, 4096], P('expert', 'tensor', 'dp'), may hold values from -0.09375 to 0.09375
Outputs:
- mixed: bfloat16 [2048, 4096], P(('groups', 'dp', 'expert'), 'tensor')
Inputs may be any that keep to these rules, and one draw needn't show every extreme that they name: `expert_ids`: each row names 2 different experts; in each aligned block of 128 rows no expert is named by more than 24 rows, and in some blocks one expert is named by exactly 24 rows.
All inputs are finite; a program needn't handle non-finite values.
Results may differ from a plain program's by a relative error of at most 0.005.
Values may be sent and summed in bfloat16 or wider, within the bound.
No kernel may reach another device: no remote copies, remote signals or barrier semaphores. Data moves between devices by JAX's collectives and lax.ppermute only.
A program may use at most 128 MiB of HBM per device.

v0:
```python
import jax
import jax.numpy as jnp
from jax import lax
from jax.sharding import PartitionSpec as P

TOP = 2
BLOCK = 128
CAP = 24


def slot_places(expert_ids, experts):
    rows = expert_ids.shape[0]
    blocks = rows // BLOCK
    flat = expert_ids.reshape(blocks, BLOCK * TOP)
    onehot = (flat[:, :, None] == jnp.arange(experts, dtype=jnp.int32)[None, None, :]).astype(
        jnp.int32
    )
    before = jnp.cumsum(onehot, axis=1) - onehot
    slot = jnp.sum(before * onehot, axis=2)
    offset = (jnp.arange(blocks, dtype=jnp.int32) * CAP)[:, None]
    return (offset + slot).reshape(rows, TOP)


def weigh_back(returned, expert_ids, place, gate_probs):
    picked = returned[expert_ids, place]
    return jnp.sum(picked * gate_probs[:, :, None], axis=1)


def on_device(tokens, expert_ids, gate_probs, w_gate, w_up, w_down):
    rows, width = tokens.shape
    experts = lax.axis_size("expert")
    blocks = rows // BLOCK
    place = slot_places(expert_ids, experts)
    spread = jnp.broadcast_to(tokens[:, None, :], (rows, TOP, tokens.shape[1]))
    outgoing = (
        jnp.zeros((experts, blocks * CAP, tokens.shape[1]), jnp.bfloat16)
        .at[expert_ids, place]
        .set(spread)
    )
    arrived = lax.all_to_all(outgoing, "expert", split_axis=0, concat_axis=0, tiled=True)
    routed = arrived.reshape(experts * blocks * CAP, width)
    gate = jnp.dot(
        routed,
        lax.all_gather(w_gate, "dp", axis=1, tiled=True)[0],
        preferred_element_type=jnp.float32,
    )
    up = jnp.dot(
        routed,
        lax.all_gather(w_up, "dp", axis=1, tiled=True)[0],
        preferred_element_type=jnp.float32,
    )
    hidden = (jax.nn.silu(gate) * up).astype(jnp.bfloat16)
    partial_value = jnp.dot(
        hidden,
        lax.all_gather(w_down, "dp", axis=2, tiled=True)[0],
        preferred_element_type=jnp.float32,
    )
    partial_value = partial_value.reshape(experts, blocks * CAP, width)
    owned = lax.psum_scatter(partial_value, "tensor", scatter_dimension=2, tiled=True)
    returned = lax.all_to_all(owned, "expert", split_axis=0, concat_axis=0, tiled=True)
    mixed = weigh_back(returned, expert_ids, place, gate_probs)
    return mixed.astype(jnp.bfloat16)


def solution(mesh):
    placed = (
        P(("groups", "dp", "expert"), None),
        P(("groups", "dp", "expert"), None),
        P(("groups", "dp", "expert"), None),
        P("expert", "dp", "tensor"),
        P("expert", "dp", "tensor"),
        P("expert", "tensor", "dp"),
    )
    return jax.shard_map(
        on_device,
        mesh=mesh,
        in_specs=placed,
        out_specs=P(("groups", "dp", "expert"), "tensor"),
        check_vma=False,
    )
```

profile of v0, /device:TPU:11, one launch (start us, length us, event | category | flops | bytes accessed | tf_op | source)
XLA Modules:
  0.0 335.3 jit_solution(4399261155421806060)
XLA Ops:
  6.5 0.8 copy.18
  7.3 0.1 eq.27
  7.5 0.6 reduce-window.6
  8.1 0.2 slice_reduce_fusion
  8.6 0.1 reshape.159
  8.8 0.7 fusion.13
  9.5 0.1 copy.25
  9.6 0.1 reshape.167
  9.7 3.3 broadcast_in_dim.8
  13.0 2.2 reshape.169
  15.3 0.4 broadcast_in_dim.6
  15.7 48.9 %scatter_fusion = bf16[16,24,4096]{2,1,0:T(8,128)(2,1)S(1)} fusion(bf16[16,24,4096]{2,1,0:T(8,128)(2,1)S(1)} %broadcast_in_dim.6, s32[256]{0:T(256)S(1)} %reshape.167, bf16[256,4096]{1,0:T(8,128)(2,1)} %reshape.169), kind=kCustom, calls=%fused_computation.1 | custom fusion | bytes 6293504 | tf_op jit(solution)/shard_map/scatter | solution.py:38
  64.5 77.0 %all_to_all.10 = bf16[16,24,4096]{2,1,0:T(8,128)(2,1)S(1)} all-to-all(bf16[16,24,4096]{2,1,0:T(8,128)(2,1)S(1)} %scatter_fusion), channel_id=1, replica_groups=mesh['groups'=1,'dp'=1,'expert'=16,'tensor'=2] {'expert'}, dimensions={0} | all-to-all | bytes 6291456 | tf_op jit(solution)/shard_map/all_to_all | solution.py:40
  141.5 9.3 %fusion.4 = f32[384,1792]{1,0:T(8,128)S(1)} fusion(bf16[384,4096]{1,0:T(8,128)(2,1)S(1)} %bitcast.45, bf16[1,4096,1792]{2,1,0:T(8,128)(2,1)} %param.9), kind=kOutput, calls=%fused_computation.6 | convolution fusion | flops 5637144576 | bytes 20578304 | tf_op jit(solution)/shard_map/dot_general | solution.py:42
  150.9 6.1 %fusion.9 = bf16[384,1792]{1,0:T(8,128)(2,1)S(1)} fusion(bf16[384,4096]{1,0:T(8,128)(2,1)S(1)} %bitcast.46, bf16[1,4096,1792]{2,1,0:T(8,128)(2,1)S(1)} %bitcast.52, f32[384,1792]{1,0:T(8,128)S(1)} %fusion.4), kind=kOutput, calls=%fused_computation.9 | convolution fusion | flops 5641273344 | bytes 21954560 | tf_op jit(solution)/shard_map/dot_general | solution.py:47
  157.0 10.8 %fusion = f32[16,24,4096]{2,1,0:T(8,128)} fusion(bf16[16,24,1792]{2,1,0:T(8,128)(2,1)S(1)} %bitcast.53, bf16[1,1792,4096]{2,1,0:T(8,128)(2,1)} %param.11), kind=kOutput, calls=%fused_computation.2 | convolution fusion | flops 5637144576 | bytes 22347776 | tf_op jit(solution)/shard_map/dot_general | solution.py:53
  167.9 75.5 %reduce-scatter.2.cloned.1.call-done = f32[16,24,2048]{2,1,0:T(8,128)} async-done(((f32[16,24,4096]{2,1,0:T(8,128)}), f32[16,24,2048]{2,1,0:T(8,128)}) %reduce-scatter.2.cloned.1.call-update) | async-done | bytes 3145744 | tf_op jit(solution)/shard_map/reduce_scatter | solution.py:59
  243.3 6.4 %all-to-all-start.1 = ((f32[16,24,2048]{2,1,0:T(8,128)}), f32[16,24,2048]{2,1,0:T(8,128)S(1)}, u32[]{:S(2)}, u32[]{:S(2)}) async-start(f32[16,24,2048]{2,1,0:T(8,128)} %reduce-scatter.2.cloned.1.call-done), calls=%async_computation.2 | async-start | bytes 6291456 | tf_op jit(solution)/shard_map/all_to_all | solution.py:60
  249.8 0.1 reshape.161
  250.0 0.1 copy.27
  250.1 67.5 %all-to-all-done.1 = f32[16,24,2048]{2,1,0:T(8,128)S(1)} async-done(((f32[16,24,2048]{2,1,0:T(8,128)}), f32[16,24,2048]{2,1,0:T(8,128)S(1)}, u32[]{:S(2)}, u32[]{:S(2)}) %all-to-all-start.1) | async-done | bytes 3145760 | tf_op jit(solution)/shard_map/all_to_all | solution.py:60
  317.6 4.5 %gather_fusion = f32[256,2048]{1,0:T(8,128)} fusion(f32[16,24,2048]{2,1,0:T(8,128)S(1)} %all-to-all-done.1, s32[256]{0:T(256)S(1)} %reshape.161), kind=kCustom, calls=%fused_computation | custom fusion | bytes 4196352 | tf_op jit(solution)/shard_map/gather | solution.py:25
  322.0 2.5 reshape.164
  324.5 3.9 %multiply_reduce_fusion = bf16[128,2048]{1,0:T(8,128)(2,1)} fusion(f32[128,2,2048]{2,1,0:T(2,128)S(1)} %reshape.164, f32[128,2]{1,0:T(8,128)S(1)} %copy.27), kind=kLoop, calls=%fused_computation.10 | loop fusion | flops 786432 | bytes 2622464 | tf_op jit(solution)/shard_map/reduce_sum | solution.py:26
  (23 shorter events, 0.5 us)
Async XLA Ops:
  6.5 236.8 %reduce-scatter.2.cloned.1.call-start = ((), (), s32[]{:S(2)}) async-start(), calls=%async_computation.3 | async-start | bytes 9437184 | tf_op jit(solution)/shard_map/reduce_scatter | solution.py:59
  64.5 86.4 %slice-start = ((s8[14680064]{0:T(1024)(128)(4,1)}), s8[4194304]{0:T(1024)(128)(4,1)S(1)}, s32[]{:S(2)}) async-start(s8[14680064]{0:T(1024)(128)(4,1)} %bitcast.51), calls=%async_computation.4 | async-start | bytes 8388608
  141.5 9.4 %slice-start.1 = ((s8[14680064]{0:T(1024)(128)(4,1)}), s8[4194304]{0:T(1024)(128)(4,1)S(1)}, s32[]{:S(2)}) async-start(s8[14680064]{0:T(1024)(128)(4,1)} %bitcast.51), calls=%async_computation.5 | async-start | bytes 8388608
  141.5 9.4 %slice-start.2 = ((s8[14680064]{0:T(1024)(128)(4,1)}), s8[4194304]{0:T(1024)(128)(4,1)S(1)}, s32[]{:S(2)}) async-start(s8[14680064]{0:T(1024)(128)(4,1)} %bitcast.51), calls=%async_computation.6 | async-start | bytes 8388608
  141.5 9.4 %slice-start.3 = ((s8[14680064]{0:T(1024)(128)(4,1)}), s8[2097152]{0:T(1024)(128)(4,1)S(1)}, s32[]{:S(2)}) async-start(s8[14680064]{0:T(1024)(128)(4,1)} %bitcast.51), calls=%async_computation.7 | async-start | bytes 4194304
  167.9 82.1 %copy-start = (f32[128,2]{0,1:T(2,128)S(1)}, f32[128,2]{0,1:T(2,128)}, u32[]{:S(2)}) copy-start(f32[128,2]{0,1:T(2,128)} %param.8) | copy-start | bytes 3076
  243.3 74.2 %all-to-all-start.1 = ((f32[16,24,2048]{2,1,0:T(8,128)}), f32[16,24,2048]{2,1,0:T(8,128)S(1)}, u32[]{:S(2)}, u32[]{:S(2)}) async-start(f32[16,24,2048]{2,1,0:T(8,128)} %reduce-scatter.2.cloned.1.call-done), calls=%async_computation.2 | async-start | bytes 6291456 | tf_op jit(solution)/shard_map/all_to_all | solution.py:60
Sparse Core Ops, SparseCore 0:
  168.0 75.3 reduce-scatter.1
where the time goes:
time: 339 us; the launch traced here: 335 us
  waiting for transfers between devices  143 us (42%)
  blocking collectives  77 us (23%)
  local copies, waits for them, and re-layouts  63.9 us (19%)
  matrix products  26.2 us (8%)
  between operations  13.6 us (4%)
  starting transfers between devices  6.39 us (2%)
  other arithmetic  5.34 us (2%)
    all_to_all x1, blocking collectives, on_device(): lax.all_to_all(outgoing, 'expert', split_axis=0, concat_axis=0, tiled=True)  77 us
    reduce_scatter x1, waiting for transfers between devices, on_device(): lax.psum_scatter(partial_value, 'tensor', scatter_dimension=2, tiled=True)  75.5 us
    all_to_all x1, waiting for transfers between devices, on_device(): lax.all_to_all(owned, 'expert', split_axis=0, concat_axis=0, tiled=True)  67.5 us
    scatter x1, local copies, waits for them, and re-layouts, on_device(): outgoing = jnp.zeros((experts, blocks * CAP, tokens.shape[1]), jnp.bfloat...  48.9 us
    dot_general x1, matrix products, on_device(): jnp.dot(hidden, lax.all_gather(w_down, 'dp', axis=2, tiled=True)[0], pref...  10.8 us
    dot_general x1, matrix products, on_device(): jnp.dot(routed, lax.all_gather(w_gate, 'dp', axis=1, tiled=True)[0], pref...  9.34 us
    gather x2, local copies, waits for them, and re-layouts, weigh_back(): picked = returned[expert_ids, place]  6.97 us
  transfers between devices with their start and end apart: 2, of which 2 were waited for; matrix products, arithmetic and copies ran while one was open for 0% of the time, Pallas kernels for 0%

commit v1 on v0

v1 whole, which is shorter than its diff:
```python
import jax
import jax.numpy as jnp
from jax import lax
from jax.sharding import PartitionSpec as P

BLOCK = 128
CAP = 24
CHUNKS = 2


def selectors(expert_ids, gate_probs, experts):
    rows = expert_ids.shape[0]
    blocks = rows // BLOCK
    match = expert_ids[:, :, None] == jnp.arange(experts, dtype=jnp.int32)
    named = jnp.any(match, axis=1)
    weight = jnp.sum(jnp.where(match, gate_probs[:, :, None], 0.0), axis=1)
    named = named.reshape(blocks, BLOCK, experts)
    weight = weight.reshape(blocks, BLOCK, experts)
    earlier = jnp.tril(jnp.ones((BLOCK, BLOCK), jnp.bfloat16), -1)
    before = jnp.einsum(
        "rs,bse->bre",
        earlier,
        named.astype(jnp.bfloat16),
        preferred_element_type=jnp.float32,
    ).astype(jnp.int32)
    slots = jnp.arange(CAP, dtype=jnp.int32)
    hit = named[..., None] & (before[..., None] == slots)
    chosen = hit.astype(jnp.bfloat16)
    high = weight.astype(jnp.bfloat16)
    rest = weight - high.astype(jnp.float32)
    middle = rest.astype(jnp.bfloat16)
    low = (rest - middle.astype(jnp.float32)).astype(jnp.bfloat16)
    weights = [jnp.where(hit, part[..., None], 0) for part in (high, middle, low)]
    return chosen, weights


def gather_over(piece, axis):
    size = lax.axis_size(axis)
    if size == 1:
        return [piece]
    me = lax.axis_index(axis)
    got = [piece]
    for step in range(1, size):
        got.append(
            lax.ppermute(piece, axis, [((i + step) % size, i) for i in range(size)])
        )
    out = []
    for rank in range(size):
        value = got[0]
        for step in range(1, size):
            value = jnp.where((me + step) % size == rank, got[step], value)
        out.append(value)
    return out


def on_device(tokens, expert_ids, gate_probs, w_gate, w_up, w_down):
    rows, width = tokens.shape
    experts = lax.axis_size("expert")
    ranks = lax.axis_size("tensor")
    me = lax.axis_index("tensor")
    blocks = rows // BLOCK
    w_gate = lax.all_gather(w_gate, "dp", axis=1, tiled=True)[0]
    w_up = lax.all_gather(w_up, "dp", axis=1, tiled=True)[0]
    w_down = lax.all_gather(w_down, "dp", axis=2, tiled=True)[0]
    chosen, weights = selectors(expert_ids, gate_probs, experts)

    share = width // ranks
    part = share // CHUNKS
    mine = lax.dynamic_slice_in_dim(tokens, me * share, share, axis=1)
    mine = mine.reshape(blocks, BLOCK, share)
    slots = experts * blocks * CAP
    gate = up = None
    for c in range(CHUNKS):
        outgoing = jnp.einsum(
            "bres,brd->ebsd",
            chosen,
            mine[:, :, c * part : (c + 1) * part],
            preferred_element_type=jnp.float32,
        ).astype(jnp.bfloat16)
        arrived = lax.all_to_all(
            outgoing.reshape(experts, blocks * CAP, part),
            "expert",
            split_axis=0,
            concat_axis=0,
            tiled=True,
        ).reshape(slots, part)
        for rank, piece in enumerate(gather_over(arrived, "tensor")):
            at = rank * share + c * part
            g = jnp.dot(piece, w_gate[at : at + part], preferred_element_type=jnp.float32)
            u = jnp.dot(piece, w_up[at : at + part], preferred_element_type=jnp.float32)
            gate = g if gate is None else gate + g
            up = u if up is None else up + u
    hidden = (jax.nn.silu(gate) * up).astype(jnp.bfloat16)

    outs = []
    for c in range(CHUNKS):
        terms = []
        for rank in range(ranks):
            at = rank * share + c * part
            terms.append(
                jnp.dot(hidden, w_down[:, at : at + part], preferred_element_type=jnp.float32)
            )
        stacked = jnp.stack(terms)
        owned = lax.dynamic_index_in_dim(stacked, me, 0, keepdims=False)
        for step in range(1, ranks):
            sent = lax.dynamic_index_in_dim(
                stacked, (me + step) % ranks, 0, keepdims=False
            ).astype(jnp.bfloat16)
            got = lax.ppermute(sent, "tensor", [(i, (i + step) % ranks) for i in range(ranks)])
            owned = owned + got.astype(jnp.float32)
        returned = lax.all_to_all(
            owned.astype(jnp.bfloat16).reshape(experts, blocks * CAP, part),
            "expert",
            split_axis=0,
            concat_axis=0,
            tiled=True,
        ).reshape(experts, blocks, CAP, part)
        mixed = sum(
            jnp.einsum("bres,ebsd->brd", w, returned, preferred_element_type=jnp.float32)
            for w in weights
        )
        outs.append(mixed.reshape(rows, part).astype(jnp.bfloat16))
    return jnp.concatenate(outs, axis=1)


def solution(mesh):
    placed = (
        P(("groups", "dp", "expert"), None),
        P(("groups", "dp", "expert"), None),
        P(("groups", "dp", "expert"), None),
        P("expert", "dp", "tensor"),
        P("expert", "dp", "tensor"),
        P("expert", "tensor", "dp"),
    )
    return jax.shard_map(
        on_device,
        mesh=mesh,
        in_specs=placed,
        out_specs=P(("groups", "dp", "expert"), "tensor"),
        check_vma=False,
    )
```

time: 339 us -> 178 us (0.53)
  blocking collectives: 77 us -> 0 us
  local copies, waits for them, and re-layouts: 63.9 us -> 1.79 us
  waiting for transfers between devices: 143 us -> 90.8 us
  matrix products: 26.2 us -> 50.9 us
  starting transfers between devices: 6.39 us -> 24.6 us
  between operations: 13.6 us -> 0.3 us
  other arithmetic: 5.34 us -> 8.96 us
    all_to_all x1 -> x0, blocking collectives: 77 us -> none  [on_device(): lax.all_to_all(outgoing, 'expert', split_axis=0, concat_axis=0, tiled=True)]
    reduce_scatter x1 -> x0, waiting for transfers between devices: 75.5 us -> none  [on_device(): lax.psum_scatter(partial_value, 'tensor', scatter_dimension=2, tiled=True)]
    scatter x1 -> x0, local copies, waits for them, and re-layouts: 48.9 us -> none  [on_device(): outgoing = jnp.zeros((experts, blocks * CAP, tokens.shape[1]), jnp.bfloat...]
    ppermute x0 -> x4, waiting for transfers between devices: none -> 35.3 us  [the longest x2 33 us: on_device(): lax.ppermute(sent, 'tensor', [(i, (i + step) % ranks) for i in range(rank...]
    dot_general x3 -> x19, matrix products: 26.2 us -> 50.2 us  [the longest x4 20.3 us: on_device(): u = jnp.dot(piece, w_up[at:at + part], preferred_element_type=jnp.float32)]
    all_to_all x1 -> x4, starting transfers between devices: 6.39 us -> 23.5 us  [the longest x2 12.3 us: on_device(): lax.all_to_all(owned.astype(jnp.bfloat16).reshape(experts, blocks * CAP,...]
    all_to_all x1 -> x4, waiting for transfers between devices: 67.5 us -> 55.5 us  [the longest x2 37.5 us: on_device(): lax.all_to_all(outgoing.reshape(experts, blocks * CAP, part), 'expert', s...]
    gather x2 -> x0, local copies, waits for them, and re-layouts: 6.97 us -> none  [weigh_back(): picked = returned[expert_ids, place]]
  transfers between devices with their start and end apart: 2 -> 8, of which waited for: 2 -> 6; matrix products, arithmetic and copies ran while one was open for 0% -> 17% of each run, Pallas kernels for 0% -> 0%
where the time goes in v1:
time: 178 us; the launch traced here: 177 us
  waiting for transfers between devices  90.8 us (51%)
  matrix products  50.9 us (29%)
  starting transfers between devices  24.6 us (14%)
  other arithmetic  8.96 us (5%)
  local copies, waits for them, and re-layouts  1.79 us (1%)
    all_to_all x2, waiting for transfers between devices, on_device(): lax.all_to_all(outgoing.reshape(experts, blocks * CAP, part), 'expert', s...  37.5 us
    ppermute x2, waiting for transfers between devices, on_device(): lax.ppermute(sent, 'tensor', [(i, (i + step) % ranks) for i in range(rank...  33 us
    dot_general x4, matrix products, on_device(): u = jnp.dot(piece, w_up[at:at + part], preferred_element_type=jnp.float32)  20.3 us
    all_to_all x2, waiting for transfers between devices, on_device(): lax.all_to_all(owned.astype(jnp.bfloat16).reshape(experts, blocks * CAP,...  18 us
    dot_general x4, matrix products, on_device(): jnp.dot(hidden, w_down[:, at:at + part], preferred_element_type=jnp.float32)  16.1 us
    all_to_all x2, starting transfers between devices, on_device(): lax.all_to_all(owned.astype(jnp.bfloat16).reshape(experts, blocks * CAP,...  12.3 us
    all_to_all x2, starting transfers between devices, on_device(): lax.all_to_all(outgoing.reshape(experts, blocks * CAP, part), 'expert', s...  11.2 us
    dot_general x4, matrix products, on_device(): g = jnp.dot(piece, w_gate[at:at + part], preferred_element_type=jnp.float32)  10.9 us
  transfers between devices with their start and end apart: 8, of which 6 were waited for; matrix products, arithmetic and copies ran while one was open for 17% of the time, Pallas kernels for 0%

profile of v1, /device:TPU:11, one launch (start us, length us, event | category | flops | bytes accessed | tf_op | source)
XLA Modules:
  0.0 177.4 jit_solution(13852309249067110418)
XLA Ops:
  2.7 6.6 %all-to-all-start.1 = ((bf16[16,24,1024]{2,1,0:T(8,128)(2,1)}), bf16[16,24,1024]{2,1,0:T(8,128)(2,1)S(1)}, u32[]{:S(2)}, u32[]{:S(2)}) async-start(bf16[16,24,1024]{2,1,0:T(8,128)(2,1)} %convert_bitcast_fusion), calls=%async_computation.1 | async-start | bytes 1572864 | tf_op jit(solution)/shard_map/all_to_all | solution.py:80
  10.7 18.2 %all-to-all-done.1 = bf16[16,24,1024]{2,1,0:T(8,128)(2,1)S(1)} async-done(((bf16[16,24,1024]{2,1,0:T(8,128)(2,1)}), bf16[16,24,1024]{2,1,0:T(8,128)(2,1)S(1)}, u32[]{:S(2)}, u32[]{:S(2)}) %all-to-all-start.1) | async-done | bytes 786464 | tf_op jit(solution)/shard_map/all_to_all | solution.py:80
  28.8 4.6 %all-to-all-start = ((bf16[16,24,1024]{2,1,0:T(8,128)(2,1)}), bf16[16,24,1024]{2,1,0:T(8,128)(2,1)S(1)}, u32[]{:S(2)}, u32[]{:S(2)}) async-start(bf16[16,24,1024]{2,1,0:T(8,128)(2,1)} %convert_bitcast_fusion.1), calls=%async_computation | async-start | bytes 1572864 | tf_op jit(solution)/shard_map/all_to_all | solution.py:80
  33.7 19.3 %all-to-all-done = bf16[16,24,1024]{2,1,0:T(8,128)(2,1)S(1)} async-done(((bf16[16,24,1024]{2,1,0:T(8,128)(2,1)}), bf16[16,24,1024]{2,1,0:T(8,128)(2,1)S(1)}, u32[]{:S(2)}, u32[]{:S(2)}) %all-to-all-start) | async-done | bytes 786464 | tf_op jit(solution)/shard_map/all_to_all | solution.py:80
  53.3 3.7 %fusion.16 = f32[384,1792]{1,0:T(8,128)S(1)} fusion(bf16[1,4096,1792]{2,1,0:T(8,128)(2,1)} %param.9, bf16[384,1024]{1,0:T(8,128)(2,1)S(1)} %collective-permute-done.1, bf16[384,1024]{1,0:T(8,128)(2,1)S(1)} %bitcast.145, pred[]{:T(512)S(6)} %eq.64), kind=kOutput, calls=%fused_computation.24 | convolution fusion | flops 1409679360 | bytes 7995393 | tf_op jit(solution)/shard_map/dot_general | solution.py:89
  57.0 3.8 %fusion.18 = f32[384,1792]{1,0:T(8,128)S(1)} fusion(bf16[1,4096,1792]{2,1,0:T(8,128)(2,1)} %param.9, bf16[384,1024]{1,0:T(8,128)(2,1)S(1)} %collective-permute-done.1, bf16[384,1024]{1,0:T(8,128)(2,1)S(1)} %bitcast.146, pred[]{:T(512)S(6)} %eq.63), kind=kOutput, calls=%fused_computation.26 | convolution fusion | flops 1409679360 | bytes 7995393 | tf_op jit(solution)/shard_map/dot_general | solution.py:89
  60.8 3.8 %fusion.8 = f32[384,1792]{1,0:T(8,128)S(1)} fusion(bf16[1,4096,1792]{2,1,0:T(8,128)(2,1)} %param.10, bf16[384,1024]{1,0:T(8,128)(2,1)S(1)} %collective-permute-done.1, bf16[384,1024]{1,0:T(8,128)(2,1)S(1)} %bitcast.147, pred[]{:T(512)S(6)} %eq.64), kind=kOutput, calls=%fused_computation.16 | convolution fusion | flops 1409679360 | bytes 7995393 | tf_op jit(solution)/shard_map/dot_general | solution.py:90
  64.7 5.4 %fusion.10 = f32[384,1792]{1,0:T(8,128)} fusion(bf16[1,4096,1792]{2,1,0:T(8,128)(2,1)} %param.10, bf16[384,1024]{1,0:T(8,128)(2,1)S(1)} %collective-permute-done.1, bf16[384,1024]{1,0:T(8,128)(2,1)S(1)} %bitcast.148, pred[]{:T(512)S(6)} %eq.63), kind=kOutput, calls=%fused_computation.18 | convolution fusion | flops 1409679360 | bytes 7995393 | tf_op jit(solution)/shard_map/dot_general | solution.py:90
  70.1 2.3 %collective-permute-done = bf16[384,1024]{1,0:T(8,128)(2,1)S(1)} collective-permute-done((bf16[384,1024]{1,0:T(8,128)(2,1)S(1)}, bf16[384,1024]{1,0:T(8,128)(2,1)S(1)}, u32[]{:S(2)}, u32[]{:S(2)}) %collective-permute-start) | collective-permute-done | bytes 786464 | tf_op jit(solution)/shard_map/ppermute | solution.py:45
  72.4 1.7 fusion.20
  74.1 5.3 %fusion.12 = f32[384,1792]{1,0:T(8,128)} fusion(bf16[1,4096,1792]{2,1,0:T(8,128)(2,1)} %param.10, bf16[384,1024]{1,0:T(8,128)(2,1)S(1)} %collective-permute-done, bf16[384,1024]{1,0:T(8,128)(2,1)S(1)} %bitcast.138, pred[]{:T(512)S(6)} %eq.64), kind=kOutput, calls=%fused_computation.20 | convolution fusion | flops 1409679360 | bytes 7995393 | tf_op jit(solution)/shard_map/dot_general | solution.py:90
  79.3 1.7 fusion.47
  81.0 5.8 %multiply_convert_fusion = bf16[384,1792]{1,0:T(8,128)(2,1)S(1)} fusion(f32[384,1792]{1,0:T(8,128)S(1)} %fusion.47, f32[384,1792]{1,0:T(8,128)S(1)} %fusion.8, f32[384,1792]{1,0:T(8,128)} %fusion.10, f32[384,1792]{1,0:T(8,128)} %fusion.12, bf16[1,4096,1792]{2,1,0:T(8,128)(2,1)} %param.10, bf16[384,1024]{1,0:T(8,128)(2,1)S(1)} %collective-permute-done, ...), kind=kOutput, calls=%fused_computation.46 | convolution fusion | flops 1415872512 | bytes 17629184 | tf_op jit(solution)/shard_map/dot_general | solution.py:90
  86.8 4.1 %fusion.68 = f32[1,384,1024]{2,1,0:T(8,128)S(1)} fusion(bf16[384,1792]{1,0:T(8,128)(2,1)S(1)} %multiply_convert_fusion, bf16[1792,4096]{1,0:T(8,128)(2,1)} %bitcast.151), kind=kOutput, calls=%fused_computation.61 | convolution fusion | flops 1409286144 | bytes 6619136 | tf_op jit(solution)/shard_map/dot_general | solution.py:101
  91.0 3.8 %fusion.71 = f32[1,384,1024]{2,1,0:T(8,128)S(1)} fusion(bf16[384,1792]{1,0:T(8,128)(2,1)S(1)} %multiply_convert_fusion, bf16[1792,4096]{1,0:T(8,128)(2,1)} %bitcast.152), kind=kOutput, calls=%fused_computation.62 | convolution fusion | flops 1409286144 | bytes 6619136 | tf_op jit(solution)/shard_map/dot_general | solution.py:101
  97.3 4.2 %fusion.62 = f32[1,384,1024]{2,1,0:T(8,128)S(1)} fusion(bf16[384,1792]{1,0:T(8,128)(2,1)} %copy-done.7, bf16[1792,4096]{1,0:T(8,128)(2,1)} %bitcast.153), kind=kOutput, calls=%fused_computation.59 | convolution fusion | flops 1409286144 | bytes 6619136 | tf_op jit(solution)/shard_map/dot_general | solution.py:101
  101.4 14.4 %collective-permute-done.3 = bf16[384,1024]{1,0:T(8,128)(2,1)} collective-permute-done((bf16[384,1024]{1,0:T(8,128)(2,1)}, bf16[384,1024]{1,0:T(8,128)(2,1)}, u32[]{:S(2)}, u32[]{:S(2)}) %collective-permute-start.3) | collective-permute-done | bytes 786464 | tf_op jit(solution)/shard_map/ppermute | solution.py:109
  115.9 2.5 %fusion.55 = bf16[384,1024]{1,0:T(8,128)(2,1)} fusion(s32[]{:T(128)S(6)} %select_n.92, f32[1,384,1024]{2,1,0:T(8,128)S(1)} %fusion.68, f32[1,384,1024]{2,1,0:T(8,128)S(1)} %copy-done.3, bf16[384,1024]{1,0:T(8,128)(2,1)} %collective-permute-done.3), kind=kLoop, calls=%fused_computation.52 | loop fusion | flops 1572864 | bytes 4718596 | tf_op jit(solution)/shard_map/convert_element_type | solution.py:112
  118.4 5.5 %all-to-all-start.3 = ((bf16[16,24,1024]{2,1,0:T(8,128)(2,1)}), bf16[16,24,1024]{2,1,0:T(8,128)(2,1)S(1)}, u32[]{:S(2)}, u32[]{:S(2)}) async-start(bf16[16,24,1024]{2,1,0:T(8,128)(2,1)} %bitcast.141), calls=%async_computation.3 | async-start | bytes 1572864 | tf_op jit(solution)/shard_map/all_to_all | solution.py:111
  123.8 4.0 %fusion.65 = f32[1,384,1024]{2,1,0:T(8,128)S(1)} fusion(bf16[384,1792]{1,0:T(8,128)(2,1)} %copy-done.7, bf16[1792,4096]{1,0:T(8,128)(2,1)} %bitcast.154), kind=kOutput, calls=%fused_computation.60 | convolution fusion | flops 1409286144 | bytes 6619136 | tf_op jit(solution)/shard_map/dot_general | solution.py:101
  128.4 18.6 %collective-permute-done.2 = bf16[384,1024]{1,0:T(8,128)(2,1)S(1)} collective-permute-done((bf16[384,1024]{1,0:T(8,128)(2,1)S(1)}, bf16[384,1024]{1,0:T(8,128)(2,1)S(1)}, u32[]{:S(2)}, u32[]{:S(2)}) %collective-permute-start.2) | collective-permute-done | bytes 786464 | tf_op jit(solution)/shard_map/ppermute | solution.py:109
  147.0 1.4 fusion.61
  148.4 6.8 %all-to-all-start.2 = ((bf16[16,24,1024]{2,1,0:T(8,128)(2,1)}), bf16[16,24,1024]{2,1,0:T(8,128)(2,1)S(1)}, u32[]{:S(2)}, u32[]{:S(2)}) async-start(bf16[16,24,1024]{2,1,0:T(8,128)(2,1)} %bitcast.31), calls=%async_computation.2 | async-start | bytes 1572864 | tf_op jit(solution)/shard_map/all_to_all | solution.py:111
  156.7 18.0 %all-to-all-done.2 = bf16[16,24,1024]{2,1,0:T(8,128)(2,1)S(1)} async-done(((bf16[16,24,1024]{2,1,0:T(8,128)(2,1)}), bf16[16,24,1024]{2,1,0:T(8,128)(2,1)S(1)}, u32[]{:S(2)}, u32[]{:S(2)}) %all-to-all-start.2) | async-done | bytes 786464 | tf_op jit(solution)/shard_map/all_to_all | solution.py:111
  (51 shorter events, 11.6 us)
Async XLA Ops:
  0.0 1.2 copy-start
  2.7 26.2 %all-to-all-start.1 = ((bf16[16,24,1024]{2,1,0:T(8,128)(2,1)}), bf16[16,24,1024]{2,1,0:T(8,128)(2,1)S(1)}, u32[]{:S(2)}, u32[]{:S(2)}) async-start(bf16[16,24,1024]{2,1,0:T(8,128)(2,1)} %convert_bitcast_fusion), calls=%async_computation.1 | async-start | bytes 1572864 | tf_op jit(solution)/shard_map/all_to_all | solution.py:80
  28.8 24.2 %all-to-all-start = ((bf16[16,24,1024]{2,1,0:T(8,128)(2,1)}), bf16[16,24,1024]{2,1,0:T(8,128)(2,1)S(1)}, u32[]{:S(2)}, u32[]{:S(2)}) async-start(bf16[16,24,1024]{2,1,0:T(8,128)(2,1)} %convert_bitcast_fusion.1), calls=%async_computation | async-start | bytes 1572864 | tf_op jit(solution)/shard_map/all_to_all | solution.py:80
  33.5 19.8 %collective-permute-start.1 = (bf16[384,1024]{1,0:T(8,128)(2,1)S(1)}, bf16[384,1024]{1,0:T(8,128)(2,1)S(1)}, u32[]{:S(2)}, u32[]{:S(2)}) collective-permute-start(bf16[384,1024]{1,0:T(8,128)(2,1)S(1)} %bitcast.144), channel_id=1, source_target_pairs={{1,0},{0,1},{3,2},{2,3},{5,4},{4,5},{7,6},{6,7},{9,8},{8,9},{11,10... | collective-permute-start | bytes 2359304 | tf_op jit(solution)/shard_map/ppermute | solution.py:45
  53.0 19.4 %collective-permute-start = (bf16[384,1024]{1,0:T(8,128)(2,1)S(1)}, bf16[384,1024]{1,0:T(8,128)(2,1)S(1)}, u32[]{:S(2)}, u32[]{:S(2)}) collective-permute-start(bf16[384,1024]{1,0:T(8,128)(2,1)S(1)} %bitcast.136), channel_id=1, source_target_pairs={{1,0},{0,1},{3,2},{2,3},{5,4},{4,5},{7,6},{6,7},{9,8},{8,9},{11,10... | collective-permute-start | bytes 2359304 | tf_op jit(solution)/shard_map/ppermute | solution.py:45
  57.0 15.4 %slice-start = ((s8[14680064]{0:T(1024)(128)(4,1)}), s8[4194304]{0:T(1024)(128)(4,1)S(1)}, s32[]{:S(2)}) async-start(s8[14680064]{0:T(1024)(128)(4,1)} %bitcast.142), calls=%async_computation.4 | async-start | bytes 8388608
  57.0 15.4 %slice-start.1 = ((s8[14680064]{0:T(1024)(128)(4,1)}), s8[4194304]{0:T(1024)(128)(4,1)S(1)}, s32[]{:S(2)}) async-start(s8[14680064]{0:T(1024)(128)(4,1)} %bitcast.142), calls=%async_computation.5 | async-start | bytes 8388608
  60.8 11.6 %slice-start.2 = ((s8[14680064]{0:T(1024)(128)(4,1)}), s8[4194304]{0:T(1024)(128)(4,1)S(1)}, s32[]{:S(2)}) async-start(s8[14680064]{0:T(1024)(128)(4,1)} %bitcast.142), calls=%async_computation.6 | async-start | bytes 8388608
  64.7 7.7 %slice-start.3 = ((s8[14680064]{0:T(1024)(128)(4,1)}), s8[2097152]{0:T(1024)(128)(4,1)S(1)}, s32[]{:S(2)}) async-start(s8[14680064]{0:T(1024)(128)(4,1)} %bitcast.142), calls=%async_computation.7 | async-start | bytes 4194304
  86.8 4.1 %copy-start.7 = (bf16[384,1792]{1,0:T(8,128)(2,1)}, bf16[384,1792]{1,0:T(8,128)(2,1)S(1)}, u32[]{:S(2)}) copy-start(bf16[384,1792]{1,0:T(8,128)(2,1)S(1)} %multiply_convert_fusion) | copy-start | bytes 4128772
  94.8 1.2 copy-start.2
  97.0 18.8 %collective-permute-start.3 = (bf16[384,1024]{1,0:T(8,128)(2,1)}, bf16[384,1024]{1,0:T(8,128)(2,1)}, u32[]{:S(2)}, u32[]{:S(2)}) collective-permute-start(bf16[384,1024]{1,0:T(8,128)(2,1)} %fusion.82), channel_id=1, source_target_pairs={{0,1},{1,0},{2,3},{3,2},{4,5},{5,4},{6,7},{7,6},{8,9},{9,8},{10,11... | collective-permute-start | bytes 2359304 | tf_op jit(solution)/shard_map/ppermute | solution.py:109
  97.3 18.6 %copy-start.3 = (f32[1,384,1024]{2,1,0:T(8,128)S(1)}, f32[1,384,1024]{2,1,0:T(8,128)}, u32[]{:S(2)}) copy-start(f32[1,384,1024]{2,1,0:T(8,128)} %copy-done.2) | copy-start | bytes 4718596
  118.4 30.0 %all-to-all-start.3 = ((bf16[16,24,1024]{2,1,0:T(8,128)(2,1)}), bf16[16,24,1024]{2,1,0:T(8,128)(2,1)S(1)}, u32[]{:S(2)}, u32[]{:S(2)}) async-start(bf16[16,24,1024]{2,1,0:T(8,128)(2,1)} %bitcast.141), calls=%async_computation.3 | async-start | bytes 1572864 | tf_op jit(solution)/shard_map/all_to_all | solution.py:111
  128.1 27.1 %copy-start.5 = (s32[128,2]{0,1:T(2,128)S(1)}, s32[128,2]{0,1:T(2,128)}, u32[]{:S(2)}) copy-start(s32[128,2]{0,1:T(2,128)} %param.7) | copy-start | bytes 3076
  128.1 27.1 %copy-start.6 = (f32[128,2]{0,1:T(2,128)S(1)}, f32[128,2]{0,1:T(2,128)}, u32[]{:S(2)}) copy-start(f32[128,2]{0,1:T(2,128)} %param.8) | copy-start | bytes 3076
  128.1 18.8 %collective-permute-start.2 = (bf16[384,1024]{1,0:T(8,128)(2,1)S(1)}, bf16[384,1024]{1,0:T(8,128)(2,1)S(1)}, u32[]{:S(2)}, u32[]{:S(2)}) collective-permute-start(bf16[384,1024]{1,0:T(8,128)(2,1)S(1)} %fusion.81), channel_id=1, source_target_pairs={{0,1},{1,0},{2,3},{3,2},{4,5},{5,4},{6,7},{7,6},{8,9},{9,8},{10,11... | collective-permute-start | bytes 2359304 | tf_op jit(solution)/shard_map/ppermute | solution.py:109
  148.4 26.4 %all-to-all-start.2 = ((bf16[16,24,1024]{2,1,0:T(8,128)(2,1)}), bf16[16,24,1024]{2,1,0:T(8,128)(2,1)S(1)}, u32[]{:S(2)}, u32[]{:S(2)}) async-start(bf16[16,24,1024]{2,1,0:T(8,128)(2,1)} %bitcast.31), calls=%async_computation.2 | async-start | bytes 1572864 | tf_op jit(solution)/shard_map/all_to_all | solution.py:111
  174.8 1.0 copy-start.4
  175.1 2.2 %copy-start.1 = (bf16[128,4096]{1,0:T(8,128)(2,1)S(1)}, bf16[128,4096]{1,0:T(8,128)(2,1)}, u32[]{:S(2)}) copy-start(bf16[128,4096]{1,0:T(8,128)(2,1)} %param.6) | copy-start | bytes 3145732

commit v2 on v0

v2 whole, which is shorter than its diff:
```python
import jax
import jax.numpy as jnp
from jax import lax
from jax.experimental import pallas as pl
from jax.experimental.pallas import tpu as pltpu
from jax.sharding import PartitionSpec as P

BLOCK = 128
CAP = 24
LANES = 256
VMEM_BYTES = 40 * 1024 * 1024


def tile_of(width):
    return LANES if width % LANES == 0 else 128


def lift_kernel(count, has_sums, last, *refs):
    refs = list(refs[1:])
    pieces, refs = refs[:count], refs[count:]
    gates, refs = refs[:count], refs[count:]
    ups, refs = refs[:count], refs[count:]
    gate = up = None
    if has_sums:
        gate, up = refs[0][...], refs[1][...]
        refs = refs[2:]
    for x, g, u in zip(pieces, gates, ups):
        more_gate = jnp.dot(x[...], g[...], preferred_element_type=jnp.float32)
        more_up = jnp.dot(x[...], u[...], preferred_element_type=jnp.float32)
        gate = more_gate if gate is None else gate + more_gate
        up = more_up if up is None else up + more_up
    if last:
        refs[0][...] = (gate / (1.0 + jnp.exp(-gate)) * up).astype(jnp.bfloat16)
    else:
        refs[0][...] = gate
        refs[1][...] = up


def lift(pieces, starts, w_gate, w_up, sums=None, last=False):
    rows = pieces[0].shape[0]
    hidden = w_gate.shape[1]
    tile = tile_of(hidden)
    count = len(pieces)

    def weight_spec(i):
        return pl.BlockSpec(
            (pl.Element(pieces[i].shape[1]), pl.Element(tile)),
            lambda n, at: (pl.multiple_of(at[i], 128), n * tile),
        )

    across = pl.BlockSpec((rows, tile), lambda n, at: (0, n))
    in_specs = [pl.BlockSpec(p.shape, lambda n, at: (0, 0)) for p in pieces]
    in_specs += [weight_spec(i) for i in range(count)] * 2
    args = list(pieces) + [w_gate] * count + [w_up] * count
    if sums is not None:
        in_specs += [across, across]
        args += list(sums)
    if last:
        out_shape = jax.ShapeDtypeStruct((rows, hidden), jnp.bfloat16)
        out_specs = across
    else:
        out_shape = [jax.ShapeDtypeStruct((rows, hidden), jnp.float32)] * 2
        out_specs = [across, across]
    depth = sum(p.shape[1] for p in pieces)
    return pl.pallas_call(
        lambda *refs: lift_kernel(count, sums is not None, last, *refs),
        out_shape=out_shape,
        grid_spec=pltpu.PrefetchScalarGridSpec(
            num_scalar_prefetch=1,
            grid=(hidden // tile,),
            in_specs=in_specs,
            out_specs=out_specs,
        ),
        compiler_params=pltpu.CompilerParams(vmem_limit_bytes=VMEM_BYTES),
        cost_estimate=pl.CostEstimate(
            flops=4 * rows * depth * hidden,
            bytes_accessed=4 * depth * hidden + 16 * rows * hidden,
            transcendentals=rows * hidden if last else 0,
        ),
        name="lift",
    )(jnp.stack(starts).astype(jnp.int32), *args)


def drop_kernel(at, hidden, weight, out):
    value = jnp.dot(hidden[...], weight[...], preferred_element_type=jnp.float32)
    out[...] = value.astype(out.dtype)


def drop(hidden, w_down, starts, width, dtype):
    rows, depth = hidden.shape
    tile = tile_of(width)
    tiles = width // tile
    count = len(starts)
    return pl.pallas_call(
        drop_kernel,
        out_shape=jax.ShapeDtypeStruct((rows, count * width), dtype),
        grid_spec=pltpu.PrefetchScalarGridSpec(
            num_scalar_prefetch=1,
            grid=(count, tiles),
            in_specs=[
                pl.BlockSpec((rows, depth), lambda i, j, at: (0, 0)),
                pl.BlockSpec(
                    (pl.Element(depth), pl.Element(tile)),
                    lambda i, j, at: (0, pl.multiple_of(at[i] + j * tile, 128)),
                ),
            ],
            out_specs=pl.BlockSpec((rows, tile), lambda i, j, at: (0, i * tiles + j)),
        ),
        compiler_params=pltpu.CompilerParams(vmem_limit_bytes=VMEM_BYTES),
        cost_estimate=pl.CostEstimate(
            flops=2 * rows * depth * count * width,
            bytes_accessed=2 * depth * count * width + 4 * rows * count * width,
            transcendentals=0,
        ),
        name="drop",
    )(jnp.stack(starts).astype(jnp.int32), hidden, w_down)


def selectors(expert_ids, gate_probs, experts):
    rows = expert_ids.shape[0]
    blocks = rows // BLOCK
    match = expert_ids.T[:, None, :] == jnp.arange(experts, dtype=jnp.int32)[None, :, None]
    named = jnp.any(match, axis=0)
    weight = jnp.sum(jnp.where(match, gate_probs.T[:, None, :], 0.0), axis=0)
    row = jnp.arange(rows, dtype=jnp.int32)
    same = row[:, None] // BLOCK == row[None, :] // BLOCK
    earlier = ((row[:, None] < row[None, :]) & same).astype(jnp.bfloat16)
    before = jnp.dot(named.astype(jnp.bfloat16), earlier, preferred_element_type=jnp.float32)
    place = before.astype(jnp.int32) + (row // BLOCK * CAP)[None, :]
    slots = jnp.arange(blocks * CAP, dtype=jnp.int32)
    hit = named[:, None, :] & (place[:, None, :] == slots[None, :, None])
    high = weight.astype(jnp.bfloat16)
    rest = weight - high.astype(jnp.float32)
    middle = rest.astype(jnp.bfloat16)
    low = (rest - middle.astype(jnp.float32)).astype(jnp.bfloat16)
    flat = (experts * blocks * CAP, rows)
    chosen = hit.astype(jnp.bfloat16).reshape(flat)
    weights = [
        jnp.where(hit, part[:, None, :], 0).astype(jnp.bfloat16).reshape(flat)
        for part in (high, middle, low)
    ]
    return chosen, weights


def swap(value, experts):
    slots, width = value.shape
    return lax.all_to_all(
        value.reshape(experts, slots // experts, width),
        "expert",
        split_axis=0,
        concat_axis=0,
        tiled=True,
    ).reshape(slots, width)


def mix(weights, returned):
    return sum(
        lax.dot_general(
            w, returned, (((0,), (0,)), ((), ())), preferred_element_type=jnp.float32
        )
        for w in weights
    )


def on_device(tokens, expert_ids, gate_probs, w_gate, w_up, w_down):
    width = tokens.shape[1]
    experts = lax.axis_size("expert")
    ranks = lax.axis_size("tensor")
    me = lax.axis_index("tensor")
    w_gate = lax.all_gather(w_gate, "dp", axis=1, tiled=True)[0]
    w_up = lax.all_gather(w_up, "dp", axis=1, tiled=True)[0]
    w_down = lax.all_gather(w_down, "dp", axis=2, tiled=True)[0]
    chosen, weights = selectors(expert_ids, gate_probs, experts)

    def rank_at(step):
        return lax.rem(me + step, ranks)

    def send_up(value, step):
        return lax.ppermute(value, "tensor", [(i, (i + step) % ranks) for i in range(ranks)])

    share = width // ranks
    shared = round(2 * share / 3 / LANES) * LANES
    direct_at = ranks * shared

    def placed(features):
        return jnp.dot(chosen, features, preferred_element_type=jnp.float32).astype(jnp.bfloat16)

    mine = lax.dynamic_slice_in_dim(tokens, me * shared, shared, axis=1)
    own = swap(placed(mine), experts)
    direct = swap(placed(tokens[:, direct_at:]), experts)
    sums = lift([own], [me * shared], w_gate, w_up)
    for step in range(1, ranks):
        other = send_up(own, ranks - step)
        sums = lift([other], [rank_at(step) * shared], w_gate, w_up, sums)
    hidden = lift([direct], [jnp.int32(direct_at)], w_gate, w_up, sums, last=True)

    early = share - shared
    partial = drop(
        hidden, w_down, [jnp.int32(rank * share) for rank in range(ranks)], early, jnp.bfloat16
    )
    returned = swap(partial, experts)
    owned = drop(hidden, w_down, [me * share + early], shared, jnp.float32)
    for step in range(1, ranks):
        sent = drop(hidden, w_down, [rank_at(step) * share + early], shared, jnp.bfloat16)
        owned = owned + send_up(sent, step).astype(jnp.float32)
    first = mix(weights, returned)

    def part_of(rank):
        return lax.dynamic_slice_in_dim(first, rank * early, early, axis=1)

    mixed = part_of(me)
    for step in range(1, ranks):
        mixed = mixed + send_up(part_of(rank_at(step)), step)
    late = mix(weights, swap(owned.astype(jnp.bfloat16), experts))
    return jnp.concatenate([mixed.astype(jnp.bfloat16), late.astype(jnp.bfloat16)], axis=1)


def solution(mesh):
    placed = (
        P(("groups", "dp", "expert"), None),
        P(("groups", "dp", "expert"), None),
        P(("groups", "dp", "expert"), None),
        P("expert", "dp", "tensor"),
        P("expert", "dp", "tensor"),
        P("expert", "tensor", "dp"),
    )
    return jax.shard_map(
        on_device,
        mesh=mesh,
        in_specs=placed,
        out_specs=P(("groups", "dp", "expert"), "tensor"),
        check_vma=False,
    )
```

time: 339 us -> 164 us (0.48)
  blocking collectives: 77 us -> 0 us
  waiting for transfers between devices: 143 us -> 74.9 us
  local copies, waits for them, and re-layouts: 63.9 us -> 6.79 us
  Pallas kernels: 0 us -> 43.3 us
  starting transfers between devices: 6.39 us -> 26.3 us
  matrix products: 26.2 us -> 7.39 us
  between operations: 13.6 us -> 0.15 us
    all_to_all x1 -> x0, blocking collectives: 77 us -> none  [on_device(): lax.all_to_all(outgoing, 'expert', split_axis=0, concat_axis=0, tiled=True)]
    reduce_scatter x1 -> x0, waiting for transfers between devices: 75.5 us -> none  [on_device(): lax.psum_scatter(partial_value, 'tensor', scatter_dimension=2, tiled=True)]
    scatter x1 -> x0, local copies, waits for them, and re-layouts: 48.9 us -> none  [on_device(): outgoing = jnp.zeros((experts, blocks * CAP, tokens.shape[1]), jnp.bfloat...]
    pallas_call x0 -> x6, Pallas kernels: none -> 43.3 us  [the longest x3 25.5 us: lift(): pl.pallas_call(lambda *refs: lift_kernel(count, sums is not None, last, *...]
    ppermute x0 -> x3, waiting for transfers between devices: none -> 42.1 us  [send_up(): lax.ppermute(value, 'tensor', [(i, (i + step) % ranks) for i in range(ran...]
    all_to_all x1 -> x4, waiting for transfers between devices: 67.5 us -> 32.7 us  [swap(): lax.all_to_all(value.reshape(experts, slots // experts, width), 'expert',...]
    all_to_all x1 -> x4, starting transfers between devices: 6.39 us -> 25.3 us  [swap(): lax.all_to_all(value.reshape(experts, slots // experts, width), 'expert',...]
    dot_general x3 -> x9, matrix products: 26.2 us -> 7.39 us  [the longest x2 4.83 us: placed(): jnp.dot(chosen, features, preferred_element_type=jnp.float32)]
  transfers between devices with their start and end apart: 2 -> 7, of which waited for: 2 -> 5; matrix products, arithmetic and copies ran while one was open for 0% -> 4% of each run, Pallas kernels for 0% -> 17%
where the time goes in v2:
time: 164 us; the launch traced here: 163 us
  waiting for transfers between devices  74.9 us (46%)
  Pallas kernels  43.3 us (26%)
  starting transfers between devices  26.3 us (16%)
  matrix products  7.39 us (5%)
  local copies, waits for them, and re-layouts  6.79 us (4%)
  other arithmetic  4.09 us (2%)
    ppermute x3, waiting for transfers between devices, send_up(): lax.ppermute(value, 'tensor', [(i, (i + step) % ranks) for i in range(ran...  42.1 us
    all_to_all x4, waiting for transfers between devices, swap(): lax.all_to_all(value.reshape(experts, slots // experts, width), 'expert',...  32.7 us
    pallas_call x3, Pallas kernels, lift(): pl.pallas_call(lambda *refs: lift_kernel(count, sums is not None, last, *...  25.5 us
    all_to_all x4, starting transfers between devices, swap(): lax.all_to_all(value.reshape(experts, slots // experts, width), 'expert',...  25.3 us
    pallas_call x3, Pallas kernels, drop(): pl.pallas_call(drop_kernel, out_shape=jax.ShapeDtypeStruct((rows, count *...  17.8 us
    unnamed x12, local copies, waits for them, and re-layouts  6.66 us
    dot_general x2, matrix products, placed(): jnp.dot(chosen, features, preferred_element_type=jnp.float32)  4.83 us
  transfers between devices with their start and end apart: 7, of which 5 were waited for; matrix products, arithmetic and copies ran while one was open for 4% of the time, Pallas kernels for 17%

profile of v2, /device:TPU:11, one launch (start us, length us, event | category | flops | bytes accessed | tf_op | source)
XLA Modules:
  0.0 162.8 jit_solution(15541761807063331962)
XLA Ops:
  0.0 0.7 fusion.48
  1.1 2.3 %convolution_convert_fusion = bf16[384,1280]{1,0:T(8,128)(2,1)} fusion(pred[384,128]{1,0:T(32,128)(4,1)S(1)} %fusion.12, bf16[128,4096]{1,0:T(8,128)(2,1)} %param.6, s32[]{:T(128)S(6)} %select_n.52), kind=kOutput, calls=%fused_computation | convolution fusion | flops 126320640 | bytes 1359876 | tf_op jit(solution)/shard_map/dot_general | solution.py:186
  3.5 6.6 %all-to-all-start.1 = ((bf16[16,24,1280]{2,1,0:T(8,128)(2,1)}), bf16[16,24,1280]{2,1,0:T(8,128)(2,1)S(1)}, u32[]{:S(2)}, u32[]{:S(2)}) async-start(bf16[16,24,1280]{2,1,0:T(8,128)(2,1)} %bitcast.9), calls=%async_computation.1 | async-start | bytes 1966080 | tf_op jit(solution)/shard_map/all_to_all | solution.py:147
  10.1 2.5 %convolution_convert_fusion.1 = bf16[384,1536]{1,0:T(8,128)(2,1)} fusion(pred[384,128]{1,0:T(32,128)(4,1)S(1)} %fusion.12, bf16[128,4096]{1,0:T(8,128)(2,1)} %param.6), kind=kOutput, calls=%fused_computation.1 | convolution fusion | flops 151584768 | bytes 1622016 | tf_op jit(solution)/shard_map/dot_general | solution.py:186
  12.6 21.0 %all-to-all-done.1 = bf16[16,24,1280]{2,1,0:T(8,128)(2,1)S(1)} async-done(((bf16[16,24,1280]{2,1,0:T(8,128)(2,1)}), bf16[16,24,1280]{2,1,0:T(8,128)(2,1)S(1)}, u32[]{:S(2)}, u32[]{:S(2)}) %all-to-all-start.1) | async-done | bytes 983072 | tf_op jit(solution)/shard_map/all_to_all | solution.py:147
  33.6 4.9 %all-to-all-start = ((bf16[16,24,1536]{2,1,0:T(8,128)(2,1)}), bf16[16,24,1536]{2,1,0:T(8,128)(2,1)S(1)}, u32[]{:S(2)}, u32[]{:S(2)}) async-start(bf16[16,24,1536]{2,1,0:T(8,128)(2,1)} %bitcast.4), calls=%async_computation | async-start | bytes 2359296 | tf_op jit(solution)/shard_map/all_to_all | solution.py:147
  38.7 8.2 %lift.3 = (f32[384,1792]{1,0:T(8,128)S(1)}, f32[384,1792]{1,0:T(8,128)S(1)}) custom-call(s32[1]{0:T(128)} %bitcast.11.refs_0_, bf16[384,1280]{1,0:T(8,128)(2,1)S(1)} %bitcast.54, bf16[4096,1792]{1,0:T(8,128)(2,1)} %bitcast.55, bf16[4096,1792]{1,0:T(8,128)(2,1)} %bitcast.58), custom_call_target="tpu_custom_call" | custom-call | flops 3523215360 | bytes 20185088 | tf_op jit(solution)/shard_map/lift/pallas_call | solution.py:65
  47.0 14.5 %collective-permute-done.refs_1_ = bf16[384,1280]{1,0:T(8,128)(2,1)S(1)} collective-permute-done((bf16[384,1280]{1,0:T(8,128)(2,1)S(1)}, bf16[384,1280]{1,0:T(8,128)(2,1)S(1)}, u32[]{:S(2)}, u32[]{:S(2)}) %collective-permute-start) | collective-permute-done | bytes 983072 | tf_op jit(solution)/shard_map/ppermute | solution.py:179
  61.5 8.3 %lift.4 = (f32[384,1792]{1,0:T(8,128)S(1)}, f32[384,1792]{1,0:T(8,128)S(1)}) custom-call(s32[1]{0:T(128)} %bitcast.8.refs_0_, bf16[384,1280]{1,0:T(8,128)(2,1)S(1)} %collective-permute-done.refs_1_, bf16[4096,1792]{1,0:T(8,128)(2,1)} %bitcast.56, bf16[4096,1792]{1,0:T(8,128)(2,1)} %bitcast.59, f32[384,1792]{1,0:T(8,128)S(1)} %get-tuple-element.9.refs_4_, ...), custom_call_target="tpu_custom_call" | custom-call | flops 3523215360 | bytes 20185088 | tf_op jit(solution)/shard_map/lift/pallas_call | solution.py:65
  69.8 1.5 copy-done
  71.3 1.6 copy-done.2
  72.9 1.8 %copy-done.1 = f32[384,1792]{1,0:T(8,128)S(1)} copy-done((f32[384,1792]{1,0:T(8,128)S(1)}, f32[384,1792]{1,0:T(8,128)}, u32[]{:S(2)}) %copy-start.1) | copy-done | bytes 2752536
  74.6 1.8 %copy-done.3 = f32[384,1792]{1,0:T(8,128)S(1)} copy-done((f32[384,1792]{1,0:T(8,128)S(1)}, f32[384,1792]{1,0:T(8,128)}, u32[]{:S(2)}) %copy-start.3) | copy-done | bytes 2752536
  76.4 9.0 %lift.5.hidden = bf16[384,1792]{1,0:T(8,128)(2,1)S(1)} custom-call(s32[1]{0:T(128)} %constant.65.clone.1.refs_0_, bf16[384,1536]{1,0:T(8,128)(2,1)S(1)} %bitcast.52, bf16[4096,1792]{1,0:T(8,128)(2,1)} %bitcast.57, bf16[4096,1792]{1,0:T(8,128)(2,1)} %bitcast.60, f32[384,1792]{1,0:T(8,128)S(1)} %copy-done.1, f32[384,1792]{1,0:T(8,128)S(1)} %copy-done.3), custom_call_target="tpu_custom_call" | custom-call | flops 4227858432 | bytes 22020096 | tf_op jit(solution)/shard_map/lift/pallas_call | solution.py:65
  85.4 7.3 %drop.3 = bf16[384,1536]{1,0:T(8,128)(2,1)} custom-call(s32[2]{0:T(128)S(1)} %iota_multiply_fusion.at, bf16[384,1792]{1,0:T(8,128)(2,1)S(1)} %lift.5.hidden, bf16[1792,4096]{1,0:T(8,128)(2,1)} %bitcast.61), custom_call_target="tpu_custom_call" | custom-call | flops 2113929216 | bytes 7864320 | tf_op jit(solution)/shard_map/drop/pallas_call | solution.py:94
  92.8 6.8 %all-to-all-start.2 = ((bf16[16,24,1536]{2,1,0:T(8,128)(2,1)}), bf16[16,24,1536]{2,1,0:T(8,128)(2,1)S(1)}, u32[]{:S(2)}, u32[]{:S(2)}) async-start(bf16[16,24,1536]{2,1,0:T(8,128)(2,1)} %bitcast.13), calls=%async_computation.2 | async-start | bytes 2359296 | tf_op jit(solution)/shard_map/all_to_all | solution.py:147
  99.6 5.2 %drop.5 = bf16[384,1280]{1,0:T(8,128)(2,1)S(1)} custom-call(s32[1]{0:T(128)} %bitcast.18.at, bf16[384,1792]{1,0:T(8,128)(2,1)S(1)} %lift.5.hidden, bf16[1792,4096]{1,0:T(8,128)(2,1)} %bitcast.62), custom_call_target="tpu_custom_call" | custom-call | flops 1761607680 | bytes 6553600 | tf_op jit(solution)/shard_map/drop/pallas_call | solution.py:94
  105.2 5.2 %drop.4 = f32[384,1280]{1,0:T(8,128)S(1)} custom-call(s32[1]{0:T(128)} %bitcast.17.at, bf16[384,1792]{1,0:T(8,128)(2,1)S(1)} %lift.5.hidden, bf16[1792,4096]{1,0:T(8,128)(2,1)} %bitcast.63), custom_call_target="tpu_custom_call" | custom-call | flops 1761607680 | bytes 6553600 | tf_op jit(solution)/shard_map/drop/pallas_call | solution.py:94
  110.4 17.6 %collective-permute-done.2 = bf16[384,1280]{1,0:T(8,128)(2,1)} collective-permute-done((bf16[384,1280]{1,0:T(8,128)(2,1)S(1)}, bf16[384,1280]{1,0:T(8,128)(2,1)}, u32[]{:S(2)}, u32[]{:S(2)}) %collective-permute-start.2) | collective-permute-done | bytes 983072 | tf_op jit(solution)/shard_map/ppermute | solution.py:179
  128.0 2.3 %add_convert_fusion = bf16[384,1280]{1,0:T(8,128)(2,1)} fusion(f32[384,1280]{1,0:T(8,128)S(1)} %drop.4, bf16[384,1280]{1,0:T(8,128)(2,1)} %collective-permute-done.2), kind=kLoop, calls=%fused_computation.13 | loop fusion | flops 1474560 | bytes 3932160 | tf_op jit(solution)/shard_map/convert_element_type | solution.py:214
  130.3 7.0 %all-to-all-start.3 = ((bf16[16,24,1280]{2,1,0:T(8,128)(2,1)}), bf16[16,24,1280]{2,1,0:T(8,128)(2,1)S(1)}, u32[]{:S(2)}, u32[]{:S(2)}) async-start(bf16[16,24,1280]{2,1,0:T(8,128)(2,1)} %bitcast.19), calls=%async_computation.3 | async-start | bytes 1966080 | tf_op jit(solution)/shard_map/all_to_all | solution.py:147
  139.0 10.1 %collective-permute-done.1 = f32[128,768]{1,0:T(8,128)S(1)} collective-permute-done((f32[128,768]{1,0:T(8,128)S(1)}, f32[128,768]{1,0:T(8,128)S(1)}, u32[]{:S(2)}, u32[]{:S(2)}) %collective-permute-start.1) | collective-permute-done | bytes 393248 | tf_op jit(solution)/shard_map/ppermute | solution.py:179
  149.1 11.7 %all-to-all-done.3 = bf16[16,24,1280]{2,1,0:T(8,128)(2,1)S(1)} async-done(((bf16[16,24,1280]{2,1,0:T(8,128)(2,1)}), bf16[16,24,1280]{2,1,0:T(8,128)(2,1)S(1)}, u32[]{:S(2)}, u32[]{:S(2)}) %all-to-all-start.3) | async-done | bytes 983072 | tf_op jit(solution)/shard_map/all_to_all | solution.py:147
  162.0 0.8 pad_maximum_fusion
  (29 shorter events, 3.8 us)
Async XLA Ops:
  3.5 30.1 %all-to-all-start.1 = ((bf16[16,24,1280]{2,1,0:T(8,128)(2,1)}), bf16[16,24,1280]{2,1,0:T(8,128)(2,1)S(1)}, u32[]{:S(2)}, u32[]{:S(2)}) async-start(bf16[16,24,1280]{2,1,0:T(8,128)(2,1)} %bitcast.9), calls=%async_computation.1 | async-start | bytes 1966080 | tf_op jit(solution)/shard_map/all_to_all | solution.py:147
  33.6 39.3 %all-to-all-start = ((bf16[16,24,1536]{2,1,0:T(8,128)(2,1)}), bf16[16,24,1536]{2,1,0:T(8,128)(2,1)S(1)}, u32[]{:S(2)}, u32[]{:S(2)}) async-start(bf16[16,24,1536]{2,1,0:T(8,128)(2,1)} %bitcast.4), calls=%async_computation | async-start | bytes 2359296 | tf_op jit(solution)/shard_map/all_to_all | solution.py:147
  38.5 23.0 %collective-permute-start = (bf16[384,1280]{1,0:T(8,128)(2,1)S(1)}, bf16[384,1280]{1,0:T(8,128)(2,1)S(1)}, u32[]{:S(2)}, u32[]{:S(2)}) collective-permute-start(bf16[384,1280]{1,0:T(8,128)(2,1)S(1)} %bitcast.53), channel_id=1, source_target_pairs={{0,1},{1,0},{2,3},{3,2},{4,5},{5,4},{6,7},{7,6},{8,9},{9,8},{10,11... | collective-permute-start | bytes 2949128 | tf_op jit(solution)/shard_map/ppermute | solution.py:179
  69.7 1.5 copy-start
  71.3 1.6 copy-start.2
  72.9 1.8 %copy-start.1 = (f32[384,1792]{1,0:T(8,128)S(1)}, f32[384,1792]{1,0:T(8,128)}, u32[]{:S(2)}) copy-start(f32[384,1792]{1,0:T(8,128)} %copy-done) | copy-start | bytes 8257540
  74.6 1.8 %copy-start.3 = (f32[384,1792]{1,0:T(8,128)S(1)}, f32[384,1792]{1,0:T(8,128)}, u32[]{:S(2)}) copy-start(f32[384,1792]{1,0:T(8,128)} %copy-done.2) | copy-start | bytes 8257540
  92.8 37.6 %all-to-all-start.2 = ((bf16[16,24,1536]{2,1,0:T(8,128)(2,1)}), bf16[16,24,1536]{2,1,0:T(8,128)(2,1)S(1)}, u32[]{:S(2)}, u32[]{:S(2)}) async-start(bf16[16,24,1536]{2,1,0:T(8,128)(2,1)} %bitcast.13), calls=%async_computation.2 | async-start | bytes 2359296 | tf_op jit(solution)/shard_map/all_to_all | solution.py:147
  104.8 23.1 %collective-permute-start.2 = (bf16[384,1280]{1,0:T(8,128)(2,1)S(1)}, bf16[384,1280]{1,0:T(8,128)(2,1)}, u32[]{:S(2)}, u32[]{:S(2)}) collective-permute-start(bf16[384,1280]{1,0:T(8,128)(2,1)S(1)} %drop.5), channel_id=1, source_target_pairs={{0,1},{1,0},{2,3},{3,2},{4,5},{5,4},{6,7},{7,6},{8,9},{9,8},{10,11... | collective-permute-start | bytes 2949128 | tf_op jit(solution)/shard_map/ppermute | solution.py:179
  130.3 7.0 %copy-start.4 = (s32[128,2]{0,1:T(2,128)S(1)}, s32[128,2]{0,1:T(2,128)}, u32[]{:S(2)}) copy-start(s32[128,2]{0,1:T(2,128)} %param.7) | copy-start | bytes 3076
  130.3 7.0 %copy-start.5 = (f32[128,2]{0,1:T(2,128)S(1)}, f32[128,2]{0,1:T(2,128)}, u32[]{:S(2)}) copy-start(f32[128,2]{0,1:T(2,128)} %param.8) | copy-start | bytes 3076
  130.3 30.5 %all-to-all-start.3 = ((bf16[16,24,1280]{2,1,0:T(8,128)(2,1)}), bf16[16,24,1280]{2,1,0:T(8,128)(2,1)S(1)}, u32[]{:S(2)}, u32[]{:S(2)}) async-start(bf16[16,24,1280]{2,1,0:T(8,128)(2,1)} %bitcast.19), calls=%async_computation.3 | async-start | bytes 1966080 | tf_op jit(solution)/shard_map/all_to_all | solution.py:147
  138.7 10.4 %collective-permute-start.1 = (f32[128,768]{1,0:T(8,128)S(1)}, f32[128,768]{1,0:T(8,128)S(1)}, u32[]{:S(2)}, u32[]{:S(2)}) collective-permute-start(f32[128,768]{1,0:T(8,128)S(1)} %constant_dynamic-slice_fusion), channel_id=1, source_target_pairs={{0,1},{1,0},{2,3},{3,2},{4,5},{5,4},{6,7},{7,6},{8,9},{9,8},{10,11... | collective-permute-start | bytes 1179656 | tf_op jit(solution)/shard_map/ppermute | solution.py:179

commit v3 on v2

v3 whole, which is shorter than its diff:
```python
import jax
import jax.numpy as jnp
from jax import lax
from jax.experimental import pallas as pl
from jax.experimental.pallas import tpu as pltpu
from jax.sharding import PartitionSpec as P

BLOCK = 128
CAP = 24
LANES = 256
VMEM_BYTES = 36 * 1024 * 1024


def tile_of(width):
    return LANES if width % LANES == 0 else 128


def fetch_rows(source, start, target, sems):
    tiles, depth, tile = target.shape

    def copy(n):
        return pltpu.make_async_copy(
            source.at[pl.ds(start, depth), pl.ds(pl.multiple_of(n * tile, 128), tile)],
            target.at[n],
            sems.at[n],
        )

    for n in range(tiles):
        copy(n).start()
    return copy


def fetch_columns(source, starts, width, target, sems):
    tiles, depth, tile = target.shape
    each = width // tile

    def copy(n):
        at = pl.multiple_of(starts[n // each] + (n % each) * tile, 128)
        return pltpu.make_async_copy(source.at[:, pl.ds(at, tile)], target.at[n], sems.at[n])

    for n in range(tiles):
        copy(n).start()
    return copy


def lift_tiles(piece, sums, gate_tiles, up_tiles, copies, write):
    tiles, depth, tile = gate_tiles.shape

    @pl.loop(0, tiles)
    def _(n):
        at = pl.ds(pl.multiple_of(n * tile, 128), tile)
        copies[0](n).wait()
        gate = jnp.dot(piece[...], gate_tiles[n], preferred_element_type=jnp.float32)
        copies[1](n).wait()
        up = jnp.dot(piece[...], up_tiles[n], preferred_element_type=jnp.float32)
        if sums is not None:
            gate = gate + sums[0][:, at]
            up = up + sums[1][:, at]
        write(at, gate, up)


def drop_tiles(hidden, down_tiles, copy, out):
    tiles, depth, tile = down_tiles.shape

    for n in range(tiles):
        copy(n).wait()
        value = jnp.dot(hidden[...], down_tiles[n], preferred_element_type=jnp.float32)
        out[:, n * tile : (n + 1) * tile] = value.astype(out.dtype)


def vmem():
    return pl.BlockSpec(memory_space=pltpu.VMEM)


def weight_scratch(tiles, depth, tile):
    return [pltpu.VMEM((tiles, depth, tile), jnp.bfloat16), pltpu.SemaphoreType.DMA((tiles,))]


def lift(piece, start, w_gate, w_up, sums=None):
    rows, depth = piece.shape
    hidden = w_gate.shape[1]
    tile = tile_of(hidden)

    def kernel(at, piece, w_gate, w_up, *refs):
        given, (gate, up), scratch = refs[:-6], refs[-6:-4], refs[-4:]
        begin = pl.multiple_of(at[0], 128)
        copies = [
            fetch_rows(w_gate, begin, scratch[0], scratch[1]),
            fetch_rows(w_up, begin, scratch[2], scratch[3]),
        ]

        def write(at, gate_tile, up_tile):
            gate[:, at] = gate_tile
            up[:, at] = up_tile

        lift_tiles(piece, given or None, scratch[0], scratch[2], copies, write)

    given = [] if sums is None else list(sums)
    return pl.pallas_call(
        kernel,
        out_shape=[jax.ShapeDtypeStruct((rows, hidden), jnp.float32)] * 2,
        in_specs=[pl.BlockSpec(memory_space=pltpu.SMEM), vmem()]
        + [pl.BlockSpec(memory_space=pltpu.HBM)] * 2
        + [vmem()] * len(given),
        out_specs=[vmem(), vmem()],
        scratch_shapes=weight_scratch(hidden // tile, depth, tile) * 2,
        compiler_params=pltpu.CompilerParams(vmem_limit_bytes=VMEM_BYTES),
        cost_estimate=pl.CostEstimate(
            flops=4 * rows * depth * hidden,
            bytes_accessed=4 * depth * hidden,
            transcendentals=0,
        ),
        name="lift",
    )(jnp.reshape(start, (1,)).astype(jnp.int32), piece, w_gate, w_up, *given)


def finish(piece, start, w_gate, w_up, sums, w_down, columns, width):
    rows, depth = piece.shape
    hidden = w_gate.shape[1]
    tile = tile_of(hidden)
    wide = tile_of(width)
    count = len(columns)

    def kernel(at, piece, w_gate, w_up, w_down, gate, up, value, out, *scratch):
        begin = pl.multiple_of(at[0], 128)
        copies = [
            fetch_rows(w_gate, begin, scratch[0], scratch[1]),
            fetch_rows(w_up, begin, scratch[2], scratch[3]),
        ]
        starts = [at[1 + i] for i in range(count)]
        down = fetch_columns(w_down, starts, width, scratch[4], scratch[5])

        def write(at, gate_tile, up_tile):
            silu = gate_tile / (1.0 + jnp.exp(-gate_tile))
            value[:, at] = (silu * up_tile).astype(jnp.bfloat16)

        lift_tiles(piece, (gate, up), scratch[0], scratch[2], copies, write)
        drop_tiles(value, scratch[4], down, out)

    return pl.pallas_call(
        kernel,
        out_shape=[
            jax.ShapeDtypeStruct((rows, hidden), jnp.bfloat16),
            jax.ShapeDtypeStruct((rows, count * width), jnp.bfloat16),
        ],
        in_specs=[pl.BlockSpec(memory_space=pltpu.SMEM), vmem()]
        + [pl.BlockSpec(memory_space=pltpu.HBM)] * 3
        + [vmem()] * 2,
        out_specs=[vmem(), vmem()],
        scratch_shapes=weight_scratch(hidden // tile, depth, tile) * 2
        + weight_scratch(count * width // wide, hidden, wide),
        compiler_params=pltpu.CompilerParams(vmem_limit_bytes=VMEM_BYTES),
        cost_estimate=pl.CostEstimate(
            flops=4 * rows * depth * hidden + 2 * rows * hidden * count * width,
            bytes_accessed=4 * depth * hidden + 2 * hidden * count * width,
            transcendentals=rows * hidden,
        ),
        name="finish",
    )(
        jnp.stack([start] + columns).astype(jnp.int32),
        piece,
        w_gate,
        w_up,
        w_down,
        *sums,
    )


def drop(hidden, w_down, start, width, dtype):
    rows, depth = hidden.shape
    tile = tile_of(width)

    def kernel(at, hidden, w_down, out, *scratch):
        copy = fetch_columns(w_down, [at[0]], width, scratch[0], scratch[1])
        drop_tiles(hidden, scratch[0], copy, out)

    return pl.pallas_call(
        kernel,
        out_shape=jax.ShapeDtypeStruct((rows, width), dtype),
        in_specs=[
            pl.BlockSpec(memory_space=pltpu.SMEM),
            vmem(),
            pl.BlockSpec(memory_space=pltpu.HBM),
        ],
        out_specs=vmem(),
        scratch_shapes=weight_scratch(width // tile, depth, tile),
        compiler_params=pltpu.CompilerParams(vmem_limit_bytes=VMEM_BYTES),
        cost_estimate=pl.CostEstimate(
            flops=2 * rows * depth * width, bytes_accessed=2 * depth * width, transcendentals=0
        ),
        name="drop",
    )(jnp.reshape(start, (1,)).astype(jnp.int32), hidden, w_down)


def selectors(expert_ids, gate_probs, experts):
    rows = expert_ids.shape[0]
    blocks = rows // BLOCK
    match = expert_ids.T[:, None, :] == jnp.arange(experts, dtype=jnp.int32)[None, :, None]
    named = jnp.any(match, axis=0)
    weight = jnp.sum(jnp.where(match, gate_probs.T[:, None, :], 0.0), axis=0)
    row = jnp.arange(rows, dtype=jnp.int32)
    same = row[:, None] // BLOCK == row[None, :] // BLOCK
    earlier = ((row[:, None] < row[None, :]) & same).astype(jnp.bfloat16)
    before = jnp.dot(named.astype(jnp.bfloat16), earlier, preferred_element_type=jnp.float32)
    place = before.astype(jnp.int32) + (row // BLOCK * CAP)[None, :]
    slots = jnp.arange(blocks * CAP, dtype=jnp.int32)
    hit = named[:, None, :] & (place[:, None, :] == slots[None, :, None])
    high = weight.astype(jnp.bfloat16)
    rest = weight - high.astype(jnp.float32)
    middle = rest.astype(jnp.bfloat16)
    low = (rest - middle.astype(jnp.float32)).astype(jnp.bfloat16)
    flat = (experts * blocks * CAP, rows)
    chosen = hit.astype(jnp.bfloat16).reshape(flat)
    weights = [
        jnp.where(hit, part[:, None, :], 0).astype(jnp.bfloat16).reshape(flat)
        for part in (high, middle, low)
    ]
    return chosen, weights


def swap(value, experts):
    slots, width = value.shape
    return lax.all_to_all(
        value.reshape(experts, slots // experts, width),
        "expert",
        split_axis=0,
        concat_axis=0,
        tiled=True,
    ).reshape(slots, width)


def mix(weights, returned):
    return sum(
        lax.dot_general(
            w, returned, (((0,), (0,)), ((), ())), preferred_element_type=jnp.float32
        )
        for w in weights
    )


def on_device(tokens, expert_ids, gate_probs, w_gate, w_up, w_down):
    width = tokens.shape[1]
    experts = lax.axis_size("expert")
    ranks = lax.axis_size("tensor")
    me = lax.axis_index("tensor")
    w_gate = lax.all_gather(w_gate, "dp", axis=1, tiled=True)[0]
    w_up = lax.all_gather(w_up, "dp", axis=1, tiled=True)[0]
    w_down = lax.all_gather(w_down, "dp", axis=2, tiled=True)[0]
    chosen, weights = selectors(expert_ids, gate_probs, experts)

    def rank_at(step):
        return lax.rem(me + step, ranks)

    def send_up(value, step):
        return lax.ppermute(value, "tensor", [(i, (i + step) % ranks) for i in range(ranks)])

    share = width // ranks
    shared = round(2 * share / 3 / LANES) * LANES
    direct_at = ranks * shared

    def placed(features):
        return jnp.dot(chosen, features, preferred_element_type=jnp.float32).astype(jnp.bfloat16)

    mine = lax.dynamic_slice_in_dim(tokens, me * shared, shared, axis=1)
    own = swap(placed(mine), experts)
    direct = swap(placed(tokens[:, direct_at:]), experts)
    sums = lift(own, me * shared, w_gate, w_up)
    for step in range(1, ranks):
        other = send_up(own, ranks - step)
        sums = lift(other, rank_at(step) * shared, w_gate, w_up, sums)
    early = share - shared
    hidden, partial = finish(
        direct,
        jnp.int32(direct_at),
        w_gate,
        w_up,
        sums,
        w_down,
        [jnp.int32(rank * share) for rank in range(ranks)],
        early,
    )
    returned = swap(partial, experts)
    owned = drop(hidden, w_down, me * share + early, shared, jnp.float32)
    for step in range(1, ranks):
        sent = drop(hidden, w_down, rank_at(step) * share + early, shared, jnp.bfloat16)
        owned = owned + send_up(sent, step).astype(jnp.float32)
    first = mix(weights, returned)

    def part_of(rank):
        return lax.dynamic_slice_in_dim(first, rank * early, early, axis=1)

    mixed = part_of(me)
    for step in range(1, ranks):
        mixed = mixed + send_up(part_of(rank_at(step)), step)
    late = mix(weights, swap(owned.astype(jnp.bfloat16), experts))
    return jnp.concatenate([mixed.astype(jnp.bfloat16), late.astype(jnp.bfloat16)], axis=1)


def solution(mesh):
    placed = (
        P(("groups", "dp", "expert"), None),
        P(("groups", "dp", "expert"), None),
        P(("groups", "dp", "expert"), None),
        P("expert", "dp", "tensor"),
        P("expert", "dp", "tensor"),
        P("expert", "tensor", "dp"),
    )
    return jax.shard_map(
        on_device,
        mesh=mesh,
        in_specs=placed,
        out_specs=P(("groups", "dp", "expert"), "tensor"),
        check_vma=False,
    )
```

time: 164 us -> 164 us (level)
  local copies, waits for them, and re-layouts: 6.79 us -> 18.1 us
  waiting for transfers between devices: 74.9 us -> 64.1 us
  matrix products: 7.39 us -> 11.2 us
  Pallas kernels: 43.3 us -> 40.2 us
    unnamed x12 -> x20, local copies, waits for them, and re-layouts: 6.66 us -> 18 us
    ppermute x3, waiting for transfers between devices: 42.1 us -> 35.2 us  [send_up(): lax.ppermute(value, 'tensor', [(i, (i + step) % ranks) for i in range(ran...]
    all_to_all x4, waiting for transfers between devices: 32.7 us -> 28.9 us  [swap(): lax.all_to_all(value.reshape(experts, slots // experts, width), 'expert',...]
    dot_general x6, matrix products: 2.36 us -> 6.15 us  [mix(): lax.dot_general(w, returned, (((0,), (0,)), ((), ())), preferred_element_...]
    pallas_call x6 -> x5, Pallas kernels: 43.3 us -> 40.2 us  [the longest x2 17.2 us: lift(): pl.pallas_call(kernel, out_shape=[jax.ShapeDtypeStruct((rows, hidden), jn...]
  transfers between devices with their start and end apart: 7 -> 7, of which waited for: 5 -> 5; matrix products, arithmetic and copies ran while one was open for 4% -> 5% of each run, Pallas kernels for 17% -> 16%
where the time goes in v3:
time: 164 us; the launch traced here: 163 us
  waiting for transfers between devices  64.1 us (39%)
  Pallas kernels  40.2 us (25%)
  starting transfers between devices  26.2 us (16%)
  local copies, waits for them, and re-layouts  18.1 us (11%)
  matrix products  11.2 us (7%)
  other arithmetic  2.89 us (2%)
    ppermute x3, waiting for transfers between devices, send_up(): lax.ppermute(value, 'tensor', [(i, (i + step) % ranks) for i in range(ran...  35.2 us
    all_to_all x4, waiting for transfers between devices, swap(): lax.all_to_all(value.reshape(experts, slots // experts, width), 'expert',...  28.9 us
    all_to_all x4, starting transfers between devices, swap(): lax.all_to_all(value.reshape(experts, slots // experts, width), 'expert',...  25.3 us
    unnamed x20, local copies, waits for them, and re-layouts  18 us
    pallas_call x2, Pallas kernels, lift(): pl.pallas_call(kernel, out_shape=[jax.ShapeDtypeStruct((rows, hidden), jn...  17.2 us
    pallas_call x1, Pallas kernels, finish(): pl.pallas_call(kernel, out_shape=[jax.ShapeDtypeStruct((rows, hidden), jn...  13.7 us
    pallas_call x2, Pallas kernels, drop(): pl.pallas_call(kernel, out_shape=jax.ShapeDtypeStruct((rows, width), dtyp...  9.33 us
    dot_general x6, matrix products, mix(): lax.dot_general(w, returned, (((0,), (0,)), ((), ())), preferred_element_...  6.15 us
  transfers between devices with their start and end apart: 7, of which 5 were waited for; matrix products, arithmetic and copies ran while one was open for 5% of the time, Pallas kernels for 16%

profile of v3, /device:TPU:11, one launch (start us, length us, event | category | flops | bytes accessed | tf_op | source)
XLA Modules:
  0.0 163.0 jit_solution(12453513738757056787)
XLA Ops:
  1.1 2.3 %convolution_convert_fusion = bf16[384,1280]{1,0:T(8,128)(2,1)} fusion(pred[384,128]{1,0:T(32,128)(4,1)S(1)} %fusion.12, bf16[128,4096]{1,0:T(8,128)(2,1)} %param.6, s32[]{:T(128)S(6)} %select_n.52), kind=kOutput, calls=%fused_computation | convolution fusion | flops 126320640 | bytes 1359876 | tf_op jit(solution)/shard_map/dot_general | solution.py:262
  3.5 6.6 %all-to-all-start.1 = ((bf16[16,24,1280]{2,1,0:T(8,128)(2,1)}), bf16[16,24,1280]{2,1,0:T(8,128)(2,1)S(1)}, u32[]{:S(2)}, u32[]{:S(2)}) async-start(bf16[16,24,1280]{2,1,0:T(8,128)(2,1)} %bitcast.10), calls=%async_computation.1 | async-start | bytes 1966080 | tf_op jit(solution)/shard_map/all_to_all | solution.py:223
  10.1 2.5 %convolution_convert_fusion.1 = bf16[384,1536]{1,0:T(8,128)(2,1)} fusion(pred[384,128]{1,0:T(32,128)(4,1)S(1)} %fusion.12, bf16[128,4096]{1,0:T(8,128)(2,1)} %param.6), kind=kOutput, calls=%fused_computation.1 | convolution fusion | flops 151584768 | bytes 1622016 | tf_op jit(solution)/shard_map/dot_general | solution.py:262
  12.6 21.0 %all-to-all-done.1 = bf16[16,24,1280]{2,1,0:T(8,128)(2,1)S(1)} async-done(((bf16[16,24,1280]{2,1,0:T(8,128)(2,1)}), bf16[16,24,1280]{2,1,0:T(8,128)(2,1)S(1)}, u32[]{:S(2)}, u32[]{:S(2)}) %all-to-all-start.1) | async-done | bytes 983072 | tf_op jit(solution)/shard_map/all_to_all | solution.py:223
  33.6 4.9 %all-to-all-start = ((bf16[16,24,1536]{2,1,0:T(8,128)(2,1)}), bf16[16,24,1536]{2,1,0:T(8,128)(2,1)S(1)}, u32[]{:S(2)}, u32[]{:S(2)}) async-start(bf16[16,24,1536]{2,1,0:T(8,128)(2,1)} %bitcast.4), calls=%async_computation | async-start | bytes 2359296 | tf_op jit(solution)/shard_map/all_to_all | solution.py:223
  38.7 10.4 %lift.2 = (f32[384,1792]{1,0:T(8,128)S(1)}, f32[384,1792]{1,0:T(8,128)S(1)}) custom-call(s32[1]{0:T(128)} %bitcast.12.at, bf16[384,1280]{1,0:T(8,128)(2,1)S(1)} %bitcast.57, bf16[4096,1792]{1,0:T(8,128)(2,1)} %bitcast.59, bf16[4096,1792]{1,0:T(8,128)(2,1)} %bitcast.62), custom_call_target="tpu_custom_call" | custom-call | flops 3523215360 | bytes 9175040 | tf_op jit(solution)/shard_map/lift/pallas_call | solution.py:99
  49.2 12.3 %collective-permute-done.piece = bf16[384,1280]{1,0:T(8,128)(2,1)S(1)} collective-permute-done((bf16[384,1280]{1,0:T(8,128)(2,1)S(1)}, bf16[384,1280]{1,0:T(8,128)(2,1)S(1)}, u32[]{:S(2)}, u32[]{:S(2)}) %collective-permute-start) | collective-permute-done | bytes 983072 | tf_op jit(solution)/shard_map/ppermute | solution.py:255
  61.5 6.8 %lift.3 = (f32[384,1792]{1,0:T(8,128)S(1)}, f32[384,1792]{1,0:T(8,128)S(1)}) custom-call(s32[1]{0:T(128)} %bitcast.9.at, bf16[384,1280]{1,0:T(8,128)(2,1)S(1)} %collective-permute-done.piece, bf16[4096,1792]{1,0:T(8,128)(2,1)} %bitcast.60, bf16[4096,1792]{1,0:T(8,128)(2,1)} %bitcast.63, f32[384,1792]{1,0:T(8,128)S(1)} %get-tuple-element.11.refs_0_, ...), custom_call_target="tpu_custom_call" | custom-call | flops 3523215360 | bytes 9175040 | tf_op jit(solution)/shard_map/lift/pallas_call | solution.py:99
  69.8 1.6 copy-done.4
  71.4 1.8 %copy-done.3 = f32[384,1792]{1,0:T(8,128)S(1)} copy-done((f32[384,1792]{1,0:T(8,128)S(1)}, f32[384,1792]{1,0:T(8,128)}, u32[]{:S(2)}) %copy-start.3) | copy-done | bytes 2752536
  73.2 1.8 %copy-done.5 = f32[384,1792]{1,0:T(8,128)S(1)} copy-done((f32[384,1792]{1,0:T(8,128)S(1)}, f32[384,1792]{1,0:T(8,128)}, u32[]{:S(2)}) %copy-start.5) | copy-done | bytes 2752536
  74.9 13.7 %finish.1 = (bf16[384,1792]{1,0:T(8,128)(2,1)S(1)}, bf16[384,1536]{1,0:T(8,128)(2,1)S(1)}) custom-call(s32[3]{0:T(128)S(1)} %copy-done.7, bf16[384,1536]{1,0:T(8,128)(2,1)S(1)} %bitcast.55, bf16[4096,1792]{1,0:T(8,128)(2,1)} %bitcast.61, bf16[4096,1792]{1,0:T(8,128)(2,1)} %bitcast.64, bf16[1792,4096]{1,0:T(8,128)(2,1)} %bitcast.52, ...), custom_call_target="tpu_custom_call" | custom-call | flops 6341787648 | bytes 16515072 | tf_op jit(solution)/shard_map/finish/pallas_call | solution.py:140
  89.6 6.8 %all-to-all-start.2 = ((bf16[16,24,1536]{2,1,0:T(8,128)(2,1)}), bf16[16,24,1536]{2,1,0:T(8,128)(2,1)}, u32[]{:S(2)}, u32[]{:S(2)}) async-start(bf16[16,24,1536]{2,1,0:T(8,128)(2,1)} %bitcast.58), calls=%async_computation.2 | async-start | bytes 2359296 | tf_op jit(solution)/shard_map/all_to_all | solution.py:223
  96.5 5.2 %copy-done = bf16[1,1792,4096]{2,1,0:T(8,128)(2,1)S(1)} copy-done((bf16[1,1792,4096]{2,1,0:T(8,128)(2,1)S(1)}, bf16[1,1792,4096]{2,1,0:T(8,128)(2,1)}, u32[]{:S(2)}) %copy-start) | copy-done | bytes 14680088
  101.6 4.7 %drop.3 = bf16[384,1280]{1,0:T(8,128)(2,1)S(1)} custom-call(s32[1]{0:T(128)} %bitcast.18.at, bf16[384,1792]{1,0:T(8,128)(2,1)S(1)} %get-tuple-element.16.hidden, bf16[1792,4096]{1,0:T(8,128)(2,1)S(1)} %bitcast.53), custom_call_target="tpu_custom_call" | custom-call | flops 1761607680 | bytes 4587520 | tf_op jit(solution)/shard_map/drop/pallas_call | solution.py:177
  106.6 5.2 %copy-done.1 = bf16[1,1792,4096]{2,1,0:T(8,128)(2,1)S(1)} copy-done((bf16[1,1792,4096]{2,1,0:T(8,128)(2,1)S(1)}, bf16[1,1792,4096]{2,1,0:T(8,128)(2,1)}, u32[]{:S(2)}) %copy-start.1) | copy-done | bytes 14680088
  111.8 4.7 %drop.2 = f32[384,1280]{1,0:T(8,128)S(1)} custom-call(s32[1]{0:T(128)} %bitcast.17.at, bf16[384,1792]{1,0:T(8,128)(2,1)S(1)} %get-tuple-element.16.hidden, bf16[1792,4096]{1,0:T(8,128)(2,1)S(1)} %bitcast.54), custom_call_target="tpu_custom_call" | custom-call | flops 1761607680 | bytes 4587520 | tf_op jit(solution)/shard_map/drop/pallas_call | solution.py:177
  116.5 12.9 %collective-permute-done.2 = bf16[384,1280]{1,0:T(8,128)(2,1)S(1)} collective-permute-done((bf16[384,1280]{1,0:T(8,128)(2,1)S(1)}, bf16[384,1280]{1,0:T(8,128)(2,1)S(1)}, u32[]{:S(2)}, u32[]{:S(2)}) %collective-permute-start.2) | collective-permute-done | bytes 983072 | tf_op jit(solution)/shard_map/ppermute | solution.py:255
  130.5 7.0 %all-to-all-start.3 = ((bf16[16,24,1280]{2,1,0:T(8,128)(2,1)}), bf16[16,24,1280]{2,1,0:T(8,128)(2,1)S(1)}, u32[]{:S(2)}, u32[]{:S(2)}) async-start(bf16[16,24,1280]{2,1,0:T(8,128)(2,1)} %bitcast.19), calls=%async_computation.3 | async-start | bytes 1966080 | tf_op jit(solution)/shard_map/all_to_all | solution.py:223
  137.5 1.7 %convolution_bitcast_fusion.3 = f32[128,1536]{1,0:T(8,128)S(1)} fusion(bf16[16,24,1536]{2,1,0:T(8,128)(2,1)} %all-to-all-done.2, s32[16,128]{1,0:T(8,128)S(1)} %fusion.5, pred[16,128]{1,0:T(8,128)(4,1)S(1)} %fusion.48, bf16[16,128]{1,0:T(8,128)(2,1)S(1)} %get-tuple-element.17), kind=kOutput, calls=%fused_computation.7 | convolution fusion | flops 151142400 | bytes 1980416 | tf_op jit(solution)/shard_map/dot_general | solution.py:234
  139.2 1.7 %convolution_bitcast_fusion.4 = f32[128,1536]{1,0:T(8,128)S(1)} fusion(bf16[16,24,1536]{2,1,0:T(8,128)(2,1)} %all-to-all-done.2, s32[16,128]{1,0:T(8,128)S(1)} %fusion.5, pred[16,128]{1,0:T(8,128)(4,1)S(1)} %fusion.48, bf16[16,128]{1,0:T(8,128)(2,1)S(1)} %get-tuple-element.18), kind=kOutput, calls=%fused_computation.8 | convolution fusion | flops 151142400 | bytes 1980416 | tf_op jit(solution)/shard_map/dot_general | solution.py:234
  140.9 1.7 %fusion.3 = f32[128,1536]{1,0:T(8,128)S(1)} fusion(f32[128,1536]{1,0:T(8,128)S(1)} %convolution_bitcast_fusion.3, f32[128,1536]{1,0:T(8,128)S(1)} %convolution_bitcast_fusion.4, bf16[16,24,1536]{2,1,0:T(8,128)(2,1)} %all-to-all-done.2, s32[16,128]{1,0:T(8,128)S(1)} %fusion.5, pred[16,128]{1,0:T(8,128)(4,1)S(1)} %fusion.48, ...), kind=kOutput, calls=%fused_computation.11 | convolution fusion | flops 151535616 | bytes 3553280 | tf_op jit(solution)/shard_map/dot_general | solution.py:234
  143.0 10.1 %collective-permute-done.1 = f32[128,768]{1,0:T(8,128)S(1)} collective-permute-done((f32[128,768]{1,0:T(8,128)S(1)}, f32[128,768]{1,0:T(8,128)S(1)}, u32[]{:S(2)}, u32[]{:S(2)}) %collective-permute-start.1) | collective-permute-done | bytes 393248 | tf_op jit(solution)/shard_map/ppermute | solution.py:255
  153.1 7.9 %all-to-all-done.3 = bf16[16,24,1280]{2,1,0:T(8,128)(2,1)S(1)} async-done(((bf16[16,24,1280]{2,1,0:T(8,128)(2,1)}), bf16[16,24,1280]{2,1,0:T(8,128)(2,1)S(1)}, u32[]{:S(2)}, u32[]{:S(2)}) %all-to-all-start.3) | async-done | bytes 983072 | tf_op jit(solution)/shard_map/all_to_all | solution.py:223
  (35 shorter events, 7.8 us)
Async XLA Ops:
  3.5 30.1 %all-to-all-start.1 = ((bf16[16,24,1280]{2,1,0:T(8,128)(2,1)}), bf16[16,24,1280]{2,1,0:T(8,128)(2,1)S(1)}, u32[]{:S(2)}, u32[]{:S(2)}) async-start(bf16[16,24,1280]{2,1,0:T(8,128)(2,1)} %bitcast.10), calls=%async_computation.1 | async-start | bytes 1966080 | tf_op jit(solution)/shard_map/all_to_all | solution.py:223
  33.6 37.8 %all-to-all-start = ((bf16[16,24,1536]{2,1,0:T(8,128)(2,1)}), bf16[16,24,1536]{2,1,0:T(8,128)(2,1)S(1)}, u32[]{:S(2)}, u32[]{:S(2)}) async-start(bf16[16,24,1536]{2,1,0:T(8,128)(2,1)} %bitcast.4), calls=%async_computation | async-start | bytes 2359296 | tf_op jit(solution)/shard_map/all_to_all | solution.py:223
  38.5 23.0 %collective-permute-start = (bf16[384,1280]{1,0:T(8,128)(2,1)S(1)}, bf16[384,1280]{1,0:T(8,128)(2,1)S(1)}, u32[]{:S(2)}, u32[]{:S(2)}) collective-permute-start(bf16[384,1280]{1,0:T(8,128)(2,1)S(1)} %bitcast.56), channel_id=1, source_target_pairs={{0,1},{1,0},{2,3},{3,2},{4,5},{5,4},{6,7},{7,6},{8,9},{9,8},{10,11... | collective-permute-start | bytes 2949128 | tf_op jit(solution)/shard_map/ppermute | solution.py:255
  61.5 9.9 %copy-start.7 = (s32[3]{0:T(128)S(1)}, s32[3]{0:T(128)}, u32[]{:S(2)}) copy-start(s32[3]{0:T(128)} %constant.62.clone.1.at) | copy-start | bytes 40
  68.2 1.5 copy-start.2
  69.8 1.6 copy-start.4
  71.4 1.8 %copy-start.3 = (f32[384,1792]{1,0:T(8,128)S(1)}, f32[384,1792]{1,0:T(8,128)}, u32[]{:S(2)}) copy-start(f32[384,1792]{1,0:T(8,128)} %copy-done.2) | copy-start | bytes 8257540
  73.2 1.8 %copy-start.5 = (f32[384,1792]{1,0:T(8,128)S(1)}, f32[384,1792]{1,0:T(8,128)}, u32[]{:S(2)}) copy-start(f32[384,1792]{1,0:T(8,128)} %copy-done.4) | copy-start | bytes 8257540
  88.6 1.0 copy-start.6
  89.6 40.9 %all-to-all-start.2 = ((bf16[16,24,1536]{2,1,0:T(8,128)(2,1)}), bf16[16,24,1536]{2,1,0:T(8,128)(2,1)}, u32[]{:S(2)}, u32[]{:S(2)}) async-start(bf16[16,24,1536]{2,1,0:T(8,128)(2,1)} %bitcast.58), calls=%async_computation.2 | async-start | bytes 2359296 | tf_op jit(solution)/shard_map/all_to_all | solution.py:223
  96.5 5.2 %copy-start = (bf16[1,1792,4096]{2,1,0:T(8,128)(2,1)S(1)}, bf16[1,1792,4096]{2,1,0:T(8,128)(2,1)}, u32[]{:S(2)}) copy-start(bf16[1,1792,4096]{2,1,0:T(8,128)(2,1)} %param.11) | copy-start | bytes 44040196
  106.3 23.0 %collective-permute-start.2 = (bf16[384,1280]{1,0:T(8,128)(2,1)S(1)}, bf16[384,1280]{1,0:T(8,128)(2,1)S(1)}, u32[]{:S(2)}, u32[]{:S(2)}) collective-permute-start(bf16[384,1280]{1,0:T(8,128)(2,1)S(1)} %drop.3), channel_id=1, source_target_pairs={{0,1},{1,0},{2,3},{3,2},{4,5},{5,4},{6,7},{7,6},{8,9},{9,8},{10,11... | collective-permute-start | bytes 2949128 | tf_op jit(solution)/shard_map/ppermute | solution.py:255
  106.6 5.2 %copy-start.1 = (bf16[1,1792,4096]{2,1,0:T(8,128)(2,1)S(1)}, bf16[1,1792,4096]{2,1,0:T(8,128)(2,1)}, u32[]{:S(2)}) copy-start(bf16[1,1792,4096]{2,1,0:T(8,128)(2,1)} %param.11) | copy-start | bytes 44040196
  130.5 7.0 %copy-start.8 = (s32[128,2]{0,1:T(2,128)S(1)}, s32[128,2]{0,1:T(2,128)}, u32[]{:S(2)}) copy-start(s32[128,2]{0,1:T(2,128)} %param.7) | copy-start | bytes 3076
  130.5 7.0 %copy-start.9 = (f32[128,2]{0,1:T(2,128)S(1)}, f32[128,2]{0,1:T(2,128)}, u32[]{:S(2)}) copy-start(f32[128,2]{0,1:T(2,128)} %param.8) | copy-start | bytes 3076
  130.5 30.5 %all-to-all-start.3 = ((bf16[16,24,1280]{2,1,0:T(8,128)(2,1)}), bf16[16,24,1280]{2,1,0:T(8,128)(2,1)S(1)}, u32[]{:S(2)}, u32[]{:S(2)}) async-start(bf16[16,24,1280]{2,1,0:T(8,128)(2,1)} %bitcast.19), calls=%async_computation.3 | async-start | bytes 1966080 | tf_op jit(solution)/shard_map/all_to_all | solution.py:223
  142.6 10.4 %collective-permute-start.1 = (f32[128,768]{1,0:T(8,128)S(1)}, f32[128,768]{1,0:T(8,128)S(1)}, u32[]{:S(2)}, u32[]{:S(2)}) collective-permute-start(f32[128,768]{1,0:T(8,128)S(1)} %constant_dynamic-slice_fusion), channel_id=1, source_target_pairs={{0,1},{1,0},{2,3},{3,2},{4,5},{5,4},{6,7},{7,6},{8,9},{9,8},{10,11... | collective-permute-start | bytes 1179656 | tf_op jit(solution)/shard_map/ppermute | solution.py:255

commit v4 on v3

v4 whole, which is shorter than its diff:
```python
import jax
import jax.numpy as jnp
from jax import lax
from jax.experimental import pallas as pl
from jax.experimental.pallas import tpu as pltpu
from jax.sharding import PartitionSpec as P

BLOCK = 128
CAP = 24
LANES = 256
STEP = 256
VMEM_BYTES = 50 * 1024 * 1024


def tile_of(width):
    return LANES if width % LANES == 0 else 128


def fetch(source, row, column, target, sems):
    depth, width = target.shape

    def copy(n):
        size = min(STEP, depth - n * STEP)
        return pltpu.make_async_copy(
            source.at[pl.ds(row + n * STEP, size), pl.ds(column, width)],
            target.at[pl.ds(n * STEP, size)],
            sems.at[n],
        )

    return [copy(n) for n in range(pl.cdiv(depth, STEP))]


def chunks_of(depth):
    steps = pl.cdiv(depth, STEP)
    count = pl.cdiv(steps, 3)
    edges = [steps * i // count for i in range(count + 1)]
    return list(zip(edges[:-1], edges[1:]))


def lift_pieces(pieces, weights, sums, gate, up, last):
    tile = tile_of(gate.shape[1])
    work = [
        (piece, weight, span)
        for piece, weight in zip(pieces, weights)
        for span in chunks_of(piece.shape[1])
    ]
    for number, (piece, (gate_rows, up_rows, gate_copies, up_copies), span) in enumerate(work):
        for n in range(*span):
            gate_copies[n].wait()
            up_copies[n].wait()
        at = pl.ds(span[0] * STEP, min(span[1] * STEP, piece.shape[1]) - span[0] * STEP)
        final = number == len(work) - 1
        before = sums if number == 0 else (gate, up)

        @pl.loop(0, gate.shape[1] // tile)
        def _(n):
            across = pl.ds(pl.multiple_of(n * tile, 128), tile)
            x = piece[:, at]
            g = jnp.dot(x, gate_rows[at, across], preferred_element_type=jnp.float32)
            u = jnp.dot(x, up_rows[at, across], preferred_element_type=jnp.float32)
            if before is not None:
                g = g + before[0][:, across]
                u = u + before[1][:, across]
            if final and last is not None:
                last[:, across] = (g / (1.0 + jnp.exp(-g)) * u).astype(jnp.bfloat16)
            else:
                gate[:, across] = g
                up[:, across] = u


def drop_columns(hidden, weight, copies, out, start):
    for copy in copies:
        copy.wait()
    width = weight.shape[1]
    for at in range(0, width, LANES):
        end = min(at + LANES, width)
        value = jnp.dot(hidden[...], weight[:, at:end], preferred_element_type=jnp.float32)
        out[:, start + at : start + end] = value.astype(out.dtype)


def vmem():
    return pl.BlockSpec(memory_space=pltpu.VMEM)


def hbm():
    return pl.BlockSpec(memory_space=pl.ANY)


def buffer(depth, width):
    return [
        pltpu.VMEM((depth, width), jnp.bfloat16),
        pltpu.SemaphoreType.DMA((pl.cdiv(depth, STEP),)),
    ]


def start_lift(at, pieces, w_gate, w_up, scratch):
    weights = []
    for i, piece in enumerate(pieces):
        begin = pl.multiple_of(at[i], 128)
        rows = scratch[4 * i : 4 * i + 4]
        gate_copies = fetch(w_gate, begin, 0, rows[0], rows[1])
        up_copies = fetch(w_up, begin, 0, rows[2], rows[3])
        for one, other in zip(gate_copies, up_copies):
            one.start()
            other.start()
        weights.append((rows[0], rows[2], gate_copies, up_copies))
    return weights


def lift(piece, start, w_gate, w_up):
    rows, depth = piece.shape
    hidden = w_gate.shape[1]

    def kernel(at, piece, w_gate, w_up, gate, up, *scratch):
        weights = start_lift(at, [piece], w_gate, w_up, scratch)
        lift_pieces([piece], weights, None, gate, up, None)

    return pl.pallas_call(
        kernel,
        out_shape=[jax.ShapeDtypeStruct((rows, hidden), jnp.float32)] * 2,
        in_specs=[pl.BlockSpec(memory_space=pltpu.SMEM), vmem(), hbm(), hbm()],
        out_specs=[vmem(), vmem()],
        scratch_shapes=buffer(depth, hidden) * 2,
        compiler_params=pltpu.CompilerParams(vmem_limit_bytes=VMEM_BYTES),
        cost_estimate=pl.CostEstimate(
            flops=4 * rows * depth * hidden,
            bytes_accessed=4 * depth * hidden,
            transcendentals=0,
        ),
        name="lift",
    )(jnp.reshape(start, (1,)).astype(jnp.int32), piece, w_gate, w_up)


def finish(pieces, starts, w_gate, w_up, sums, w_down, columns, width):
    rows = pieces[0].shape[0]
    depth = sum(piece.shape[1] for piece in pieces)
    hidden = w_gate.shape[1]
    count = len(pieces)

    def kernel(at, *refs):
        given, refs = refs[:count], refs[count:]
        w_gate, w_up, w_down, gate, up, value, out = refs[:7]
        gate_sum, up_sum = refs[7:9]
        scratch = refs[9:]
        weights = start_lift(at, given, w_gate, w_up, scratch)
        scratch = scratch[4 * count :]
        downs = []
        for i in range(len(columns)):
            begin = pl.multiple_of(at[count + i], 128)
            copies = fetch(w_down, 0, begin, scratch[2 * i], scratch[2 * i + 1])
            for copy in copies:
                copy.start()
            downs.append(copies)
        lift_pieces(given, weights, (gate, up), gate_sum, up_sum, value)
        for i, copies in enumerate(downs):
            drop_columns(value, scratch[2 * i], copies, out, i * width)

    scratch = [pltpu.VMEM((rows, hidden), jnp.float32)] * 2
    for piece in pieces:
        scratch += buffer(piece.shape[1], hidden) * 2
    for _ in columns:
        scratch += buffer(hidden, width)
    return pl.pallas_call(
        kernel,
        out_shape=[
            jax.ShapeDtypeStruct((rows, hidden), jnp.bfloat16),
            jax.ShapeDtypeStruct((rows, len(columns) * width), jnp.bfloat16),
        ],
        in_specs=[pl.BlockSpec(memory_space=pltpu.SMEM)]
        + [vmem()] * count
        + [hbm()] * 3
        + [vmem()] * 2,
        out_specs=[vmem(), vmem()],
        scratch_shapes=scratch,
        compiler_params=pltpu.CompilerParams(vmem_limit_bytes=VMEM_BYTES - 10 * 1024 * 1024),
        cost_estimate=pl.CostEstimate(
            flops=4 * rows * depth * hidden + 2 * rows * hidden * len(columns) * width,
            bytes_accessed=4 * depth * hidden + 2 * hidden * len(columns) * width,
            transcendentals=rows * hidden,
        ),
        name="finish",
    )(
        jnp.stack(list(starts) + list(columns)).astype(jnp.int32),
        *pieces,
        w_gate,
        w_up,
        w_down,
        *sums,
    )


def drop(hidden, w_down, start, width, dtype):
    rows, depth = hidden.shape

    def kernel(at, hidden, w_down, out, weight, sems):
        copies = fetch(w_down, 0, pl.multiple_of(at[0], 128), weight, sems)
        for copy in copies:
            copy.start()
        drop_columns(hidden, weight, copies, out, 0)

    return pl.pallas_call(
        kernel,
        out_shape=jax.ShapeDtypeStruct((rows, width), dtype),
        in_specs=[pl.BlockSpec(memory_space=pltpu.SMEM), vmem(), hbm()],
        out_specs=vmem(),
        scratch_shapes=buffer(depth, width),
        compiler_params=pltpu.CompilerParams(vmem_limit_bytes=VMEM_BYTES),
        cost_estimate=pl.CostEstimate(
            flops=2 * rows * depth * width, bytes_accessed=2 * depth * width, transcendentals=0
        ),
        name="drop",
    )(jnp.reshape(start, (1,)).astype(jnp.int32), hidden, w_down)


def selectors(expert_ids, gate_probs, experts):
    rows = expert_ids.shape[0]
    blocks = rows // BLOCK
    match = expert_ids.T[:, None, :] == jnp.arange(experts, dtype=jnp.int32)[None, :, None]
    named = jnp.any(match, axis=0)
    weight = jnp.sum(jnp.where(match, gate_probs.T[:, None, :], 0.0), axis=0)
    row = jnp.arange(rows, dtype=jnp.int32)
    same = row[:, None] // BLOCK == row[None, :] // BLOCK
    earlier = ((row[:, None] < row[None, :]) & same).astype(jnp.bfloat16)
    before = jnp.dot(named.astype(jnp.bfloat16), earlier, preferred_element_type=jnp.float32)
    place = before.astype(jnp.int32) + (row // BLOCK * CAP)[None, :]
    slots = jnp.arange(blocks * CAP, dtype=jnp.int32)
    hit = named[:, None, :] & (place[:, None, :] == slots[None, :, None])
    high = weight.astype(jnp.bfloat16)
    rest = weight - high.astype(jnp.float32)
    middle = rest.astype(jnp.bfloat16)
    low = (rest - middle.astype(jnp.float32)).astype(jnp.bfloat16)
    flat = (experts * blocks * CAP, rows)
    chosen = hit.astype(jnp.bfloat16).reshape(flat)
    weights = [
        jnp.where(hit, part[:, None, :], 0).astype(jnp.bfloat16).reshape(flat)
        for part in (high, middle, low)
    ]
    return chosen, weights


def swap(value, experts):
    slots, width = value.shape
    return lax.all_to_all(
        value.reshape(experts, slots // experts, width),
        "expert",
        split_axis=0,
        concat_axis=0,
        tiled=True,
    ).reshape(slots, width)


def mix(weights, returned):
    return sum(
        lax.dot_general(
            w, returned, (((0,), (0,)), ((), ())), preferred_element_type=jnp.float32
        )
        for w in weights
    )


def on_device(tokens, expert_ids, gate_probs, w_gate, w_up, w_down):
    width = tokens.shape[1]
    experts = lax.axis_size("expert")
    ranks = lax.axis_size("tensor")
    me = lax.axis_index("tensor")
    w_gate = lax.all_gather(w_gate, "dp", axis=1, tiled=True)[0]
    w_up = lax.all_gather(w_up, "dp", axis=1, tiled=True)[0]
    w_down = lax.all_gather(w_down, "dp", axis=2, tiled=True)[0]
    chosen, weights = selectors(expert_ids, gate_probs, experts)

    def rank_at(step):
        return lax.rem(me + step, ranks)

    def send_up(value, step):
        return lax.ppermute(value, "tensor", [(i, (i + step) % ranks) for i in range(ranks)])

    share = width // ranks
    shared = round(2 * share / 3 / LANES) * LANES
    direct_at = ranks * shared

    def placed(features):
        return jnp.dot(chosen, features, preferred_element_type=jnp.float32).astype(jnp.bfloat16)

    mine = lax.dynamic_slice_in_dim(tokens, me * shared, shared, axis=1)
    own = swap(placed(mine), experts)
    direct = swap(placed(tokens[:, direct_at:]), experts)
    sums = lift(own, me * shared, w_gate, w_up)
    pieces, starts = [], []
    for step in range(1, ranks):
        pieces.append(send_up(own, ranks - step))
        starts.append(rank_at(step) * shared)
    pieces.append(direct)
    starts.append(jnp.int32(direct_at))
    reduced = round(share * 9 / 16 / 128) * 128
    early = share - reduced
    columns = [jnp.int32(rank * share) for rank in range(ranks)]
    hidden, partial = finish(pieces, starts, w_gate, w_up, sums, w_down, columns, early)
    returned = swap(partial, experts)
    owned = drop(hidden, w_down, me * share + early, reduced, jnp.float32)
    for step in range(1, ranks):
        sent = drop(hidden, w_down, rank_at(step) * share + early, reduced, jnp.bfloat16)
        owned = owned + send_up(sent, step).astype(jnp.float32)
    first = mix(weights, returned)

    def part_of(rank):
        return lax.dynamic_slice_in_dim(first, rank * early, early, axis=1)

    mixed = part_of(me)
    for step in range(1, ranks):
        mixed = mixed + send_up(part_of(rank_at(step)), step)
    late = mix(weights, swap(owned.astype(jnp.bfloat16), experts))
    return jnp.concatenate([mixed.astype(jnp.bfloat16), late.astype(jnp.bfloat16)], axis=1)


def solution(mesh):
    placed = (
        P(("groups", "dp", "expert"), None),
        P(("groups", "dp", "expert"), None),
        P(("groups", "dp", "expert"), None),
        P("expert", "dp", "tensor"),
        P("expert", "dp", "tensor"),
        P("expert", "tensor", "dp"),
    )
    return jax.shard_map(
        on_device,
        mesh=mesh,
        in_specs=placed,
        out_specs=P(("groups", "dp", "expert"), "tensor"),
        check_vma=False,
    )
```

time: 164 us -> 198 us (1.21)
  waiting for transfers between devices: 64.1 us -> 96.2 us
  blocking collectives: 0 us -> 27.2 us
  local copies, waits for them, and re-layouts: 18.1 us -> 5.27 us
  starting transfers between devices: 26.2 us -> 17.1 us
  matrix products: 11.2 us -> 7.5 us
    all_to_all x4 -> x3, waiting for transfers between devices: 28.9 us -> 68.1 us  [swap(): lax.all_to_all(value.reshape(experts, slots // experts, width), 'expert',...]
    all_to_all x0 -> x1, blocking collectives: none -> 27.2 us  [swap(): lax.all_to_all(value.reshape(experts, slots // experts, width), 'expert',...]
    unnamed x20 -> x10, local copies, waits for them, and re-layouts: 18 us -> 5.14 us
    pallas_call x1, Pallas kernels: 13.7 us -> 23.2 us  [finish(): pl.pallas_call(kernel, out_shape=[jax.ShapeDtypeStruct((rows, hidden), jn...]
    all_to_all x4 -> x3, starting transfers between devices: 25.3 us -> 16 us  [swap(): lax.all_to_all(value.reshape(experts, slots // experts, width), 'expert',...]
    pallas_call x2 -> x1, Pallas kernels: 17.2 us -> 9.63 us  [lift(): pl.pallas_call(kernel, out_shape=[jax.ShapeDtypeStruct((rows, hidden), jn...]
    ppermute x3, waiting for transfers between devices: 35.2 us -> 28.1 us  [send_up(): lax.ppermute(value, 'tensor', [(i, (i + step) % ranks) for i in range(ran...]
    dot_general x6, matrix products: 6.15 us -> 2.48 us  [mix(): lax.dot_general(w, returned, (((0,), (0,)), ((), ())), preferred_element_...]
  transfers between devices with their start and end apart: 7 -> 6, of which waited for: 5 -> 5; matrix products, arithmetic and copies ran while one was open for 5% -> 2% of each run, Pallas kernels for 16% -> 7%
where the time goes in v4:
time: 198 us; the launch traced here: 197 us
  waiting for transfers between devices  96.2 us (49%)
  Pallas kernels  41.1 us (21%)
  blocking collectives  27.2 us (14%)
  starting transfers between devices  17.1 us (9%)
  matrix products  7.5 us (4%)
  local copies, waits for them, and re-layouts  5.27 us (3%)
  other arithmetic  2.04 us (1%)
    all_to_all x3, waiting for transfers between devices, swap(): lax.all_to_all(value.reshape(experts, slots // experts, width), 'expert',...  68.1 us
    ppermute x3, waiting for transfers between devices, send_up(): lax.ppermute(value, 'tensor', [(i, (i + step) % ranks) for i in range(ran...  28.1 us
    all_to_all x1, blocking collectives, swap(): lax.all_to_all(value.reshape(experts, slots // experts, width), 'expert',...  27.2 us
    pallas_call x1, Pallas kernels, finish(): pl.pallas_call(kernel, out_shape=[jax.ShapeDtypeStruct((rows, hidden), jn...  23.2 us
    all_to_all x3, starting transfers between devices, swap(): lax.all_to_all(value.reshape(experts, slots // experts, width), 'expert',...  16 us
    pallas_call x1, Pallas kernels, lift(): pl.pallas_call(kernel, out_shape=[jax.ShapeDtypeStruct((rows, hidden), jn...  9.63 us
    pallas_call x2, Pallas kernels, drop(): pl.pallas_call(kernel, out_shape=jax.ShapeDtypeStruct((rows, width), dtyp...  8.31 us
    unnamed x10, local copies, waits for them, and re-layouts  5.14 us
  transfers between devices with their start and end apart: 6, of which 5 were waited for; matrix products, arithmetic and copies ran while one was open for 2% of the time, Pallas kernels for 7%

profile of v4, /device:TPU:11, one launch (start us, length us, event | category | flops | bytes accessed | tf_op | source)
XLA Modules:
  0.0 196.7 jit_solution(17512262779561330288)
XLA Ops:
  0.0 0.7 fusion.48
  1.1 2.3 %convolution_convert_fusion = bf16[384,1280]{1,0:T(8,128)(2,1)} fusion(pred[384,128]{1,0:T(32,128)(4,1)S(1)} %fusion.12, bf16[128,4096]{1,0:T(8,128)(2,1)} %param.6, s32[]{:T(128)S(6)} %select_n.52), kind=kOutput, calls=%fused_computation | convolution fusion | flops 126320640 | bytes 1359876 | tf_op jit(solution)/shard_map/dot_general | solution.py:282
  3.5 6.6 %all-to-all-start = ((bf16[16,24,1280]{2,1,0:T(8,128)(2,1)}), bf16[16,24,1280]{2,1,0:T(8,128)(2,1)S(1)}, u32[]{:S(2)}, u32[]{:S(2)}) async-start(bf16[16,24,1280]{2,1,0:T(8,128)(2,1)} %bitcast.5), calls=%async_computation | async-start | bytes 1966080 | tf_op jit(solution)/shard_map/all_to_all | solution.py:243
  10.1 2.5 %convolution_convert_fusion.1 = bf16[384,1536]{1,0:T(8,128)(2,1)} fusion(pred[384,128]{1,0:T(32,128)(4,1)S(1)} %fusion.12, bf16[128,4096]{1,0:T(8,128)(2,1)} %param.6), kind=kOutput, calls=%fused_computation.1 | convolution fusion | flops 151584768 | bytes 1622016 | tf_op jit(solution)/shard_map/dot_general | solution.py:282
  12.6 21.0 %all-to-all-done = bf16[16,24,1280]{2,1,0:T(8,128)(2,1)S(1)} async-done(((bf16[16,24,1280]{2,1,0:T(8,128)(2,1)}), bf16[16,24,1280]{2,1,0:T(8,128)(2,1)S(1)}, u32[]{:S(2)}, u32[]{:S(2)}) %all-to-all-start) | async-done | bytes 983072 | tf_op jit(solution)/shard_map/all_to_all | solution.py:243
  33.6 4.9 %all-to-all-start.1 = ((bf16[16,24,1536]{2,1,0:T(8,128)(2,1)}), bf16[16,24,1536]{2,1,0:T(8,128)(2,1)S(1)}, u32[]{:S(2)}, u32[]{:S(2)}) async-start(bf16[16,24,1536]{2,1,0:T(8,128)(2,1)} %bitcast.62), calls=%async_computation.1 | async-start | bytes 2359296 | tf_op jit(solution)/shard_map/all_to_all | solution.py:243
  38.8 9.6 %lift.1 = (f32[384,1792]{1,0:T(8,128)S(1)}, f32[384,1792]{1,0:T(8,128)}) custom-call(s32[1]{0:T(128)} %bitcast.12.at, bf16[384,1280]{1,0:T(8,128)(2,1)S(1)} %bitcast.54, bf16[4096,1792]{1,0:T(8,128)(2,1)} %bitcast.58, bf16[4096,1792]{1,0:T(8,128)(2,1)} %bitcast.60), custom_call_target="tpu_custom_call" | custom-call | flops 3523215360 | bytes 9175040 | tf_op jit(solution)/shard_map/lift/pallas_call | solution.py:118
  48.5 1.6 copy-done
  50.0 16.0 %all-to-all-done.1 = bf16[16,24,1536]{2,1,0:T(8,128)(2,1)S(1)} async-done(((bf16[16,24,1536]{2,1,0:T(8,128)(2,1)}), bf16[16,24,1536]{2,1,0:T(8,128)(2,1)S(1)}, u32[]{:S(2)}, u32[]{:S(2)}) %all-to-all-start.1) | async-done | bytes 1179680 | tf_op jit(solution)/shard_map/all_to_all | solution.py:243
  66.0 1.8 copy-done.1
  67.8 1.8 copy-done.2
  69.6 23.2 %finish.1 = (bf16[384,1792]{1,0:T(8,128)(2,1)S(1)}, bf16[384,1792]{1,0:T(8,128)(2,1)}) custom-call(s32[4]{0:T(128)S(1)} %pad_add_fusion.at, bf16[384,1280]{1,0:T(8,128)(2,1)S(1)} %collective-permute-done.refs_0_, bf16[384,1536]{1,0:T(8,128)(2,1)S(1)} %bitcast.52, bf16[4096,1792]{1,0:T(8,128)(2,1)} %bitcast.59, bf16[4096,1792]{1,0:T(8,128)(2,1)} %bitcast.61, ...), custom_call_target="tpu_custom_call" | custom-call | flops 10217324544 | bytes 26607616 | tf_op jit(solution)/shard_map/finish/pallas_call | solution.py:163
  92.8 4.2 %drop.3 = bf16[384,1152]{1,0:T(8,128)(2,1)S(1)} custom-call(s32[1]{0:T(128)} %bitcast.18.at, bf16[384,1792]{1,0:T(8,128)(2,1)S(1)} %get-tuple-element.12.hidden, bf16[1792,4096]{1,0:T(8,128)(2,1)} %bitcast.56), custom_call_target="tpu_custom_call" | custom-call | flops 1585446912 | bytes 4128768 | tf_op jit(solution)/shard_map/drop/pallas_call | solution.py:201
  97.0 0.4 collective-permute-start.2
  97.4 4.2 %drop.2 = f32[384,1152]{1,0:T(8,128)S(1)} custom-call(s32[1]{0:T(128)} %bitcast.17.at, bf16[384,1792]{1,0:T(8,128)(2,1)S(1)} %get-tuple-element.12.hidden, bf16[1792,4096]{1,0:T(8,128)(2,1)} %bitcast.57), custom_call_target="tpu_custom_call" | custom-call | flops 1585446912 | bytes 4128768 | tf_op jit(solution)/shard_map/drop/pallas_call | solution.py:201
  101.6 16.9 %collective-permute-done.2 = bf16[384,1152]{1,0:T(8,128)(2,1)S(1)} collective-permute-done((bf16[384,1152]{1,0:T(8,128)(2,1)S(1)}, bf16[384,1152]{1,0:T(8,128)(2,1)S(1)}, u32[]{:S(2)}, u32[]{:S(2)}) %collective-permute-start.2) | collective-permute-done | bytes 884768 | tf_op jit(solution)/shard_map/ppermute | solution.py:275
  118.7 27.2 %all_to_all.20 = bf16[16,24,1152]{2,1,0:T(8,128)(2,1)S(1)} all-to-all(bf16[16,24,1152]{2,1,0:T(8,128)(2,1)S(1)} %bitcast.63), channel_id=1, replica_groups=mesh['groups'=1,'dp'=1,'expert'=16,'tensor'=2] {'expert'}, dimensions={0} | all-to-all | bytes 1769472 | tf_op jit(solution)/shard_map/all_to_all | solution.py:243
  146.0 4.5 %all-to-all-start.2 = ((bf16[16,24,1792]{2,1,0:T(8,128)(2,1)}), bf16[16,24,1792]{2,1,0:T(8,128)(2,1)S(1)}, u32[]{:S(2)}, u32[]{:S(2)}) async-start(bf16[16,24,1792]{2,1,0:T(8,128)(2,1)} %bitcast.13), calls=%async_computation.2 | async-start | bytes 2752512 | tf_op jit(solution)/shard_map/all_to_all | solution.py:243
  150.9 31.1 %all-to-all-done.2 = bf16[16,24,1792]{2,1,0:T(8,128)(2,1)S(1)} async-done(((bf16[16,24,1792]{2,1,0:T(8,128)(2,1)}), bf16[16,24,1792]{2,1,0:T(8,128)(2,1)S(1)}, u32[]{:S(2)}, u32[]{:S(2)}) %all-to-all-start.2) | async-done | bytes 1376288 | tf_op jit(solution)/shard_map/all_to_all | solution.py:243
  181.9 0.4 convolution_bitcast_fusion.3
  182.4 0.4 convolution_bitcast_fusion.4
  182.8 0.5 fusion.3
  184.6 11.2 %collective-permute-done.1 = f32[128,896]{1,0:T(8,128)S(1)} collective-permute-done((f32[128,896]{1,0:T(8,128)S(1)}, f32[128,896]{1,0:T(8,128)S(1)}, u32[]{:S(2)}, u32[]{:S(2)}) %collective-permute-start.1) | collective-permute-done | bytes 458784 | tf_op jit(solution)/shard_map/ppermute | solution.py:275
  195.8 0.9 pad_maximum_fusion
  (24 shorter events, 2.7 us)
Async XLA Ops:
  3.5 30.1 %all-to-all-start = ((bf16[16,24,1280]{2,1,0:T(8,128)(2,1)}), bf16[16,24,1280]{2,1,0:T(8,128)(2,1)S(1)}, u32[]{:S(2)}, u32[]{:S(2)}) async-start(bf16[16,24,1280]{2,1,0:T(8,128)(2,1)} %bitcast.5), calls=%async_computation | async-start | bytes 1966080 | tf_op jit(solution)/shard_map/all_to_all | solution.py:243
  33.6 32.4 %all-to-all-start.1 = ((bf16[16,24,1536]{2,1,0:T(8,128)(2,1)}), bf16[16,24,1536]{2,1,0:T(8,128)(2,1)S(1)}, u32[]{:S(2)}, u32[]{:S(2)}) async-start(bf16[16,24,1536]{2,1,0:T(8,128)(2,1)} %bitcast.62), calls=%async_computation.1 | async-start | bytes 2359296 | tf_op jit(solution)/shard_map/all_to_all | solution.py:243
  38.5 27.6 %collective-permute-start = (bf16[384,1280]{1,0:T(8,128)(2,1)S(1)}, bf16[384,1280]{1,0:T(8,128)(2,1)S(1)}, u32[]{:S(2)}, u32[]{:S(2)}) collective-permute-start(bf16[384,1280]{1,0:T(8,128)(2,1)S(1)} %bitcast.53), channel_id=1, source_target_pairs={{0,1},{1,0},{2,3},{3,2},{4,5},{5,4},{6,7},{7,6},{8,9},{9,8},{10,11... | collective-permute-start | bytes 2949128 | tf_op jit(solution)/shard_map/ppermute | solution.py:275
  48.4 1.6 copy-start
  66.0 1.8 copy-start.1
  67.8 1.8 copy-start.2
  97.0 21.5 %collective-permute-start.2 = (bf16[384,1152]{1,0:T(8,128)(2,1)S(1)}, bf16[384,1152]{1,0:T(8,128)(2,1)S(1)}, u32[]{:S(2)}, u32[]{:S(2)}) collective-permute-start(bf16[384,1152]{1,0:T(8,128)(2,1)S(1)} %drop.3), channel_id=1, source_target_pairs={{0,1},{1,0},{2,3},{3,2},{4,5},{5,4},{6,7},{7,6},{8,9},{9,8},{10,11... | collective-permute-start | bytes 2654216 | tf_op jit(solution)/shard_map/ppermute | solution.py:275
  145.9 4.5 %copy-start.3 = (s32[128,2]{0,1:T(2,128)S(1)}, s32[128,2]{0,1:T(2,128)}, u32[]{:S(2)}) copy-start(s32[128,2]{0,1:T(2,128)} %param.7) | copy-start | bytes 3076
  146.0 4.5 %copy-start.4 = (f32[128,2]{0,1:T(2,128)S(1)}, f32[128,2]{0,1:T(2,128)}, u32[]{:S(2)}) copy-start(f32[128,2]{0,1:T(2,128)} %param.8) | copy-start | bytes 3076
  146.0 36.0 %all-to-all-start.2 = ((bf16[16,24,1792]{2,1,0:T(8,128)(2,1)}), bf16[16,24,1792]{2,1,0:T(8,128)(2,1)S(1)}, u32[]{:S(2)}, u32[]{:S(2)}) async-start(bf16[16,24,1792]{2,1,0:T(8,128)(2,1)} %bitcast.13), calls=%async_computation.2 | async-start | bytes 2752512 | tf_op jit(solution)/shard_map/all_to_all | solution.py:243
  183.4 12.4 %collective-permute-start.1 = (f32[128,896]{1,0:T(8,128)S(1)}, f32[128,896]{1,0:T(8,128)S(1)}, u32[]{:S(2)}, u32[]{:S(2)}) collective-permute-start(f32[128,896]{1,0:T(8,128)S(1)} %constant_dynamic-slice_fusion), channel_id=1, source_target_pairs={{0,1},{1,0},{2,3},{3,2},{4,5},{5,4},{6,7},{7,6},{8,9},{9,8},{10,11... | collective-permute-start | bytes 1376264 | tf_op jit(solution)/shard_map/ppermute | solution.py:275

commit v5 on v4

--- a/solution.py
+++ b/solution.py
@@ -55,9 +55,9 @@
         @pl.loop(0, gate.shape[1] // tile)
         def _(n):
             across = pl.ds(pl.multiple_of(n * tile, 128), tile)
-            x = piece[:, at]
-            g = jnp.dot(x, gate_rows[at, across], preferred_element_type=jnp.float32)
-            u = jnp.dot(x, up_rows[at, across], preferred_element_type=jnp.float32)
+            both = jnp.concatenate([gate_rows[at, across], up_rows[at, across]], axis=1)
+            product = jnp.dot(piece[:, at], both, preferred_element_type=jnp.float32)
+            g, u = product[:, :tile], product[:, tile:]
             if before is not None:
                 g = g + before[0][:, across]
                 u = u + before[1][:, across]
@@ -72,8 +72,8 @@
     for copy in copies:
         copy.wait()
     width = weight.shape[1]
-    for at in range(0, width, LANES):
-        end = min(at + LANES, width)
+    for at in range(0, width, 2 * LANES):
+        end = min(at + 2 * LANES, width)
         value = jnp.dot(hidden[...], weight[:, at:end], preferred_element_type=jnp.float32)
         out[:, start + at : start + end] = value.astype(out.dtype)
 
@@ -212,10 +212,11 @@
     )(jnp.reshape(start, (1,)).astype(jnp.int32), hidden, w_down)
 
 
-def selectors(expert_ids, gate_probs, experts):
+def selectors(expert_ids, gate_probs, order):
+    experts = order.shape[0]
     rows = expert_ids.shape[0]
     blocks = rows // BLOCK
-    match = expert_ids.T[:, None, :] == jnp.arange(experts, dtype=jnp.int32)[None, :, None]
+    match = expert_ids.T[:, None, :] == order[None, :, None]
     named = jnp.any(match, axis=0)
     weight = jnp.sum(jnp.where(match, gate_probs.T[:, None, :], 0.0), axis=0)
     row = jnp.arange(rows, dtype=jnp.int32)
@@ -238,15 +239,39 @@
     return chosen, weights
 
 
-def swap(value, experts):
-    slots, width = value.shape
-    return lax.all_to_all(
-        value.reshape(experts, slots // experts, width),
-        "expert",
-        split_axis=0,
-        concat_axis=0,
-        tiled=True,
-    ).reshape(slots, width)
+def flip(value, bits):
+    size = lax.axis_size("expert")
+    return lax.ppermute(value, "expert", [(i, i ^ bits) for i in range(size)])
+
+
+def far_first(pairs):
+    return list(range(pairs - 1, 0, -1))
+
+
+def dispatch(even, odd, pairs):
+    slots = even.shape[0] // pairs
+    other = flip(odd, 1)
+
+    def both(j):
+        at = slice(j * slots, (j + 1) * slots)
+        return jnp.concatenate([even[at], other[at]], axis=0)
+
+    arrived = {j: flip(both(j), 2 * j) for j in far_first(pairs)}
+    arrived[0] = both(0)
+    return jnp.concatenate([arrived[j] for j in range(pairs)], axis=0)
+
+
+def give_back(value, pairs):
+    slots = value.shape[0] // (2 * pairs)
+
+    def of(j):
+        return value[2 * j * slots : 2 * (j + 1) * slots]
+
+    arrived = {j: flip(of(j), 2 * j) for j in far_first(pairs)}
+    arrived[0] = of(0)
+    even = jnp.concatenate([arrived[j][:slots] for j in range(pairs)], axis=0)
+    odd = jnp.concatenate([arrived[j][slots:] for j in range(pairs)], axis=0)
+    return jnp.concatenate([even, flip(odd, 1)], axis=0)
 
 
 def mix(weights, returned):
@@ -266,7 +291,12 @@
     w_gate = lax.all_gather(w_gate, "dp", axis=1, tiled=True)[0]
     w_up = lax.all_gather(w_up, "dp", axis=1, tiled=True)[0]
     w_down = lax.all_gather(w_down, "dp", axis=2, tiled=True)[0]
-    chosen, weights = selectors(expert_ids, gate_probs, experts)
+    pairs = experts // 2
+    near = jnp.arange(experts, dtype=jnp.int32)
+    near = jnp.where(near < pairs, 2 * near, 2 * (near - pairs) + 1)
+    order = near ^ lax.axis_index("expert").astype(jnp.int32)
+    chosen, weights = selectors(expert_ids, gate_probs, order)
+    half = chosen.shape[0] // 2
 
     def rank_at(step):
         return lax.rem(me + step, ranks)
@@ -279,11 +309,15 @@
     direct_at = ranks * shared
 
     def placed(features):
-        return jnp.dot(chosen, features, preferred_element_type=jnp.float32).astype(jnp.bfloat16)
+        def rows_of(part):
+            value = jnp.dot(part, features, preferred_element_type=jnp.float32)
+            return value.astype(jnp.bfloat16)
+
+        return dispatch(rows_of(chosen[:half]), rows_of(chosen[half:]), pairs)
 
     mine = lax.dynamic_slice_in_dim(tokens, me * shared, shared, axis=1)
-    own = swap(placed(mine), experts)
-    direct = swap(placed(tokens[:, direct_at:]), experts)
+    own = placed(mine)
+    direct = placed(tokens[:, direct_at:])
     sums = lift(own, me * shared, w_gate, w_up)
     pieces, starts = [], []
     for step in range(1, ranks):
@@ -295,7 +329,7 @@
     early = share - reduced
     columns = [jnp.int32(rank * share) for rank in range(ranks)]
     hidden, partial = finish(pieces, starts, w_gate, w_up, sums, w_down, columns, early)
-    returned = swap(partial, experts)
+    returned = give_back(partial, pairs)
     owned = drop(hidden, w_down, me * share + early, reduced, jnp.float32)
     for step in range(1, ranks):
         sent = drop(hidden, w_down, rank_at(step) * share + early, reduced, jnp.bfloat16)
@@ -308,7 +342,7 @@
     mixed = part_of(me)
     for step in range(1, ranks):
         mixed = mixed + send_up(part_of(rank_at(step)), step)
-    late = mix(weights, swap(owned.astype(jnp.bfloat16), experts))
+    late = mix(weights, give_back(owned.astype(jnp.bfloat16), pairs))
     return jnp.concatenate([mixed.astype(jnp.bfloat16), late.astype(jnp.bfloat16)], axis=1)
 
 

time: 198 us -> 187 us (0.944)
  blocking collectives: 27.2 us -> 0 us
  starting transfers between devices: 17.1 us -> 42 us
  waiting for transfers between devices: 96.2 us -> 80 us
  local copies, waits for them, and re-layouts: 5.27 us -> 14.9 us
    all_to_all x3 -> x0, waiting for transfers between devices: 68.1 us -> none  [swap(): lax.all_to_all(value.reshape(experts, slots // experts, width), 'expert',...]
    ppermute x0 -> x32, waiting for transfers between devices: none -> 60.2 us  [flip(): return lax.ppermute(value, 'expert', [(i, i ^ bits) for i in range(size)])]
    ppermute x0 -> x32, starting transfers between devices: none -> 40.1 us  [flip(): return lax.ppermute(value, 'expert', [(i, i ^ bits) for i in range(size)])]
    all_to_all x1 -> x0, blocking collectives: 27.2 us -> none  [swap(): lax.all_to_all(value.reshape(experts, slots // experts, width), 'expert',...]
    all_to_all x3 -> x0, starting transfers between devices: 16 us -> none  [swap(): lax.all_to_all(value.reshape(experts, slots // experts, width), 'expert',...]
    ppermute x3, waiting for transfers between devices: 28.1 us -> 19.8 us  [send_up(): lax.ppermute(value, 'tensor', [(i, (i + step) % ranks) for i in range(ran...]
    unnamed x10 -> x38, local copies, waits for them, and re-layouts: 5.14 us -> 10.9 us
    concatenate x0 -> x6, local copies, waits for them, and re-layouts: none -> 2.48 us  [the longest x2 1.28 us: give_back(): odd = jnp.concatenate([arrived[j][slots:] for j in range(pairs)], axis=0)]
  transfers between devices with their start and end apart: 6 -> 35, of which waited for: 5 -> 17; matrix products, arithmetic and copies ran while one was open for 2% -> 9% of each run, Pallas kernels for 7% -> 10%
where the time goes in v5:
time: 187 us; the launch traced here: 186 us
  waiting for transfers between devices  80 us (43%)
  starting transfers between devices  42 us (22%)
  Pallas kernels  40 us (21%)
  local copies, waits for them, and re-layouts  14.9 us (8%)
  matrix products  6.4 us (3%)
  other arithmetic  2.44 us (1%)
    ppermute x32, waiting for transfers between devices, flip(): return lax.ppermute(value, 'expert', [(i, i ^ bits) for i in range(size)])  60.2 us
    ppermute x32, starting transfers between devices, flip(): return lax.ppermute(value, 'expert', [(i, i ^ bits) for i in range(size)])  40.1 us
    pallas_call x1, Pallas kernels, finish(): pl.pallas_call(kernel, out_shape=[jax.ShapeDtypeStruct((rows, hidden), jn...  22.1 us
    ppermute x3, waiting for transfers between devices, send_up(): lax.ppermute(value, 'tensor', [(i, (i + step) % ranks) for i in range(ran...  19.8 us
    unnamed x38, local copies, waits for them, and re-layouts  10.9 us
    pallas_call x1, Pallas kernels, lift(): pl.pallas_call(kernel, out_shape=[jax.ShapeDtypeStruct((rows, hidden), jn...  9.6 us
    pallas_call x2, Pallas kernels, drop(): pl.pallas_call(kernel, out_shape=jax.ShapeDtypeStruct((rows, width), dtyp...  8.31 us
    dot_general x4, matrix products, rows_of(): value = jnp.dot(part, features, preferred_element_type=jnp.float32)  3.79 us
  transfers between devices with their start and end apart: 35, of which 17 were waited for; matrix products, arithmetic and copies ran while one was open for 9% of the time, Pallas kernels for 10%

profile of v5, /device:TPU:11, one launch (start us, length us, event | category | flops | bytes accessed | tf_op | source)
XLA Modules:
  0.0 186.3 jit_solution(194566312124775813)
XLA Ops:
  1.1 2.1 %convolution_convert_fusion = bf16[192,1536]{1,0:T(8,128)(2,1)} fusion(pred[192,128]{1,0:T(8,128)(4,1)S(1)} %bitcast.61, bf16[128,4096]{1,0:T(8,128)(2,1)} %param.6), kind=kOutput, calls=%fused_computation.2 | convolution fusion | flops 75792384 | bytes 1007616 | tf_op jit(solution)/shard_map/dot_general | solution.py:313
  10.0 2.4 %collective-permute-start.4 = (bf16[48,1280]{1,0:T(8,128)(2,1)S(1)}, bf16[48,1280]{1,0:T(8,128)(2,1)S(1)}, u32[]{:S(2)}, u32[]{:S(2)}) collective-permute-start(bf16[48,1280]{1,0:T(8,128)(2,1)S(1)} %pad_maximum_fusion.11), channel_id=1, source_target_pairs={{0,16},{2,18},{4,20},{6,22},{8,24},{10,26},{12,28},{14,30},{16,0},... | collective-permute-start | bytes 368648 | tf_op jit(solution)/shard_map/ppermute | solution.py:244
  21.2 6.0 %collective-permute-done.5 = bf16[48,1280]{1,0:T(8,128)(2,1)S(1)} collective-permute-done((bf16[48,1280]{1,0:T(8,128)(2,1)S(1)}, bf16[48,1280]{1,0:T(8,128)(2,1)S(1)}, u32[]{:S(2)}, u32[]{:S(2)}) %collective-permute-start.5) | collective-permute-done | bytes 122912 | tf_op jit(solution)/shard_map/ppermute | solution.py:244
  27.2 3.4 %collective-permute-done.6 = bf16[48,1280]{1,0:T(8,128)(2,1)S(1)} collective-permute-done((bf16[48,1280]{1,0:T(8,128)(2,1)S(1)}, bf16[48,1280]{1,0:T(8,128)(2,1)S(1)}, u32[]{:S(2)}, u32[]{:S(2)}) %collective-permute-start.6) | collective-permute-done | bytes 122912 | tf_op jit(solution)/shard_map/ppermute | solution.py:244
  31.8 2.4 %collective-permute-done.7 = bf16[48,1280]{1,0:T(8,128)(2,1)S(1)} collective-permute-done((bf16[48,1280]{1,0:T(8,128)(2,1)S(1)}, bf16[48,1280]{1,0:T(8,128)(2,1)S(1)}, u32[]{:S(2)}, u32[]{:S(2)}) %collective-permute-start.7) | collective-permute-done | bytes 122912 | tf_op jit(solution)/shard_map/ppermute | solution.py:244
  34.2 9.6 %lift.1 = (f32[384,1792]{1,0:T(8,128)S(1)}, f32[384,1792]{1,0:T(8,128)}) custom-call(s32[1]{0:T(128)} %bitcast.11.at, bf16[384,1280]{1,0:T(8,128)(2,1)S(1)} %constant_dynamic-update-slice_fusion.piece, bf16[4096,1792]{1,0:T(8,128)(2,1)} %bitcast.55, bf16[4096,1792]{1,0:T(8,128)(2,1)} %bitcast.57), custom_call_target="tpu_custom_call" | custom-call | flops 3523215360 | bytes 9175040 | tf_op jit(solution)/shard_map/lift/pallas_call | solution.py:118
  46.3 4.1 %collective-permute-done.15 = bf16[48,1536]{1,0:T(8,128)(2,1)S(1)} collective-permute-done((bf16[48,1536]{1,0:T(8,128)(2,1)S(1)}, bf16[48,1536]{1,0:T(8,128)(2,1)S(1)}, u32[]{:S(2)}, u32[]{:S(2)}) %collective-permute-start.15) | collective-permute-done | bytes 147488 | tf_op jit(solution)/shard_map/ppermute | solution.py:244
  50.4 4.1 %collective-permute-done.16 = bf16[48,1536]{1,0:T(8,128)(2,1)S(1)} collective-permute-done((bf16[48,1536]{1,0:T(8,128)(2,1)S(1)}, bf16[48,1536]{1,0:T(8,128)(2,1)S(1)}, u32[]{:S(2)}, u32[]{:S(2)}) %collective-permute-start.16) | collective-permute-done | bytes 147488 | tf_op jit(solution)/shard_map/ppermute | solution.py:244
  54.5 6.7 %collective-permute-done.8.refs_0_ = bf16[384,1280]{1,0:T(8,128)(2,1)S(1)} collective-permute-done((bf16[384,1280]{1,0:T(8,128)(2,1)S(1)}, bf16[384,1280]{1,0:T(8,128)(2,1)S(1)}, u32[]{:S(2)}, u32[]{:S(2)}) %collective-permute-start.8) | collective-permute-done | bytes 983072 | tf_op jit(solution)/shard_map/ppermute | solution.py:305
  63.0 22.1 %finish.1 = (bf16[384,1792]{1,0:T(8,128)(2,1)S(1)}, bf16[384,1792]{1,0:T(8,128)(2,1)S(1)}) custom-call(s32[4]{0:T(128)S(1)} %pad_add_fusion.at, bf16[384,1280]{1,0:T(8,128)(2,1)S(1)} %collective-permute-done.8.refs_0_, bf16[384,1536]{1,0:T(8,128)(2,1)S(1)} %constant_dynamic-update-slice_fusion.9.refs_1_, bf16[4096,1792]{1,0:T(8,128)(2,1)} %bitcast.56, ...), custom_call_target="tpu_custom_call" | custom-call | flops 10217324544 | bytes 26607616 | tf_op jit(solution)/shard_map/finish/pallas_call | solution.py:163
  85.3 2.1 %collective-permute-start.17 = (bf16[48,1792]{1,0:T(8,128)(2,1)S(1)}, bf16[48,1792]{1,0:T(8,128)(2,1)S(1)}, u32[]{:S(2)}, u32[]{:S(2)}) collective-permute-start(bf16[48,1792]{1,0:T(8,128)(2,1)S(1)} %get-tuple-element.21), channel_id=1, source_target_pairs={{0,4},{2,6},{4,0},{6,2},{8,12},{10,14},{12,8},{14,10},{16,20},{18,... | collective-permute-start | bytes 516104 | tf_op jit(solution)/shard_map/ppermute | solution.py:244
  88.1 6.2 %collective-permute-start.18 = (bf16[48,1792]{1,0:T(8,128)(2,1)S(1)}, bf16[48,1792]{1,0:T(8,128)(2,1)S(1)}, u32[]{:S(2)}, u32[]{:S(2)}) collective-permute-start(bf16[48,1792]{1,0:T(8,128)(2,1)S(1)} %get-tuple-element.20), channel_id=1, source_target_pairs={{0,8},{2,10},{4,12},{6,14},{8,0},{10,2},{12,4},{14,6},{16,24},{18,... | collective-permute-start | bytes 516104 | tf_op jit(solution)/shard_map/ppermute | solution.py:244
  95.4 2.4 %collective-permute-start.21 = (bf16[48,1792]{1,0:T(8,128)(2,1)S(1)}, bf16[48,1792]{1,0:T(8,128)(2,1)S(1)}, u32[]{:S(2)}, u32[]{:S(2)}) collective-permute-start(bf16[48,1792]{1,0:T(8,128)(2,1)S(1)} %get-tuple-element.17), channel_id=1, source_target_pairs={{0,20},{2,22},{4,16},{6,18},{8,28},{10,30},{12,24},{14,26},{16,4},... | collective-permute-start | bytes 516104 | tf_op jit(solution)/shard_map/ppermute | solution.py:244
  98.7 2.1 %collective-permute-start.23 = (bf16[48,1792]{1,0:T(8,128)(2,1)S(1)}, bf16[48,1792]{1,0:T(8,128)(2,1)S(1)}, u32[]{:S(2)}, u32[]{:S(2)}) collective-permute-start(bf16[48,1792]{1,0:T(8,128)(2,1)S(1)} %get-tuple-element.15), channel_id=1, source_target_pairs={{0,28},{2,30},{4,24},{6,26},{8,20},{10,22},{12,16},{14,18},{16,12}... | collective-permute-start | bytes 516104 | tf_op jit(solution)/shard_map/ppermute | solution.py:244
  103.4 18.6 %collective-permute-done.22 = bf16[48,1792]{1,0:T(8,128)(2,1)S(1)} collective-permute-done((bf16[48,1792]{1,0:T(8,128)(2,1)S(1)}, bf16[48,1792]{1,0:T(8,128)(2,1)S(1)}, u32[]{:S(2)}, u32[]{:S(2)}) %collective-permute-start.22) | collective-permute-done | bytes 172064 | tf_op jit(solution)/shard_map/ppermute | solution.py:244
  122.6 3.5 %collective-permute-done.23 = bf16[48,1792]{1,0:T(8,128)(2,1)S(1)} collective-permute-done((bf16[48,1792]{1,0:T(8,128)(2,1)S(1)}, bf16[48,1792]{1,0:T(8,128)(2,1)S(1)}, u32[]{:S(2)}, u32[]{:S(2)}) %collective-permute-start.23) | collective-permute-done | bytes 172064 | tf_op jit(solution)/shard_map/ppermute | solution.py:244
  126.8 2.8 %collective-permute-start.24 = (bf16[192,1792]{1,0:T(8,128)(2,1)}, bf16[192,1792]{1,0:T(8,128)(2,1)}, u32[]{:S(2)}, u32[]{:S(2)}) collective-permute-start(bf16[192,1792]{1,0:T(8,128)(2,1)} %get-tuple-element.63), channel_id=1, source_target_pairs={{0,2},{2,0},{4,6},{6,4},{8,10},{10,8},{12,14},{14,12},{16,18},{18,... | collective-permute-start | bytes 2064392 | tf_op jit(solution)/shard_map/ppermute | solution.py:244
  129.9 4.2 %drop.3 = bf16[384,1152]{1,0:T(8,128)(2,1)S(1)} custom-call(s32[1]{0:T(128)} %bitcast.15.at, bf16[384,1792]{1,0:T(8,128)(2,1)S(1)} %get-tuple-element.12.hidden, bf16[1792,4096]{1,0:T(8,128)(2,1)} %bitcast.53), custom_call_target="tpu_custom_call" | custom-call | flops 1585446912 | bytes 4128768 | tf_op jit(solution)/shard_map/drop/pallas_call | solution.py:201
  134.5 4.2 %drop.2 = f32[384,1152]{1,0:T(8,128)S(1)} custom-call(s32[1]{0:T(128)} %bitcast.14.at, bf16[384,1792]{1,0:T(8,128)(2,1)S(1)} %get-tuple-element.12.hidden, bf16[1792,4096]{1,0:T(8,128)(2,1)} %bitcast.54), custom_call_target="tpu_custom_call" | custom-call | flops 1585446912 | bytes 4128768 | tf_op jit(solution)/shard_map/drop/pallas_call | solution.py:201
  142.4 13.0 %collective-permute-done.26 = bf16[384,1152]{1,0:T(8,128)(2,1)S(1)} collective-permute-done((bf16[384,1152]{1,0:T(8,128)(2,1)S(1)}, bf16[384,1152]{1,0:T(8,128)(2,1)S(1)}, u32[]{:S(2)}, u32[]{:S(2)}) %collective-permute-start.26) | collective-permute-done | bytes 884768 | tf_op jit(solution)/shard_map/ppermute | solution.py:305
  159.7 2.7 %collective-permute-start.31 = (bf16[48,1152]{1,0:T(8,128)(2,1)S(1)}, bf16[48,1152]{1,0:T(8,128)(2,1)S(1)}, u32[]{:S(2)}, u32[]{:S(2)}) collective-permute-start(bf16[48,1152]{1,0:T(8,128)(2,1)S(1)} %get-tuple-element.26), channel_id=1, source_target_pairs={{0,20},{2,22},{4,16},{6,18},{8,28},{10,30},{12,24},{14,26},{16,4},... | collective-permute-start | bytes 331784 | tf_op jit(solution)/shard_map/ppermute | solution.py:244
  166.3 7.8 %collective-permute-done.31 = bf16[48,1152]{1,0:T(8,128)(2,1)S(1)} collective-permute-done((bf16[48,1152]{1,0:T(8,128)(2,1)S(1)}, bf16[48,1152]{1,0:T(8,128)(2,1)S(1)}, u32[]{:S(2)}, u32[]{:S(2)}) %collective-permute-start.31) | collective-permute-done | bytes 110624 | tf_op jit(solution)/shard_map/ppermute | solution.py:244
  177.3 2.6 %collective-permute-done.33 = bf16[48,1152]{1,0:T(8,128)(2,1)S(1)} collective-permute-done((bf16[48,1152]{1,0:T(8,128)(2,1)S(1)}, bf16[48,1152]{1,0:T(8,128)(2,1)S(1)}, u32[]{:S(2)}, u32[]{:S(2)}) %collective-permute-start.33) | collective-permute-done | bytes 110624 | tf_op jit(solution)/shard_map/ppermute | solution.py:244
  180.5 2.1 %collective-permute-start.34 = (bf16[192,1152]{1,0:T(8,128)(2,1)}, bf16[192,1152]{1,0:T(8,128)(2,1)S(1)}, u32[]{:S(2)}, u32[]{:S(2)}) collective-permute-start(bf16[192,1152]{1,0:T(8,128)(2,1)} %get-tuple-element.77), channel_id=1, source_target_pairs={{0,2},{2,0},{4,6},{6,4},{8,10},{10,8},{12,14},{14,12},{16,18},{18,... | collective-permute-start | bytes 1327112 | tf_op jit(solution)/shard_map/ppermute | solution.py:244
  (140 shorter events, 48.6 us)
Async XLA Ops:
  3.3 9.2 %collective-permute-start.9 = (bf16[192,1536]{1,0:T(8,128)(2,1)}, bf16[192,1536]{1,0:T(8,128)(2,1)}, u32[]{:S(2)}, u32[]{:S(2)}) collective-permute-start(bf16[192,1536]{1,0:T(8,128)(2,1)} %convolution_convert_fusion), channel_id=1, source_target_pairs={{0,2},{2,0},{4,6},{6,4},{8,10},{10,8},{12,14},{14,12},{16,18},{18,... | collective-permute-start | bytes 1769480 | tf_op jit(solution)/shard_map/ppermute | solution.py:244
  8.5 7.8 %collective-permute-start.2 = (bf16[48,1280]{1,0:T(8,128)(2,1)S(1)}, bf16[48,1280]{1,0:T(8,128)(2,1)S(1)}, u32[]{:S(2)}, u32[]{:S(2)}) collective-permute-start(bf16[48,1280]{1,0:T(8,128)(2,1)S(1)} %pad_maximum_fusion.9), channel_id=1, source_target_pairs={{0,8},{2,10},{4,12},{6,14},{8,0},{10,2},{12,4},{14,6},{16,24},{18,... | collective-permute-start | bytes 368648 | tf_op jit(solution)/shard_map/ppermute | solution.py:244
  8.7 8.8 %collective-permute-start.3 = (bf16[48,1280]{1,0:T(8,128)(2,1)S(1)}, bf16[48,1280]{1,0:T(8,128)(2,1)S(1)}, u32[]{:S(2)}, u32[]{:S(2)}) collective-permute-start(bf16[48,1280]{1,0:T(8,128)(2,1)S(1)} %pad_maximum_fusion.10), channel_id=1, source_target_pairs={{0,12},{2,14},{4,8},{6,10},{8,4},{10,6},{12,0},{14,2},{16,28},{18,... | collective-permute-start | bytes 368648 | tf_op jit(solution)/shard_map/ppermute | solution.py:244
  10.0 9.2 %collective-permute-start.4 = (bf16[48,1280]{1,0:T(8,128)(2,1)S(1)}, bf16[48,1280]{1,0:T(8,128)(2,1)S(1)}, u32[]{:S(2)}, u32[]{:S(2)}) collective-permute-start(bf16[48,1280]{1,0:T(8,128)(2,1)S(1)} %pad_maximum_fusion.11), channel_id=1, source_target_pairs={{0,16},{2,18},{4,20},{6,22},{8,24},{10,26},{12,28},{14,30},{16,0},... | collective-permute-start | bytes 368648 | tf_op jit(solution)/shard_map/ppermute | solution.py:244
  12.5 14.8 %collective-permute-start.5 = (bf16[48,1280]{1,0:T(8,128)(2,1)S(1)}, bf16[48,1280]{1,0:T(8,128)(2,1)S(1)}, u32[]{:S(2)}, u32[]{:S(2)}) collective-permute-start(bf16[48,1280]{1,0:T(8,128)(2,1)S(1)} %pad_maximum_fusion.12), channel_id=1, source_target_pairs={{0,20},{2,22},{4,16},{6,18},{8,28},{10,30},{12,24},{14,26},{16,4},... | collective-permute-start | bytes 368648 | tf_op jit(solution)/shard_map/ppermute | solution.py:244
  14.9 15.8 %collective-permute-start.6 = (bf16[48,1280]{1,0:T(8,128)(2,1)S(1)}, bf16[48,1280]{1,0:T(8,128)(2,1)S(1)}, u32[]{:S(2)}, u32[]{:S(2)}) collective-permute-start(bf16[48,1280]{1,0:T(8,128)(2,1)S(1)} %pad_maximum_fusion.13), channel_id=1, source_target_pairs={{0,24},{2,26},{4,28},{6,30},{8,16},{10,18},{12,20},{14,22},{16,8},... | collective-permute-start | bytes 368648 | tf_op jit(solution)/shard_map/ppermute | solution.py:244
  16.3 17.9 %collective-permute-start.7 = (bf16[48,1280]{1,0:T(8,128)(2,1)S(1)}, bf16[48,1280]{1,0:T(8,128)(2,1)S(1)}, u32[]{:S(2)}, u32[]{:S(2)}) collective-permute-start(bf16[48,1280]{1,0:T(8,128)(2,1)S(1)} %pad_maximum_fusion.14), channel_id=1, source_target_pairs={{0,28},{2,30},{4,24},{6,26},{8,20},{10,22},{12,16},{14,18},{16,12}... | collective-permute-start | bytes 368648 | tf_op jit(solution)/shard_map/ppermute | solution.py:244
  17.5 26.3 %collective-permute-start.10 = (bf16[48,1536]{1,0:T(8,128)(2,1)S(1)}, bf16[48,1536]{1,0:T(8,128)(2,1)S(1)}, u32[]{:S(2)}, u32[]{:S(2)}) collective-permute-start(bf16[48,1536]{1,0:T(8,128)(2,1)S(1)} %pad_maximum_fusion.1), channel_id=1, source_target_pairs={{0,4},{2,6},{4,0},{6,2},{8,12},{10,14},{12,8},{14,10},{16,20},{18,... | collective-permute-start | bytes 442376 | tf_op jit(solution)/shard_map/ppermute | solution.py:244
  19.3 26.5 %collective-permute-start.11 = (bf16[48,1536]{1,0:T(8,128)(2,1)S(1)}, bf16[48,1536]{1,0:T(8,128)(2,1)S(1)}, u32[]{:S(2)}, u32[]{:S(2)}) collective-permute-start(bf16[48,1536]{1,0:T(8,128)(2,1)S(1)} %pad_maximum_fusion.2), channel_id=1, source_target_pairs={{0,8},{2,10},{4,12},{6,14},{8,0},{10,2},{12,4},{14,6},{16,24},{18,... | collective-permute-start | bytes 442376 | tf_op jit(solution)/shard_map/ppermute | solution.py:244
  27.2 18.7 %collective-permute-start.12 = (bf16[48,1536]{1,0:T(8,128)(2,1)S(1)}, bf16[48,1536]{1,0:T(8,128)(2,1)S(1)}, u32[]{:S(2)}, u32[]{:S(2)}) collective-permute-start(bf16[48,1536]{1,0:T(8,128)(2,1)S(1)} %pad_maximum_fusion.3), channel_id=1, source_target_pairs={{0,12},{2,14},{4,8},{6,10},{8,4},{10,6},{12,0},{14,2},{16,28},{18,... | collective-permute-start | bytes 442376 | tf_op jit(solution)/shard_map/ppermute | solution.py:244
  30.7 15.6 %collective-permute-start.13 = (bf16[48,1536]{1,0:T(8,128)(2,1)S(1)}, bf16[48,1536]{1,0:T(8,128)(2,1)S(1)}, u32[]{:S(2)}, u32[]{:S(2)}) collective-permute-start(bf16[48,1536]{1,0:T(8,128)(2,1)S(1)} %pad_maximum_fusion.4), channel_id=1, source_target_pairs={{0,16},{2,18},{4,20},{6,22},{8,24},{10,26},{12,28},{14,30},{16,0},... | collective-permute-start | bytes 442376 | tf_op jit(solution)/shard_map/ppermute | solution.py:244
  34.2 12.1 %collective-permute-start.14 = (bf16[48,1536]{1,0:T(8,128)(2,1)S(1)}, bf16[48,1536]{1,0:T(8,128)(2,1)S(1)}, u32[]{:S(2)}, u32[]{:S(2)}) collective-permute-start(bf16[48,1536]{1,0:T(8,128)(2,1)S(1)} %pad_maximum_fusion.5), channel_id=1, source_target_pairs={{0,20},{2,22},{4,16},{6,18},{8,28},{10,30},{12,24},{14,26},{16,4},... | collective-permute-start | bytes 442376 | tf_op jit(solution)/shard_map/ppermute | solution.py:244
  45.8 8.7 %collective-permute-start.16 = (bf16[48,1536]{1,0:T(8,128)(2,1)S(1)}, bf16[48,1536]{1,0:T(8,128)(2,1)S(1)}, u32[]{:S(2)}, u32[]{:S(2)}) collective-permute-start(bf16[48,1536]{1,0:T(8,128)(2,1)S(1)} %pad_maximum_fusion.7), channel_id=1, source_target_pairs={{0,28},{2,30},{4,24},{6,26},{8,20},{10,22},{12,16},{14,18},{16,12}... | collective-permute-start | bytes 442376 | tf_op jit(solution)/shard_map/ppermute | solution.py:244
  45.9 15.3 %collective-permute-start.8 = (bf16[384,1280]{1,0:T(8,128)(2,1)S(1)}, bf16[384,1280]{1,0:T(8,128)(2,1)S(1)}, u32[]{:S(2)}, u32[]{:S(2)}) collective-permute-start(bf16[384,1280]{1,0:T(8,128)(2,1)S(1)} %constant_dynamic-update-slice_fusion.piece), channel_id=1, source_target_pairs={{0,1},{1,0},{2,3},{3,2},{4,5},{5,4},{6,7},{7,6},{8,9},{9,8},{10,11... | collective-permute-start | bytes 2949128 | tf_op jit(solution)/shard_map/ppermute | solution.py:305
  85.3 12.5 %collective-permute-start.17 = (bf16[48,1792]{1,0:T(8,128)(2,1)S(1)}, bf16[48,1792]{1,0:T(8,128)(2,1)S(1)}, u32[]{:S(2)}, u32[]{:S(2)}) collective-permute-start(bf16[48,1792]{1,0:T(8,128)(2,1)S(1)} %get-tuple-element.21), channel_id=1, source_target_pairs={{0,4},{2,6},{4,0},{6,2},{8,12},{10,14},{12,8},{14,10},{16,20},{18,... | collective-permute-start | bytes 516104 | tf_op jit(solution)/shard_map/ppermute | solution.py:244
  88.1 10.6 %collective-permute-start.18 = (bf16[48,1792]{1,0:T(8,128)(2,1)S(1)}, bf16[48,1792]{1,0:T(8,128)(2,1)S(1)}, u32[]{:S(2)}, u32[]{:S(2)}) collective-permute-start(bf16[48,1792]{1,0:T(8,128)(2,1)S(1)} %get-tuple-element.20), channel_id=1, source_target_pairs={{0,8},{2,10},{4,12},{6,14},{8,0},{10,2},{12,4},{14,6},{16,24},{18,... | collective-permute-start | bytes 516104 | tf_op jit(solution)/shard_map/ppermute | solution.py:244
  97.8 24.2 %collective-permute-start.22 = (bf16[48,1792]{1,0:T(8,128)(2,1)S(1)}, bf16[48,1792]{1,0:T(8,128)(2,1)S(1)}, u32[]{:S(2)}, u32[]{:S(2)}) collective-permute-start(bf16[48,1792]{1,0:T(8,128)(2,1)S(1)} %get-tuple-element.16), channel_id=1, source_target_pairs={{0,24},{2,26},{4,28},{6,30},{8,16},{10,18},{12,20},{14,22},{16,8},... | collective-permute-start | bytes 516104 | tf_op jit(solution)/shard_map/ppermute | solution.py:244
  98.7 27.5 %collective-permute-start.23 = (bf16[48,1792]{1,0:T(8,128)(2,1)S(1)}, bf16[48,1792]{1,0:T(8,128)(2,1)S(1)}, u32[]{:S(2)}, u32[]{:S(2)}) collective-permute-start(bf16[48,1792]{1,0:T(8,128)(2,1)S(1)} %get-tuple-element.15), channel_id=1, source_target_pairs={{0,28},{2,30},{4,24},{6,26},{8,20},{10,22},{12,16},{14,18},{16,12}... | collective-permute-start | bytes 516104 | tf_op jit(solution)/shard_map/ppermute | solution.py:244
  126.8 11.9 %collective-permute-start.24 = (bf16[192,1792]{1,0:T(8,128)(2,1)}, bf16[192,1792]{1,0:T(8,128)(2,1)}, u32[]{:S(2)}, u32[]{:S(2)}) collective-permute-start(bf16[192,1792]{1,0:T(8,128)(2,1)} %get-tuple-element.63), channel_id=1, source_target_pairs={{0,2},{2,0},{4,6},{6,4},{8,10},{10,8},{12,14},{14,12},{16,18},{18,... | collective-permute-start | bytes 2064392 | tf_op jit(solution)/shard_map/ppermute | solution.py:244
  134.1 21.3 %collective-permute-start.26 = (bf16[384,1152]{1,0:T(8,128)(2,1)S(1)}, bf16[384,1152]{1,0:T(8,128)(2,1)S(1)}, u32[]{:S(2)}, u32[]{:S(2)}) collective-permute-start(bf16[384,1152]{1,0:T(8,128)(2,1)S(1)} %drop.3), channel_id=1, source_target_pairs={{0,1},{1,0},{2,3},{3,2},{4,5},{5,4},{6,7},{7,6},{8,9},{9,8},{10,11... | collective-permute-start | bytes 2654216 | tf_op jit(solution)/shard_map/ppermute | solution.py:305
  141.2 41.4 %collective-permute-start.25 = (f32[128,896]{1,0:T(8,128)S(1)}, f32[128,896]{1,0:T(8,128)S(1)}, u32[]{:S(2)}, u32[]{:S(2)}) collective-permute-start(f32[128,896]{1,0:T(8,128)S(1)} %constant_dynamic-slice_fusion), channel_id=1, source_target_pairs={{0,1},{1,0},{2,3},{3,2},{4,5},{5,4},{6,7},{7,6},{8,9},{9,8},{10,11... | collective-permute-start | bytes 1376264 | tf_op jit(solution)/shard_map/ppermute | solution.py:305
  159.7 14.5 %collective-permute-start.31 = (bf16[48,1152]{1,0:T(8,128)(2,1)S(1)}, bf16[48,1152]{1,0:T(8,128)(2,1)S(1)}, u32[]{:S(2)}, u32[]{:S(2)}) collective-permute-start(bf16[48,1152]{1,0:T(8,128)(2,1)S(1)} %get-tuple-element.26), channel_id=1, source_target_pairs={{0,20},{2,22},{4,16},{6,18},{8,28},{10,30},{12,24},{14,26},{16,4},... | collective-permute-start | bytes 331784 | tf_op jit(solution)/shard_map/ppermute | solution.py:244
  163.0 13.7 %collective-permute-start.32 = (bf16[48,1152]{1,0:T(8,128)(2,1)S(1)}, bf16[48,1152]{1,0:T(8,128)(2,1)S(1)}, u32[]{:S(2)}, u32[]{:S(2)}) collective-permute-start(bf16[48,1152]{1,0:T(8,128)(2,1)S(1)} %get-tuple-element.25), channel_id=1, source_target_pairs={{0,24},{2,26},{4,28},{6,30},{8,16},{10,18},{12,20},{14,22},{16,8},... | collective-permute-start | bytes 331784 | tf_op jit(solution)/shard_map/ppermute | solution.py:244
  163.6 16.3 %collective-permute-start.33 = (bf16[48,1152]{1,0:T(8,128)(2,1)S(1)}, bf16[48,1152]{1,0:T(8,128)(2,1)S(1)}, u32[]{:S(2)}, u32[]{:S(2)}) collective-permute-start(bf16[48,1152]{1,0:T(8,128)(2,1)S(1)} %get-tuple-element.24), channel_id=1, source_target_pairs={{0,28},{2,30},{4,24},{6,26},{8,20},{10,22},{12,16},{14,18},{16,12}... | collective-permute-start | bytes 331784 | tf_op jit(solution)/shard_map/ppermute | solution.py:244
  (17 other events, 199.4 us)

commit v6 on v3

v6 whole, which is shorter than its diff:
```python
import jax
import jax.numpy as jnp
from jax import lax
from jax.experimental import pallas as pl
from jax.experimental.pallas import tpu as pltpu
from jax.sharding import PartitionSpec as P

BLOCK = 128
CAP = 24
LANES = 256
VMEM_BYTES = 50 * 1024 * 1024
CUTS = 3


def tile_of(width):
    for tile in (LANES, 128):
        if width % tile == 0:
            return tile
    return width


def tile_copies(tiles, copy):
    for n in range(tiles):
        copy(n).start()
    return copy


def span(n, tile):
    return pl.ds(pl.multiple_of(n * tile, 128), tile)


def fetch_rows(source, start, target, column, sems):
    tiles, depth, both = target.shape
    tile = both // 2
    return tile_copies(
        tiles,
        lambda n: pltpu.make_async_copy(
            source.at[pl.ds(start, depth), span(n, tile)],
            target.at[n, :, pl.ds(column, tile)],
            sems.at[n],
        ),
    )


def fetch_sums(source, target, sems):
    tiles, rows, tile = target.shape
    return tile_copies(
        tiles,
        lambda n: pltpu.make_async_copy(source.at[:, span(n, tile)], target.at[n], sems.at[n]),
    )


def fetch_columns(source, starts, width, target, sems):
    tiles, depth, tile = target.shape
    each = width // tile

    def copy(n):
        at = pl.multiple_of(starts[n // each] + (n % each) * tile, 128)
        return pltpu.make_async_copy(source.at[:, pl.ds(at, tile)], target.at[n], sems.at[n])

    return tile_copies(tiles, copy)


def drop_tiles(hidden, down_tiles, copy, out):
    tiles, depth, tile = down_tiles.shape
    for n in range(tiles):
        copy(n).wait()
        value = jnp.dot(hidden[...], down_tiles[n], preferred_element_type=jnp.float32)
        out[:, n * tile : (n + 1) * tile] = value.astype(out.dtype)


def vmem():
    return pl.BlockSpec(memory_space=pltpu.VMEM)


def hbm():
    return pl.BlockSpec(memory_space=pl.ANY)


def buffer(shape, dtype=jnp.bfloat16):
    return [pltpu.VMEM(shape, dtype), pltpu.SemaphoreType.DMA((shape[0],))]


def lift(piece, start, w_gate, w_up, sums=None, back=None):
    rows, depth = piece.shape
    hidden = w_gate.shape[1]
    tile = tile_of(hidden)
    tiles = hidden // tile
    given = [] if sums is None else list(sums)
    scalars = [start]
    scratch = buffer((tiles, depth, 2 * tile)) + [pltpu.SemaphoreType.DMA((tiles,))]
    for _ in given:
        scratch += buffer((tiles, rows, tile), jnp.float32)
    flops = 4 * rows * depth * hidden
    moved = 4 * depth * hidden + 16 * rows * hidden
    if back is None:
        for _ in range(2):
            scratch += buffer((tiles, rows, tile), jnp.float32)
        args = [piece, w_gate, w_up] + given
        out_shape = [jax.ShapeDtypeStruct((rows, hidden), jnp.float32)] * 2
        out_specs = [hbm(), hbm()]
    else:
        w_down, columns, width = back
        wide = tile_of(width)
        scratch += buffer((len(columns) * width // wide, hidden, wide))
        scalars += list(columns)
        args = [piece, w_gate, w_up] + given + [w_down]
        out_shape = [
            jax.ShapeDtypeStruct((rows, hidden), jnp.bfloat16),
            jax.ShapeDtypeStruct((rows, len(columns) * width), jnp.bfloat16),
        ]
        out_specs = [vmem(), vmem()]
        flops += 2 * rows * hidden * len(columns) * width
        moved += 2 * hidden * len(columns) * width

    def kernel(at, *refs):
        piece, w_gate, w_up = refs[:3]
        sums = refs[3 : 3 + len(given)]
        first, second = refs[len(args) : len(args) + 2]
        both, gate_sems, up_sems = refs[len(args) + 2 : len(args) + 5]
        extra = refs[len(args) + 5 :]
        begin = pl.multiple_of(at[0], 128)
        waits = [
            fetch_rows(w_gate, begin, both, 0, gate_sems),
            fetch_rows(w_up, begin, both, tile, up_sems),
        ]
        for i, source in enumerate(sums):
            waits.append(fetch_sums(source, extra[2 * i], extra[2 * i + 1]))
        before, extra = extra[: 2 * len(given) : 2], extra[2 * len(given) :]
        if back is not None:
            starts = [at[1 + i] for i in range(len(columns))]
            down = fetch_columns(refs[len(args) - 1], starts, width, extra[0], extra[1])

        def store(i, n):
            target = (first, second)[i]
            return pltpu.make_async_copy(
                extra[2 * i].at[n], target.at[:, span(n, tile)], extra[2 * i + 1].at[n]
            )

        @pl.loop(0, tiles)
        def _(n):
            for wait in waits:
                wait(n).wait()
            product = jnp.dot(piece[...], both[n], preferred_element_type=jnp.float32)
            gate, up = product[:, :tile], product[:, tile:]
            if given:
                gate = gate + before[0][n]
                up = up + before[1][n]
            if back is None:
                extra[0][n] = gate
                extra[2][n] = up
                store(0, n).start()
                store(1, n).start()
            else:
                silu = gate / (1.0 + jnp.exp(-gate))
                first[:, span(n, tile)] = (silu * up).astype(jnp.bfloat16)

        if back is None:
            for n in range(tiles):
                store(0, n).wait()
                store(1, n).wait()
        else:
            drop_tiles(first, extra[0], down, second)

    return pl.pallas_call(
        kernel,
        out_shape=out_shape,
        in_specs=[pl.BlockSpec(memory_space=pltpu.SMEM), vmem()] + [hbm()] * (len(args) - 1),
        out_specs=out_specs,
        scratch_shapes=scratch,
        compiler_params=pltpu.CompilerParams(vmem_limit_bytes=VMEM_BYTES),
        cost_estimate=pl.CostEstimate(
            flops=flops,
            bytes_accessed=moved,
            transcendentals=rows * hidden,
        ),
        name="lift",
    )(jnp.stack(scalars).astype(jnp.int32), *args)


def drop(hidden, w_down, start, width, dtype):
    rows, depth = hidden.shape
    tile = tile_of(width)

    def kernel(at, hidden, w_down, out, *scratch):
        copy = fetch_columns(w_down, [at[0]], width, scratch[0], scratch[1])
        drop_tiles(hidden, scratch[0], copy, out)

    return pl.pallas_call(
        kernel,
        out_shape=jax.ShapeDtypeStruct((rows, width), dtype),
        in_specs=[pl.BlockSpec(memory_space=pltpu.SMEM), vmem(), hbm()],
        out_specs=vmem(),
        scratch_shapes=buffer((width // tile, depth, tile)),
        compiler_params=pltpu.CompilerParams(vmem_limit_bytes=VMEM_BYTES),
        cost_estimate=pl.CostEstimate(
            flops=2 * rows * depth * width, bytes_accessed=2 * depth * width, transcendentals=0
        ),
        name="drop",
    )(jnp.reshape(start, (1,)).astype(jnp.int32), hidden, w_down)


def selectors(expert_ids, gate_probs, experts):
    rows = expert_ids.shape[0]
    blocks = rows // BLOCK
    match = expert_ids.T[:, None, :] == jnp.arange(experts, dtype=jnp.int32)[None, :, None]
    named = jnp.any(match, axis=0)
    weight = jnp.sum(jnp.where(match, gate_probs.T[:, None, :], 0.0), axis=0)
    row = jnp.arange(rows, dtype=jnp.int32)
    same = row[:, None] // BLOCK == row[None, :] // BLOCK
    earlier = ((row[:, None] < row[None, :]) & same).astype(jnp.bfloat16)
    before = jnp.dot(named.astype(jnp.bfloat16), earlier, preferred_element_type=jnp.float32)
    place = before.astype(jnp.int32) + (row // BLOCK * CAP)[None, :]
    slots = jnp.arange(blocks * CAP, dtype=jnp.int32)
    hit = named[:, None, :] & (place[:, None, :] == slots[None, :, None])
    high = weight.astype(jnp.bfloat16)
    rest = weight - high.astype(jnp.float32)
    middle = rest.astype(jnp.bfloat16)
    low = (rest - middle.astype(jnp.float32)).astype(jnp.bfloat16)
    flat = (experts * blocks * CAP, rows)
    chosen = hit.astype(jnp.bfloat16).reshape(flat)
    weights = [
        jnp.where(hit, part[:, None, :], 0).astype(jnp.bfloat16).reshape(flat)
        for part in (high, middle, low)
    ]
    return chosen, weights


def swap(value, experts):
    slots, width = value.shape
    return lax.all_to_all(
        value.reshape(experts, slots // experts, width),
        "expert",
        split_axis=0,
        concat_axis=0,
        tiled=True,
    ).reshape(slots, width)


def mix(weights, returned):
    return sum(
        lax.dot_general(
            w, returned, (((0,), (0,)), ((), ())), preferred_element_type=jnp.float32
        )
        for w in weights
    )


def on_device(tokens, expert_ids, gate_probs, w_gate, w_up, w_down):
    width = tokens.shape[1]
    experts = lax.axis_size("expert")
    ranks = lax.axis_size("tensor")
    me = lax.axis_index("tensor")
    w_gate = lax.all_gather(w_gate, "dp", axis=1, tiled=True)[0]
    w_up = lax.all_gather(w_up, "dp", axis=1, tiled=True)[0]
    w_down = lax.all_gather(w_down, "dp", axis=2, tiled=True)[0]
    chosen, weights = selectors(expert_ids, gate_probs, experts)

    def rank_at(step):
        return lax.rem(me + step, ranks)

    def send_up(value, step):
        return lax.ppermute(value, "tensor", [(i, (i + step) % ranks) for i in range(ranks)])

    share = width // ranks
    shared = share // 4 * 3
    direct_at = ranks * shared

    def placed(features):
        return jnp.dot(chosen, features, preferred_element_type=jnp.float32).astype(jnp.bfloat16)

    mine = lax.dynamic_slice_in_dim(tokens, me * shared, shared, axis=1)
    own = swap(placed(mine), experts)
    cut = shared // CUTS
    others = []
    for at in range(0, shared, cut):
        for step in range(1, ranks):
            sent = send_up(own[:, at : at + cut], ranks - step)
            others.append((sent, rank_at(step) * shared + at))
    direct = swap(placed(tokens[:, direct_at:]), experts)
    sums = lift(own, me * shared, w_gate, w_up)
    for piece, at in others[: 1 - ranks]:
        sums = lift(piece, at, w_gate, w_up, sums)
    sums = lift(direct, jnp.int32(direct_at), w_gate, w_up, sums)
    for piece, at in others[1 - ranks : -1]:
        sums = lift(piece, at, w_gate, w_up, sums)

    early = share // 8 * 3
    columns = [jnp.int32(rank * share) for rank in range(ranks)]
    piece, at = others[-1]
    hidden, partial = lift(piece, at, w_gate, w_up, sums, (w_down, columns, early))
    returned = swap(partial, experts)
    cut = pl.cdiv(share - early, 2 * LANES) * LANES
    owned = []
    for at in range(early, share, cut):
        cut = min(cut, share - at)
        arrived = [
            send_up(drop(hidden, w_down, rank_at(step) * share + at, cut, jnp.bfloat16), step)
            for step in range(1, ranks)
        ]
        value = drop(hidden, w_down, me * share + at, cut, jnp.float32)
        for other in arrived:
            value = value + other.astype(jnp.float32)
        owned.append(value.astype(jnp.bfloat16))
    returned, *owned = lax.optimization_barrier((returned, *owned))
    first = mix(weights, returned)

    def part_of(rank):
        return lax.dynamic_slice_in_dim(first, rank * early, early, axis=1)

    mixed = part_of(me)
    for step in range(1, ranks):
        mixed = mixed + send_up(part_of(rank_at(step)), step)
    late = mix(weights, swap(jnp.concatenate(owned, axis=1), experts))
    return jnp.concatenate([mixed.astype(jnp.bfloat16), late.astype(jnp.bfloat16)], axis=1)


def solution(mesh):
    placed = (
        P(("groups", "dp", "expert"), None),
        P(("groups", "dp", "expert"), None),
        P(("groups", "dp", "expert"), None),
        P("expert", "dp", "tensor"),
        P("expert", "dp", "tensor"),
        P("expert", "tensor", "dp"),
    )
    return jax.shard_map(
        on_device,
        mesh=mesh,
        in_specs=placed,
        out_specs=P(("groups", "dp", "expert"), "tensor"),
        check_vma=False,
    )
```

time: 164 us -> 162 us (0.988)
  Pallas kernels: 40.2 us -> 54.3 us
  local copies, waits for them, and re-layouts: 18.1 us -> 6.45 us
  waiting for transfers between devices: 64.1 us -> 55.4 us
  matrix products: 11.2 us -> 7.28 us
  other arithmetic: 2.89 us -> 6.6 us
  starting transfers between devices: 26.2 us -> 29.9 us
    ppermute x3 -> x6, waiting for transfers between devices: 35.2 us -> 18.4 us  [send_up(): lax.ppermute(value, 'tensor', [(i, (i + step) % ranks) for i in range(ran...]
    unnamed x20 -> x24, local copies, waits for them, and re-layouts: 18 us -> 6.25 us
    pallas_call x3 -> x5, Pallas kernels: 30.9 us -> 41.6 us  [lift(): pl.pallas_call(kernel, out_shape=out_shape, in_specs=[pl.BlockSpec(memory...]
    all_to_all x4, waiting for transfers between devices: 28.9 us -> 37.1 us  [swap(): lax.all_to_all(value.reshape(experts, slots // experts, width), 'expert',...]
    dot_general x6, matrix products: 6.15 us -> 2.33 us  [mix(): lax.dot_general(w, returned, (((0,), (0,)), ((), ())), preferred_element_...]
    ppermute x3 -> x6, starting transfers between devices: 0.9 us -> 4.69 us  [send_up(): lax.ppermute(value, 'tensor', [(i, (i + step) % ranks) for i in range(ran...]
    pallas_call x2 -> x4, Pallas kernels: 9.33 us -> 12.8 us  [drop(): pl.pallas_call(kernel, out_shape=jax.ShapeDtypeStruct((rows, width), dtyp...]
  transfers between devices with their start and end apart: 7 -> 10, of which waited for: 5 -> 5; matrix products, arithmetic and copies ran while one was open for 5% -> 5% of each run, Pallas kernels for 16% -> 26%
where the time goes in v6:
time: 162 us; the launch traced here: 160 us
  waiting for transfers between devices  55.4 us (34%)
  Pallas kernels  54.3 us (34%)
  starting transfers between devices  29.9 us (18%)
  matrix products  7.28 us (4%)
  other arithmetic  6.6 us (4%)
  local copies, waits for them, and re-layouts  6.45 us (4%)
    pallas_call x5, Pallas kernels, lift(): pl.pallas_call(kernel, out_shape=out_shape, in_specs=[pl.BlockSpec(memory...  41.6 us
    all_to_all x4, waiting for transfers between devices, swap(): lax.all_to_all(value.reshape(experts, slots // experts, width), 'expert',...  37.1 us
    all_to_all x4, starting transfers between devices, swap(): lax.all_to_all(value.reshape(experts, slots // experts, width), 'expert',...  25.3 us
    ppermute x6, waiting for transfers between devices, send_up(): lax.ppermute(value, 'tensor', [(i, (i + step) % ranks) for i in range(ran...  18.4 us
    pallas_call x4, Pallas kernels, drop(): pl.pallas_call(kernel, out_shape=jax.ShapeDtypeStruct((rows, width), dtyp...  12.8 us
    unnamed x24, local copies, waits for them, and re-layouts  6.25 us
    dot_general x2, matrix products, placed(): jnp.dot(chosen, features, preferred_element_type=jnp.float32)  4.75 us
    ppermute x6, starting transfers between devices, send_up(): lax.ppermute(value, 'tensor', [(i, (i + step) % ranks) for i in range(ran...  4.69 us
  transfers between devices with their start and end apart: 10, of which 5 were waited for; matrix products, arithmetic and copies ran while one was open for 5% of the time, Pallas kernels for 26%

profile of v6, /device:TPU:11, one launch (start us, length us, event | category | flops | bytes accessed | tf_op | source)
XLA Modules:
  0.0 160.3 jit_solution(4864857788839943393)
XLA Ops:
  1.1 2.5 %convolution_convert_fusion = bf16[384,1536]{1,0:T(8,128)(2,1)} fusion(pred[384,128]{1,0:T(32,128)(4,1)S(1)} %fusion.10, bf16[128,4096]{1,0:T(8,128)(2,1)} %param.6, s32[]{:T(128)S(6)} %select_n.61), kind=kOutput, calls=%fused_computation | convolution fusion | flops 151584768 | bytes 1622020 | tf_op jit(solution)/shard_map/dot_general | solution.py:270
  3.6 6.6 %all-to-all-start = ((bf16[16,24,1536]{2,1,0:T(8,128)(2,1)}), bf16[16,24,1536]{2,1,0:T(8,128)(2,1)S(1)}, u32[]{:S(2)}, u32[]{:S(2)}) async-start(bf16[16,24,1536]{2,1,0:T(8,128)(2,1)} %bitcast.6), calls=%async_computation | async-start | bytes 2359296 | tf_op jit(solution)/shard_map/all_to_all | solution.py:231
  10.2 2.3 %convolution_convert_fusion.1 = bf16[384,1024]{1,0:T(8,128)(2,1)} fusion(pred[384,128]{1,0:T(32,128)(4,1)S(1)} %fusion.10, bf16[128,4096]{1,0:T(8,128)(2,1)} %param.6), kind=kOutput, calls=%fused_computation.9 | convolution fusion | flops 101056512 | bytes 1097728 | tf_op jit(solution)/shard_map/dot_general | solution.py:270
  12.5 25.3 %all-to-all-done = bf16[16,24,1536]{2,1,0:T(8,128)(2,1)S(1)} async-done(((bf16[16,24,1536]{2,1,0:T(8,128)(2,1)}), bf16[16,24,1536]{2,1,0:T(8,128)(2,1)S(1)}, u32[]{:S(2)}, u32[]{:S(2)}) %all-to-all-start) | async-done | bytes 1179680 | tf_op jit(solution)/shard_map/all_to_all | solution.py:231
  37.8 5.1 %all-to-all-start.1 = ((bf16[16,24,1024]{2,1,0:T(8,128)(2,1)}), bf16[16,24,1024]{2,1,0:T(8,128)(2,1)S(1)}, u32[]{:S(2)}, u32[]{:S(2)}) async-start(bf16[16,24,1024]{2,1,0:T(8,128)(2,1)} %bitcast.10), calls=%async_computation.1 | async-start | bytes 1572864 | tf_op jit(solution)/shard_map/all_to_all | solution.py:231
  44.8 9.5 %lift.5 = (f32[384,1792]{1,0:T(8,128)S(1)}, f32[384,1792]{1,0:T(8,128)}) custom-call(s32[1]{0:T(128)} %bitcast.14.at, bf16[384,1536]{1,0:T(8,128)(2,1)S(1)} %bitcast.69, bf16[4096,1792]{1,0:T(8,128)(2,1)} %bitcast.71, bf16[4096,1792]{1,0:T(8,128)(2,1)} %bitcast.76), custom_call_target="tpu_custom_call" | custom-call | flops 4227858432 | bytes 22020096 | tf_op jit(solution)/shard_map/lift/pallas_call | solution.py:165
  54.4 1.6 copy-done.3
  55.9 5.8 %lift.6 = (f32[384,1792]{1,0:T(8,128)S(1)}, f32[384,1792]{1,0:T(8,128)}) custom-call(s32[1]{0:T(128)} %bitcast.13.at, bf16[384,512]{1,0:T(8,128)(2,1)S(1)} %collective-permute-done.2.refs_0_, bf16[4096,1792]{1,0:T(8,128)(2,1)} %bitcast.72, bf16[4096,1792]{1,0:T(8,128)(2,1)} %bitcast.77, f32[384,1792]{1,0:T(8,128)} %copy-done.3, ...), custom_call_target="tpu_custom_call" | custom-call | flops 1409286144 | bytes 14680064 | tf_op jit(solution)/shard_map/lift/pallas_call | solution.py:165
  61.8 1.6 copy-done.1
  63.3 5.8 %lift.7 = (f32[384,1792]{1,0:T(8,128)S(1)}, f32[384,1792]{1,0:T(8,128)}) custom-call(s32[1]{0:T(128)} %bitcast.12.at, bf16[384,512]{1,0:T(8,128)(2,1)S(1)} %collective-permute-done.1.refs_0_, bf16[4096,1792]{1,0:T(8,128)(2,1)} %bitcast.73, bf16[4096,1792]{1,0:T(8,128)(2,1)} %bitcast.78, f32[384,1792]{1,0:T(8,128)} %copy-done.1, ...), custom_call_target="tpu_custom_call" | custom-call | flops 1409286144 | bytes 14680064 | tf_op jit(solution)/shard_map/lift/pallas_call | solution.py:165
  69.1 1.6 copy-done
  70.7 7.9 %lift.8 = (f32[384,1792]{1,0:T(8,128)S(1)}, f32[384,1792]{1,0:T(8,128)}) custom-call(s32[1]{0:T(128)} %constant.71.clone.1.at, bf16[384,1024]{1,0:T(8,128)(2,1)S(1)} %bitcast.70, bf16[4096,1792]{1,0:T(8,128)(2,1)} %bitcast.74, bf16[4096,1792]{1,0:T(8,128)(2,1)} %bitcast.79, f32[384,1792]{1,0:T(8,128)} %copy-done, f32[384,1792]{1,0:T(8,128)} %get-tuple-element.23.refs_4_), custom_call_target="tpu_custom_call" | custom-call | flops 2818572288 | bytes 18350080 | tf_op jit(solution)/shard_map/lift/pallas_call | solution.py:165
  78.6 1.5 copy-done.2
  80.1 12.5 %lift.9 = (bf16[384,1792]{1,0:T(8,128)(2,1)S(1)}, bf16[384,1536]{1,0:T(8,128)(2,1)}) custom-call(s32[3]{0:T(128)S(1)} %pad_add_fusion.at, bf16[384,512]{1,0:T(8,128)(2,1)S(1)} %collective-permute-done.refs_0_, bf16[4096,1792]{1,0:T(8,128)(2,1)} %bitcast.75, bf16[4096,1792]{1,0:T(8,128)(2,1)} %bitcast.80, f32[384,1792]{1,0:T(8,128)} %copy-done.2, ...), custom_call_target="tpu_custom_call" | custom-call | flops 3523215360 | bytes 20185088 | tf_op jit(solution)/shard_map/lift/pallas_call | solution.py:165
  92.7 6.8 %all-to-all-start.2 = ((bf16[16,24,1536]{2,1,0:T(8,128)(2,1)}), bf16[16,24,1536]{2,1,0:T(8,128)(2,1)S(1)}, u32[]{:S(2)}, u32[]{:S(2)}) async-start(bf16[16,24,1536]{2,1,0:T(8,128)(2,1)} %bitcast.16), calls=%async_computation.2 | async-start | bytes 2359296 | tf_op jit(solution)/shard_map/all_to_all | solution.py:231
  99.5 2.9 %drop.7 = bf16[384,512]{1,0:T(8,128)(2,1)S(1)} custom-call(s32[1]{0:T(128)} %bitcast.21.at, bf16[384,1792]{1,0:T(8,128)(2,1)S(1)} %get-tuple-element.27.hidden, bf16[1792,4096]{1,0:T(8,128)(2,1)} %bitcast.82), custom_call_target="tpu_custom_call" | custom-call | flops 704643072 | bytes 1835008 | tf_op jit(solution)/shard_map/drop/pallas_call | solution.py:189
  103.7 3.5 %drop.5 = bf16[384,768]{1,0:T(8,128)(2,1)S(1)} custom-call(s32[1]{0:T(128)} %bitcast.19.at, bf16[384,1792]{1,0:T(8,128)(2,1)S(1)} %get-tuple-element.27.hidden, bf16[1792,4096]{1,0:T(8,128)(2,1)} %bitcast.83), custom_call_target="tpu_custom_call" | custom-call | flops 1056964608 | bytes 2752512 | tf_op jit(solution)/shard_map/drop/pallas_call | solution.py:189
  107.5 1.3 select_reduce_fusion
  108.8 2.9 %drop.6 = f32[384,512]{1,0:T(8,128)S(1)} custom-call(s32[1]{0:T(128)} %bitcast.20.at, bf16[384,1792]{1,0:T(8,128)(2,1)S(1)} %get-tuple-element.27.hidden, bf16[1792,4096]{1,0:T(8,128)(2,1)} %bitcast.84), custom_call_target="tpu_custom_call" | custom-call | flops 704643072 | bytes 1835008 | tf_op jit(solution)/shard_map/drop/pallas_call | solution.py:189
  111.7 3.5 %drop.4 = f32[384,768]{1,0:T(8,128)S(1)} custom-call(s32[1]{0:T(128)} %bitcast.18.at, bf16[384,1792]{1,0:T(8,128)(2,1)S(1)} %get-tuple-element.27.hidden, bf16[1792,4096]{1,0:T(8,128)(2,1)} %bitcast.85), custom_call_target="tpu_custom_call" | custom-call | flops 1056964608 | bytes 2752512 | tf_op jit(solution)/shard_map/drop/pallas_call | solution.py:189
  116.4 9.2 %collective-permute-done.3 = bf16[384,768]{1,0:T(8,128)(2,1)} collective-permute-done((bf16[384,768]{1,0:T(8,128)(2,1)S(1)}, bf16[384,768]{1,0:T(8,128)(2,1)}, u32[]{:S(2)}, u32[]{:S(2)}) %collective-permute-start.3) | collective-permute-done | bytes 589856 | tf_op jit(solution)/shard_map/ppermute | solution.py:263
  128.1 6.7 %all-to-all-start.3 = ((bf16[16,24,1280]{2,1,0:T(8,128)(2,1)}), bf16[16,24,1280]{2,1,0:T(8,128)(2,1)S(1)}, u32[]{:S(2)}, u32[]{:S(2)}) async-start(bf16[16,24,1280]{2,1,0:T(8,128)(2,1)} %bitcast.24), calls=%async_computation.3 | async-start | bytes 1966080 | tf_op jit(solution)/shard_map/all_to_all | solution.py:231
  137.6 9.1 %collective-permute-done.5 = f32[128,768]{1,0:T(8,128)S(1)} collective-permute-done((f32[128,768]{1,0:T(8,128)S(1)}, f32[128,768]{1,0:T(8,128)S(1)}, u32[]{:S(2)}, u32[]{:S(2)}) %collective-permute-start.5) | collective-permute-done | bytes 393248 | tf_op jit(solution)/shard_map/ppermute | solution.py:263
  146.8 11.5 %all-to-all-done.3 = bf16[16,24,1280]{2,1,0:T(8,128)(2,1)S(1)} async-done(((bf16[16,24,1280]{2,1,0:T(8,128)(2,1)}), bf16[16,24,1280]{2,1,0:T(8,128)(2,1)S(1)}, u32[]{:S(2)}, u32[]{:S(2)}) %all-to-all-start.3) | async-done | bytes 983072 | tf_op jit(solution)/shard_map/all_to_all | solution.py:231
  (54 shorter events, 13.1 us)
Async XLA Ops:
  0.8 2.8 %copy-start.9 = (s32[384]{0:T(512)}, s32[384]{0:T(512)S(1)}, u32[]{:S(2)}) copy-start(s32[384]{0:T(512)S(1)} %eq.62) | copy-start | bytes 4612
  3.6 34.2 %all-to-all-start = ((bf16[16,24,1536]{2,1,0:T(8,128)(2,1)}), bf16[16,24,1536]{2,1,0:T(8,128)(2,1)S(1)}, u32[]{:S(2)}, u32[]{:S(2)}) async-start(bf16[16,24,1536]{2,1,0:T(8,128)(2,1)} %bitcast.6), calls=%async_computation | async-start | bytes 2359296 | tf_op jit(solution)/shard_map/all_to_all | solution.py:231
  37.8 32.9 %all-to-all-start.1 = ((bf16[16,24,1024]{2,1,0:T(8,128)(2,1)}), bf16[16,24,1024]{2,1,0:T(8,128)(2,1)S(1)}, u32[]{:S(2)}, u32[]{:S(2)}) async-start(bf16[16,24,1024]{2,1,0:T(8,128)(2,1)} %bitcast.10), calls=%async_computation.1 | async-start | bytes 1572864 | tf_op jit(solution)/shard_map/all_to_all | solution.py:231
  43.0 12.9 %collective-permute-start.2 = (bf16[384,512]{1,0:T(8,128)(2,1)S(1)}, bf16[384,512]{1,0:T(8,128)(2,1)S(1)}, u32[]{:S(2)}, u32[]{:S(2)}) collective-permute-start(bf16[384,512]{1,0:T(8,128)(2,1)S(1)} %get-tuple-element.31), channel_id=1, source_target_pairs={{0,1},{1,0},{2,3},{3,2},{4,5},{5,4},{6,7},{7,6},{8,9},{9,8},{10,11... | collective-permute-start | bytes 1179656 | tf_op jit(solution)/shard_map/ppermute | solution.py:263
  43.3 20.0 %collective-permute-start.1 = (bf16[384,512]{1,0:T(8,128)(2,1)S(1)}, bf16[384,512]{1,0:T(8,128)(2,1)S(1)}, u32[]{:S(2)}, u32[]{:S(2)}) collective-permute-start(bf16[384,512]{1,0:T(8,128)(2,1)S(1)} %get-tuple-element.32), channel_id=1, source_target_pairs={{0,1},{1,0},{2,3},{3,2},{4,5},{5,4},{6,7},{7,6},{8,9},{9,8},{10,11... | collective-permute-start | bytes 1179656 | tf_op jit(solution)/shard_map/ppermute | solution.py:263
  44.5 35.6 %collective-permute-start = (bf16[384,512]{1,0:T(8,128)(2,1)S(1)}, bf16[384,512]{1,0:T(8,128)(2,1)S(1)}, u32[]{:S(2)}, u32[]{:S(2)}) collective-permute-start(bf16[384,512]{1,0:T(8,128)(2,1)S(1)} %get-tuple-element.33), channel_id=1, source_target_pairs={{0,1},{1,0},{2,3},{3,2},{4,5},{5,4},{6,7},{7,6},{8,9},{9,8},{10,11... | collective-permute-start | bytes 1179656 | tf_op jit(solution)/shard_map/ppermute | solution.py:263
  54.4 1.6 copy-start.3
  61.8 1.6 copy-start.1
  69.1 1.6 copy-start
  78.6 1.5 copy-start.2
  92.7 34.4 %all-to-all-start.2 = ((bf16[16,24,1536]{2,1,0:T(8,128)(2,1)}), bf16[16,24,1536]{2,1,0:T(8,128)(2,1)S(1)}, u32[]{:S(2)}, u32[]{:S(2)}) async-start(bf16[16,24,1536]{2,1,0:T(8,128)(2,1)} %bitcast.16), calls=%async_computation.2 | async-start | bytes 2359296 | tf_op jit(solution)/shard_map/all_to_all | solution.py:231
  102.4 12.8 %collective-permute-start.4 = (bf16[384,512]{1,0:T(8,128)(2,1)S(1)}, bf16[384,512]{1,0:T(8,128)(2,1)}, u32[]{:S(2)}, u32[]{:S(2)}) collective-permute-start(bf16[384,512]{1,0:T(8,128)(2,1)S(1)} %drop.7), channel_id=1, source_target_pairs={{0,1},{1,0},{2,3},{3,2},{4,5},{5,4},{6,7},{7,6},{8,9},{9,8},{10,11... | collective-permute-start | bytes 1179656 | tf_op jit(solution)/shard_map/ppermute | solution.py:263
  103.7 3.8 %copy-start.11 = (s32[128,2]{0,1:T(2,128)S(1)}, s32[128,2]{0,1:T(2,128)}, u32[]{:S(2)}) copy-start(s32[128,2]{0,1:T(2,128)} %param.7) | copy-start | bytes 3076
  107.2 18.4 %collective-permute-start.3 = (bf16[384,768]{1,0:T(8,128)(2,1)S(1)}, bf16[384,768]{1,0:T(8,128)(2,1)}, u32[]{:S(2)}, u32[]{:S(2)}) collective-permute-start(bf16[384,768]{1,0:T(8,128)(2,1)S(1)} %drop.5), channel_id=1, source_target_pairs={{0,1},{1,0},{2,3},{3,2},{4,5},{5,4},{6,7},{7,6},{8,9},{9,8},{10,11... | collective-permute-start | bytes 1769480 | tf_op jit(solution)/shard_map/ppermute | solution.py:263
  128.1 6.7 %copy-start.8 = (f32[16,128]{1,0:T(8,128)S(1)}, f32[16,128]{1,0:T(8,128)}, u32[]{:S(2)}) copy-start(f32[16,128]{1,0:T(8,128)} %select_reduce_fusion) | copy-start | bytes 24580
  128.1 6.8 %copy-start.10 = (s32[384]{0:T(512)S(1)}, s32[384]{0:T(512)}, u32[]{:S(2)}) copy-start(s32[384]{0:T(512)} %copy-done.9) | copy-start | bytes 4612
  128.1 30.2 %all-to-all-start.3 = ((bf16[16,24,1280]{2,1,0:T(8,128)(2,1)}), bf16[16,24,1280]{2,1,0:T(8,128)(2,1)S(1)}, u32[]{:S(2)}, u32[]{:S(2)}) async-start(bf16[16,24,1280]{2,1,0:T(8,128)(2,1)} %bitcast.24), calls=%async_computation.3 | async-start | bytes 1966080 | tf_op jit(solution)/shard_map/all_to_all | solution.py:231
  134.9 0.6 copy-start.4
  134.9 0.6 copy-start.6
  136.3 22.1 %copy-start.7 = (bf16[16,128]{1,0:T(8,128)(2,1)S(1)}, bf16[16,128]{1,0:T(8,128)(2,1)}, u32[]{:S(2)}) copy-start(bf16[16,128]{1,0:T(8,128)(2,1)} %copy-done.6) | copy-start | bytes 12292
  136.3 10.4 %collective-permute-start.5 = (f32[128,768]{1,0:T(8,128)S(1)}, f32[128,768]{1,0:T(8,128)S(1)}, u32[]{:S(2)}, u32[]{:S(2)}) collective-permute-start(f32[128,768]{1,0:T(8,128)S(1)} %constant_dynamic-slice_fusion), channel_id=1, source_target_pairs={{0,1},{1,0},{2,3},{3,2},{4,5},{5,4},{6,7},{7,6},{8,9},{9,8},{10,11... | collective-permute-start | bytes 1179656 | tf_op jit(solution)/shard_map/ppermute | solution.py:263
  137.6 21.1 %copy-start.5 = (bf16[16,128]{1,0:T(8,128)(2,1)S(1)}, bf16[16,128]{1,0:T(8,128)(2,1)}, u32[]{:S(2)}) copy-start(bf16[16,128]{1,0:T(8,128)(2,1)} %copy-done.4) | copy-start | bytes 12292

commit v7 on v6

--- a/solution.py
+++ b/solution.py
@@ -9,11 +9,10 @@
 CAP = 24
 LANES = 256
 VMEM_BYTES = 50 * 1024 * 1024
-CUTS = 3
-
-
-def tile_of(width):
-    for tile in (LANES, 128):
+
+
+def tile_of(width, most=LANES):
+    for tile in range(most, 127, -128):
         if width % tile == 0:
             return tile
     return width
@@ -29,14 +28,14 @@
     return pl.ds(pl.multiple_of(n * tile, 128), tile)
 
 
-def fetch_rows(source, start, target, column, sems):
-    tiles, depth, both = target.shape
+def fetch_rows(source, start, target, row, depth, column, sems):
+    tiles, _, both = target.shape
     tile = both // 2
     return tile_copies(
         tiles,
         lambda n: pltpu.make_async_copy(
             source.at[pl.ds(start, depth), span(n, tile)],
-            target.at[n, :, pl.ds(column, tile)],
+            target.at[n, pl.ds(row, depth), pl.ds(column, tile)],
             sems.at[n],
         ),
     )
@@ -81,14 +80,19 @@
     return [pltpu.VMEM(shape, dtype), pltpu.SemaphoreType.DMA((shape[0],))]
 
 
-def lift(piece, start, w_gate, w_up, sums=None, back=None):
-    rows, depth = piece.shape
+def lift(pieces, starts, w_gate, w_up, sums=None, back=None):
+    rows = pieces[0].shape[0]
+    depths = [piece.shape[1] for piece in pieces]
+    depth = sum(depths)
+    count = len(pieces)
     hidden = w_gate.shape[1]
     tile = tile_of(hidden)
     tiles = hidden // tile
     given = [] if sums is None else list(sums)
-    scalars = [start]
-    scratch = buffer((tiles, depth, 2 * tile)) + [pltpu.SemaphoreType.DMA((tiles,))]
+    scalars = list(starts)
+    scratch = [pltpu.VMEM((rows, depth), jnp.bfloat16)]
+    scratch += [pltpu.VMEM((tiles, depth, 2 * tile), jnp.bfloat16)]
+    scratch += [pltpu.SemaphoreType.DMA((tiles,))] * (2 * count)
     for _ in given:
         scratch += buffer((tiles, rows, tile), jnp.float32)
     flops = 4 * rows * depth * hidden
@@ -96,15 +100,15 @@
     if back is None:
         for _ in range(2):
             scratch += buffer((tiles, rows, tile), jnp.float32)
-        args = [piece, w_gate, w_up] + given
+        args = [*pieces, w_gate, w_up] + given
         out_shape = [jax.ShapeDtypeStruct((rows, hidden), jnp.float32)] * 2
         out_specs = [hbm(), hbm()]
     else:
         w_down, columns, width = back
-        wide = tile_of(width)
+        wide = tile_of(width, 1024)
         scratch += buffer((len(columns) * width // wide, hidden, wide))
         scalars += list(columns)
-        args = [piece, w_gate, w_up] + given + [w_down]
+        args = [*pieces, w_gate, w_up] + given + [w_down]
         out_shape = [
             jax.ShapeDtypeStruct((rows, hidden), jnp.bfloat16),
             jax.ShapeDtypeStruct((rows, len(columns) * width), jnp.bfloat16),
@@ -114,22 +118,29 @@
         moved += 2 * hidden * len(columns) * width
 
     def kernel(at, *refs):
-        piece, w_gate, w_up = refs[:3]
-        sums = refs[3 : 3 + len(given)]
+        parts, (w_gate, w_up) = refs[:count], refs[count : count + 2]
+        sums = refs[count + 2 : count + 2 + len(given)]
         first, second = refs[len(args) : len(args) + 2]
-        both, gate_sems, up_sems = refs[len(args) + 2 : len(args) + 5]
-        extra = refs[len(args) + 5 :]
-        begin = pl.multiple_of(at[0], 128)
-        waits = [
-            fetch_rows(w_gate, begin, both, 0, gate_sems),
-            fetch_rows(w_up, begin, both, tile, up_sems),
-        ]
+        whole, both = refs[len(args) + 2 : len(args) + 4]
+        sems = refs[len(args) + 4 : len(args) + 4 + 2 * count]
+        extra = refs[len(args) + 4 + 2 * count :]
+        waits = []
+        row = 0
+        for i, part in enumerate(parts):
+            begin = pl.multiple_of(at[i], 128)
+            for source, column, sem in ((w_gate, 0, sems[2 * i]), (w_up, tile, sems[2 * i + 1])):
+                waits.append(fetch_rows(source, begin, both, row, depths[i], column, sem))
+            row += depths[i]
         for i, source in enumerate(sums):
             waits.append(fetch_sums(source, extra[2 * i], extra[2 * i + 1]))
         before, extra = extra[: 2 * len(given) : 2], extra[2 * len(given) :]
         if back is not None:
-            starts = [at[1 + i] for i in range(len(columns))]
-            down = fetch_columns(refs[len(args) - 1], starts, width, extra[0], extra[1])
+            ranges = [at[count + i] for i in range(len(columns))]
+            down = fetch_columns(refs[len(args) - 1], ranges, width, extra[0], extra[1])
+        row = 0
+        for part, size in zip(parts, depths):
+            whole[:, row : row + size] = part[...]
+            row += size
 
         def store(i, n):
             target = (first, second)[i]
@@ -141,7 +152,7 @@
         def _(n):
             for wait in waits:
                 wait(n).wait()
-            product = jnp.dot(piece[...], both[n], preferred_element_type=jnp.float32)
+            product = jnp.dot(whole[...], both[n], preferred_element_type=jnp.float32)
             gate, up = product[:, :tile], product[:, tile:]
             if given:
                 gate = gate + before[0][n]
@@ -165,7 +176,9 @@
     return pl.pallas_call(
         kernel,
         out_shape=out_shape,
-        in_specs=[pl.BlockSpec(memory_space=pltpu.SMEM), vmem()] + [hbm()] * (len(args) - 1),
+        in_specs=[pl.BlockSpec(memory_space=pltpu.SMEM)]
+        + [vmem()] * count
+        + [hbm()] * (len(args) - count),
         out_specs=out_specs,
         scratch_shapes=scratch,
         compiler_params=pltpu.CompilerParams(vmem_limit_bytes=VMEM_BYTES),
@@ -180,7 +193,7 @@
 
 def drop(hidden, w_down, start, width, dtype):
     rows, depth = hidden.shape
-    tile = tile_of(width)
+    tile = tile_of(width, 1024)
 
     def kernel(at, hidden, w_down, out, *scratch):
         copy = fetch_columns(w_down, [at[0]], width, scratch[0], scratch[1])
@@ -263,7 +276,7 @@
         return lax.ppermute(value, "tensor", [(i, (i + step) % ranks) for i in range(ranks)])
 
     share = width // ranks
-    shared = share // 4 * 3
+    shared = round(share * 5 / 8 / LANES) * LANES
     direct_at = ranks * shared
 
     def placed(features):
@@ -271,29 +284,33 @@
 
     mine = lax.dynamic_slice_in_dim(tokens, me * shared, shared, axis=1)
     own = swap(placed(mine), experts)
-    cut = shared // CUTS
+    cut = pl.cdiv(shared, 2 * LANES) * LANES
     others = []
-    for at in range(0, shared, cut):
+    for begin, end in ((0, cut), (cut, shared)):
         for step in range(1, ranks):
-            sent = send_up(own[:, at : at + cut], ranks - step)
-            others.append((sent, rank_at(step) * shared + at))
+            sent = send_up(own[:, begin:end], ranks - step)
+            others.append((sent, rank_at(step) * shared + begin))
     direct = swap(placed(tokens[:, direct_at:]), experts)
-    sums = lift(own, me * shared, w_gate, w_up)
-    for piece, at in others[: 1 - ranks]:
-        sums = lift(piece, at, w_gate, w_up, sums)
-    sums = lift(direct, jnp.int32(direct_at), w_gate, w_up, sums)
-    for piece, at in others[1 - ranks : -1]:
-        sums = lift(piece, at, w_gate, w_up, sums)
-
-    early = share // 8 * 3
+    sums = lift([own], [me * shared], w_gate, w_up)
+    for piece, at in others[:-1]:
+        sums = lift([piece], [at], w_gate, w_up, sums)
+
+    early = round(share * 7 / 16 / 128) * 128
     columns = [jnp.int32(rank * share) for rank in range(ranks)]
-    piece, at = others[-1]
-    hidden, partial = lift(piece, at, w_gate, w_up, sums, (w_down, columns, early))
+    last, last_at = others[-1]
+    hidden, partial = lift(
+        [last, direct],
+        [last_at, jnp.int32(direct_at)],
+        w_gate,
+        w_up,
+        sums,
+        (w_down, columns, early),
+    )
     returned = swap(partial, experts)
-    cut = pl.cdiv(share - early, 2 * LANES) * LANES
+    edges = [early, early + pl.cdiv(share - early, 256) * 128, share]
     owned = []
-    for at in range(early, share, cut):
-        cut = min(cut, share - at)
+    for at, end in zip(edges[:-1], edges[1:]):
+        cut = end - at
         arrived = [
             send_up(drop(hidden, w_down, rank_at(step) * share + at, cut, jnp.bfloat16), step)
             for step in range(1, ranks)

time: 162 us -> 150 us (0.926)
  Pallas kernels: 54.3 us -> 42.5 us
  waiting for transfers between devices: 55.4 us -> 61.6 us
  starting transfers between devices: 29.9 us -> 25.3 us
  matrix products: 7.28 us -> 11.5 us
  other arithmetic: 6.6 us -> 3.15 us
    pallas_call x5 -> x3, Pallas kernels: 41.6 us -> 31.9 us  [lift(): pl.pallas_call(kernel, out_shape=out_shape, in_specs=[pl.BlockSpec(memory...]
    ppermute x6 -> x5, waiting for transfers between devices: 18.4 us -> 24.9 us  [send_up(): lax.ppermute(value, 'tensor', [(i, (i + step) % ranks) for i in range(ran...]
    dot_general x6, matrix products: 2.33 us -> 6.43 us  [mix(): lax.dot_general(w, returned, (((0,), (0,)), ((), ())), preferred_element_...]
    all_to_all x4, starting transfers between devices: 25.3 us -> 21.9 us  [swap(): lax.all_to_all(value.reshape(experts, slots // experts, width), 'expert',...]
    unnamed x24 -> x12, local copies, waits for them, and re-layouts: 6.25 us -> 3.13 us
    pallas_call x4, Pallas kernels: 12.8 us -> 10.6 us  [drop(): pl.pallas_call(kernel, out_shape=jax.ShapeDtypeStruct((rows, width), dtyp...]
    convert_element_type x2, other arithmetic: 2.35 us -> 0.21 us  [on_device(): owned.append(value.astype(jnp.bfloat16))]
    ppermute x6 -> x5, starting transfers between devices: 4.69 us -> 3.4 us  [send_up(): lax.ppermute(value, 'tensor', [(i, (i + step) % ranks) for i in range(ran...]
  transfers between devices with their start and end apart: 10 -> 9, of which waited for: 5 -> 8; matrix products, arithmetic and copies ran while one was open for 5% -> 7% of each run, Pallas kernels for 26% -> 17%
where the time goes in v7:
time: 150 us; the launch traced here: 149 us
  waiting for transfers between devices  61.6 us (41%)
  Pallas kernels  42.5 us (28%)
  starting transfers between devices  25.3 us (17%)
  matrix products  11.5 us (8%)
  local copies, waits for them, and re-layouts  4.9 us (3%)
  other arithmetic  3.15 us (2%)
    all_to_all x4, waiting for transfers between devices, swap(): lax.all_to_all(value.reshape(experts, slots // experts, width), 'expert',...  36.8 us
    pallas_call x3, Pallas kernels, lift(): pl.pallas_call(kernel, out_shape=out_shape, in_specs=[pl.BlockSpec(memory...  31.9 us
    ppermute x5, waiting for transfers between devices, send_up(): lax.ppermute(value, 'tensor', [(i, (i + step) % ranks) for i in range(ran...  24.9 us
    all_to_all x4, starting transfers between devices, swap(): lax.all_to_all(value.reshape(experts, slots // experts, width), 'expert',...  21.9 us
    pallas_call x4, Pallas kernels, drop(): pl.pallas_call(kernel, out_shape=jax.ShapeDtypeStruct((rows, width), dtyp...  10.6 us
    dot_general x6, matrix products, mix(): lax.dot_general(w, returned, (((0,), (0,)), ((), ())), preferred_element_...  6.43 us
    dot_general x2, matrix products, placed(): jnp.dot(chosen, features, preferred_element_type=jnp.float32)  4.89 us
    ppermute x5, starting transfers between devices, send_up(): lax.ppermute(value, 'tensor', [(i, (i + step) % ranks) for i in range(ran...  3.4 us
  transfers between devices with their start and end apart: 9, of which 8 were waited for; matrix products, arithmetic and copies ran while one was open for 7% of the time, Pallas kernels for 17%

profile of v7, /device:TPU:11, one launch (start us, length us, event | category | flops | bytes accessed | tf_op | source)
XLA Modules:
  0.0 149.2 jit_solution(328250132412845451)
XLA Ops:
  1.1 2.3 %convolution_convert_fusion = bf16[384,1280]{1,0:T(8,128)(2,1)} fusion(pred[384,128]{1,0:T(32,128)(4,1)S(1)} %fusion.10, bf16[128,4096]{1,0:T(8,128)(2,1)} %param.6, s32[]{:T(128)S(6)} %select_n.61), kind=kOutput, calls=%fused_computation | convolution fusion | flops 126320640 | bytes 1359876 | tf_op jit(solution)/shard_map/dot_general | solution.py:283
  3.5 6.6 %all-to-all-start = ((bf16[16,24,1280]{2,1,0:T(8,128)(2,1)}), bf16[16,24,1280]{2,1,0:T(8,128)(2,1)S(1)}, u32[]{:S(2)}, u32[]{:S(2)}) async-start(bf16[16,24,1280]{2,1,0:T(8,128)(2,1)} %bitcast.6), calls=%async_computation | async-start | bytes 1966080 | tf_op jit(solution)/shard_map/all_to_all | solution.py:244
  10.1 2.5 %convolution_convert_fusion.1 = bf16[384,1536]{1,0:T(8,128)(2,1)} fusion(pred[384,128]{1,0:T(32,128)(4,1)S(1)} %fusion.10, bf16[128,4096]{1,0:T(8,128)(2,1)} %param.6), kind=kOutput, calls=%fused_computation.1 | convolution fusion | flops 151584768 | bytes 1622016 | tf_op jit(solution)/shard_map/dot_general | solution.py:283
  12.6 21.0 %all-to-all-done = bf16[16,24,1280]{2,1,0:T(8,128)(2,1)S(1)} async-done(((bf16[16,24,1280]{2,1,0:T(8,128)(2,1)}), bf16[16,24,1280]{2,1,0:T(8,128)(2,1)S(1)}, u32[]{:S(2)}, u32[]{:S(2)}) %all-to-all-start) | async-done | bytes 983072 | tf_op jit(solution)/shard_map/all_to_all | solution.py:244
  33.6 4.9 %all-to-all-start.1 = ((bf16[16,24,1536]{2,1,0:T(8,128)(2,1)}), bf16[16,24,1536]{2,1,0:T(8,128)(2,1)S(1)}, u32[]{:S(2)}, u32[]{:S(2)}) async-start(bf16[16,24,1536]{2,1,0:T(8,128)(2,1)} %bitcast.82), calls=%async_computation.1 | async-start | bytes 2359296 | tf_op jit(solution)/shard_map/all_to_all | solution.py:244
  41.7 8.5 %lift.3 = (f32[384,1792]{1,0:T(8,128)S(1)}, f32[384,1792]{1,0:T(8,128)}) custom-call(s32[1]{0:T(128)} %bitcast.13.at, bf16[384,1280]{1,0:T(8,128)(2,1)S(1)} %bitcast.69, bf16[4096,1792]{1,0:T(8,128)(2,1)} %bitcast.76, bf16[4096,1792]{1,0:T(8,128)(2,1)} %bitcast.79), custom_call_target="tpu_custom_call" | custom-call | flops 3523215360 | bytes 20185088 | tf_op jit(solution)/shard_map/lift/pallas_call | solution.py:176
  51.7 2.4 %collective-permute-done.1.refs_0_ = bf16[384,768]{1,0:T(8,128)(2,1)S(1)} collective-permute-done((bf16[384,768]{1,0:T(8,128)(2,1)}, bf16[384,768]{1,0:T(8,128)(2,1)S(1)}, u32[]{:S(2)}, u32[]{:S(2)}) %collective-permute-start.1) | collective-permute-done | bytes 589856 | tf_op jit(solution)/shard_map/ppermute | solution.py:276
  54.1 6.8 %lift.4 = (f32[384,1792]{1,0:T(8,128)S(1)}, f32[384,1792]{1,0:T(8,128)}) custom-call(s32[1]{0:T(128)} %bitcast.12.at, bf16[384,768]{1,0:T(8,128)(2,1)S(1)} %collective-permute-done.1.refs_0_, bf16[4096,1792]{1,0:T(8,128)(2,1)} %bitcast.77, bf16[4096,1792]{1,0:T(8,128)(2,1)} %bitcast.80, f32[384,1792]{1,0:T(8,128)} %copy-done.1, ...), custom_call_target="tpu_custom_call" | custom-call | flops 2113929216 | bytes 16515072 | tf_op jit(solution)/shard_map/lift/pallas_call | solution.py:176
  61.0 1.6 %copy-done = f32[384,1792]{1,0:T(8,128)} copy-done((f32[384,1792]{1,0:T(8,128)}, f32[384,1792]{1,0:T(8,128)S(1)}, u32[]{:S(2)}) %copy-start) | copy-done | bytes 2752536
  62.6 3.5 %all-to-all-done.1 = bf16[16,24,1536]{2,1,0:T(8,128)(2,1)S(1)} async-done(((bf16[16,24,1536]{2,1,0:T(8,128)(2,1)}), bf16[16,24,1536]{2,1,0:T(8,128)(2,1)S(1)}, u32[]{:S(2)}, u32[]{:S(2)}) %all-to-all-start.1) | async-done | bytes 1179680 | tf_op jit(solution)/shard_map/all_to_all | solution.py:244
  66.1 16.6 %lift.5 = (bf16[384,1792]{1,0:T(8,128)(2,1)S(1)}, bf16[384,1792]{1,0:T(8,128)(2,1)}) custom-call(s32[4]{0:T(128)S(1)} %pad_add_fusion.at, bf16[384,512]{1,0:T(8,128)(2,1)S(1)} %collective-permute-done.refs_0_, bf16[384,1536]{1,0:T(8,128)(2,1)S(1)} %bitcast.70, bf16[4096,1792]{1,0:T(8,128)(2,1)} %bitcast.78, bf16[4096,1792]{1,0:T(8,128)(2,1)} %bitcast.81, ...), custom_call_target="tpu_custom_call" | custom-call | flops 8103395328 | bytes 32112640 | tf_op jit(solution)/shard_map/lift/pallas_call | solution.py:176
  82.7 5.1 %all-to-all-start.2 = ((bf16[16,24,1792]{2,1,0:T(8,128)(2,1)}), bf16[16,24,1792]{2,1,0:T(8,128)(2,1)}, u32[]{:S(2)}, u32[]{:S(2)}) async-start(bf16[16,24,1792]{2,1,0:T(8,128)(2,1)} %bitcast.83), calls=%async_computation.2 | async-start | bytes 2752512 | tf_op jit(solution)/shard_map/all_to_all | solution.py:244
  87.8 2.4 %drop.7 = bf16[384,512]{1,0:T(8,128)(2,1)S(1)} custom-call(s32[1]{0:T(128)} %bitcast.20.at, bf16[384,1792]{1,0:T(8,128)(2,1)S(1)} %get-tuple-element.19.hidden, bf16[1792,4096]{1,0:T(8,128)(2,1)} %bitcast.72), custom_call_target="tpu_custom_call" | custom-call | flops 704643072 | bytes 1835008 | tf_op jit(solution)/shard_map/drop/pallas_call | solution.py:202
  90.5 2.9 %drop.5 = bf16[384,640]{1,0:T(8,128)(2,1)S(1)} custom-call(s32[1]{0:T(128)} %bitcast.18.at, bf16[384,1792]{1,0:T(8,128)(2,1)S(1)} %get-tuple-element.19.hidden, bf16[1792,4096]{1,0:T(8,128)(2,1)} %bitcast.73), custom_call_target="tpu_custom_call" | custom-call | flops 880803840 | bytes 2293760 | tf_op jit(solution)/shard_map/drop/pallas_call | solution.py:202
  94.8 2.4 %drop.6 = f32[384,512]{1,0:T(8,128)S(1)} custom-call(s32[1]{0:T(128)} %bitcast.19.at, bf16[384,1792]{1,0:T(8,128)(2,1)S(1)} %get-tuple-element.19.hidden, bf16[1792,4096]{1,0:T(8,128)(2,1)} %bitcast.74), custom_call_target="tpu_custom_call" | custom-call | flops 704643072 | bytes 1835008 | tf_op jit(solution)/shard_map/drop/pallas_call | solution.py:202
  97.2 2.9 %drop.4 = f32[384,640]{1,0:T(8,128)S(1)} custom-call(s32[1]{0:T(128)} %bitcast.17.at, bf16[384,1792]{1,0:T(8,128)(2,1)S(1)} %get-tuple-element.19.hidden, bf16[1792,4096]{1,0:T(8,128)(2,1)} %bitcast.75), custom_call_target="tpu_custom_call" | custom-call | flops 880803840 | bytes 2293760 | tf_op jit(solution)/shard_map/drop/pallas_call | solution.py:202
  100.8 10.4 %collective-permute-done.2 = bf16[384,640]{1,0:T(8,128)(2,1)S(1)} collective-permute-done((bf16[384,640]{1,0:T(8,128)(2,1)S(1)}, bf16[384,640]{1,0:T(8,128)(2,1)S(1)}, u32[]{:S(2)}, u32[]{:S(2)}) %collective-permute-start.2) | collective-permute-done | bytes 491552 | tf_op jit(solution)/shard_map/ppermute | solution.py:276
  111.3 8.0 %all-to-all-done.2 = bf16[16,24,1792]{2,1,0:T(8,128)(2,1)} async-done(((bf16[16,24,1792]{2,1,0:T(8,128)(2,1)}), bf16[16,24,1792]{2,1,0:T(8,128)(2,1)}, u32[]{:S(2)}, u32[]{:S(2)}) %all-to-all-start.2) | async-done | bytes 1376288 | tf_op jit(solution)/shard_map/all_to_all | solution.py:244
  120.3 5.3 %all-to-all-start.3 = ((bf16[16,24,1152]{2,1,0:T(8,128)(2,1)}), bf16[16,24,1152]{2,1,0:T(8,128)(2,1)S(1)}, u32[]{:S(2)}, u32[]{:S(2)}) async-start(bf16[16,24,1152]{2,1,0:T(8,128)(2,1)} %bitcast.23), calls=%async_computation.3 | async-start | bytes 1769472 | tf_op jit(solution)/shard_map/all_to_all | solution.py:244
  125.7 1.8 %fusion.37 = f32[128,1792]{1,0:T(8,128)S(1)} fusion(bf16[384,128]{1,0:T(8,128)(2,1)S(1)} %get-tuple-element.24, bf16[384,1792]{1,0:T(8,128)(2,1)} %bitcast.16), kind=kOutput, calls=%fused_computation.63 | convolution fusion | flops 176160768 | bytes 2392064 | tf_op jit(solution)/shard_map/dot_general | solution.py:255
  127.4 1.8 %convolution_add_fusion.1 = f32[128,1792]{1,0:T(8,128)S(1)} fusion(f32[128,1792]{1,0:T(8,128)S(1)} %fusion.37, bf16[384,128]{1,0:T(8,128)(2,1)S(1)} %get-tuple-element.25, bf16[384,1792]{1,0:T(8,128)(2,1)} %bitcast.16), kind=kOutput, calls=%fused_computation.3 | convolution fusion | flops 176390144 | bytes 3309568 | tf_op jit(solution)/shard_map/dot_general | solution.py:255
  129.2 1.8 %convolution_add_fusion = f32[128,1792]{1,0:T(8,128)S(1)} fusion(f32[128,1792]{1,0:T(8,128)S(1)} %convolution_add_fusion.1, bf16[384,128]{1,0:T(8,128)(2,1)S(1)} %get-tuple-element.23, bf16[384,1792]{1,0:T(8,128)(2,1)} %bitcast.16), kind=kOutput, calls=%fused_computation.2 | convolution fusion | flops 176390144 | bytes 3309568 | tf_op jit(solution)/shard_map/dot_general | solution.py:255
  131.4 11.5 %collective-permute-done.4 = f32[128,896]{1,0:T(8,128)S(1)} collective-permute-done((f32[128,896]{1,0:T(8,128)S(1)}, f32[128,896]{1,0:T(8,128)S(1)}, u32[]{:S(2)}, u32[]{:S(2)}) %collective-permute-start.4) | collective-permute-done | bytes 458784 | tf_op jit(solution)/shard_map/ppermute | solution.py:276
  142.9 4.3 %all-to-all-done.3 = bf16[16,24,1152]{2,1,0:T(8,128)(2,1)S(1)} async-done(((bf16[16,24,1152]{2,1,0:T(8,128)(2,1)}), bf16[16,24,1152]{2,1,0:T(8,128)(2,1)S(1)}, u32[]{:S(2)}, u32[]{:S(2)}) %all-to-all-start.3) | async-done | bytes 884768 | tf_op jit(solution)/shard_map/all_to_all | solution.py:244
  (39 shorter events, 11.7 us)
Async XLA Ops:
  0.8 2.7 %copy-start.2 = (s32[384]{0:T(512)}, s32[384]{0:T(512)S(1)}, u32[]{:S(2)}) copy-start(s32[384]{0:T(512)S(1)} %eq.62) | copy-start | bytes 4612
  3.5 30.1 %all-to-all-start = ((bf16[16,24,1280]{2,1,0:T(8,128)(2,1)}), bf16[16,24,1280]{2,1,0:T(8,128)(2,1)S(1)}, u32[]{:S(2)}, u32[]{:S(2)}) async-start(bf16[16,24,1280]{2,1,0:T(8,128)(2,1)} %bitcast.6), calls=%async_computation | async-start | bytes 1966080 | tf_op jit(solution)/shard_map/all_to_all | solution.py:244
  33.6 32.4 %all-to-all-start.1 = ((bf16[16,24,1536]{2,1,0:T(8,128)(2,1)}), bf16[16,24,1536]{2,1,0:T(8,128)(2,1)S(1)}, u32[]{:S(2)}, u32[]{:S(2)}) async-start(bf16[16,24,1536]{2,1,0:T(8,128)(2,1)} %bitcast.82), calls=%async_computation.1 | async-start | bytes 2359296 | tf_op jit(solution)/shard_map/all_to_all | solution.py:244
  39.4 14.8 %collective-permute-start.1 = (bf16[384,768]{1,0:T(8,128)(2,1)}, bf16[384,768]{1,0:T(8,128)(2,1)S(1)}, u32[]{:S(2)}, u32[]{:S(2)}) collective-permute-start(bf16[384,768]{1,0:T(8,128)(2,1)} %slice.13), channel_id=1, source_target_pairs={{0,1},{1,0},{2,3},{3,2},{4,5},{5,4},{6,7},{7,6},{8,9},{9,8},{10,11... | collective-permute-start | bytes 1769480 | tf_op jit(solution)/shard_map/ppermute | solution.py:276
  40.5 25.6 %collective-permute-start = (bf16[384,512]{1,0:T(8,128)(2,1)}, bf16[384,512]{1,0:T(8,128)(2,1)S(1)}, u32[]{:S(2)}, u32[]{:S(2)}) collective-permute-start(bf16[384,512]{1,0:T(8,128)(2,1)} %slice.12), channel_id=1, source_target_pairs={{0,1},{1,0},{2,3},{3,2},{4,5},{5,4},{6,7},{7,6},{8,9},{9,8},{10,11... | collective-permute-start | bytes 1179656 | tf_op jit(solution)/shard_map/ppermute | solution.py:276
  50.2 1.5 %copy-start.1 = (f32[384,1792]{1,0:T(8,128)}, f32[384,1792]{1,0:T(8,128)S(1)}, u32[]{:S(2)}) copy-start(f32[384,1792]{1,0:T(8,128)S(1)} %get-tuple-element.14.refs_3_) | copy-start | bytes 8257540
  61.0 1.6 %copy-start = (f32[384,1792]{1,0:T(8,128)}, f32[384,1792]{1,0:T(8,128)S(1)}, u32[]{:S(2)}) copy-start(f32[384,1792]{1,0:T(8,128)S(1)} %get-tuple-element.16.refs_4_) | copy-start | bytes 8257540
  82.6 5.1 %copy-start.4 = (s32[128,2]{0,1:T(2,128)S(1)}, s32[128,2]{0,1:T(2,128)}, u32[]{:S(2)}) copy-start(s32[128,2]{0,1:T(2,128)} %param.7) | copy-start | bytes 3076
  82.6 5.1 %copy-start.5 = (f32[128,2]{0,1:T(2,128)S(1)}, f32[128,2]{0,1:T(2,128)}, u32[]{:S(2)}) copy-start(f32[128,2]{0,1:T(2,128)} %param.8) | copy-start | bytes 3076
  82.7 36.7 %all-to-all-start.2 = ((bf16[16,24,1792]{2,1,0:T(8,128)(2,1)}), bf16[16,24,1792]{2,1,0:T(8,128)(2,1)}, u32[]{:S(2)}, u32[]{:S(2)}) async-start(bf16[16,24,1792]{2,1,0:T(8,128)(2,1)} %bitcast.83), calls=%async_computation.2 | async-start | bytes 2752512 | tf_op jit(solution)/shard_map/all_to_all | solution.py:244
  90.2 10.5 %collective-permute-start.3 = (bf16[384,512]{1,0:T(8,128)(2,1)S(1)}, bf16[384,512]{1,0:T(8,128)(2,1)S(1)}, u32[]{:S(2)}, u32[]{:S(2)}) collective-permute-start(bf16[384,512]{1,0:T(8,128)(2,1)S(1)} %drop.7), channel_id=1, source_target_pairs={{0,1},{1,0},{2,3},{3,2},{4,5},{5,4},{6,7},{7,6},{8,9},{9,8},{10,11... | collective-permute-start | bytes 1179656 | tf_op jit(solution)/shard_map/ppermute | solution.py:276
  90.5 4.2 %copy-start.3 = (s32[384]{0:T(512)S(1)}, s32[384]{0:T(512)}, u32[]{:S(2)}) copy-start(s32[384]{0:T(512)} %copy-done.2) | copy-start | bytes 4612
  93.4 17.8 %collective-permute-start.2 = (bf16[384,640]{1,0:T(8,128)(2,1)S(1)}, bf16[384,640]{1,0:T(8,128)(2,1)S(1)}, u32[]{:S(2)}, u32[]{:S(2)}) collective-permute-start(bf16[384,640]{1,0:T(8,128)(2,1)S(1)} %drop.5), channel_id=1, source_target_pairs={{0,1},{1,0},{2,3},{3,2},{4,5},{5,4},{6,7},{7,6},{8,9},{9,8},{10,11... | collective-permute-start | bytes 1474568 | tf_op jit(solution)/shard_map/ppermute | solution.py:276
  120.3 26.9 %all-to-all-start.3 = ((bf16[16,24,1152]{2,1,0:T(8,128)(2,1)}), bf16[16,24,1152]{2,1,0:T(8,128)(2,1)S(1)}, u32[]{:S(2)}, u32[]{:S(2)}) async-start(bf16[16,24,1152]{2,1,0:T(8,128)(2,1)} %bitcast.23), calls=%async_computation.3 | async-start | bytes 1769472 | tf_op jit(solution)/shard_map/all_to_all | solution.py:244
  131.0 11.8 %collective-permute-start.4 = (f32[128,896]{1,0:T(8,128)S(1)}, f32[128,896]{1,0:T(8,128)S(1)}, u32[]{:S(2)}, u32[]{:S(2)}) collective-permute-start(f32[128,896]{1,0:T(8,128)S(1)} %constant_dynamic-slice_fusion), channel_id=1, source_target_pairs={{0,1},{1,0},{2,3},{3,2},{4,5},{5,4},{6,7},{7,6},{8,9},{9,8},{10,11... | collective-permute-start | bytes 1376264 | tf_op jit(solution)/shard_map/ppermute | solution.py:276

commit v8 on v7

--- a/solution.py
+++ b/solution.py
@@ -18,66 +18,51 @@
     return width
 
 
-def tile_copies(tiles, copy):
-    for n in range(tiles):
-        copy(n).start()
-    return copy
-
-
-def span(n, tile):
-    return pl.ds(pl.multiple_of(n * tile, 128), tile)
-
-
-def fetch_rows(source, start, target, row, depth, column, sems):
-    tiles, _, both = target.shape
-    tile = both // 2
-    return tile_copies(
-        tiles,
-        lambda n: pltpu.make_async_copy(
-            source.at[pl.ds(start, depth), span(n, tile)],
-            target.at[n, pl.ds(row, depth), pl.ds(column, tile)],
-            sems.at[n],
-        ),
-    )
-
-
-def fetch_sums(source, target, sems):
-    tiles, rows, tile = target.shape
-    return tile_copies(
-        tiles,
-        lambda n: pltpu.make_async_copy(source.at[:, span(n, tile)], target.at[n], sems.at[n]),
-    )
-
-
-def fetch_columns(source, starts, width, target, sems):
+def vmem():
+    return pl.BlockSpec(memory_space=pltpu.VMEM)
+
+
+def hbm():
+    return pl.BlockSpec(memory_space=pl.ANY)
+
+
+def dma(count):
+    return pltpu.SemaphoreType.DMA((count,))
+
+
+def in_turn(groups, ahead):
+    for group in groups[:ahead]:
+        for copy in group:
+            copy.start()
+    left = iter(range(len(groups)))
+
+    def wait():
+        now = next(left)
+        if now + ahead < len(groups):
+            for copy in groups[now + ahead]:
+                copy.start()
+        for copy in groups[now]:
+            copy.wait()
+
+    return wait
+
+
+def column_groups(source, starts, width, target, sems):
     tiles, depth, tile = target.shape
     each = width // tile
-
-    def copy(n):
+    groups = []
+    for n in range(tiles):
         at = pl.multiple_of(starts[n // each] + (n % each) * tile, 128)
-        return pltpu.make_async_copy(source.at[:, pl.ds(at, tile)], target.at[n], sems.at[n])
-
-    return tile_copies(tiles, copy)
-
-
-def drop_tiles(hidden, down_tiles, copy, out):
-    tiles, depth, tile = down_tiles.shape
-    for n in range(tiles):
-        copy(n).wait()
-        value = jnp.dot(hidden[...], down_tiles[n], preferred_element_type=jnp.float32)
-        out[:, n * tile : (n + 1) * tile] = value.astype(out.dtype)
-
-
-def vmem():
-    return pl.BlockSpec(memory_space=pltpu.VMEM)
-
-
-def hbm():
-    return pl.BlockSpec(memory_space=pl.ANY)
-
-
-def buffer(shape, dtype=jnp.bfloat16):
-    return [pltpu.VMEM(shape, dtype), pltpu.SemaphoreType.DMA((shape[0],))]
+        groups.append(
+            [pltpu.make_async_copy(source.at[:, pl.ds(at, tile)], target.at[n], sems.at[n])]
+        )
+    return groups
+
+
+def drop_tile(hidden, tiles, n, out):
+    tile = tiles.shape[2]
+    value = jnp.dot(hidden[...], tiles[n], preferred_element_type=jnp.float32)
+    out[:, n * tile : (n + 1) * tile] = value.astype(out.dtype)
 
 
 def lift(pieces, starts, w_gate, w_up, sums=None, back=None):
@@ -88,27 +73,27 @@
     hidden = w_gate.shape[1]
     tile = tile_of(hidden)
     tiles = hidden // tile
-    given = [] if sums is None else list(sums)
+    given = [] if sums is None else [sums]
     scalars = list(starts)
-    scratch = [pltpu.VMEM((rows, depth), jnp.bfloat16)]
-    scratch += [pltpu.VMEM((tiles, depth, 2 * tile), jnp.bfloat16)]
-    scratch += [pltpu.SemaphoreType.DMA((tiles,))] * (2 * count)
-    for _ in given:
-        scratch += buffer((tiles, rows, tile), jnp.float32)
+    args = [*pieces, w_gate, w_up, *given]
+    scratch = [
+        pltpu.VMEM((rows, depth), jnp.bfloat16),
+        pltpu.VMEM((tiles, depth, 2 * tile), jnp.bfloat16),
+        pltpu.VMEM((tiles, rows, 2 * tile), jnp.float32),
+    ]
+    scratch += [dma(tiles)] * (2 * count + 2)
     flops = 4 * rows * depth * hidden
     moved = 4 * depth * hidden + 16 * rows * hidden
     if back is None:
-        for _ in range(2):
-            scratch += buffer((tiles, rows, tile), jnp.float32)
-        args = [*pieces, w_gate, w_up] + given
-        out_shape = [jax.ShapeDtypeStruct((rows, hidden), jnp.float32)] * 2
-        out_specs = [hbm(), hbm()]
+        out_shape = [jax.ShapeDtypeStruct((tiles, rows, 2 * tile), jnp.float32)]
+        out_specs = [hbm()]
     else:
         w_down, columns, width = back
         wide = tile_of(width, 1024)
-        scratch += buffer((len(columns) * width // wide, hidden, wide))
+        drops = len(columns) * width // wide
+        scratch += [pltpu.VMEM((drops, hidden, wide), jnp.bfloat16), dma(drops)]
         scalars += list(columns)
-        args = [*pieces, w_gate, w_up] + given + [w_down]
+        args += [w_down]
         out_shape = [
             jax.ShapeDtypeStruct((rows, hidden), jnp.bfloat16),
             jax.ShapeDtypeStruct((rows, len(columns) * width), jnp.bfloat16),
@@ -118,60 +103,73 @@
         moved += 2 * hidden * len(columns) * width
 
     def kernel(at, *refs):
-        parts, (w_gate, w_up) = refs[:count], refs[count : count + 2]
-        sums = refs[count + 2 : count + 2 + len(given)]
-        first, second = refs[len(args) : len(args) + 2]
-        whole, both = refs[len(args) + 2 : len(args) + 4]
-        sems = refs[len(args) + 4 : len(args) + 4 + 2 * count]
-        extra = refs[len(args) + 4 + 2 * count :]
-        waits = []
-        row = 0
-        for i, part in enumerate(parts):
-            begin = pl.multiple_of(at[i], 128)
-            for source, column, sem in ((w_gate, 0, sems[2 * i]), (w_up, tile, sems[2 * i + 1])):
-                waits.append(fetch_rows(source, begin, both, row, depths[i], column, sem))
-            row += depths[i]
-        for i, source in enumerate(sums):
-            waits.append(fetch_sums(source, extra[2 * i], extra[2 * i + 1]))
-        before, extra = extra[: 2 * len(given) : 2], extra[2 * len(given) :]
+        parts, refs = refs[:count], refs[count:]
+        (gate_from, up_from), refs = refs[:2], refs[2:]
+        before, refs = refs[: len(given)], refs[len(given) :]
+        more = len(args) - count - 2 - len(given)
+        down_from, refs = refs[:more], refs[more:]
+        outs, refs = refs[: len(out_shape)], refs[len(out_shape) :]
+        whole, both, totals = refs[:3]
+        sems, (sum_sems, out_sems) = refs[3 : 3 + 2 * count], refs[3 + 2 * count : 5 + 2 * count]
+        groups = []
+        for n in range(tiles):
+            across = pl.ds(n * tile, tile)
+            group = []
+            row = 0
+            for i, size in enumerate(depths):
+                begin = pl.multiple_of(at[i], 128)
+                for side, source in enumerate((gate_from, up_from)):
+                    group.append(
+                        pltpu.make_async_copy(
+                            source.at[pl.ds(begin, size), across],
+                            both.at[n, pl.ds(row, size), pl.ds(side * tile, tile)],
+                            sems[2 * i + side].at[n],
+                        )
+                    )
+                row += size
+            for source in before:
+                group.append(
+                    pltpu.make_async_copy(source.at[n], totals.at[n], sum_sems.at[n])
+                )
+            groups.append(group)
         if back is not None:
             ranges = [at[count + i] for i in range(len(columns))]
-            down = fetch_columns(refs[len(args) - 1], ranges, width, extra[0], extra[1])
+            groups += column_groups(down_from[0], ranges, width, refs[-2], refs[-1])
+        wait = in_turn(groups, 2)
         row = 0
         for part, size in zip(parts, depths):
             whole[:, row : row + size] = part[...]
             row += size
 
-        def store(i, n):
-            target = (first, second)[i]
-            return pltpu.make_async_copy(
-                extra[2 * i].at[n], target.at[:, span(n, tile)], extra[2 * i + 1].at[n]
-            )
-
-        @pl.loop(0, tiles)
-        def _(n):
-            for wait in waits:
-                wait(n).wait()
+        def store(n):
+            return pltpu.make_async_copy(totals.at[n], outs[0].at[n], out_sems.at[n])
+
+        def settle(n, product):
+            if given:
+                product = product + totals[n]
+            if back is None:
+                totals[n] = product
+                store(n).start()
+            else:
+                gate, up = product[:, :tile], product[:, tile:]
+                value = gate / (1.0 + jnp.exp(-gate)) * up
+                outs[0][:, n * tile : (n + 1) * tile] = value.astype(jnp.bfloat16)
+
+        held = None
+        for n in range(tiles):
+            wait()
             product = jnp.dot(whole[...], both[n], preferred_element_type=jnp.float32)
-            gate, up = product[:, :tile], product[:, tile:]
-            if given:
-                gate = gate + before[0][n]
-                up = up + before[1][n]
-            if back is None:
-                extra[0][n] = gate
-                extra[2][n] = up
-                store(0, n).start()
-                store(1, n).start()
-            else:
-                silu = gate / (1.0 + jnp.exp(-gate))
-                first[:, span(n, tile)] = (silu * up).astype(jnp.bfloat16)
-
+            if held is not None:
+                settle(n - 1, held)
+            held = product
+        settle(tiles - 1, held)
         if back is None:
             for n in range(tiles):
-                store(0, n).wait()
-                store(1, n).wait()
+                store(n).wait()
         else:
-            drop_tiles(first, extra[0], down, second)
+            for n in range(drops):
+                wait()
+                drop_tile(outs[0], refs[-2], n, outs[1])
 
     return pl.pallas_call(
         kernel,
@@ -195,16 +193,21 @@
     rows, depth = hidden.shape
     tile = tile_of(width, 1024)
 
-    def kernel(at, hidden, w_down, out, *scratch):
-        copy = fetch_columns(w_down, [at[0]], width, scratch[0], scratch[1])
-        drop_tiles(hidden, scratch[0], copy, out)
+    def kernel(at, hidden, w_down, out, weight, sems):
+        wait = in_turn(column_groups(w_down, [at[0]], width, weight, sems), 2)
+        for n in range(width // tile):
+            wait()
+            drop_tile(hidden, weight, n, out)
 
     return pl.pallas_call(
         kernel,
         out_shape=jax.ShapeDtypeStruct((rows, width), dtype),
         in_specs=[pl.BlockSpec(memory_space=pltpu.SMEM), vmem(), hbm()],
         out_specs=vmem(),
-        scratch_shapes=buffer((width // tile, depth, tile)),
+        scratch_shapes=[
+            pltpu.VMEM((width // tile, depth, tile), jnp.bfloat16),
+            dma(width // tile),
+        ],
         compiler_params=pltpu.CompilerParams(vmem_limit_bytes=VMEM_BYTES),
         cost_estimate=pl.CostEstimate(
             flops=2 * rows * depth * width, bytes_accessed=2 * depth * width, transcendentals=0
@@ -291,9 +294,9 @@
             sent = send_up(own[:, begin:end], ranks - step)
             others.append((sent, rank_at(step) * shared + begin))
     direct = swap(placed(tokens[:, direct_at:]), experts)
-    sums = lift([own], [me * shared], w_gate, w_up)
+    (sums,) = lift([own], [me * shared], w_gate, w_up)
     for piece, at in others[:-1]:
-        sums = lift([piece], [at], w_gate, w_up, sums)
+        (sums,) = lift([piece], [at], w_gate, w_up, sums)
 
     early = round(share * 7 / 16 / 128) * 128
     columns = [jnp.int32(rank * share) for rank in range(ranks)]

time: 150 us -> 149 us (level)
  waiting for transfers between devices: 61.6 us -> 65 us
  local copies, waits for them, and re-layouts: 4.9 us -> 1.77 us
  Pallas kernels: 42.5 us -> 40.8 us
    unnamed x12 -> x8, local copies, waits for them, and re-layouts: 3.13 us -> 0.02 us
    ppermute x5, waiting for transfers between devices: 24.9 us -> 27.4 us  [send_up(): lax.ppermute(value, 'tensor', [(i, (i + step) % ranks) for i in range(ran...]
    pallas_call x3, Pallas kernels: 31.9 us -> 30.3 us  [lift(): pl.pallas_call(kernel, out_shape=out_shape, in_specs=[pl.BlockSpec(memory...]
where the time goes in v8:
time: 149 us; the launch traced here: 148 us
  waiting for transfers between devices  65 us (44%)
  Pallas kernels  40.8 us (27%)
  starting transfers between devices  25.5 us (17%)
  matrix products  11.4 us (8%)
  other arithmetic  3.15 us (2%)
  local copies, waits for them, and re-layouts  1.77 us (1%)
    all_to_all x4, waiting for transfers between devices, swap(): lax.all_to_all(value.reshape(experts, slots // experts, width), 'expert',...  37.6 us
    pallas_call x3, Pallas kernels, lift(): pl.pallas_call(kernel, out_shape=out_shape, in_specs=[pl.BlockSpec(memory...  30.3 us
    ppermute x5, waiting for transfers between devices, send_up(): lax.ppermute(value, 'tensor', [(i, (i + step) % ranks) for i in range(ran...  27.4 us
    all_to_all x4, starting transfers between devices, swap(): lax.all_to_all(value.reshape(experts, slots // experts, width), 'expert',...  22.1 us
    pallas_call x4, Pallas kernels, drop(): pl.pallas_call(kernel, out_shape=jax.ShapeDtypeStruct((rows, width), dtyp...  10.6 us
    dot_general x6, matrix products, mix(): lax.dot_general(w, returned, (((0,), (0,)), ((), ())), preferred_element_...  6.45 us
    dot_general x2, matrix products, placed(): jnp.dot(chosen, features, preferred_element_type=jnp.float32)  4.78 us
    ppermute x5, starting transfers between devices, send_up(): lax.ppermute(value, 'tensor', [(i, (i + step) % ranks) for i in range(ran...  3.38 us
  transfers between devices with their start and end apart: 9, of which 8 were waited for; matrix products, arithmetic and copies ran while one was open for 7% of the time, Pallas kernels for 17%

profile of v8, /device:TPU:11, one launch (start us, length us, event | category | flops | bytes accessed | tf_op | source)
XLA Modules:
  0.0 147.9 jit_solution(14608677678542566988)
XLA Ops:
  1.1 2.3 %convolution_convert_fusion = bf16[384,1280]{1,0:T(8,128)(2,1)} fusion(pred[384,128]{1,0:T(32,128)(4,1)S(1)} %fusion.10, bf16[128,4096]{1,0:T(8,128)(2,1)} %param.6, s32[]{:T(128)S(6)} %select_n.61), kind=kOutput, calls=%fused_computation | convolution fusion | flops 126320640 | bytes 1359876 | tf_op jit(solution)/shard_map/dot_general | solution.py:286
  3.5 6.6 %all-to-all-start = ((bf16[16,24,1280]{2,1,0:T(8,128)(2,1)}), bf16[16,24,1280]{2,1,0:T(8,128)(2,1)S(1)}, u32[]{:S(2)}, u32[]{:S(2)}) async-start(bf16[16,24,1280]{2,1,0:T(8,128)(2,1)} %bitcast.6), calls=%async_computation | async-start | bytes 1966080 | tf_op jit(solution)/shard_map/all_to_all | solution.py:247
  10.1 2.4 %convolution_convert_fusion.1 = bf16[384,1536]{1,0:T(8,128)(2,1)} fusion(pred[384,128]{1,0:T(32,128)(4,1)S(1)} %fusion.10, bf16[128,4096]{1,0:T(8,128)(2,1)} %param.6), kind=kOutput, calls=%fused_computation.1 | convolution fusion | flops 151584768 | bytes 1622016 | tf_op jit(solution)/shard_map/dot_general | solution.py:286
  12.5 21.1 %all-to-all-done = bf16[16,24,1280]{2,1,0:T(8,128)(2,1)S(1)} async-done(((bf16[16,24,1280]{2,1,0:T(8,128)(2,1)}), bf16[16,24,1280]{2,1,0:T(8,128)(2,1)S(1)}, u32[]{:S(2)}, u32[]{:S(2)}) %all-to-all-start) | async-done | bytes 983072 | tf_op jit(solution)/shard_map/all_to_all | solution.py:247
  33.6 4.9 %all-to-all-start.1 = ((bf16[16,24,1536]{2,1,0:T(8,128)(2,1)}), bf16[16,24,1536]{2,1,0:T(8,128)(2,1)S(1)}, u32[]{:S(2)}, u32[]{:S(2)}) async-start(bf16[16,24,1536]{2,1,0:T(8,128)(2,1)} %bitcast.82), calls=%async_computation.1 | async-start | bytes 2359296 | tf_op jit(solution)/shard_map/all_to_all | solution.py:247
  41.7 7.5 %lift.3.refs_3_ = f32[7,384,512]{2,1,0:T(8,128)} custom-call(s32[1]{0:T(128)} %bitcast.13.at, bf16[384,1280]{1,0:T(8,128)(2,1)S(1)} %bitcast.69, bf16[4096,1792]{1,0:T(8,128)(2,1)} %bitcast.76, bf16[4096,1792]{1,0:T(8,128)(2,1)} %bitcast.79), custom_call_target="tpu_custom_call" | custom-call | flops 3523215360 | bytes 20185088 | tf_op jit(solution)/shard_map/lift/pallas_call | solution.py:174
  49.1 5.0 %collective-permute-done.1.refs_0_ = bf16[384,768]{1,0:T(8,128)(2,1)S(1)} collective-permute-done((bf16[384,768]{1,0:T(8,128)(2,1)}, bf16[384,768]{1,0:T(8,128)(2,1)S(1)}, u32[]{:S(2)}, u32[]{:S(2)}) %collective-permute-start.1) | collective-permute-done | bytes 589856 | tf_op jit(solution)/shard_map/ppermute | solution.py:279
  54.1 7.7 %lift.4.refs_4_ = f32[7,384,512]{2,1,0:T(8,128)} custom-call(s32[1]{0:T(128)} %bitcast.12.at, bf16[384,768]{1,0:T(8,128)(2,1)S(1)} %collective-permute-done.1.refs_0_, bf16[4096,1792]{1,0:T(8,128)(2,1)} %bitcast.77, bf16[4096,1792]{1,0:T(8,128)(2,1)} %bitcast.80, f32[7,384,512]{2,1,0:T(8,128)} %lift.3.refs_3_), custom_call_target="tpu_custom_call" | custom-call | flops 2113929216 | bytes 16515072 | tf_op jit(solution)/shard_map/lift/pallas_call | solution.py:174
  61.8 4.2 %all-to-all-done.1 = bf16[16,24,1536]{2,1,0:T(8,128)(2,1)S(1)} async-done(((bf16[16,24,1536]{2,1,0:T(8,128)(2,1)}), bf16[16,24,1536]{2,1,0:T(8,128)(2,1)S(1)}, u32[]{:S(2)}, u32[]{:S(2)}) %all-to-all-start.1) | async-done | bytes 1179680 | tf_op jit(solution)/shard_map/all_to_all | solution.py:247
  66.0 15.1 %lift.5 = (bf16[384,1792]{1,0:T(8,128)(2,1)S(1)}, bf16[384,1792]{1,0:T(8,128)(2,1)}) custom-call(s32[4]{0:T(128)S(1)} %pad_add_fusion.at, bf16[384,512]{1,0:T(8,128)(2,1)S(1)} %collective-permute-done.refs_0_, bf16[384,1536]{1,0:T(8,128)(2,1)S(1)} %bitcast.70, bf16[4096,1792]{1,0:T(8,128)(2,1)} %bitcast.78, bf16[4096,1792]{1,0:T(8,128)(2,1)} %bitcast.81, ...), custom_call_target="tpu_custom_call" | custom-call | flops 8103395328 | bytes 32112640 | tf_op jit(solution)/shard_map/lift/pallas_call | solution.py:174
  81.2 5.3 %all-to-all-start.2 = ((bf16[16,24,1792]{2,1,0:T(8,128)(2,1)}), bf16[16,24,1792]{2,1,0:T(8,128)(2,1)}, u32[]{:S(2)}, u32[]{:S(2)}) async-start(bf16[16,24,1792]{2,1,0:T(8,128)(2,1)} %bitcast.83), calls=%async_computation.2 | async-start | bytes 2752512 | tf_op jit(solution)/shard_map/all_to_all | solution.py:247
  86.5 2.4 %drop.7 = bf16[384,512]{1,0:T(8,128)(2,1)S(1)} custom-call(s32[1]{0:T(128)} %bitcast.20.at, bf16[384,1792]{1,0:T(8,128)(2,1)S(1)} %get-tuple-element.11.hidden, bf16[1792,4096]{1,0:T(8,128)(2,1)} %bitcast.72), custom_call_target="tpu_custom_call" | custom-call | flops 704643072 | bytes 1835008 | tf_op jit(solution)/shard_map/drop/pallas_call | solution.py:202
  89.2 2.9 %drop.5 = bf16[384,640]{1,0:T(8,128)(2,1)S(1)} custom-call(s32[1]{0:T(128)} %bitcast.18.at, bf16[384,1792]{1,0:T(8,128)(2,1)S(1)} %get-tuple-element.11.hidden, bf16[1792,4096]{1,0:T(8,128)(2,1)} %bitcast.73), custom_call_target="tpu_custom_call" | custom-call | flops 880803840 | bytes 2293760 | tf_op jit(solution)/shard_map/drop/pallas_call | solution.py:202
  92.1 1.3 collective-permute-start.2
  93.5 2.4 %drop.6 = f32[384,512]{1,0:T(8,128)S(1)} custom-call(s32[1]{0:T(128)} %bitcast.19.at, bf16[384,1792]{1,0:T(8,128)(2,1)S(1)} %get-tuple-element.11.hidden, bf16[1792,4096]{1,0:T(8,128)(2,1)} %bitcast.74), custom_call_target="tpu_custom_call" | custom-call | flops 704643072 | bytes 1835008 | tf_op jit(solution)/shard_map/drop/pallas_call | solution.py:202
  95.9 2.9 %drop.4 = f32[384,640]{1,0:T(8,128)S(1)} custom-call(s32[1]{0:T(128)} %bitcast.17.at, bf16[384,1792]{1,0:T(8,128)(2,1)S(1)} %get-tuple-element.11.hidden, bf16[1792,4096]{1,0:T(8,128)(2,1)} %bitcast.75), custom_call_target="tpu_custom_call" | custom-call | flops 880803840 | bytes 2293760 | tf_op jit(solution)/shard_map/drop/pallas_call | solution.py:202
  99.5 10.4 %collective-permute-done.2 = bf16[384,640]{1,0:T(8,128)(2,1)S(1)} collective-permute-done((bf16[384,640]{1,0:T(8,128)(2,1)S(1)}, bf16[384,640]{1,0:T(8,128)(2,1)S(1)}, u32[]{:S(2)}, u32[]{:S(2)}) %collective-permute-start.2) | collective-permute-done | bytes 491552 | tf_op jit(solution)/shard_map/ppermute | solution.py:279
  110.0 8.0 %all-to-all-done.2 = bf16[16,24,1792]{2,1,0:T(8,128)(2,1)} async-done(((bf16[16,24,1792]{2,1,0:T(8,128)(2,1)}), bf16[16,24,1792]{2,1,0:T(8,128)(2,1)}, u32[]{:S(2)}, u32[]{:S(2)}) %all-to-all-start.2) | async-done | bytes 1376288 | tf_op jit(solution)/shard_map/all_to_all | solution.py:247
  119.0 5.3 %all-to-all-start.3 = ((bf16[16,24,1152]{2,1,0:T(8,128)(2,1)}), bf16[16,24,1152]{2,1,0:T(8,128)(2,1)S(1)}, u32[]{:S(2)}, u32[]{:S(2)}) async-start(bf16[16,24,1152]{2,1,0:T(8,128)(2,1)} %bitcast.23), calls=%async_computation.3 | async-start | bytes 1769472 | tf_op jit(solution)/shard_map/all_to_all | solution.py:247
  124.4 1.8 %fusion.37 = f32[128,1792]{1,0:T(8,128)S(1)} fusion(bf16[384,128]{1,0:T(8,128)(2,1)S(1)} %get-tuple-element.16, bf16[384,1792]{1,0:T(8,128)(2,1)} %bitcast.16), kind=kOutput, calls=%fused_computation.63 | convolution fusion | flops 176160768 | bytes 2392064 | tf_op jit(solution)/shard_map/dot_general | solution.py:258
  126.2 1.8 %convolution_add_fusion.1 = f32[128,1792]{1,0:T(8,128)S(1)} fusion(f32[128,1792]{1,0:T(8,128)S(1)} %fusion.37, bf16[384,128]{1,0:T(8,128)(2,1)S(1)} %get-tuple-element.17, bf16[384,1792]{1,0:T(8,128)(2,1)} %bitcast.16), kind=kOutput, calls=%fused_computation.3 | convolution fusion | flops 176390144 | bytes 3309568 | tf_op jit(solution)/shard_map/dot_general | solution.py:258
  127.9 1.8 %convolution_add_fusion = f32[128,1792]{1,0:T(8,128)S(1)} fusion(f32[128,1792]{1,0:T(8,128)S(1)} %convolution_add_fusion.1, bf16[384,128]{1,0:T(8,128)(2,1)S(1)} %get-tuple-element.15, bf16[384,1792]{1,0:T(8,128)(2,1)} %bitcast.16), kind=kOutput, calls=%fused_computation.2 | convolution fusion | flops 176390144 | bytes 3309568 | tf_op jit(solution)/shard_map/dot_general | solution.py:258
  130.1 11.5 %collective-permute-done.4 = f32[128,896]{1,0:T(8,128)S(1)} collective-permute-done((f32[128,896]{1,0:T(8,128)S(1)}, f32[128,896]{1,0:T(8,128)S(1)}, u32[]{:S(2)}, u32[]{:S(2)}) %collective-permute-start.4) | collective-permute-done | bytes 458784 | tf_op jit(solution)/shard_map/ppermute | solution.py:279
  141.6 4.3 %all-to-all-done.3 = bf16[16,24,1152]{2,1,0:T(8,128)(2,1)S(1)} async-done(((bf16[16,24,1152]{2,1,0:T(8,128)(2,1)}), bf16[16,24,1152]{2,1,0:T(8,128)(2,1)S(1)}, u32[]{:S(2)}, u32[]{:S(2)}) %all-to-all-start.3) | async-done | bytes 884768 | tf_op jit(solution)/shard_map/all_to_all | solution.py:247
  (35 shorter events, 8.9 us)
Async XLA Ops:
  0.8 2.7 %copy-start = (s32[384]{0:T(512)}, s32[384]{0:T(512)S(1)}, u32[]{:S(2)}) copy-start(s32[384]{0:T(512)S(1)} %eq.62) | copy-start | bytes 4612
  3.5 30.1 %all-to-all-start = ((bf16[16,24,1280]{2,1,0:T(8,128)(2,1)}), bf16[16,24,1280]{2,1,0:T(8,128)(2,1)S(1)}, u32[]{:S(2)}, u32[]{:S(2)}) async-start(bf16[16,24,1280]{2,1,0:T(8,128)(2,1)} %bitcast.6), calls=%async_computation | async-start | bytes 1966080 | tf_op jit(solution)/shard_map/all_to_all | solution.py:247
  33.6 32.4 %all-to-all-start.1 = ((bf16[16,24,1536]{2,1,0:T(8,128)(2,1)}), bf16[16,24,1536]{2,1,0:T(8,128)(2,1)S(1)}, u32[]{:S(2)}, u32[]{:S(2)}) async-start(bf16[16,24,1536]{2,1,0:T(8,128)(2,1)} %bitcast.82), calls=%async_computation.1 | async-start | bytes 2359296 | tf_op jit(solution)/shard_map/all_to_all | solution.py:247
  39.3 14.8 %collective-permute-start.1 = (bf16[384,768]{1,0:T(8,128)(2,1)}, bf16[384,768]{1,0:T(8,128)(2,1)S(1)}, u32[]{:S(2)}, u32[]{:S(2)}) collective-permute-start(bf16[384,768]{1,0:T(8,128)(2,1)} %slice.13), channel_id=1, source_target_pairs={{0,1},{1,0},{2,3},{3,2},{4,5},{5,4},{6,7},{7,6},{8,9},{9,8},{10,11... | collective-permute-start | bytes 1769480 | tf_op jit(solution)/shard_map/ppermute | solution.py:279
  40.4 25.6 %collective-permute-start = (bf16[384,512]{1,0:T(8,128)(2,1)}, bf16[384,512]{1,0:T(8,128)(2,1)S(1)}, u32[]{:S(2)}, u32[]{:S(2)}) collective-permute-start(bf16[384,512]{1,0:T(8,128)(2,1)} %slice.12), channel_id=1, source_target_pairs={{0,1},{1,0},{2,3},{3,2},{4,5},{5,4},{6,7},{7,6},{8,9},{9,8},{10,11... | collective-permute-start | bytes 1179656 | tf_op jit(solution)/shard_map/ppermute | solution.py:279
  81.2 5.3 %copy-start.2 = (s32[128,2]{0,1:T(2,128)S(1)}, s32[128,2]{0,1:T(2,128)}, u32[]{:S(2)}) copy-start(s32[128,2]{0,1:T(2,128)} %param.7) | copy-start | bytes 3076
  81.2 5.3 %copy-start.3 = (f32[128,2]{0,1:T(2,128)S(1)}, f32[128,2]{0,1:T(2,128)}, u32[]{:S(2)}) copy-start(f32[128,2]{0,1:T(2,128)} %param.8) | copy-start | bytes 3076
  81.2 36.9 %all-to-all-start.2 = ((bf16[16,24,1792]{2,1,0:T(8,128)(2,1)}), bf16[16,24,1792]{2,1,0:T(8,128)(2,1)}, u32[]{:S(2)}, u32[]{:S(2)}) async-start(bf16[16,24,1792]{2,1,0:T(8,128)(2,1)} %bitcast.83), calls=%async_computation.2 | async-start | bytes 2752512 | tf_op jit(solution)/shard_map/all_to_all | solution.py:247
  88.9 10.5 %collective-permute-start.3 = (bf16[384,512]{1,0:T(8,128)(2,1)S(1)}, bf16[384,512]{1,0:T(8,128)(2,1)S(1)}, u32[]{:S(2)}, u32[]{:S(2)}) collective-permute-start(bf16[384,512]{1,0:T(8,128)(2,1)S(1)} %drop.7), channel_id=1, source_target_pairs={{0,1},{1,0},{2,3},{3,2},{4,5},{5,4},{6,7},{7,6},{8,9},{9,8},{10,11... | collective-permute-start | bytes 1179656 | tf_op jit(solution)/shard_map/ppermute | solution.py:279
  89.2 4.2 %copy-start.1 = (s32[384]{0:T(512)S(1)}, s32[384]{0:T(512)}, u32[]{:S(2)}) copy-start(s32[384]{0:T(512)} %copy-done) | copy-start | bytes 4612
  92.1 17.8 %collective-permute-start.2 = (bf16[384,640]{1,0:T(8,128)(2,1)S(1)}, bf16[384,640]{1,0:T(8,128)(2,1)S(1)}, u32[]{:S(2)}, u32[]{:S(2)}) collective-permute-start(bf16[384,640]{1,0:T(8,128)(2,1)S(1)} %drop.5), channel_id=1, source_target_pairs={{0,1},{1,0},{2,3},{3,2},{4,5},{5,4},{6,7},{7,6},{8,9},{9,8},{10,11... | collective-permute-start | bytes 1474568 | tf_op jit(solution)/shard_map/ppermute | solution.py:279
  119.0 26.9 %all-to-all-start.3 = ((bf16[16,24,1152]{2,1,0:T(8,128)(2,1)}), bf16[16,24,1152]{2,1,0:T(8,128)(2,1)S(1)}, u32[]{:S(2)}, u32[]{:S(2)}) async-start(bf16[16,24,1152]{2,1,0:T(8,128)(2,1)} %bitcast.23), calls=%async_computation.3 | async-start | bytes 1769472 | tf_op jit(solution)/shard_map/all_to_all | solution.py:247
  129.8 11.8 %collective-permute-start.4 = (f32[128,896]{1,0:T(8,128)S(1)}, f32[128,896]{1,0:T(8,128)S(1)}, u32[]{:S(2)}, u32[]{:S(2)}) collective-permute-start(f32[128,896]{1,0:T(8,128)S(1)} %constant_dynamic-slice_fusion), channel_id=1, source_target_pairs={{0,1},{1,0},{2,3},{3,2},{4,5},{5,4},{6,7},{7,6},{8,9},{9,8},{10,11... | collective-permute-start | bytes 1376264 | tf_op jit(solution)/shard_map/ppermute | solution.py:279

commit v9 on v8

--- a/solution.py
+++ b/solution.py
@@ -216,10 +216,11 @@
     )(jnp.reshape(start, (1,)).astype(jnp.int32), hidden, w_down)
 
 
-def selectors(expert_ids, gate_probs, experts):
+def selectors(expert_ids, gate_probs, order):
+    experts = order.shape[0]
     rows = expert_ids.shape[0]
     blocks = rows // BLOCK
-    match = expert_ids.T[:, None, :] == jnp.arange(experts, dtype=jnp.int32)[None, :, None]
+    match = expert_ids.T[:, None, :] == order[None, :, None]
     named = jnp.any(match, axis=0)
     weight = jnp.sum(jnp.where(match, gate_probs.T[:, None, :], 0.0), axis=0)
     row = jnp.arange(rows, dtype=jnp.int32)
@@ -253,6 +254,64 @@
     ).reshape(slots, width)
 
 
+def flip(value, bits):
+    size = lax.axis_size("expert")
+    return lax.ppermute(value, "expert", [(i, i ^ bits) for i in range(size)])
+
+
+def near_order(experts):
+    place = jnp.arange(experts, dtype=jnp.int32)
+    pairs = experts // 2
+    apart = jnp.where(place < pairs, 2 * place, 2 * (place - pairs) + 1)
+    return apart ^ lax.axis_index("expert").astype(jnp.int32)
+
+
+def send_pairs(value, experts):
+    pairs = experts // 2
+    rows = value.shape[0] // pairs
+    pair = lax.axis_index("expert") // 2
+
+    def of(j):
+        return lax.dynamic_slice_in_dim(value, (pair ^ j) * rows, rows, axis=0)
+
+    arrived = {j: flip(of(j), 2 * j) for j in range(pairs - 1, 0, -1)}
+    arrived[0] = of(0)
+    return [arrived[j] for j in range(pairs)]
+
+
+def split_pairs(arrived):
+    pairs = len(arrived)
+    both, width = arrived[0].shape
+    slots = both // 2
+
+    def kernel(core, *refs):
+        pieces, (mine, other) = refs[:pairs], refs[pairs:]
+        first = core[0] == 0
+        for j in range(0, pairs, 2):
+            values = [piece[...].astype(jnp.float32) for piece in pieces[j : j + 2]]
+            top = jnp.concatenate([value[:slots] for value in values], axis=0)
+            bottom = jnp.concatenate([value[slots:] for value in values], axis=0)
+            at = slice(j * slots, (j + 2) * slots)
+            mine[at] = jnp.where(first, top, bottom).astype(jnp.bfloat16)
+            other[at] = jnp.where(first, bottom, top).astype(jnp.bfloat16)
+
+    core = lax.axis_index("expert").astype(jnp.int32) % 2
+    mine, other = pl.pallas_call(
+        kernel,
+        out_shape=[jax.ShapeDtypeStruct((pairs * slots, width), jnp.bfloat16)] * 2,
+        in_specs=[pl.BlockSpec(memory_space=pltpu.SMEM)] + [vmem()] * pairs,
+        out_specs=[vmem(), vmem()],
+        compiler_params=pltpu.CompilerParams(vmem_limit_bytes=VMEM_BYTES // 2),
+        cost_estimate=pl.CostEstimate(
+            flops=2 * pairs * both * width,
+            bytes_accessed=4 * pairs * both * width,
+            transcendentals=0,
+        ),
+        name="split_pairs",
+    )(core.reshape(1), *arrived)
+    return mine, flip(other, 1)
+
+
 def mix(weights, returned):
     return sum(
         lax.dot_general(
@@ -270,7 +329,8 @@
     w_gate = lax.all_gather(w_gate, "dp", axis=1, tiled=True)[0]
     w_up = lax.all_gather(w_up, "dp", axis=1, tiled=True)[0]
     w_down = lax.all_gather(w_down, "dp", axis=2, tiled=True)[0]
-    chosen, weights = selectors(expert_ids, gate_probs, experts)
+    chosen, weights = selectors(expert_ids, gate_probs, jnp.arange(experts, dtype=jnp.int32))
+    near_weights = selectors(expert_ids, gate_probs, near_order(experts))[1]
 
     def rank_at(step):
         return lax.rem(me + step, ranks)
@@ -298,7 +358,7 @@
     for piece, at in others[:-1]:
         (sums,) = lift([piece], [at], w_gate, w_up, sums)
 
-    early = round(share * 7 / 16 / 128) * 128
+    early = round(share * 3 / 8 / 128) * 128
     columns = [jnp.int32(rank * share) for rank in range(ranks)]
     last, last_at = others[-1]
     hidden, partial = lift(
@@ -309,21 +369,24 @@
         sums,
         (w_down, columns, early),
     )
-    returned = swap(partial, experts)
+    arrived = send_pairs(partial, experts)
     edges = [early, early + pl.cdiv(share - early, 256) * 128, share]
     owned = []
     for at, end in zip(edges[:-1], edges[1:]):
         cut = end - at
-        arrived = [
+        received = [
             send_up(drop(hidden, w_down, rank_at(step) * share + at, cut, jnp.bfloat16), step)
             for step in range(1, ranks)
         ]
         value = drop(hidden, w_down, me * share + at, cut, jnp.float32)
-        for other in arrived:
+        for other in received:
             value = value + other.astype(jnp.float32)
         owned.append(value.astype(jnp.bfloat16))
-    returned, *owned = lax.optimization_barrier((returned, *owned))
-    first = mix(weights, returned)
+    arrived, owned = lax.optimization_barrier((arrived, owned))
+    mine, passed = split_pairs(arrived)
+    half = mine.shape[0]
+    first = mix([w[:half] for w in near_weights], mine)
+    first = first + mix([w[half:] for w in near_weights], passed)
 
     def part_of(rank):
         return lax.dynamic_slice_in_dim(first, rank * early, early, axis=1)

time: 149 us -> 159 us (1.067)
  waiting for transfers between devices: 65 us -> 72.4 us
  matrix products: 11.4 us -> 8.09 us
  local copies, waits for them, and re-layouts: 1.77 us -> 4.83 us
  starting transfers between devices: 25.5 us -> 27.2 us
    ppermute x0 -> x8, waiting for transfers between devices: none -> 17.1 us  [flip(): return lax.ppermute(value, 'expert', [(i, i ^ bits) for i in range(size)])]
    ppermute x0 -> x8, starting transfers between devices: none -> 8.14 us  [flip(): return lax.ppermute(value, 'expert', [(i, i ^ bits) for i in range(size)])]
    all_to_all x4 -> x3, starting transfers between devices: 22.1 us -> 15.6 us  [swap(): lax.all_to_all(value.reshape(experts, slots // experts, width), 'expert',...]
    ppermute x5, waiting for transfers between devices: 27.4 us -> 21.6 us  [send_up(): lax.ppermute(value, 'tensor', [(i, (i + step) % ranks) for i in range(ran...]
    all_to_all x4 -> x3, waiting for transfers between devices: 37.6 us -> 33.7 us  [swap(): lax.all_to_all(value.reshape(experts, slots // experts, width), 'expert',...]
    dot_general x6 -> x9, matrix products: 6.45 us -> 2.83 us  [mix(): lax.dot_general(w, returned, (((0,), (0,)), ((), ())), preferred_element_...]
    slice x0 -> x3, local copies, waits for them, and re-layouts: none -> 1.96 us  [on_device(): first = first + mix([w[half:] for w in near_weights], passed)]
    unnamed x8 -> x20, local copies, waits for them, and re-layouts: 0.02 us -> 1.77 us
  transfers between devices with their start and end apart: 9 -> 16, of which waited for: 8 -> 10; matrix products, arithmetic and copies ran while one was open for 7% -> 6% of each run, Pallas kernels for 17% -> 15%
where the time goes in v9:
time: 159 us; the launch traced here: 158 us
  waiting for transfers between devices  72.4 us (46%)
  Pallas kernels  41.3 us (26%)
  starting transfers between devices  27.2 us (17%)
  matrix products  8.09 us (5%)
  local copies, waits for them, and re-layouts  4.83 us (3%)
  other arithmetic  3.86 us (2%)
    all_to_all x3, waiting for transfers between devices, swap(): lax.all_to_all(value.reshape(experts, slots // experts, width), 'expert',...  33.7 us
    pallas_call x3, Pallas kernels, lift(): pl.pallas_call(kernel, out_shape=out_shape, in_specs=[pl.BlockSpec(memory...  29.4 us
    ppermute x5, waiting for transfers between devices, send_up(): lax.ppermute(value, 'tensor', [(i, (i + step) % ranks) for i in range(ran...  21.6 us
    ppermute x8, waiting for transfers between devices, flip(): return lax.ppermute(value, 'expert', [(i, i ^ bits) for i in range(size)])  17.1 us
    all_to_all x3, starting transfers between devices, swap(): lax.all_to_all(value.reshape(experts, slots // experts, width), 'expert',...  15.6 us
    pallas_call x4, Pallas kernels, drop(): pl.pallas_call(kernel, out_shape=jax.ShapeDtypeStruct((rows, width), dtyp...  11.6 us
    ppermute x8, starting transfers between devices, flip(): return lax.ppermute(value, 'expert', [(i, i ^ bits) for i in range(size)])  8.14 us
    dot_general x2, matrix products, placed(): jnp.dot(chosen, features, preferred_element_type=jnp.float32)  4.85 us
  transfers between devices with their start and end apart: 16, of which 10 were waited for; matrix products, arithmetic and copies ran while one was open for 6% of the time, Pallas kernels for 15%

profile of v9, /device:TPU:11, one launch (start us, length us, event | category | flops | bytes accessed | tf_op | source)
XLA Modules:
  0.0 158.0 jit_solution(16539447767505744001)
XLA Ops:
  1.2 2.4 %convolution_convert_fusion = bf16[384,1280]{1,0:T(8,128)(2,1)} fusion(pred[384,128]{1,0:T(32,128)(4,1)S(1)} %fusion.17, bf16[128,4096]{1,0:T(8,128)(2,1)} %param.6, s32[]{:T(128)S(6)} %select_n.116), kind=kOutput, calls=%fused_computation | convolution fusion | flops 126320640 | bytes 1359876 | tf_op jit(solution)/shard_map/dot_general | solution.py:346
  3.6 6.6 %all-to-all-start = ((bf16[16,24,1280]{2,1,0:T(8,128)(2,1)}), bf16[16,24,1280]{2,1,0:T(8,128)(2,1)S(1)}, u32[]{:S(2)}, u32[]{:S(2)}) async-start(bf16[16,24,1280]{2,1,0:T(8,128)(2,1)} %bitcast.7), calls=%async_computation | async-start | bytes 1966080 | tf_op jit(solution)/shard_map/all_to_all | solution.py:248
  10.2 2.5 %convolution_convert_fusion.1 = bf16[384,1536]{1,0:T(8,128)(2,1)} fusion(pred[384,128]{1,0:T(32,128)(4,1)S(1)} %fusion.17, bf16[128,4096]{1,0:T(8,128)(2,1)} %param.6), kind=kOutput, calls=%fused_computation.1 | convolution fusion | flops 151584768 | bytes 1622016 | tf_op jit(solution)/shard_map/dot_general | solution.py:346
  12.7 21.0 %all-to-all-done = bf16[16,24,1280]{2,1,0:T(8,128)(2,1)S(1)} async-done(((bf16[16,24,1280]{2,1,0:T(8,128)(2,1)}), bf16[16,24,1280]{2,1,0:T(8,128)(2,1)S(1)}, u32[]{:S(2)}, u32[]{:S(2)}) %all-to-all-start) | async-done | bytes 983072 | tf_op jit(solution)/shard_map/all_to_all | solution.py:248
  33.7 4.9 %all-to-all-start.1 = ((bf16[16,24,1536]{2,1,0:T(8,128)(2,1)}), bf16[16,24,1536]{2,1,0:T(8,128)(2,1)S(1)}, u32[]{:S(2)}, u32[]{:S(2)}) async-start(bf16[16,24,1536]{2,1,0:T(8,128)(2,1)} %bitcast.9), calls=%async_computation.1 | async-start | bytes 2359296 | tf_op jit(solution)/shard_map/all_to_all | solution.py:248
  44.0 7.5 %lift.3.refs_3_ = f32[7,384,512]{2,1,0:T(8,128)} custom-call(s32[1]{0:T(128)} %bitcast.14.at, bf16[384,1280]{1,0:T(8,128)(2,1)S(1)} %bitcast.63, bf16[4096,1792]{1,0:T(8,128)(2,1)} %bitcast.70, bf16[4096,1792]{1,0:T(8,128)(2,1)} %bitcast.73), custom_call_target="tpu_custom_call" | custom-call | flops 3523215360 | bytes 20185088 | tf_op jit(solution)/shard_map/lift/pallas_call | solution.py:174
  51.5 5.0 %collective-permute-done.1.refs_0_ = bf16[384,768]{1,0:T(8,128)(2,1)S(1)} collective-permute-done((bf16[384,768]{1,0:T(8,128)(2,1)}, bf16[384,768]{1,0:T(8,128)(2,1)S(1)}, u32[]{:S(2)}, u32[]{:S(2)}) %collective-permute-start.1) | collective-permute-done | bytes 589856 | tf_op jit(solution)/shard_map/ppermute | solution.py:339
  56.5 7.7 %lift.4.refs_4_ = f32[7,384,512]{2,1,0:T(8,128)} custom-call(s32[1]{0:T(128)} %bitcast.13.at, bf16[384,768]{1,0:T(8,128)(2,1)S(1)} %collective-permute-done.1.refs_0_, bf16[4096,1792]{1,0:T(8,128)(2,1)} %bitcast.71, bf16[4096,1792]{1,0:T(8,128)(2,1)} %bitcast.74, f32[7,384,512]{2,1,0:T(8,128)} %lift.3.refs_3_), custom_call_target="tpu_custom_call" | custom-call | flops 2113929216 | bytes 16515072 | tf_op jit(solution)/shard_map/lift/pallas_call | solution.py:174
  64.2 1.9 %all-to-all-done.1 = bf16[16,24,1536]{2,1,0:T(8,128)(2,1)S(1)} async-done(((bf16[16,24,1536]{2,1,0:T(8,128)(2,1)}), bf16[16,24,1536]{2,1,0:T(8,128)(2,1)S(1)}, u32[]{:S(2)}, u32[]{:S(2)}) %all-to-all-start.1) | async-done | bytes 1179680 | tf_op jit(solution)/shard_map/all_to_all | solution.py:248
  66.1 14.2 %lift.5 = (bf16[384,1792]{1,0:T(8,128)(2,1)}, bf16[384,1536]{1,0:T(8,128)(2,1)S(1)}) custom-call(s32[4]{0:T(128)S(1)} %pad_add_fusion.at, bf16[384,512]{1,0:T(8,128)(2,1)S(1)} %collective-permute-done.refs_0_, bf16[384,1536]{1,0:T(8,128)(2,1)S(1)} %bitcast.64, bf16[4096,1792]{1,0:T(8,128)(2,1)} %bitcast.72, bf16[4096,1792]{1,0:T(8,128)(2,1)} %bitcast.75, ...), custom_call_target="tpu_custom_call" | custom-call | flops 7751073792 | bytes 31195136 | tf_op jit(solution)/shard_map/lift/pallas_call | solution.py:174
  81.7 2.9 %drop.7 = bf16[384,640]{1,0:T(8,128)(2,1)S(1)} custom-call(s32[1]{0:T(128)} %bitcast.19.at, bf16[384,1792]{1,0:T(8,128)(2,1)S(1)} %copy-done, bf16[1792,4096]{1,0:T(8,128)(2,1)} %bitcast.66), custom_call_target="tpu_custom_call" | custom-call | flops 880803840 | bytes 2293760 | tf_op jit(solution)/shard_map/drop/pallas_call | solution.py:202
  84.9 2.9 %drop.5 = bf16[384,640]{1,0:T(8,128)(2,1)S(1)} custom-call(s32[1]{0:T(128)} %bitcast.17.at, bf16[384,1792]{1,0:T(8,128)(2,1)S(1)} %copy-done, bf16[1792,4096]{1,0:T(8,128)(2,1)} %bitcast.67), custom_call_target="tpu_custom_call" | custom-call | flops 880803840 | bytes 2293760 | tf_op jit(solution)/shard_map/drop/pallas_call | solution.py:202
  91.9 2.9 %drop.6 = f32[384,640]{1,0:T(8,128)S(1)} custom-call(s32[1]{0:T(128)} %bitcast.18.at, bf16[384,1792]{1,0:T(8,128)(2,1)S(1)} %copy-done, bf16[1792,4096]{1,0:T(8,128)(2,1)} %bitcast.68), custom_call_target="tpu_custom_call" | custom-call | flops 880803840 | bytes 2293760 | tf_op jit(solution)/shard_map/drop/pallas_call | solution.py:202
  94.8 2.9 %drop.4 = f32[384,640]{1,0:T(8,128)S(1)} custom-call(s32[1]{0:T(128)} %bitcast.16.at, bf16[384,1792]{1,0:T(8,128)(2,1)S(1)} %copy-done, bf16[1792,4096]{1,0:T(8,128)(2,1)} %bitcast.69), custom_call_target="tpu_custom_call" | custom-call | flops 880803840 | bytes 2293760 | tf_op jit(solution)/shard_map/drop/pallas_call | solution.py:202
  99.0 2.5 %collective-permute-start.6 = (bf16[48,1536]{1,0:T(8,128)(2,1)S(1)}, bf16[48,1536]{1,0:T(8,128)(2,1)S(1)}, u32[]{:S(2)}, u32[]{:S(2)}) collective-permute-start(bf16[48,1536]{1,0:T(8,128)(2,1)S(1)} %get-tuple-element.39), channel_id=1, source_target_pairs={{0,20},{2,22},{4,16},{6,18},{8,28},{10,30},{12,24},{14,26},{16,4},... | collective-permute-start | bytes 442376 | tf_op jit(solution)/shard_map/ppermute | solution.py:259
  101.5 6.5 %collective-permute-done.9 = bf16[384,640]{1,0:T(8,128)(2,1)S(1)} collective-permute-done((bf16[384,640]{1,0:T(8,128)(2,1)S(1)}, bf16[384,640]{1,0:T(8,128)(2,1)S(1)}, u32[]{:S(2)}, u32[]{:S(2)}) %collective-permute-start.9) | collective-permute-done | bytes 491552 | tf_op jit(solution)/shard_map/ppermute | solution.py:339
  108.1 2.8 %collective-permute-done.5.refs_4_ = bf16[48,1536]{1,0:T(8,128)(2,1)S(1)} collective-permute-done((bf16[48,1536]{1,0:T(8,128)(2,1)S(1)}, bf16[48,1536]{1,0:T(8,128)(2,1)S(1)}, u32[]{:S(2)}, u32[]{:S(2)}) %collective-permute-start.5) | collective-permute-done | bytes 147488 | tf_op jit(solution)/shard_map/ppermute | solution.py:259
  110.9 6.4 %collective-permute-done.6.refs_5_ = bf16[48,1536]{1,0:T(8,128)(2,1)S(1)} collective-permute-done((bf16[48,1536]{1,0:T(8,128)(2,1)S(1)}, bf16[48,1536]{1,0:T(8,128)(2,1)S(1)}, u32[]{:S(2)}, u32[]{:S(2)}) %collective-permute-start.6) | collective-permute-done | bytes 147488 | tf_op jit(solution)/shard_map/ppermute | solution.py:259
  117.3 4.2 %collective-permute-done.7.refs_6_ = bf16[48,1536]{1,0:T(8,128)(2,1)S(1)} collective-permute-done((bf16[48,1536]{1,0:T(8,128)(2,1)S(1)}, bf16[48,1536]{1,0:T(8,128)(2,1)S(1)}, u32[]{:S(2)}, u32[]{:S(2)}) %collective-permute-start.7) | collective-permute-done | bytes 147488 | tf_op jit(solution)/shard_map/ppermute | solution.py:259
  121.4 3.8 %collective-permute-done.8.refs_7_ = bf16[48,1536]{1,0:T(8,128)(2,1)S(1)} collective-permute-done((bf16[48,1536]{1,0:T(8,128)(2,1)S(1)}, bf16[48,1536]{1,0:T(8,128)(2,1)S(1)}, u32[]{:S(2)}, u32[]{:S(2)}) %collective-permute-start.8) | collective-permute-done | bytes 147488 | tf_op jit(solution)/shard_map/ppermute | solution.py:259
  125.5 1.8 %collective-permute-start.11 = (bf16[192,1536]{1,0:T(8,128)(2,1)S(1)}, bf16[192,1536]{1,0:T(8,128)(2,1)S(1)}, u32[]{:S(2)}, u32[]{:S(2)}) collective-permute-start(bf16[192,1536]{1,0:T(8,128)(2,1)S(1)} %get-tuple-element.30), channel_id=1, source_target_pairs={{0,2},{2,0},{4,6},{6,4},{8,10},{10,8},{12,14},{14,12},{16,18},{18,... | collective-permute-start | bytes 1769480 | tf_op jit(solution)/shard_map/ppermute | solution.py:259
  128.4 4.1 %all-to-all-start.2 = ((bf16[16,24,1280]{2,1,0:T(8,128)(2,1)}), bf16[16,24,1280]{2,1,0:T(8,128)(2,1)S(1)}, u32[]{:S(2)}, u32[]{:S(2)}) async-start(bf16[16,24,1280]{2,1,0:T(8,128)(2,1)} %bitcast.76), calls=%async_computation.2 | async-start | bytes 1966080 | tf_op jit(solution)/shard_map/all_to_all | solution.py:248
  135.1 10.1 %collective-permute-done.12 = f32[128,768]{1,0:T(8,128)S(1)} collective-permute-done((f32[128,768]{1,0:T(8,128)S(1)}, f32[128,768]{1,0:T(8,128)S(1)}, u32[]{:S(2)}, u32[]{:S(2)}) %collective-permute-start.12) | collective-permute-done | bytes 393248 | tf_op jit(solution)/shard_map/ppermute | solution.py:339
  145.2 10.8 %all-to-all-done.2 = bf16[16,24,1280]{2,1,0:T(8,128)(2,1)S(1)} async-done(((bf16[16,24,1280]{2,1,0:T(8,128)(2,1)}), bf16[16,24,1280]{2,1,0:T(8,128)(2,1)S(1)}, u32[]{:S(2)}, u32[]{:S(2)}) %all-to-all-start.2) | async-done | bytes 983072 | tf_op jit(solution)/shard_map/all_to_all | solution.py:248
  (72 shorter events, 19.5 us)
Async XLA Ops:
  3.6 30.1 %all-to-all-start = ((bf16[16,24,1280]{2,1,0:T(8,128)(2,1)}), bf16[16,24,1280]{2,1,0:T(8,128)(2,1)S(1)}, u32[]{:S(2)}, u32[]{:S(2)}) async-start(bf16[16,24,1280]{2,1,0:T(8,128)(2,1)} %bitcast.7), calls=%async_computation | async-start | bytes 1966080 | tf_op jit(solution)/shard_map/all_to_all | solution.py:248
  10.2 28.4 %copy-start.8 = (s32[128,2]{0,1:T(2,128)S(1)}, s32[128,2]{0,1:T(2,128)}, u32[]{:S(2)}) copy-start(s32[128,2]{0,1:T(2,128)} %param.7) | copy-start | bytes 3076
  10.2 28.4 %copy-start.9 = (f32[128,2]{0,1:T(2,128)S(1)}, f32[128,2]{0,1:T(2,128)}, u32[]{:S(2)}) copy-start(f32[128,2]{0,1:T(2,128)} %param.8) | copy-start | bytes 3076
  33.7 32.4 %all-to-all-start.1 = ((bf16[16,24,1536]{2,1,0:T(8,128)(2,1)}), bf16[16,24,1536]{2,1,0:T(8,128)(2,1)S(1)}, u32[]{:S(2)}, u32[]{:S(2)}) async-start(bf16[16,24,1536]{2,1,0:T(8,128)(2,1)} %bitcast.9), calls=%async_computation.1 | async-start | bytes 2359296 | tf_op jit(solution)/shard_map/all_to_all | solution.py:248
  41.7 14.8 %collective-permute-start.1 = (bf16[384,768]{1,0:T(8,128)(2,1)}, bf16[384,768]{1,0:T(8,128)(2,1)S(1)}, u32[]{:S(2)}, u32[]{:S(2)}) collective-permute-start(bf16[384,768]{1,0:T(8,128)(2,1)} %slice.62), channel_id=1, source_target_pairs={{0,1},{1,0},{2,3},{3,2},{4,5},{5,4},{6,7},{7,6},{8,9},{9,8},{10,11... | collective-permute-start | bytes 1769480 | tf_op jit(solution)/shard_map/ppermute | solution.py:339
  42.7 23.4 %collective-permute-start = (bf16[384,512]{1,0:T(8,128)(2,1)S(1)}, bf16[384,512]{1,0:T(8,128)(2,1)S(1)}, u32[]{:S(2)}, u32[]{:S(2)}) collective-permute-start(bf16[384,512]{1,0:T(8,128)(2,1)S(1)} %slice.61), channel_id=1, source_target_pairs={{0,1},{1,0},{2,3},{3,2},{4,5},{5,4},{6,7},{7,6},{8,9},{9,8},{10,11... | collective-permute-start | bytes 1179656 | tf_op jit(solution)/shard_map/ppermute | solution.py:339
  80.4 1.3 copy-start
  84.6 13.1 %collective-permute-start.10 = (bf16[384,640]{1,0:T(8,128)(2,1)S(1)}, bf16[384,640]{1,0:T(8,128)(2,1)S(1)}, u32[]{:S(2)}, u32[]{:S(2)}) collective-permute-start(bf16[384,640]{1,0:T(8,128)(2,1)S(1)} %drop.7), channel_id=1, source_target_pairs={{0,1},{1,0},{2,3},{3,2},{4,5},{5,4},{6,7},{7,6},{8,9},{9,8},{10,11... | collective-permute-start | bytes 1474568 | tf_op jit(solution)/shard_map/ppermute | solution.py:339
  87.8 20.2 %collective-permute-start.9 = (bf16[384,640]{1,0:T(8,128)(2,1)S(1)}, bf16[384,640]{1,0:T(8,128)(2,1)S(1)}, u32[]{:S(2)}, u32[]{:S(2)}) collective-permute-start(bf16[384,640]{1,0:T(8,128)(2,1)S(1)} %drop.5), channel_id=1, source_target_pairs={{0,1},{1,0},{2,3},{3,2},{4,5},{5,4},{6,7},{7,6},{8,9},{9,8},{10,11... | collective-permute-start | bytes 1474568 | tf_op jit(solution)/shard_map/ppermute | solution.py:339
  89.2 9.8 %collective-permute-start.2 = (bf16[48,1536]{1,0:T(8,128)(2,1)S(1)}, bf16[48,1536]{1,0:T(8,128)(2,1)S(1)}, u32[]{:S(2)}, u32[]{:S(2)}) collective-permute-start(bf16[48,1536]{1,0:T(8,128)(2,1)S(1)} %get-tuple-element.43), channel_id=1, source_target_pairs={{0,4},{2,6},{4,0},{6,2},{8,12},{10,14},{12,8},{14,10},{16,20},{18,... | collective-permute-start | bytes 442376 | tf_op jit(solution)/shard_map/ppermute | solution.py:259
  90.6 10.8 %collective-permute-start.3 = (bf16[48,1536]{1,0:T(8,128)(2,1)S(1)}, bf16[48,1536]{1,0:T(8,128)(2,1)S(1)}, u32[]{:S(2)}, u32[]{:S(2)}) collective-permute-start(bf16[48,1536]{1,0:T(8,128)(2,1)S(1)} %get-tuple-element.42), channel_id=1, source_target_pairs={{0,8},{2,10},{4,12},{6,14},{8,0},{10,2},{12,4},{14,6},{16,24},{18,... | collective-permute-start | bytes 442376 | tf_op jit(solution)/shard_map/ppermute | solution.py:259
  90.6 17.5 %collective-permute-start.4 = (bf16[48,1536]{1,0:T(8,128)(2,1)S(1)}, bf16[48,1536]{1,0:T(8,128)(2,1)S(1)}, u32[]{:S(2)}, u32[]{:S(2)}) collective-permute-start(bf16[48,1536]{1,0:T(8,128)(2,1)S(1)} %get-tuple-element.41), channel_id=1, source_target_pairs={{0,12},{2,14},{4,8},{6,10},{8,4},{10,6},{12,0},{14,2},{16,28},{18,... | collective-permute-start | bytes 442376 | tf_op jit(solution)/shard_map/ppermute | solution.py:259
  97.7 13.2 %collective-permute-start.5 = (bf16[48,1536]{1,0:T(8,128)(2,1)S(1)}, bf16[48,1536]{1,0:T(8,128)(2,1)S(1)}, u32[]{:S(2)}, u32[]{:S(2)}) collective-permute-start(bf16[48,1536]{1,0:T(8,128)(2,1)S(1)} %get-tuple-element.40), channel_id=1, source_target_pairs={{0,16},{2,18},{4,20},{6,22},{8,24},{10,26},{12,28},{14,30},{16,0},... | collective-permute-start | bytes 442376 | tf_op jit(solution)/shard_map/ppermute | solution.py:259
  99.0 18.3 %collective-permute-start.6 = (bf16[48,1536]{1,0:T(8,128)(2,1)S(1)}, bf16[48,1536]{1,0:T(8,128)(2,1)S(1)}, u32[]{:S(2)}, u32[]{:S(2)}) collective-permute-start(bf16[48,1536]{1,0:T(8,128)(2,1)S(1)} %get-tuple-element.39), channel_id=1, source_target_pairs={{0,20},{2,22},{4,16},{6,18},{8,28},{10,30},{12,24},{14,26},{16,4},... | collective-permute-start | bytes 442376 | tf_op jit(solution)/shard_map/ppermute | solution.py:259
  101.5 19.9 %collective-permute-start.7 = (bf16[48,1536]{1,0:T(8,128)(2,1)S(1)}, bf16[48,1536]{1,0:T(8,128)(2,1)S(1)}, u32[]{:S(2)}, u32[]{:S(2)}) collective-permute-start(bf16[48,1536]{1,0:T(8,128)(2,1)S(1)} %get-tuple-element.38), channel_id=1, source_target_pairs={{0,24},{2,26},{4,28},{6,30},{8,16},{10,18},{12,20},{14,22},{16,8},... | collective-permute-start | bytes 442376 | tf_op jit(solution)/shard_map/ppermute | solution.py:259
  108.0 17.3 %collective-permute-start.8 = (bf16[48,1536]{1,0:T(8,128)(2,1)S(1)}, bf16[48,1536]{1,0:T(8,128)(2,1)S(1)}, u32[]{:S(2)}, u32[]{:S(2)}) collective-permute-start(bf16[48,1536]{1,0:T(8,128)(2,1)S(1)} %get-tuple-element.37), channel_id=1, source_target_pairs={{0,28},{2,30},{4,24},{6,26},{8,20},{10,22},{12,16},{14,18},{16,12}... | collective-permute-start | bytes 442376 | tf_op jit(solution)/shard_map/ppermute | solution.py:259
  125.5 7.0 %copy-start.2 = (bf16[8,24,128]{2,1,0:T(8,128)(2,1)S(1)}, bf16[8,24,128]{2,1,0:T(8,128)(2,1)}, u32[]{:S(2)}) copy-start(bf16[8,24,128]{2,1,0:T(8,128)(2,1)} %get-tuple-element.46) | copy-start | bytes 147460
  125.5 8.0 %collective-permute-start.11 = (bf16[192,1536]{1,0:T(8,128)(2,1)S(1)}, bf16[192,1536]{1,0:T(8,128)(2,1)S(1)}, u32[]{:S(2)}, u32[]{:S(2)}) collective-permute-start(bf16[192,1536]{1,0:T(8,128)(2,1)S(1)} %get-tuple-element.30), channel_id=1, source_target_pairs={{0,2},{2,0},{4,6},{6,4},{8,10},{10,8},{12,14},{14,12},{16,18},{18,... | collective-permute-start | bytes 1769480 | tf_op jit(solution)/shard_map/ppermute | solution.py:259
  128.4 4.4 %copy-start.4 = (bf16[8,24,128]{2,1,0:T(8,128)(2,1)S(1)}, bf16[8,24,128]{2,1,0:T(8,128)(2,1)}, u32[]{:S(2)}) copy-start(bf16[8,24,128]{2,1,0:T(8,128)(2,1)} %get-tuple-element.48) | copy-start | bytes 147460
  128.4 27.6 %all-to-all-start.2 = ((bf16[16,24,1280]{2,1,0:T(8,128)(2,1)}), bf16[16,24,1280]{2,1,0:T(8,128)(2,1)S(1)}, u32[]{:S(2)}, u32[]{:S(2)}) async-start(bf16[16,24,1280]{2,1,0:T(8,128)(2,1)} %bitcast.76), calls=%async_computation.2 | async-start | bytes 1966080 | tf_op jit(solution)/shard_map/all_to_all | solution.py:248
  132.8 0.8 copy-start.1
  133.1 0.8 copy-start.3
  133.6 0.8 copy-start.6
  134.7 10.4 %collective-permute-start.12 = (f32[128,768]{1,0:T(8,128)S(1)}, f32[128,768]{1,0:T(8,128)S(1)}, u32[]{:S(2)}, u32[]{:S(2)}) collective-permute-start(f32[128,768]{1,0:T(8,128)S(1)} %constant_dynamic-slice_fusion), channel_id=1, source_target_pairs={{0,1},{1,0},{2,3},{3,2},{4,5},{5,4},{6,7},{7,6},{8,9},{9,8},{10,11... | collective-permute-start | bytes 1179656 | tf_op jit(solution)/shard_map/ppermute | solution.py:339
  (2 other events, 1.5 us)

commit v10 on v8

--- a/solution.py
+++ b/solution.py
@@ -5,6 +5,7 @@
 from jax.experimental.pallas import tpu as pltpu
 from jax.sharding import PartitionSpec as P
 
+TOP = 2
 BLOCK = 128
 CAP = 24
 LANES = 256
@@ -234,12 +235,62 @@
     middle = rest.astype(jnp.bfloat16)
     low = (rest - middle.astype(jnp.float32)).astype(jnp.bfloat16)
     flat = (experts * blocks * CAP, rows)
-    chosen = hit.astype(jnp.bfloat16).reshape(flat)
-    weights = [
+    return [
         jnp.where(hit, part[:, None, :], 0).astype(jnp.bfloat16).reshape(flat)
         for part in (high, middle, low)
     ]
-    return chosen, weights
+
+
+def place(tokens, expert_ids, experts, start, width):
+    rows = tokens.shape[0]
+    slots = rows // BLOCK * CAP
+
+    def kernel(at, ids, tokens, chosen, out, part, picked, sem):
+        begin = pl.multiple_of(at[0], 128)
+        copy = pltpu.make_async_copy(tokens.at[:, pl.ds(begin, width)], part, sem)
+        copy.start()
+        expert = lax.broadcasted_iota(jnp.int32, (experts, rows), 0)
+        named = jnp.zeros((experts, rows), jnp.float32)
+        for k in range(TOP):
+            named = named + jnp.where(ids[k : k + 1] == expert, 1.0, 0.0)
+        row = lax.broadcasted_iota(jnp.int32, (rows, rows), 0)
+        later = lax.broadcasted_iota(jnp.int32, (rows, rows), 1)
+        same = row // BLOCK == later // BLOCK
+        earlier = jnp.where((row < later) & same, 1.0, 0.0).astype(jnp.bfloat16)
+        before = jnp.dot(
+            named.astype(jnp.bfloat16), earlier, preferred_element_type=jnp.float32
+        ).astype(jnp.int32)
+        block = lax.broadcasted_iota(jnp.int32, (experts, rows), 1) // BLOCK
+        where = jnp.where(named > 0.0, before + block * CAP, -1)
+        slot = lax.broadcasted_iota(jnp.int32, (slots, rows), 0)
+        for e in range(experts):
+            picked[e * slots : (e + 1) * slots] = jnp.where(where[e : e + 1] == slot, 1.0, 0.0)
+        chosen[...] = picked[...].astype(jnp.bfloat16)
+        copy.wait()
+        value = jnp.dot(chosen[...], part[...], preferred_element_type=jnp.float32)
+        out[...] = value.astype(jnp.bfloat16)
+
+    return pl.pallas_call(
+        kernel,
+        out_shape=[
+            jax.ShapeDtypeStruct((experts * slots, rows), jnp.bfloat16),
+            jax.ShapeDtypeStruct((experts * slots, width), jnp.bfloat16),
+        ],
+        in_specs=[pl.BlockSpec(memory_space=pltpu.SMEM), vmem(), hbm()],
+        out_specs=[vmem(), vmem()],
+        scratch_shapes=[
+            pltpu.VMEM((rows, width), jnp.bfloat16),
+            pltpu.VMEM((experts * slots, rows), jnp.float32),
+            pltpu.SemaphoreType.DMA,
+        ],
+        compiler_params=pltpu.CompilerParams(vmem_limit_bytes=VMEM_BYTES // 2),
+        cost_estimate=pl.CostEstimate(
+            flops=2 * experts * slots * rows * width,
+            bytes_accessed=2 * rows * width,
+            transcendentals=0,
+        ),
+        name="place",
+    )(jnp.reshape(start, (1,)).astype(jnp.int32), expert_ids.T, tokens)
 
 
 def swap(value, experts):
@@ -270,7 +321,7 @@
     w_gate = lax.all_gather(w_gate, "dp", axis=1, tiled=True)[0]
     w_up = lax.all_gather(w_up, "dp", axis=1, tiled=True)[0]
     w_down = lax.all_gather(w_down, "dp", axis=2, tiled=True)[0]
-    chosen, weights = selectors(expert_ids, gate_probs, experts)
+    weights = selectors(expert_ids, gate_probs, experts)
 
     def rank_at(step):
         return lax.rem(me + step, ranks)
@@ -282,18 +333,16 @@
     shared = round(share * 5 / 8 / LANES) * LANES
     direct_at = ranks * shared
 
-    def placed(features):
-        return jnp.dot(chosen, features, preferred_element_type=jnp.float32).astype(jnp.bfloat16)
-
-    mine = lax.dynamic_slice_in_dim(tokens, me * shared, shared, axis=1)
-    own = swap(placed(mine), experts)
+    chosen, placed = place(tokens, expert_ids, experts, me * shared, shared)
+    own = swap(placed, experts)
     cut = pl.cdiv(shared, 2 * LANES) * LANES
     others = []
     for begin, end in ((0, cut), (cut, shared)):
         for step in range(1, ranks):
             sent = send_up(own[:, begin:end], ranks - step)
             others.append((sent, rank_at(step) * shared + begin))
-    direct = swap(placed(tokens[:, direct_at:]), experts)
+    placed = jnp.dot(chosen, tokens[:, direct_at:], preferred_element_type=jnp.float32)
+    direct = swap(placed.astype(jnp.bfloat16), experts)
     (sums,) = lift([own], [me * shared], w_gate, w_up)
     for piece, at in others[:-1]:
         (sums,) = lift([piece], [at], w_gate, w_up, sums)
@@ -322,7 +371,7 @@
         for other in arrived:
             value = value + other.astype(jnp.float32)
         owned.append(value.astype(jnp.bfloat16))
-    returned, *owned = lax.optimization_barrier((returned, *owned))
+    returned, owned = lax.optimization_barrier((returned, jnp.concatenate(owned, axis=1)))
     first = mix(weights, returned)
 
     def part_of(rank):
@@ -331,7 +380,7 @@
     mixed = part_of(me)
     for step in range(1, ranks):
         mixed = mixed + send_up(part_of(rank_at(step)), step)
-    late = mix(weights, swap(jnp.concatenate(owned, axis=1), experts))
+    late = mix(weights, swap(owned, experts))
     return jnp.concatenate([mixed.astype(jnp.bfloat16), late.astype(jnp.bfloat16)], axis=1)
 
 

time: 149 us -> 148 us (level)
  matrix products: 11.4 us -> 9.09 us
  local copies, waits for them, and re-layouts: 1.77 us -> 3.69 us
  Pallas kernels: 40.8 us -> 42.4 us
    dot_general x2 -> x1, matrix products: 4.78 us -> 2.47 us  [on_device(): jnp.dot(chosen, tokens[:, direct_at:], preferred_element_type=jnp.float32)]
    unnamed x8, local copies, waits for them, and re-layouts: 0.02 us -> 1.92 us
    pallas_call x0 -> x1, Pallas kernels: none -> 1.57 us  [place(): pl.pallas_call(kernel, out_shape=[jax.ShapeDtypeStruct((experts * slots,...]
  transfers between devices with their start and end apart: 9 -> 9, of which waited for: 8 -> 8; matrix products, arithmetic and copies ran while one was open for 7% -> 8% of each run, Pallas kernels for 17% -> 18%
where the time goes in v10:
time: 148 us; the launch traced here: 147 us
  waiting for transfers between devices  63.7 us (43%)
  Pallas kernels  42.4 us (29%)
  starting transfers between devices  25.5 us (17%)
  matrix products  9.09 us (6%)
  local copies, waits for them, and re-layouts  3.69 us (2%)
  other arithmetic  2.37 us (2%)
    all_to_all x4, waiting for transfers between devices, swap(): lax.all_to_all(value.reshape(experts, slots // experts, width), 'expert',...  36.6 us
    pallas_call x3, Pallas kernels, lift(): pl.pallas_call(kernel, out_shape=out_shape, in_specs=[pl.BlockSpec(memory...  30.3 us
    ppermute x5, waiting for transfers between devices, send_up(): lax.ppermute(value, 'tensor', [(i, (i + step) % ranks) for i in range(ran...  27.1 us
    all_to_all x4, starting transfers between devices, swap(): lax.all_to_all(value.reshape(experts, slots // experts, width), 'expert',...  22.1 us
    pallas_call x4, Pallas kernels, drop(): pl.pallas_call(kernel, out_shape=jax.ShapeDtypeStruct((rows, width), dtyp...  10.6 us
    dot_general x6, matrix products, mix(): lax.dot_general(w, returned, (((0,), (0,)), ((), ())), preferred_element_...  6.42 us
    ppermute x5, starting transfers between devices, send_up(): lax.ppermute(value, 'tensor', [(i, (i + step) % ranks) for i in range(ran...  3.38 us
  transfers between devices with their start and end apart: 9, of which 8 were waited for; matrix products, arithmetic and copies ran while one was open for 8% of the time, Pallas kernels for 18%

profile of v10, /device:TPU:11, one launch (start us, length us, event | category | flops | bytes accessed | tf_op | source)
XLA Modules:
  0.0 147.0 jit_solution(16147625561242431993)
XLA Ops:
  1.9 1.6 %place.1 = (bf16[384,128]{1,0:T(8,128)(2,1)S(1)}, bf16[384,1280]{1,0:T(8,128)(2,1)}) custom-call(s32[1]{0:T(128)} %bitcast.6.at, s32[2,128]{1,0:T(2,128)S(1)} %bitcast.70, bf16[128,4096]{1,0:T(8,128)(2,1)S(1)} %copy-done), custom_call_target="tpu_custom_call" | custom-call | flops 125829120 | bytes 327680 | tf_op jit(solution)/shard_map/place/pallas_call | solution.py:273
  3.5 6.6 %all-to-all-start = ((bf16[16,24,1280]{2,1,0:T(8,128)(2,1)}), bf16[16,24,1280]{2,1,0:T(8,128)(2,1)S(1)}, u32[]{:S(2)}, u32[]{:S(2)}) async-start(bf16[16,24,1280]{2,1,0:T(8,128)(2,1)} %bitcast.7), calls=%async_computation | async-start | bytes 1966080 | tf_op jit(solution)/shard_map/all_to_all | solution.py:298
  10.1 2.5 %convolution_convert_fusion = bf16[384,1536]{1,0:T(8,128)(2,1)} fusion(bf16[384,128]{1,0:T(8,128)(2,1)S(1)} %get-tuple-element.12, bf16[128,4096]{1,0:T(8,128)(2,1)} %tokens.1), kind=kOutput, calls=%fused_computation | convolution fusion | flops 151584768 | bytes 1671168 | tf_op jit(solution)/shard_map/dot_general | solution.py:344
  12.6 21.0 %all-to-all-done = bf16[16,24,1280]{2,1,0:T(8,128)(2,1)S(1)} async-done(((bf16[16,24,1280]{2,1,0:T(8,128)(2,1)}), bf16[16,24,1280]{2,1,0:T(8,128)(2,1)S(1)}, u32[]{:S(2)}, u32[]{:S(2)}) %all-to-all-start) | async-done | bytes 983072 | tf_op jit(solution)/shard_map/all_to_all | solution.py:298
  33.6 4.9 %all-to-all-start.1 = ((bf16[16,24,1536]{2,1,0:T(8,128)(2,1)}), bf16[16,24,1536]{2,1,0:T(8,128)(2,1)S(1)}, u32[]{:S(2)}, u32[]{:S(2)}) async-start(bf16[16,24,1536]{2,1,0:T(8,128)(2,1)} %bitcast.84), calls=%async_computation.1 | async-start | bytes 2359296 | tf_op jit(solution)/shard_map/all_to_all | solution.py:298
  41.7 7.5 %lift.3.refs_3_ = f32[7,384,512]{2,1,0:T(8,128)} custom-call(s32[1]{0:T(128)} %bitcast.6.at, bf16[384,1280]{1,0:T(8,128)(2,1)S(1)} %bitcast.68, bf16[4096,1792]{1,0:T(8,128)(2,1)} %bitcast.78, bf16[4096,1792]{1,0:T(8,128)(2,1)} %bitcast.81), custom_call_target="tpu_custom_call" | custom-call | flops 3523215360 | bytes 20185088 | tf_op jit(solution)/shard_map/lift/pallas_call | solution.py:175
  49.1 5.0 %collective-permute-done.1.refs_0_ = bf16[384,768]{1,0:T(8,128)(2,1)S(1)} collective-permute-done((bf16[384,768]{1,0:T(8,128)(2,1)}, bf16[384,768]{1,0:T(8,128)(2,1)S(1)}, u32[]{:S(2)}, u32[]{:S(2)}) %collective-permute-start.1) | collective-permute-done | bytes 589856 | tf_op jit(solution)/shard_map/ppermute | solution.py:330
  54.1 7.7 %lift.4.refs_4_ = f32[7,384,512]{2,1,0:T(8,128)} custom-call(s32[1]{0:T(128)} %bitcast.13.at, bf16[384,768]{1,0:T(8,128)(2,1)S(1)} %collective-permute-done.1.refs_0_, bf16[4096,1792]{1,0:T(8,128)(2,1)} %bitcast.79, bf16[4096,1792]{1,0:T(8,128)(2,1)} %bitcast.82, f32[7,384,512]{2,1,0:T(8,128)} %lift.3.refs_3_), custom_call_target="tpu_custom_call" | custom-call | flops 2113929216 | bytes 16515072 | tf_op jit(solution)/shard_map/lift/pallas_call | solution.py:175
  61.9 4.2 %all-to-all-done.1 = bf16[16,24,1536]{2,1,0:T(8,128)(2,1)S(1)} async-done(((bf16[16,24,1536]{2,1,0:T(8,128)(2,1)}), bf16[16,24,1536]{2,1,0:T(8,128)(2,1)S(1)}, u32[]{:S(2)}, u32[]{:S(2)}) %all-to-all-start.1) | async-done | bytes 1179680 | tf_op jit(solution)/shard_map/all_to_all | solution.py:298
  66.1 15.1 %lift.5 = (bf16[384,1792]{1,0:T(8,128)(2,1)S(1)}, bf16[384,1792]{1,0:T(8,128)(2,1)}) custom-call(s32[4]{0:T(128)S(1)} %pad_add_fusion.at, bf16[384,512]{1,0:T(8,128)(2,1)S(1)} %collective-permute-done.refs_0_, bf16[384,1536]{1,0:T(8,128)(2,1)S(1)} %bitcast.69, bf16[4096,1792]{1,0:T(8,128)(2,1)} %bitcast.80, bf16[4096,1792]{1,0:T(8,128)(2,1)} %bitcast.83, ...), custom_call_target="tpu_custom_call" | custom-call | flops 8103395328 | bytes 32112640 | tf_op jit(solution)/shard_map/lift/pallas_call | solution.py:175
  81.2 5.3 %all-to-all-start.2 = ((bf16[16,24,1792]{2,1,0:T(8,128)(2,1)}), bf16[16,24,1792]{2,1,0:T(8,128)(2,1)}, u32[]{:S(2)}, u32[]{:S(2)}) async-start(bf16[16,24,1792]{2,1,0:T(8,128)(2,1)} %bitcast.85), calls=%async_computation.2 | async-start | bytes 2752512 | tf_op jit(solution)/shard_map/all_to_all | solution.py:298
  86.6 2.4 %drop.7 = bf16[384,512]{1,0:T(8,128)(2,1)S(1)} custom-call(s32[1]{0:T(128)} %bitcast.20.at, bf16[384,1792]{1,0:T(8,128)(2,1)S(1)} %get-tuple-element.14.hidden, bf16[1792,4096]{1,0:T(8,128)(2,1)} %bitcast.74), custom_call_target="tpu_custom_call" | custom-call | flops 704643072 | bytes 1835008 | tf_op jit(solution)/shard_map/drop/pallas_call | solution.py:203
  89.3 2.9 %drop.5 = bf16[384,640]{1,0:T(8,128)(2,1)S(1)} custom-call(s32[1]{0:T(128)} %bitcast.18.at, bf16[384,1792]{1,0:T(8,128)(2,1)S(1)} %get-tuple-element.14.hidden, bf16[1792,4096]{1,0:T(8,128)(2,1)} %bitcast.75), custom_call_target="tpu_custom_call" | custom-call | flops 880803840 | bytes 2293760 | tf_op jit(solution)/shard_map/drop/pallas_call | solution.py:203
  92.2 1.3 collective-permute-start.2
  93.9 2.4 %drop.6 = f32[384,512]{1,0:T(8,128)S(1)} custom-call(s32[1]{0:T(128)} %bitcast.19.at, bf16[384,1792]{1,0:T(8,128)(2,1)S(1)} %get-tuple-element.14.hidden, bf16[1792,4096]{1,0:T(8,128)(2,1)} %bitcast.76), custom_call_target="tpu_custom_call" | custom-call | flops 704643072 | bytes 1835008 | tf_op jit(solution)/shard_map/drop/pallas_call | solution.py:203
  96.3 2.9 %drop.4 = f32[384,640]{1,0:T(8,128)S(1)} custom-call(s32[1]{0:T(128)} %bitcast.17.at, bf16[384,1792]{1,0:T(8,128)(2,1)S(1)} %get-tuple-element.14.hidden, bf16[1792,4096]{1,0:T(8,128)(2,1)} %bitcast.77), custom_call_target="tpu_custom_call" | custom-call | flops 880803840 | bytes 2293760 | tf_op jit(solution)/shard_map/drop/pallas_call | solution.py:203
  99.6 10.4 %collective-permute-done.2 = bf16[384,640]{1,0:T(8,128)(2,1)S(1)} collective-permute-done((bf16[384,640]{1,0:T(8,128)(2,1)S(1)}, bf16[384,640]{1,0:T(8,128)(2,1)S(1)}, u32[]{:S(2)}, u32[]{:S(2)}) %collective-permute-start.2) | collective-permute-done | bytes 491552 | tf_op jit(solution)/shard_map/ppermute | solution.py:330
  111.1 7.0 %all-to-all-done.2 = bf16[16,24,1792]{2,1,0:T(8,128)(2,1)} async-done(((bf16[16,24,1792]{2,1,0:T(8,128)(2,1)}), bf16[16,24,1792]{2,1,0:T(8,128)(2,1)}, u32[]{:S(2)}, u32[]{:S(2)}) %all-to-all-start.2) | async-done | bytes 1376288 | tf_op jit(solution)/shard_map/all_to_all | solution.py:298
  118.1 5.3 %all-to-all-start.3 = ((bf16[16,24,1152]{2,1,0:T(8,128)(2,1)}), bf16[16,24,1152]{2,1,0:T(8,128)(2,1)S(1)}, u32[]{:S(2)}, u32[]{:S(2)}) async-start(bf16[16,24,1152]{2,1,0:T(8,128)(2,1)} %bitcast.23), calls=%async_computation.3 | async-start | bytes 1769472 | tf_op jit(solution)/shard_map/all_to_all | solution.py:298
  123.4 1.8 %fusion.38 = f32[128,1792]{1,0:T(8,128)S(1)} fusion(bf16[384,128]{1,0:T(8,128)(2,1)S(1)} %get-tuple-element.19, bf16[384,1792]{1,0:T(8,128)(2,1)} %bitcast.16), kind=kOutput, calls=%fused_computation.60 | convolution fusion | flops 176160768 | bytes 2392064 | tf_op jit(solution)/shard_map/dot_general | solution.py:309
  125.2 1.8 %convolution_add_fusion.1 = f32[128,1792]{1,0:T(8,128)S(1)} fusion(f32[128,1792]{1,0:T(8,128)S(1)} %fusion.38, bf16[384,128]{1,0:T(8,128)(2,1)S(1)} %get-tuple-element.18, bf16[384,1792]{1,0:T(8,128)(2,1)} %bitcast.16), kind=kOutput, calls=%fused_computation.2 | convolution fusion | flops 176390144 | bytes 3309568 | tf_op jit(solution)/shard_map/dot_general | solution.py:309
  127.0 1.8 %convolution_add_fusion = f32[128,1792]{1,0:T(8,128)S(1)} fusion(f32[128,1792]{1,0:T(8,128)S(1)} %convolution_add_fusion.1, bf16[384,128]{1,0:T(8,128)(2,1)S(1)} %get-tuple-element.17, bf16[384,1792]{1,0:T(8,128)(2,1)} %bitcast.16), kind=kOutput, calls=%fused_computation.1 | convolution fusion | flops 176390144 | bytes 3309568 | tf_op jit(solution)/shard_map/dot_general | solution.py:309
  129.1 11.5 %collective-permute-done.4 = f32[128,896]{1,0:T(8,128)S(1)} collective-permute-done((f32[128,896]{1,0:T(8,128)S(1)}, f32[128,896]{1,0:T(8,128)S(1)}, u32[]{:S(2)}, u32[]{:S(2)}) %collective-permute-start.4) | collective-permute-done | bytes 458784 | tf_op jit(solution)/shard_map/ppermute | solution.py:330
  140.7 4.3 %all-to-all-done.3 = bf16[16,24,1152]{2,1,0:T(8,128)(2,1)S(1)} async-done(((bf16[16,24,1152]{2,1,0:T(8,128)(2,1)}), bf16[16,24,1152]{2,1,0:T(8,128)(2,1)S(1)}, u32[]{:S(2)}, u32[]{:S(2)}) %all-to-all-start.3) | async-done | bytes 884768 | tf_op jit(solution)/shard_map/all_to_all | solution.py:298
  (34 shorter events, 9.7 us)
Async XLA Ops:
  0.0 1.2 copy-start
  1.2 0.7 copy-start.1
  3.5 30.1 %all-to-all-start = ((bf16[16,24,1280]{2,1,0:T(8,128)(2,1)}), bf16[16,24,1280]{2,1,0:T(8,128)(2,1)S(1)}, u32[]{:S(2)}, u32[]{:S(2)}) async-start(bf16[16,24,1280]{2,1,0:T(8,128)(2,1)} %bitcast.7), calls=%async_computation | async-start | bytes 1966080 | tf_op jit(solution)/shard_map/all_to_all | solution.py:298
  33.6 32.4 %all-to-all-start.1 = ((bf16[16,24,1536]{2,1,0:T(8,128)(2,1)}), bf16[16,24,1536]{2,1,0:T(8,128)(2,1)S(1)}, u32[]{:S(2)}, u32[]{:S(2)}) async-start(bf16[16,24,1536]{2,1,0:T(8,128)(2,1)} %bitcast.84), calls=%async_computation.1 | async-start | bytes 2359296 | tf_op jit(solution)/shard_map/all_to_all | solution.py:298
  39.4 14.8 %collective-permute-start.1 = (bf16[384,768]{1,0:T(8,128)(2,1)}, bf16[384,768]{1,0:T(8,128)(2,1)S(1)}, u32[]{:S(2)}, u32[]{:S(2)}) collective-permute-start(bf16[384,768]{1,0:T(8,128)(2,1)} %slice.13), channel_id=1, source_target_pairs={{0,1},{1,0},{2,3},{3,2},{4,5},{5,4},{6,7},{7,6},{8,9},{9,8},{10,11... | collective-permute-start | bytes 1769480 | tf_op jit(solution)/shard_map/ppermute | solution.py:330
  40.5 25.6 %collective-permute-start = (bf16[384,512]{1,0:T(8,128)(2,1)}, bf16[384,512]{1,0:T(8,128)(2,1)S(1)}, u32[]{:S(2)}, u32[]{:S(2)}) collective-permute-start(bf16[384,512]{1,0:T(8,128)(2,1)} %slice.12), channel_id=1, source_target_pairs={{0,1},{1,0},{2,3},{3,2},{4,5},{5,4},{6,7},{7,6},{8,9},{9,8},{10,11... | collective-permute-start | bytes 1179656 | tf_op jit(solution)/shard_map/ppermute | solution.py:330
  81.2 5.3 %copy-start.2 = (s32[128,2]{0,1:T(2,128)S(1)}, s32[128,2]{0,1:T(2,128)}, u32[]{:S(2)}) copy-start(s32[128,2]{0,1:T(2,128)} %param.7) | copy-start | bytes 3076
  81.2 5.3 %copy-start.3 = (f32[128,2]{0,1:T(2,128)S(1)}, f32[128,2]{0,1:T(2,128)}, u32[]{:S(2)}) copy-start(f32[128,2]{0,1:T(2,128)} %param.8) | copy-start | bytes 3076
  81.2 36.9 %all-to-all-start.2 = ((bf16[16,24,1792]{2,1,0:T(8,128)(2,1)}), bf16[16,24,1792]{2,1,0:T(8,128)(2,1)}, u32[]{:S(2)}, u32[]{:S(2)}) async-start(bf16[16,24,1792]{2,1,0:T(8,128)(2,1)} %bitcast.85), calls=%async_computation.2 | async-start | bytes 2752512 | tf_op jit(solution)/shard_map/all_to_all | solution.py:298
  89.0 10.5 %collective-permute-start.3 = (bf16[384,512]{1,0:T(8,128)(2,1)S(1)}, bf16[384,512]{1,0:T(8,128)(2,1)S(1)}, u32[]{:S(2)}, u32[]{:S(2)}) collective-permute-start(bf16[384,512]{1,0:T(8,128)(2,1)S(1)} %drop.7), channel_id=1, source_target_pairs={{0,1},{1,0},{2,3},{3,2},{4,5},{5,4},{6,7},{7,6},{8,9},{9,8},{10,11... | collective-permute-start | bytes 1179656 | tf_op jit(solution)/shard_map/ppermute | solution.py:330
  92.2 17.8 %collective-permute-start.2 = (bf16[384,640]{1,0:T(8,128)(2,1)S(1)}, bf16[384,640]{1,0:T(8,128)(2,1)S(1)}, u32[]{:S(2)}, u32[]{:S(2)}) collective-permute-start(bf16[384,640]{1,0:T(8,128)(2,1)S(1)} %drop.5), channel_id=1, source_target_pairs={{0,1},{1,0},{2,3},{3,2},{4,5},{5,4},{6,7},{7,6},{8,9},{9,8},{10,11... | collective-permute-start | bytes 1474568 | tf_op jit(solution)/shard_map/ppermute | solution.py:330
  118.1 26.9 %all-to-all-start.3 = ((bf16[16,24,1152]{2,1,0:T(8,128)(2,1)}), bf16[16,24,1152]{2,1,0:T(8,128)(2,1)S(1)}, u32[]{:S(2)}, u32[]{:S(2)}) async-start(bf16[16,24,1152]{2,1,0:T(8,128)(2,1)} %bitcast.23), calls=%async_computation.3 | async-start | bytes 1769472 | tf_op jit(solution)/shard_map/all_to_all | solution.py:298
  128.8 11.8 %collective-permute-start.4 = (f32[128,896]{1,0:T(8,128)S(1)}, f32[128,896]{1,0:T(8,128)S(1)}, u32[]{:S(2)}, u32[]{:S(2)}) collective-permute-start(f32[128,896]{1,0:T(8,128)S(1)} %constant_dynamic-slice_fusion), channel_id=1, source_target_pairs={{0,1},{1,0},{2,3},{3,2},{4,5},{5,4},{6,7},{7,6},{8,9},{9,8},{10,11... | collective-permute-start | bytes 1376264 | tf_op jit(solution)/shard_map/ppermute | solution.py:330

commit v11 on v10

--- a/solution.py
+++ b/solution.py
@@ -334,6 +334,8 @@
     direct_at = ranks * shared
 
     chosen, placed = place(tokens, expert_ids, experts, me * shared, shared)
+    later = jnp.dot(chosen, tokens[:, direct_at:], preferred_element_type=jnp.float32)
+    placed, later = lax.optimization_barrier((placed, later.astype(jnp.bfloat16)))
     own = swap(placed, experts)
     cut = pl.cdiv(shared, 2 * LANES) * LANES
     others = []
@@ -341,8 +343,7 @@
         for step in range(1, ranks):
             sent = send_up(own[:, begin:end], ranks - step)
             others.append((sent, rank_at(step) * shared + begin))
-    placed = jnp.dot(chosen, tokens[:, direct_at:], preferred_element_type=jnp.float32)
-    direct = swap(placed.astype(jnp.bfloat16), experts)
+    direct = swap(later, experts)
     (sums,) = lift([own], [me * shared], w_gate, w_up)
     for piece, at in others[:-1]:
         (sums,) = lift([piece], [at], w_gate, w_up, sums)

time: 148 us -> 148 us (level)
  blocking collectives: 0 us -> 30.4 us
  waiting for transfers between devices: 63.7 us -> 42.6 us
  starting transfers between devices: 25.5 us -> 18.4 us
    all_to_all x0 -> x1, blocking collectives: none -> 30.4 us  [swap(): lax.all_to_all(value.reshape(experts, slots // experts, width), 'expert',...]
    all_to_all x4 -> x3, waiting for transfers between devices: 36.6 us -> 15.5 us  [swap(): lax.all_to_all(value.reshape(experts, slots // experts, width), 'expert',...]
    all_to_all x4 -> x3, starting transfers between devices: 22.1 us -> 15 us  [swap(): lax.all_to_all(value.reshape(experts, slots // experts, width), 'expert',...]
  transfers between devices with their start and end apart: 9 -> 8, of which waited for: 8 -> 7; matrix products, arithmetic and copies ran while one was open for 8% -> 6% of each run, Pallas kernels for 18% -> 17%
where the time goes in v11:
time: 148 us; the launch traced here: 147 us
  waiting for transfers between devices  42.6 us (29%)
  Pallas kernels  41.5 us (28%)
  blocking collectives  30.4 us (21%)
  starting transfers between devices  18.4 us (12%)
  matrix products  8.09 us (5%)
  local copies, waits for them, and re-layouts  3.68 us (2%)
  other arithmetic  2.37 us (2%)
    all_to_all x1, blocking collectives, swap(): lax.all_to_all(value.reshape(experts, slots // experts, width), 'expert',...  30.4 us
    pallas_call x3, Pallas kernels, lift(): pl.pallas_call(kernel, out_shape=out_shape, in_specs=[pl.BlockSpec(memory...  30.3 us
    ppermute x5, waiting for transfers between devices, send_up(): lax.ppermute(value, 'tensor', [(i, (i + step) % ranks) for i in range(ran...  27.1 us
    all_to_all x3, waiting for transfers between devices, swap(): lax.all_to_all(value.reshape(experts, slots // experts, width), 'expert',...  15.5 us
    all_to_all x3, starting transfers between devices, swap(): lax.all_to_all(value.reshape(experts, slots // experts, width), 'expert',...  15 us
    pallas_call x4, Pallas kernels, drop(): pl.pallas_call(kernel, out_shape=jax.ShapeDtypeStruct((rows, width), dtyp...  10.6 us
    dot_general x6, matrix products, mix(): lax.dot_general(w, returned, (((0,), (0,)), ((), ())), preferred_element_...  6.43 us
    ppermute x5, starting transfers between devices, send_up(): lax.ppermute(value, 'tensor', [(i, (i + step) % ranks) for i in range(ran...  3.38 us
  transfers between devices with their start and end apart: 8, of which 7 were waited for; matrix products, arithmetic and copies ran while one was open for 6% of the time, Pallas kernels for 17%

profile of v11, /device:TPU:11, one launch (start us, length us, event | category | flops | bytes accessed | tf_op | source)
XLA Modules:
  0.0 147.3 jit_solution(4483345639766332390)
XLA Ops:
  0.0 1.2 copy-done
  2.5 1.5 convolution_convert_fusion
  4.0 30.4 %all_to_all.20 = bf16[16,24,1280]{2,1,0:T(8,128)(2,1)S(1)} all-to-all(bf16[16,24,1280]{2,1,0:T(8,128)(2,1)S(1)} %bitcast.70), channel_id=1, replica_groups=mesh['groups'=1,'dp'=1,'expert'=16,'tensor'=2] {'expert'}, dimensions={0} | all-to-all | bytes 1966080 | tf_op jit(solution)/shard_map/all_to_all | solution.py:298
  34.4 4.4 %all-to-all-start.1 = ((bf16[16,24,1536]{2,1,0:T(8,128)(2,1)}), bf16[16,24,1536]{2,1,0:T(8,128)(2,1)S(1)}, u32[]{:S(2)}, u32[]{:S(2)}) async-start(bf16[16,24,1536]{2,1,0:T(8,128)(2,1)} %bitcast.85), calls=%async_computation.1 | async-start | bytes 2359296 | tf_op jit(solution)/shard_map/all_to_all | solution.py:298
  40.8 1.2 collective-permute-start
  42.0 7.5 %lift.3.refs_3_ = f32[7,384,512]{2,1,0:T(8,128)} custom-call(s32[1]{0:T(128)} %bitcast.6.at, bf16[384,1280]{1,0:T(8,128)(2,1)S(1)} %bitcast.68, bf16[4096,1792]{1,0:T(8,128)(2,1)} %bitcast.79, bf16[4096,1792]{1,0:T(8,128)(2,1)} %bitcast.82), custom_call_target="tpu_custom_call" | custom-call | flops 3523215360 | bytes 20185088 | tf_op jit(solution)/shard_map/lift/pallas_call | solution.py:175
  49.5 5.0 %collective-permute-done.1.refs_0_ = bf16[384,768]{1,0:T(8,128)(2,1)S(1)} collective-permute-done((bf16[384,768]{1,0:T(8,128)(2,1)}, bf16[384,768]{1,0:T(8,128)(2,1)S(1)}, u32[]{:S(2)}, u32[]{:S(2)}) %collective-permute-start.1) | collective-permute-done | bytes 589856 | tf_op jit(solution)/shard_map/ppermute | solution.py:330
  54.4 7.7 %lift.4.refs_4_ = f32[7,384,512]{2,1,0:T(8,128)} custom-call(s32[1]{0:T(128)} %bitcast.13.at, bf16[384,768]{1,0:T(8,128)(2,1)S(1)} %collective-permute-done.1.refs_0_, bf16[4096,1792]{1,0:T(8,128)(2,1)} %bitcast.80, bf16[4096,1792]{1,0:T(8,128)(2,1)} %bitcast.83, f32[7,384,512]{2,1,0:T(8,128)} %lift.3.refs_3_), custom_call_target="tpu_custom_call" | custom-call | flops 2113929216 | bytes 16515072 | tf_op jit(solution)/shard_map/lift/pallas_call | solution.py:175
  62.2 4.2 %all-to-all-done.1 = bf16[16,24,1536]{2,1,0:T(8,128)(2,1)S(1)} async-done(((bf16[16,24,1536]{2,1,0:T(8,128)(2,1)}), bf16[16,24,1536]{2,1,0:T(8,128)(2,1)S(1)}, u32[]{:S(2)}, u32[]{:S(2)}) %all-to-all-start.1) | async-done | bytes 1179680 | tf_op jit(solution)/shard_map/all_to_all | solution.py:298
  66.4 15.1 %lift.5 = (bf16[384,1792]{1,0:T(8,128)(2,1)S(1)}, bf16[384,1792]{1,0:T(8,128)(2,1)}) custom-call(s32[4]{0:T(128)S(1)} %pad_add_fusion.at, bf16[384,512]{1,0:T(8,128)(2,1)S(1)} %collective-permute-done.refs_0_, bf16[384,1536]{1,0:T(8,128)(2,1)S(1)} %bitcast.69, bf16[4096,1792]{1,0:T(8,128)(2,1)} %bitcast.81, bf16[4096,1792]{1,0:T(8,128)(2,1)} %bitcast.84, ...), custom_call_target="tpu_custom_call" | custom-call | flops 8103395328 | bytes 32112640 | tf_op jit(solution)/shard_map/lift/pallas_call | solution.py:175
  81.6 5.3 %all-to-all-start.2 = ((bf16[16,24,1792]{2,1,0:T(8,128)(2,1)}), bf16[16,24,1792]{2,1,0:T(8,128)(2,1)}, u32[]{:S(2)}, u32[]{:S(2)}) async-start(bf16[16,24,1792]{2,1,0:T(8,128)(2,1)} %bitcast.86), calls=%async_computation.2 | async-start | bytes 2752512 | tf_op jit(solution)/shard_map/all_to_all | solution.py:298
  86.9 2.4 %drop.7 = bf16[384,512]{1,0:T(8,128)(2,1)S(1)} custom-call(s32[1]{0:T(128)} %bitcast.20.at, bf16[384,1792]{1,0:T(8,128)(2,1)S(1)} %get-tuple-element.18.hidden, bf16[1792,4096]{1,0:T(8,128)(2,1)} %bitcast.75), custom_call_target="tpu_custom_call" | custom-call | flops 704643072 | bytes 1835008 | tf_op jit(solution)/shard_map/drop/pallas_call | solution.py:203
  89.6 2.9 %drop.5 = bf16[384,640]{1,0:T(8,128)(2,1)S(1)} custom-call(s32[1]{0:T(128)} %bitcast.18.at, bf16[384,1792]{1,0:T(8,128)(2,1)S(1)} %get-tuple-element.18.hidden, bf16[1792,4096]{1,0:T(8,128)(2,1)} %bitcast.76), custom_call_target="tpu_custom_call" | custom-call | flops 880803840 | bytes 2293760 | tf_op jit(solution)/shard_map/drop/pallas_call | solution.py:203
  92.5 1.3 collective-permute-start.2
  94.2 2.4 %drop.6 = f32[384,512]{1,0:T(8,128)S(1)} custom-call(s32[1]{0:T(128)} %bitcast.19.at, bf16[384,1792]{1,0:T(8,128)(2,1)S(1)} %get-tuple-element.18.hidden, bf16[1792,4096]{1,0:T(8,128)(2,1)} %bitcast.77), custom_call_target="tpu_custom_call" | custom-call | flops 704643072 | bytes 1835008 | tf_op jit(solution)/shard_map/drop/pallas_call | solution.py:203
  96.6 2.9 %drop.4 = f32[384,640]{1,0:T(8,128)S(1)} custom-call(s32[1]{0:T(128)} %bitcast.17.at, bf16[384,1792]{1,0:T(8,128)(2,1)S(1)} %get-tuple-element.18.hidden, bf16[1792,4096]{1,0:T(8,128)(2,1)} %bitcast.78), custom_call_target="tpu_custom_call" | custom-call | flops 880803840 | bytes 2293760 | tf_op jit(solution)/shard_map/drop/pallas_call | solution.py:203
  99.9 10.4 %collective-permute-done.2 = bf16[384,640]{1,0:T(8,128)(2,1)S(1)} collective-permute-done((bf16[384,640]{1,0:T(8,128)(2,1)S(1)}, bf16[384,640]{1,0:T(8,128)(2,1)S(1)}, u32[]{:S(2)}, u32[]{:S(2)}) %collective-permute-start.2) | collective-permute-done | bytes 491552 | tf_op jit(solution)/shard_map/ppermute | solution.py:330
  111.4 7.0 %all-to-all-done.2 = bf16[16,24,1792]{2,1,0:T(8,128)(2,1)} async-done(((bf16[16,24,1792]{2,1,0:T(8,128)(2,1)}), bf16[16,24,1792]{2,1,0:T(8,128)(2,1)}, u32[]{:S(2)}, u32[]{:S(2)}) %all-to-all-start.2) | async-done | bytes 1376288 | tf_op jit(solution)/shard_map/all_to_all | solution.py:298
  118.4 5.3 %all-to-all-start.3 = ((bf16[16,24,1152]{2,1,0:T(8,128)(2,1)}), bf16[16,24,1152]{2,1,0:T(8,128)(2,1)S(1)}, u32[]{:S(2)}, u32[]{:S(2)}) async-start(bf16[16,24,1152]{2,1,0:T(8,128)(2,1)} %bitcast.23), calls=%async_computation.3 | async-start | bytes 1769472 | tf_op jit(solution)/shard_map/all_to_all | solution.py:298
  123.8 1.8 %fusion.38 = f32[128,1792]{1,0:T(8,128)S(1)} fusion(bf16[384,128]{1,0:T(8,128)(2,1)S(1)} %get-tuple-element.23, bf16[384,1792]{1,0:T(8,128)(2,1)} %bitcast.16), kind=kOutput, calls=%fused_computation.60 | convolution fusion | flops 176160768 | bytes 2392064 | tf_op jit(solution)/shard_map/dot_general | solution.py:309
  125.5 1.8 %convolution_add_fusion.1 = f32[128,1792]{1,0:T(8,128)S(1)} fusion(f32[128,1792]{1,0:T(8,128)S(1)} %fusion.38, bf16[384,128]{1,0:T(8,128)(2,1)S(1)} %get-tuple-element.22, bf16[384,1792]{1,0:T(8,128)(2,1)} %bitcast.16), kind=kOutput, calls=%fused_computation.2 | convolution fusion | flops 176390144 | bytes 3309568 | tf_op jit(solution)/shard_map/dot_general | solution.py:309
  127.3 1.8 %convolution_add_fusion = f32[128,1792]{1,0:T(8,128)S(1)} fusion(f32[128,1792]{1,0:T(8,128)S(1)} %convolution_add_fusion.1, bf16[384,128]{1,0:T(8,128)(2,1)S(1)} %get-tuple-element.21, bf16[384,1792]{1,0:T(8,128)(2,1)} %bitcast.16), kind=kOutput, calls=%fused_computation.1 | convolution fusion | flops 176390144 | bytes 3309568 | tf_op jit(solution)/shard_map/dot_general | solution.py:309
  129.4 11.5 %collective-permute-done.4 = f32[128,896]{1,0:T(8,128)S(1)} collective-permute-done((f32[128,896]{1,0:T(8,128)S(1)}, f32[128,896]{1,0:T(8,128)S(1)}, u32[]{:S(2)}, u32[]{:S(2)}) %collective-permute-start.4) | collective-permute-done | bytes 458784 | tf_op jit(solution)/shard_map/ppermute | solution.py:330
  141.0 4.3 %all-to-all-done.3 = bf16[16,24,1152]{2,1,0:T(8,128)(2,1)S(1)} async-done(((bf16[16,24,1152]{2,1,0:T(8,128)(2,1)}), bf16[16,24,1152]{2,1,0:T(8,128)(2,1)S(1)}, u32[]{:S(2)}, u32[]{:S(2)}) %all-to-all-start.3) | async-done | bytes 884768 | tf_op jit(solution)/shard_map/all_to_all | solution.py:298
  (33 shorter events, 7.9 us)
Async XLA Ops:
  0.0 1.2 copy-start
  1.2 0.7 copy-start.1
  34.4 32.0 %all-to-all-start.1 = ((bf16[16,24,1536]{2,1,0:T(8,128)(2,1)}), bf16[16,24,1536]{2,1,0:T(8,128)(2,1)S(1)}, u32[]{:S(2)}, u32[]{:S(2)}) async-start(bf16[16,24,1536]{2,1,0:T(8,128)(2,1)} %bitcast.85), calls=%async_computation.1 | async-start | bytes 2359296 | tf_op jit(solution)/shard_map/all_to_all | solution.py:298
  39.7 14.8 %collective-permute-start.1 = (bf16[384,768]{1,0:T(8,128)(2,1)}, bf16[384,768]{1,0:T(8,128)(2,1)S(1)}, u32[]{:S(2)}, u32[]{:S(2)}) collective-permute-start(bf16[384,768]{1,0:T(8,128)(2,1)} %slice.13), channel_id=1, source_target_pairs={{0,1},{1,0},{2,3},{3,2},{4,5},{5,4},{6,7},{7,6},{8,9},{9,8},{10,11... | collective-permute-start | bytes 1769480 | tf_op jit(solution)/shard_map/ppermute | solution.py:330
  40.8 25.6 %collective-permute-start = (bf16[384,512]{1,0:T(8,128)(2,1)}, bf16[384,512]{1,0:T(8,128)(2,1)S(1)}, u32[]{:S(2)}, u32[]{:S(2)}) collective-permute-start(bf16[384,512]{1,0:T(8,128)(2,1)} %slice.12), channel_id=1, source_target_pairs={{0,1},{1,0},{2,3},{3,2},{4,5},{5,4},{6,7},{7,6},{8,9},{9,8},{10,11... | collective-permute-start | bytes 1179656 | tf_op jit(solution)/shard_map/ppermute | solution.py:330
  81.5 5.3 %copy-start.2 = (s32[128,2]{0,1:T(2,128)S(1)}, s32[128,2]{0,1:T(2,128)}, u32[]{:S(2)}) copy-start(s32[128,2]{0,1:T(2,128)} %param.7) | copy-start | bytes 3076
  81.5 5.3 %copy-start.3 = (f32[128,2]{0,1:T(2,128)S(1)}, f32[128,2]{0,1:T(2,128)}, u32[]{:S(2)}) copy-start(f32[128,2]{0,1:T(2,128)} %param.8) | copy-start | bytes 3076
  81.6 36.9 %all-to-all-start.2 = ((bf16[16,24,1792]{2,1,0:T(8,128)(2,1)}), bf16[16,24,1792]{2,1,0:T(8,128)(2,1)}, u32[]{:S(2)}, u32[]{:S(2)}) async-start(bf16[16,24,1792]{2,1,0:T(8,128)(2,1)} %bitcast.86), calls=%async_computation.2 | async-start | bytes 2752512 | tf_op jit(solution)/shard_map/all_to_all | solution.py:298
  89.3 10.5 %collective-permute-start.3 = (bf16[384,512]{1,0:T(8,128)(2,1)S(1)}, bf16[384,512]{1,0:T(8,128)(2,1)S(1)}, u32[]{:S(2)}, u32[]{:S(2)}) collective-permute-start(bf16[384,512]{1,0:T(8,128)(2,1)S(1)} %drop.7), channel_id=1, source_target_pairs={{0,1},{1,0},{2,3},{3,2},{4,5},{5,4},{6,7},{7,6},{8,9},{9,8},{10,11... | collective-permute-start | bytes 1179656 | tf_op jit(solution)/shard_map/ppermute | solution.py:330
  92.5 17.8 %collective-permute-start.2 = (bf16[384,640]{1,0:T(8,128)(2,1)S(1)}, bf16[384,640]{1,0:T(8,128)(2,1)S(1)}, u32[]{:S(2)}, u32[]{:S(2)}) collective-permute-start(bf16[384,640]{1,0:T(8,128)(2,1)S(1)} %drop.5), channel_id=1, source_target_pairs={{0,1},{1,0},{2,3},{3,2},{4,5},{5,4},{6,7},{7,6},{8,9},{9,8},{10,11... | collective-permute-start | bytes 1474568 | tf_op jit(solution)/shard_map/ppermute | solution.py:330
  118.4 26.9 %all-to-all-start.3 = ((bf16[16,24,1152]{2,1,0:T(8,128)(2,1)}), bf16[16,24,1152]{2,1,0:T(8,128)(2,1)S(1)}, u32[]{:S(2)}, u32[]{:S(2)}) async-start(bf16[16,24,1152]{2,1,0:T(8,128)(2,1)} %bitcast.23), calls=%async_computation.3 | async-start | bytes 1769472 | tf_op jit(solution)/shard_map/all_to_all | solution.py:298
  129.1 11.8 %collective-permute-start.4 = (f32[128,896]{1,0:T(8,128)S(1)}, f32[128,896]{1,0:T(8,128)S(1)}, u32[]{:S(2)}, u32[]{:S(2)}) collective-permute-start(f32[128,896]{1,0:T(8,128)S(1)} %constant_dynamic-slice_fusion), channel_id=1, source_target_pairs={{0,1},{1,0},{2,3},{3,2},{4,5},{5,4},{6,7},{7,6},{8,9},{9,8},{10,11... | collective-permute-start | bytes 1376264 | tf_op jit(solution)/shard_map/ppermute | solution.py:330

commit v12 on v10

--- a/solution.py
+++ b/solution.py
@@ -313,6 +313,36 @@
     )
 
 
+def mix_last(weights, returned, first):
+    rows = weights[0].shape[1]
+    early = first[0].shape[1]
+    late = returned.shape[1]
+    count = len(weights)
+
+    def kernel(*refs):
+        parts, back, terms, out = refs[:count], refs[count], refs[count + 1 : -1], refs[-1]
+        out[:, :early] = sum(term[...] for term in terms).astype(jnp.bfloat16)
+        for at in range(0, late, 2 * LANES):
+            end = min(at + 2 * LANES, late)
+            out[:, early + at : early + end] = mix(
+                [part[...] for part in parts], back[:, at:end]
+            ).astype(jnp.bfloat16)
+
+    return pl.pallas_call(
+        kernel,
+        out_shape=jax.ShapeDtypeStruct((rows, early + late), jnp.bfloat16),
+        in_specs=[vmem()] * (count + 1 + len(first)),
+        out_specs=vmem(),
+        compiler_params=pltpu.CompilerParams(vmem_limit_bytes=VMEM_BYTES // 2),
+        cost_estimate=pl.CostEstimate(
+            flops=2 * count * returned.shape[0] * rows * late,
+            bytes_accessed=2 * rows * (early + late),
+            transcendentals=0,
+        ),
+        name="mix_last",
+    )(*weights, returned, *first)
+
+
 def on_device(tokens, expert_ids, gate_probs, w_gate, w_up, w_down):
     width = tokens.shape[1]
     experts = lax.axis_size("expert")
@@ -347,7 +377,7 @@
     for piece, at in others[:-1]:
         (sums,) = lift([piece], [at], w_gate, w_up, sums)
 
-    early = round(share * 7 / 16 / 128) * 128
+    early = round(share * 3 / 8 / 128) * 128
     columns = [jnp.int32(rank * share) for rank in range(ranks)]
     last, last_at = others[-1]
     hidden, partial = lift(
@@ -359,7 +389,7 @@
         (w_down, columns, early),
     )
     returned = swap(partial, experts)
-    edges = [early, early + pl.cdiv(share - early, 256) * 128, share]
+    edges = [early, early + (share - early) // 512 * 256, share] if share - early >= 512 else [early, share]
     owned = []
     for at, end in zip(edges[:-1], edges[1:]):
         cut = end - at
@@ -377,11 +407,10 @@
     def part_of(rank):
         return lax.dynamic_slice_in_dim(first, rank * early, early, axis=1)
 
-    mixed = part_of(me)
+    terms = [part_of(me)]
     for step in range(1, ranks):
-        mixed = mixed + send_up(part_of(rank_at(step)), step)
-    late = mix(weights, swap(owned, experts))
-    return jnp.concatenate([mixed.astype(jnp.bfloat16), late.astype(jnp.bfloat16)], axis=1)
+        terms.append(send_up(part_of(rank_at(step)), step))
+    return mix_last(weights, swap(owned, experts), terms)
 
 
 def solution(mesh):

time: 148 us -> 148 us (level)
  matrix products: 9.09 us -> 3.84 us
  other arithmetic: 2.37 us -> 5.39 us
  Pallas kernels: 42.4 us -> 44.3 us
  starting transfers between devices: 25.5 us -> 27 us
    dot_general x6 -> x3, matrix products: 6.42 us -> 1.18 us  [mix(): lax.dot_general(w, returned, (((0,), (0,)), ((), ())), preferred_element_...]
    convert_element_type x2, other arithmetic: 0.21 us -> 2.29 us  [on_device(): owned.append(value.astype(jnp.bfloat16))]
    pallas_call x0 -> x1, Pallas kernels: none -> 1.51 us  [mix_last(): pl.pallas_call(kernel, out_shape=jax.ShapeDtypeStruct((rows, early + late...]
  transfers between devices with their start and end apart: 9 -> 9, of which waited for: 8 -> 6; matrix products, arithmetic and copies ran while one was open for 8% -> 7% of each run, Pallas kernels for 18% -> 18%
where the time goes in v12:
time: 148 us; the launch traced here: 147 us
  waiting for transfers between devices  63.1 us (43%)
  Pallas kernels  44.3 us (30%)
  starting transfers between devices  27 us (18%)
  other arithmetic  5.39 us (4%)
  matrix products  3.84 us (3%)
  local copies, waits for them, and re-layouts  2.97 us (2%)
    all_to_all x4, waiting for transfers between devices, swap(): lax.all_to_all(value.reshape(experts, slots // experts, width), 'expert',...  36.7 us
    pallas_call x3, Pallas kernels, lift(): pl.pallas_call(kernel, out_shape=out_shape, in_specs=[pl.BlockSpec(memory...  30.4 us
    ppermute x5, waiting for transfers between devices, send_up(): lax.ppermute(value, 'tensor', [(i, (i + step) % ranks) for i in range(ran...  26.4 us
    all_to_all x4, starting transfers between devices, swap(): lax.all_to_all(value.reshape(experts, slots // experts, width), 'expert',...  23.6 us
    pallas_call x4, Pallas kernels, drop(): pl.pallas_call(kernel, out_shape=jax.ShapeDtypeStruct((rows, width), dtyp...  10.8 us
    ppermute x5, starting transfers between devices, send_up(): lax.ppermute(value, 'tensor', [(i, (i + step) % ranks) for i in range(ran...  3.44 us
  transfers between devices with their start and end apart: 9, of which 6 were waited for; matrix products, arithmetic and copies ran while one was open for 7% of the time, Pallas kernels for 18%

profile of v12, /device:TPU:11, one launch (start us, length us, event | category | flops | bytes accessed | tf_op | source)
XLA Modules:
  0.0 146.8 jit_solution(7440335494629668333)
XLA Ops:
  0.0 1.2 copy-done.1
  1.9 1.6 %place.1 = (bf16[384,128]{1,0:T(8,128)(2,1)S(1)}, bf16[384,1280]{1,0:T(8,128)(2,1)}) custom-call(s32[1]{0:T(128)} %bitcast.8.at, s32[2,128]{1,0:T(2,128)S(1)} %bitcast.57, bf16[128,4096]{1,0:T(8,128)(2,1)S(1)} %copy-done.1), custom_call_target="tpu_custom_call" | custom-call | flops 125829120 | bytes 327680 | tf_op jit(solution)/shard_map/place/pallas_call | solution.py:273
  3.5 6.6 %all-to-all-start = ((bf16[16,24,1280]{2,1,0:T(8,128)(2,1)}), bf16[16,24,1280]{2,1,0:T(8,128)(2,1)S(1)}, u32[]{:S(2)}, u32[]{:S(2)}) async-start(bf16[16,24,1280]{2,1,0:T(8,128)(2,1)} %bitcast.9), calls=%async_computation | async-start | bytes 1966080 | tf_op jit(solution)/shard_map/all_to_all | solution.py:298
  10.1 2.5 %convolution_convert_fusion = bf16[384,1536]{1,0:T(8,128)(2,1)} fusion(bf16[384,128]{1,0:T(8,128)(2,1)S(1)} %get-tuple-element.12, bf16[128,4096]{1,0:T(8,128)(2,1)} %tokens.1), kind=kOutput, calls=%fused_computation | convolution fusion | flops 151584768 | bytes 1671168 | tf_op jit(solution)/shard_map/dot_general | solution.py:374
  12.6 21.1 %all-to-all-done = bf16[16,24,1280]{2,1,0:T(8,128)(2,1)S(1)} async-done(((bf16[16,24,1280]{2,1,0:T(8,128)(2,1)}), bf16[16,24,1280]{2,1,0:T(8,128)(2,1)S(1)}, u32[]{:S(2)}, u32[]{:S(2)}) %all-to-all-start) | async-done | bytes 983072 | tf_op jit(solution)/shard_map/all_to_all | solution.py:298
  33.6 4.9 %all-to-all-start.1 = ((bf16[16,24,1536]{2,1,0:T(8,128)(2,1)}), bf16[16,24,1536]{2,1,0:T(8,128)(2,1)S(1)}, u32[]{:S(2)}, u32[]{:S(2)}) async-start(bf16[16,24,1536]{2,1,0:T(8,128)(2,1)} %bitcast.11), calls=%async_computation.1 | async-start | bytes 2359296 | tf_op jit(solution)/shard_map/all_to_all | solution.py:298
  39.7 1.3 collective-permute-start
  41.0 7.4 %lift.3.refs_3_ = f32[7,384,512]{2,1,0:T(8,128)} custom-call(s32[1]{0:T(128)} %bitcast.8.at, bf16[384,1280]{1,0:T(8,128)(2,1)S(1)} %bitcast.54, bf16[4096,1792]{1,0:T(8,128)(2,1)} %bitcast.65, bf16[4096,1792]{1,0:T(8,128)(2,1)} %bitcast.68), custom_call_target="tpu_custom_call" | custom-call | flops 3523215360 | bytes 20185088 | tf_op jit(solution)/shard_map/lift/pallas_call | solution.py:175
  48.5 5.7 %collective-permute-done.1.refs_0_ = bf16[384,768]{1,0:T(8,128)(2,1)S(1)} collective-permute-done((bf16[384,768]{1,0:T(8,128)(2,1)}, bf16[384,768]{1,0:T(8,128)(2,1)S(1)}, u32[]{:S(2)}, u32[]{:S(2)}) %collective-permute-start.1) | collective-permute-done | bytes 589856 | tf_op jit(solution)/shard_map/ppermute | solution.py:360
  54.1 7.7 %lift.4.refs_4_ = f32[7,384,512]{2,1,0:T(8,128)} custom-call(s32[1]{0:T(128)} %bitcast.15.at, bf16[384,768]{1,0:T(8,128)(2,1)S(1)} %collective-permute-done.1.refs_0_, bf16[4096,1792]{1,0:T(8,128)(2,1)} %bitcast.66, bf16[4096,1792]{1,0:T(8,128)(2,1)} %bitcast.69, f32[7,384,512]{2,1,0:T(8,128)} %lift.3.refs_3_), custom_call_target="tpu_custom_call" | custom-call | flops 2113929216 | bytes 16515072 | tf_op jit(solution)/shard_map/lift/pallas_call | solution.py:175
  61.9 4.2 %all-to-all-done.1 = bf16[16,24,1536]{2,1,0:T(8,128)(2,1)S(1)} async-done(((bf16[16,24,1536]{2,1,0:T(8,128)(2,1)}), bf16[16,24,1536]{2,1,0:T(8,128)(2,1)S(1)}, u32[]{:S(2)}, u32[]{:S(2)}) %all-to-all-start.1) | async-done | bytes 1179680 | tf_op jit(solution)/shard_map/all_to_all | solution.py:298
  66.1 15.2 %lift.5 = (bf16[384,1792]{1,0:T(8,128)(2,1)}, bf16[384,1536]{1,0:T(8,128)(2,1)}) custom-call(s32[4]{0:T(128)S(1)} %pad_add_fusion.at, bf16[384,512]{1,0:T(8,128)(2,1)S(1)} %collective-permute-done.refs_0_, bf16[384,1536]{1,0:T(8,128)(2,1)S(1)} %bitcast.55, bf16[4096,1792]{1,0:T(8,128)(2,1)} %bitcast.67, bf16[4096,1792]{1,0:T(8,128)(2,1)} %bitcast.70, ...), custom_call_target="tpu_custom_call" | custom-call | flops 7751073792 | bytes 31195136 | tf_op jit(solution)/shard_map/lift/pallas_call | solution.py:175
  81.3 5.2 %all-to-all-start.2 = ((bf16[16,24,1536]{2,1,0:T(8,128)(2,1)}), bf16[16,24,1536]{2,1,0:T(8,128)(2,1)S(1)}, u32[]{:S(2)}, u32[]{:S(2)}) async-start(bf16[16,24,1536]{2,1,0:T(8,128)(2,1)} %bitcast.17), calls=%async_computation.2 | async-start | bytes 2359296 | tf_op jit(solution)/shard_map/all_to_all | solution.py:298
  87.1 2.4 %drop.5 = bf16[384,512]{1,0:T(8,128)(2,1)S(1)} custom-call(s32[1]{0:T(128)} %bitcast.20.at, bf16[384,1792]{1,0:T(8,128)(2,1)S(1)} %copy-done, bf16[1792,4096]{1,0:T(8,128)(2,1)} %bitcast.61), custom_call_target="tpu_custom_call" | custom-call | flops 704643072 | bytes 1835008 | tf_op jit(solution)/shard_map/drop/pallas_call | solution.py:203
  89.8 3.0 %drop.7 = bf16[384,768]{1,0:T(8,128)(2,1)S(1)} custom-call(s32[1]{0:T(128)} %bitcast.22.at, bf16[384,1792]{1,0:T(8,128)(2,1)S(1)} %copy-done, bf16[1792,4096]{1,0:T(8,128)(2,1)} %bitcast.62), custom_call_target="tpu_custom_call" | custom-call | flops 1056964608 | bytes 2752512 | tf_op jit(solution)/shard_map/drop/pallas_call | solution.py:203
  92.9 1.3 collective-permute-start.3
  95.5 2.4 %drop.4 = f32[384,512]{1,0:T(8,128)S(1)} custom-call(s32[1]{0:T(128)} %bitcast.19.at, bf16[384,1792]{1,0:T(8,128)(2,1)S(1)} %copy-done, bf16[1792,4096]{1,0:T(8,128)(2,1)} %bitcast.63), custom_call_target="tpu_custom_call" | custom-call | flops 704643072 | bytes 1835008 | tf_op jit(solution)/shard_map/drop/pallas_call | solution.py:203
  97.9 3.0 %drop.6 = f32[384,768]{1,0:T(8,128)S(1)} custom-call(s32[1]{0:T(128)} %bitcast.21.at, bf16[384,1792]{1,0:T(8,128)(2,1)S(1)} %copy-done, bf16[1792,4096]{1,0:T(8,128)(2,1)} %bitcast.64), custom_call_target="tpu_custom_call" | custom-call | flops 1056964608 | bytes 2752512 | tf_op jit(solution)/shard_map/drop/pallas_call | solution.py:203
  102.1 10.6 %collective-permute-done.3 = bf16[384,768]{1,0:T(8,128)(2,1)} collective-permute-done((bf16[384,768]{1,0:T(8,128)(2,1)S(1)}, bf16[384,768]{1,0:T(8,128)(2,1)}, u32[]{:S(2)}, u32[]{:S(2)}) %collective-permute-start.3) | collective-permute-done | bytes 589856 | tf_op jit(solution)/shard_map/ppermute | solution.py:360
  112.7 1.2 add_convert_fusion
  114.9 6.9 %all-to-all-start.3 = ((bf16[16,24,1280]{2,1,0:T(8,128)(2,1)}), bf16[16,24,1280]{2,1,0:T(8,128)(2,1)S(1)}, u32[]{:S(2)}, u32[]{:S(2)}) async-start(bf16[16,24,1280]{2,1,0:T(8,128)(2,1)} %bitcast.23), calls=%async_computation.3 | async-start | bytes 1966080 | tf_op jit(solution)/shard_map/all_to_all | solution.py:298
  123.7 10.1 %collective-permute-done.4.refs_5_ = f32[128,768]{1,0:T(8,128)S(1)} collective-permute-done((f32[128,768]{1,0:T(8,128)S(1)}, f32[128,768]{1,0:T(8,128)S(1)}, u32[]{:S(2)}, u32[]{:S(2)}) %collective-permute-start.4) | collective-permute-done | bytes 393248 | tf_op jit(solution)/shard_map/ppermute | solution.py:360
  133.8 11.4 %all-to-all-done.3 = bf16[16,24,1280]{2,1,0:T(8,128)(2,1)S(1)} async-done(((bf16[16,24,1280]{2,1,0:T(8,128)(2,1)}), bf16[16,24,1280]{2,1,0:T(8,128)(2,1)S(1)}, u32[]{:S(2)}, u32[]{:S(2)}) %all-to-all-start.3) | async-done | bytes 983072 | tf_op jit(solution)/shard_map/all_to_all | solution.py:298
  145.3 1.5 %mix_last.1 = bf16[128,2048]{1,0:T(8,128)(2,1)} custom-call(bf16[384,128]{1,0:T(8,128)(2,1)S(1)} %get-tuple-element.21.refs_0_, bf16[384,128]{1,0:T(8,128)(2,1)S(1)} %get-tuple-element.20.refs_1_, bf16[384,128]{1,0:T(8,128)(2,1)S(1)} %get-tuple-element.19.refs_2_, bf16[384,1280]{1,0:T(8,128)(2,1)S(1)} %bitcast.56, f32[128,768]{1,0:T(8,128)S(1)} %get-tuple-element.18.refs_4_, ...), custom_call_target="tpu_custom_call" | custom-call | flops 377487360 | bytes 524288 | tf_op jit(solution)/shard_map/mix_last/pallas_call | solution.py:331
  (36 shorter events, 8.2 us)
Async XLA Ops:
  0.0 1.2 copy-start.1
  1.2 0.7 copy-start.2
  3.5 30.1 %all-to-all-start = ((bf16[16,24,1280]{2,1,0:T(8,128)(2,1)}), bf16[16,24,1280]{2,1,0:T(8,128)(2,1)S(1)}, u32[]{:S(2)}, u32[]{:S(2)}) async-start(bf16[16,24,1280]{2,1,0:T(8,128)(2,1)} %bitcast.9), calls=%async_computation | async-start | bytes 1966080 | tf_op jit(solution)/shard_map/all_to_all | solution.py:298
  33.6 32.4 %all-to-all-start.1 = ((bf16[16,24,1536]{2,1,0:T(8,128)(2,1)}), bf16[16,24,1536]{2,1,0:T(8,128)(2,1)S(1)}, u32[]{:S(2)}, u32[]{:S(2)}) async-start(bf16[16,24,1536]{2,1,0:T(8,128)(2,1)} %bitcast.11), calls=%async_computation.1 | async-start | bytes 2359296 | tf_op jit(solution)/shard_map/all_to_all | solution.py:298
  39.4 14.8 %collective-permute-start.1 = (bf16[384,768]{1,0:T(8,128)(2,1)}, bf16[384,768]{1,0:T(8,128)(2,1)S(1)}, u32[]{:S(2)}, u32[]{:S(2)}) collective-permute-start(bf16[384,768]{1,0:T(8,128)(2,1)} %slice.13), channel_id=1, source_target_pairs={{0,1},{1,0},{2,3},{3,2},{4,5},{5,4},{6,7},{7,6},{8,9},{9,8},{10,11... | collective-permute-start | bytes 1769480 | tf_op jit(solution)/shard_map/ppermute | solution.py:360
  39.7 26.3 %collective-permute-start = (bf16[384,512]{1,0:T(8,128)(2,1)S(1)}, bf16[384,512]{1,0:T(8,128)(2,1)S(1)}, u32[]{:S(2)}, u32[]{:S(2)}) collective-permute-start(bf16[384,512]{1,0:T(8,128)(2,1)S(1)} %slice.12), channel_id=1, source_target_pairs={{0,1},{1,0},{2,3},{3,2},{4,5},{5,4},{6,7},{7,6},{8,9},{9,8},{10,11... | collective-permute-start | bytes 1179656 | tf_op jit(solution)/shard_map/ppermute | solution.py:360
  81.3 5.2 %copy-start.3 = (s32[128,2]{0,1:T(2,128)S(1)}, s32[128,2]{0,1:T(2,128)}, u32[]{:S(2)}) copy-start(s32[128,2]{0,1:T(2,128)} %param.7) | copy-start | bytes 3076
  81.3 5.8 %copy-start = (bf16[384,1792]{1,0:T(8,128)(2,1)S(1)}, bf16[384,1792]{1,0:T(8,128)(2,1)}, u32[]{:S(2)}) copy-start(bf16[384,1792]{1,0:T(8,128)(2,1)} %get-tuple-element.14.hidden) | copy-start | bytes 4128772
  81.3 33.6 %all-to-all-start.2 = ((bf16[16,24,1536]{2,1,0:T(8,128)(2,1)}), bf16[16,24,1536]{2,1,0:T(8,128)(2,1)S(1)}, u32[]{:S(2)}, u32[]{:S(2)}) async-start(bf16[16,24,1536]{2,1,0:T(8,128)(2,1)} %bitcast.17), calls=%async_computation.2 | async-start | bytes 2359296 | tf_op jit(solution)/shard_map/all_to_all | solution.py:298
  89.5 11.4 %collective-permute-start.2 = (bf16[384,512]{1,0:T(8,128)(2,1)S(1)}, bf16[384,512]{1,0:T(8,128)(2,1)}, u32[]{:S(2)}, u32[]{:S(2)}) collective-permute-start(bf16[384,512]{1,0:T(8,128)(2,1)S(1)} %drop.5), channel_id=1, source_target_pairs={{0,1},{1,0},{2,3},{3,2},{4,5},{5,4},{6,7},{7,6},{8,9},{9,8},{10,11... | collective-permute-start | bytes 1179656 | tf_op jit(solution)/shard_map/ppermute | solution.py:360
  92.9 19.8 %collective-permute-start.3 = (bf16[384,768]{1,0:T(8,128)(2,1)S(1)}, bf16[384,768]{1,0:T(8,128)(2,1)}, u32[]{:S(2)}, u32[]{:S(2)}) collective-permute-start(bf16[384,768]{1,0:T(8,128)(2,1)S(1)} %drop.7), channel_id=1, source_target_pairs={{0,1},{1,0},{2,3},{3,2},{4,5},{5,4},{6,7},{7,6},{8,9},{9,8},{10,11... | collective-permute-start | bytes 1769480 | tf_op jit(solution)/shard_map/ppermute | solution.py:360
  114.9 6.9 %copy-start.4 = (pred[16,128]{1,0:T(8,128)(4,1)S(1)}, pred[16,128]{1,0:T(8,128)(4,1)}, u32[]{:S(2)}) copy-start(pred[16,128]{1,0:T(8,128)(4,1)} %fusion.11) | copy-start | bytes 6148
  114.9 6.9 %copy-start.5 = (s32[128]{0:T(128)S(1)}, s32[128]{0:T(128)}, u32[]{:S(2)}) copy-start(s32[128]{0:T(128)} %get-tuple-element.25) | copy-start | bytes 1540
  114.9 6.9 %copy-start.6 = (s32[128]{0:T(128)S(1)}, s32[128]{0:T(128)}, u32[]{:S(2)}) copy-start(s32[128]{0:T(128)} %get-tuple-element.26) | copy-start | bytes 1540
  114.9 30.4 %all-to-all-start.3 = ((bf16[16,24,1280]{2,1,0:T(8,128)(2,1)}), bf16[16,24,1280]{2,1,0:T(8,128)(2,1)S(1)}, u32[]{:S(2)}, u32[]{:S(2)}) async-start(bf16[16,24,1280]{2,1,0:T(8,128)(2,1)} %bitcast.23), calls=%async_computation.3 | async-start | bytes 1966080 | tf_op jit(solution)/shard_map/all_to_all | solution.py:298
  123.4 10.4 %collective-permute-start.4 = (f32[128,768]{1,0:T(8,128)S(1)}, f32[128,768]{1,0:T(8,128)S(1)}, u32[]{:S(2)}, u32[]{:S(2)}) collective-permute-start(f32[128,768]{1,0:T(8,128)S(1)} %get-tuple-element.17), channel_id=1, source_target_pairs={{0,1},{1,0},{2,3},{3,2},{4,5},{5,4},{6,7},{7,6},{8,9},{9,8},{10,11... | collective-permute-start | bytes 1179656 | tf_op jit(solution)/shard_map/ppermute | solution.py:360

commit v13 on v12

--- a/solution.py
+++ b/solution.py
@@ -313,6 +313,37 @@
     )
 
 
+def add_join(groups):
+    rows = groups[0][0].shape[0]
+    widths = [group[0].shape[1] for group in groups]
+    count = len(groups[0])
+    flat = [term for group in groups for term in group]
+
+    def kernel(*refs):
+        out = refs[-1]
+        at = 0
+        for i, width in enumerate(widths):
+            value = refs[i * count][...]
+            for term in refs[i * count + 1 : (i + 1) * count]:
+                value = value + term[...].astype(jnp.float32)
+            out[:, at : at + width] = value.astype(jnp.bfloat16)
+            at += width
+
+    return pl.pallas_call(
+        kernel,
+        out_shape=jax.ShapeDtypeStruct((rows, sum(widths)), jnp.bfloat16),
+        in_specs=[vmem()] * len(flat),
+        out_specs=vmem(),
+        compiler_params=pltpu.CompilerParams(vmem_limit_bytes=VMEM_BYTES // 2),
+        cost_estimate=pl.CostEstimate(
+            flops=count * rows * sum(widths),
+            bytes_accessed=8 * rows * sum(widths),
+            transcendentals=0,
+        ),
+        name="add_join",
+    )(*flat)
+
+
 def mix_last(weights, returned, first):
     rows = weights[0].shape[1]
     early = first[0].shape[1]
@@ -398,10 +429,8 @@
             for step in range(1, ranks)
         ]
         value = drop(hidden, w_down, me * share + at, cut, jnp.float32)
-        for other in arrived:
-            value = value + other.astype(jnp.float32)
-        owned.append(value.astype(jnp.bfloat16))
-    returned, owned = lax.optimization_barrier((returned, jnp.concatenate(owned, axis=1)))
+        owned.append([value, *arrived])
+    returned, owned = lax.optimization_barrier((returned, add_join(owned)))
     first = mix(weights, returned)
 
     def part_of(rank):

time: 148 us -> 146 us (0.986)
  other arithmetic: 5.39 us -> 0.24 us
  matrix products: 3.84 us -> 7.63 us
    dot_general x3, matrix products: 1.18 us -> 4.98 us  [mix(): lax.dot_general(w, returned, (((0,), (0,)), ((), ())), preferred_element_...]
    all_to_all x4, waiting for transfers between devices: 36.7 us -> 33.2 us  [swap(): lax.all_to_all(value.reshape(experts, slots // experts, width), 'expert',...]
    ppermute x5, waiting for transfers between devices: 26.4 us -> 29.3 us  [send_up(): lax.ppermute(value, 'tensor', [(i, (i + step) % ranks) for i in range(ran...]
    convert_element_type x2 -> x0, other arithmetic: 2.29 us -> none  [on_device(): owned.append(value.astype(jnp.bfloat16))]
  transfers between devices with their start and end apart: 9 -> 9, of which waited for: 6 -> 7; matrix products, arithmetic and copies ran while one was open for 7% -> 6% of each run, Pallas kernels for 18% -> 19%
where the time goes in v13:
time: 146 us
  waiting for transfers between devices  62.5 us (43%)
  Pallas kernels  45.5 us (31%)
  starting transfers between devices  26.6 us (18%)
  matrix products  7.63 us (5%)
  local copies, waits for them, and re-layouts  2.96 us (2%)
    all_to_all x4, waiting for transfers between devices, swap(): lax.all_to_all(value.reshape(experts, slots // experts, width), 'expert',...  33.2 us
    pallas_call x3, Pallas kernels, lift(): pl.pallas_call(kernel, out_shape=out_shape, in_specs=[pl.BlockSpec(memory...  30.4 us
    ppermute x5, waiting for transfers between devices, send_up(): lax.ppermute(value, 'tensor', [(i, (i + step) % ranks) for i in range(ran...  29.3 us
    all_to_all x4, starting transfers between devices, swap(): lax.all_to_all(value.reshape(experts, slots // experts, width), 'expert',...  23.2 us
    pallas_call x4, Pallas kernels, drop(): pl.pallas_call(kernel, out_shape=jax.ShapeDtypeStruct((rows, width), dtyp...  10.9 us
    dot_general x3, matrix products, mix(): lax.dot_general(w, returned, (((0,), (0,)), ((), ())), preferred_element_...  4.98 us
    ppermute x5, starting transfers between devices, send_up(): lax.ppermute(value, 'tensor', [(i, (i + step) % ranks) for i in range(ran...  3.44 us
  transfers between devices with their start and end apart: 9, of which 7 were waited for; matrix products, arithmetic and copies ran while one was open for 6% of the time, Pallas kernels for 19%

profile of v13, /device:TPU:11, one launch (start us, length us, event | category | flops | bytes accessed | tf_op | source)
XLA Modules:
  0.0 145.6 jit_solution(4267640433889248360)
XLA Ops:
  1.9 1.6 %place.1 = (bf16[384,128]{1,0:T(8,128)(2,1)S(1)}, bf16[384,1280]{1,0:T(8,128)(2,1)}) custom-call(s32[1]{0:T(128)} %bitcast.8.at, s32[2,128]{1,0:T(2,128)S(1)} %bitcast.57, bf16[128,4096]{1,0:T(8,128)(2,1)S(1)} %copy-done.1), custom_call_target="tpu_custom_call" | custom-call | flops 125829120 | bytes 327680 | tf_op jit(solution)/shard_map/place/pallas_call | solution.py:273
  3.5 6.6 %all-to-all-start = ((bf16[16,24,1280]{2,1,0:T(8,128)(2,1)}), bf16[16,24,1280]{2,1,0:T(8,128)(2,1)S(1)}, u32[]{:S(2)}, u32[]{:S(2)}) async-start(bf16[16,24,1280]{2,1,0:T(8,128)(2,1)} %bitcast.9), calls=%async_computation | async-start | bytes 1966080 | tf_op jit(solution)/shard_map/all_to_all | solution.py:298
  10.1 2.5 %convolution_convert_fusion = bf16[384,1536]{1,0:T(8,128)(2,1)} fusion(bf16[384,128]{1,0:T(8,128)(2,1)S(1)} %get-tuple-element.12, bf16[128,4096]{1,0:T(8,128)(2,1)} %tokens.1), kind=kOutput, calls=%fused_computation | convolution fusion | flops 151584768 | bytes 1671168 | tf_op jit(solution)/shard_map/dot_general | solution.py:405
  12.6 21.1 %all-to-all-done = bf16[16,24,1280]{2,1,0:T(8,128)(2,1)S(1)} async-done(((bf16[16,24,1280]{2,1,0:T(8,128)(2,1)}), bf16[16,24,1280]{2,1,0:T(8,128)(2,1)S(1)}, u32[]{:S(2)}, u32[]{:S(2)}) %all-to-all-start) | async-done | bytes 983072 | tf_op jit(solution)/shard_map/all_to_all | solution.py:298
  33.6 4.9 %all-to-all-start.1 = ((bf16[16,24,1536]{2,1,0:T(8,128)(2,1)}), bf16[16,24,1536]{2,1,0:T(8,128)(2,1)S(1)}, u32[]{:S(2)}, u32[]{:S(2)}) async-start(bf16[16,24,1536]{2,1,0:T(8,128)(2,1)} %bitcast.11), calls=%async_computation.1 | async-start | bytes 2359296 | tf_op jit(solution)/shard_map/all_to_all | solution.py:298
  41.0 7.4 %lift.3.refs_3_ = f32[7,384,512]{2,1,0:T(8,128)} custom-call(s32[1]{0:T(128)} %bitcast.8.at, bf16[384,1280]{1,0:T(8,128)(2,1)S(1)} %bitcast.54, bf16[4096,1792]{1,0:T(8,128)(2,1)} %bitcast.65, bf16[4096,1792]{1,0:T(8,128)(2,1)} %bitcast.68), custom_call_target="tpu_custom_call" | custom-call | flops 3523215360 | bytes 20185088 | tf_op jit(solution)/shard_map/lift/pallas_call | solution.py:175
  48.5 5.7 %collective-permute-done.1.refs_0_ = bf16[384,768]{1,0:T(8,128)(2,1)S(1)} collective-permute-done((bf16[384,768]{1,0:T(8,128)(2,1)}, bf16[384,768]{1,0:T(8,128)(2,1)S(1)}, u32[]{:S(2)}, u32[]{:S(2)}) %collective-permute-start.1) | collective-permute-done | bytes 589856 | tf_op jit(solution)/shard_map/ppermute | solution.py:391
  54.1 7.7 %lift.4.refs_4_ = f32[7,384,512]{2,1,0:T(8,128)} custom-call(s32[1]{0:T(128)} %bitcast.15.at, bf16[384,768]{1,0:T(8,128)(2,1)S(1)} %collective-permute-done.1.refs_0_, bf16[4096,1792]{1,0:T(8,128)(2,1)} %bitcast.66, bf16[4096,1792]{1,0:T(8,128)(2,1)} %bitcast.69, f32[7,384,512]{2,1,0:T(8,128)} %lift.3.refs_3_), custom_call_target="tpu_custom_call" | custom-call | flops 2113929216 | bytes 16515072 | tf_op jit(solution)/shard_map/lift/pallas_call | solution.py:175
  61.9 4.2 %all-to-all-done.1 = bf16[16,24,1536]{2,1,0:T(8,128)(2,1)S(1)} async-done(((bf16[16,24,1536]{2,1,0:T(8,128)(2,1)}), bf16[16,24,1536]{2,1,0:T(8,128)(2,1)S(1)}, u32[]{:S(2)}, u32[]{:S(2)}) %all-to-all-start.1) | async-done | bytes 1179680 | tf_op jit(solution)/shard_map/all_to_all | solution.py:298
  66.1 15.2 %lift.5 = (bf16[384,1792]{1,0:T(8,128)(2,1)}, bf16[384,1536]{1,0:T(8,128)(2,1)}) custom-call(s32[4]{0:T(128)S(1)} %pad_add_fusion.at, bf16[384,512]{1,0:T(8,128)(2,1)S(1)} %collective-permute-done.refs_0_, bf16[384,1536]{1,0:T(8,128)(2,1)S(1)} %bitcast.55, bf16[4096,1792]{1,0:T(8,128)(2,1)} %bitcast.67, bf16[4096,1792]{1,0:T(8,128)(2,1)} %bitcast.70, ...), custom_call_target="tpu_custom_call" | custom-call | flops 7751073792 | bytes 31195136 | tf_op jit(solution)/shard_map/lift/pallas_call | solution.py:175
  81.3 5.2 %all-to-all-start.2 = ((bf16[16,24,1536]{2,1,0:T(8,128)(2,1)}), bf16[16,24,1536]{2,1,0:T(8,128)(2,1)}, u32[]{:S(2)}, u32[]{:S(2)}) async-start(bf16[16,24,1536]{2,1,0:T(8,128)(2,1)} %bitcast.17), calls=%async_computation.2 | async-start | bytes 2359296 | tf_op jit(solution)/shard_map/all_to_all | solution.py:298
  86.5 3.0 %drop.7 = bf16[384,768]{1,0:T(8,128)(2,1)S(1)} custom-call(s32[1]{0:T(128)} %bitcast.22.at, bf16[384,1792]{1,0:T(8,128)(2,1)S(1)} %copy-done, bf16[1792,4096]{1,0:T(8,128)(2,1)} %bitcast.61), custom_call_target="tpu_custom_call" | custom-call | flops 1056964608 | bytes 2752512 | tf_op jit(solution)/shard_map/drop/pallas_call | solution.py:203
  89.9 2.4 %drop.5 = bf16[384,512]{1,0:T(8,128)(2,1)S(1)} custom-call(s32[1]{0:T(128)} %bitcast.20.at, bf16[384,1792]{1,0:T(8,128)(2,1)S(1)} %copy-done, bf16[1792,4096]{1,0:T(8,128)(2,1)} %bitcast.62), custom_call_target="tpu_custom_call" | custom-call | flops 704643072 | bytes 1835008 | tf_op jit(solution)/shard_map/drop/pallas_call | solution.py:203
  92.3 1.3 collective-permute-start.2
  93.7 2.4 %drop.4.refs_0_ = f32[384,512]{1,0:T(8,128)S(1)} custom-call(s32[1]{0:T(128)} %bitcast.19.at, bf16[384,1792]{1,0:T(8,128)(2,1)S(1)} %copy-done, bf16[1792,4096]{1,0:T(8,128)(2,1)} %bitcast.63), custom_call_target="tpu_custom_call" | custom-call | flops 704643072 | bytes 1835008 | tf_op jit(solution)/shard_map/drop/pallas_call | solution.py:203
  96.1 3.0 %drop.6.refs_2_ = f32[384,768]{1,0:T(8,128)S(1)} custom-call(s32[1]{0:T(128)} %bitcast.21.at, bf16[384,1792]{1,0:T(8,128)(2,1)S(1)} %copy-done, bf16[1792,4096]{1,0:T(8,128)(2,1)} %bitcast.64), custom_call_target="tpu_custom_call" | custom-call | flops 1056964608 | bytes 2752512 | tf_op jit(solution)/shard_map/drop/pallas_call | solution.py:203
  99.2 13.6 %collective-permute-done.2.refs_1_ = bf16[384,512]{1,0:T(8,128)(2,1)S(1)} collective-permute-done((bf16[384,512]{1,0:T(8,128)(2,1)S(1)}, bf16[384,512]{1,0:T(8,128)(2,1)S(1)}, u32[]{:S(2)}, u32[]{:S(2)}) %collective-permute-start.2) | collective-permute-done | bytes 393248 | tf_op jit(solution)/shard_map/ppermute | solution.py:391
  114.2 6.4 %all-to-all-start.3 = ((bf16[16,24,1280]{2,1,0:T(8,128)(2,1)}), bf16[16,24,1280]{2,1,0:T(8,128)(2,1)S(1)}, u32[]{:S(2)}, u32[]{:S(2)}) async-start(bf16[16,24,1280]{2,1,0:T(8,128)(2,1)} %bitcast.23), calls=%async_computation.3 | async-start | bytes 1966080 | tf_op jit(solution)/shard_map/all_to_all | solution.py:298
  121.0 1.7 %fusion.13 = f32[128,1536]{1,0:T(8,128)S(1)} fusion(bf16[384,128]{1,0:T(8,128)(2,1)S(1)} %get-tuple-element.20.refs_1_, bf16[384,1536]{1,0:T(8,128)(2,1)} %bitcast.18), kind=kOutput, calls=%fused_computation.30 | convolution fusion | flops 150994944 | bytes 2064384 | tf_op jit(solution)/shard_map/dot_general | solution.py:309
  122.6 1.7 %convolution_add_fusion.1 = f32[128,1536]{1,0:T(8,128)S(1)} fusion(f32[128,1536]{1,0:T(8,128)S(1)} %fusion.13, bf16[384,128]{1,0:T(8,128)(2,1)S(1)} %get-tuple-element.21.refs_0_, bf16[384,1536]{1,0:T(8,128)(2,1)} %bitcast.18), kind=kOutput, calls=%fused_computation.2 | convolution fusion | flops 151191552 | bytes 2850816 | tf_op jit(solution)/shard_map/dot_general | solution.py:309
  124.3 1.7 %convolution_add_fusion = f32[128,1536]{1,0:T(8,128)S(1)} fusion(f32[128,1536]{1,0:T(8,128)S(1)} %convolution_add_fusion.1, bf16[384,128]{1,0:T(8,128)(2,1)S(1)} %get-tuple-element.19.refs_2_, bf16[384,1536]{1,0:T(8,128)(2,1)} %bitcast.18), kind=kOutput, calls=%fused_computation.1 | convolution fusion | flops 151191552 | bytes 2850816 | tf_op jit(solution)/shard_map/dot_general | solution.py:309
  126.4 10.1 %collective-permute-done.4.refs_5_ = f32[128,768]{1,0:T(8,128)S(1)} collective-permute-done((f32[128,768]{1,0:T(8,128)S(1)}, f32[128,768]{1,0:T(8,128)S(1)}, u32[]{:S(2)}, u32[]{:S(2)}) %collective-permute-start.4) | collective-permute-done | bytes 393248 | tf_op jit(solution)/shard_map/ppermute | solution.py:391
  136.4 7.7 %all-to-all-done.3 = bf16[16,24,1280]{2,1,0:T(8,128)(2,1)S(1)} async-done(((bf16[16,24,1280]{2,1,0:T(8,128)(2,1)}), bf16[16,24,1280]{2,1,0:T(8,128)(2,1)S(1)}, u32[]{:S(2)}, u32[]{:S(2)}) %all-to-all-start.3) | async-done | bytes 983072 | tf_op jit(solution)/shard_map/all_to_all | solution.py:298
  144.1 1.5 %mix_last.1 = bf16[128,2048]{1,0:T(8,128)(2,1)} custom-call(bf16[384,128]{1,0:T(8,128)(2,1)S(1)} %get-tuple-element.21.refs_0_, bf16[384,128]{1,0:T(8,128)(2,1)S(1)} %get-tuple-element.20.refs_1_, bf16[384,128]{1,0:T(8,128)(2,1)S(1)} %get-tuple-element.19.refs_2_, bf16[384,1280]{1,0:T(8,128)(2,1)S(1)} %bitcast.56, f32[128,768]{1,0:T(8,128)S(1)} %get-tuple-element.18.refs_4_, ...), custom_call_target="tpu_custom_call" | custom-call | flops 377487360 | bytes 524288 | tf_op jit(solution)/shard_map/mix_last/pallas_call | solution.py:362
  (30 shorter events, 7.0 us)
Async XLA Ops:
  0.0 1.2 copy-start.1
  1.2 0.7 copy-start.2
  3.5 30.1 %all-to-all-start = ((bf16[16,24,1280]{2,1,0:T(8,128)(2,1)}), bf16[16,24,1280]{2,1,0:T(8,128)(2,1)S(1)}, u32[]{:S(2)}, u32[]{:S(2)}) async-start(bf16[16,24,1280]{2,1,0:T(8,128)(2,1)} %bitcast.9), calls=%async_computation | async-start | bytes 1966080 | tf_op jit(solution)/shard_map/all_to_all | solution.py:298
  33.6 32.4 %all-to-all-start.1 = ((bf16[16,24,1536]{2,1,0:T(8,128)(2,1)}), bf16[16,24,1536]{2,1,0:T(8,128)(2,1)S(1)}, u32[]{:S(2)}, u32[]{:S(2)}) async-start(bf16[16,24,1536]{2,1,0:T(8,128)(2,1)} %bitcast.11), calls=%async_computation.1 | async-start | bytes 2359296 | tf_op jit(solution)/shard_map/all_to_all | solution.py:298
  39.4 14.8 %collective-permute-start.1 = (bf16[384,768]{1,0:T(8,128)(2,1)}, bf16[384,768]{1,0:T(8,128)(2,1)S(1)}, u32[]{:S(2)}, u32[]{:S(2)}) collective-permute-start(bf16[384,768]{1,0:T(8,128)(2,1)} %slice.13), channel_id=1, source_target_pairs={{0,1},{1,0},{2,3},{3,2},{4,5},{5,4},{6,7},{7,6},{8,9},{9,8},{10,11... | collective-permute-start | bytes 1769480 | tf_op jit(solution)/shard_map/ppermute | solution.py:391
  39.7 26.3 %collective-permute-start = (bf16[384,512]{1,0:T(8,128)(2,1)S(1)}, bf16[384,512]{1,0:T(8,128)(2,1)S(1)}, u32[]{:S(2)}, u32[]{:S(2)}) collective-permute-start(bf16[384,512]{1,0:T(8,128)(2,1)S(1)} %slice.12), channel_id=1, source_target_pairs={{0,1},{1,0},{2,3},{3,2},{4,5},{5,4},{6,7},{7,6},{8,9},{9,8},{10,11... | collective-permute-start | bytes 1179656 | tf_op jit(solution)/shard_map/ppermute | solution.py:391
  81.3 5.2 %copy-start = (bf16[384,1792]{1,0:T(8,128)(2,1)S(1)}, bf16[384,1792]{1,0:T(8,128)(2,1)}, u32[]{:S(2)}) copy-start(bf16[384,1792]{1,0:T(8,128)(2,1)} %get-tuple-element.14.hidden) | copy-start | bytes 4128772
  81.3 32.9 %all-to-all-start.2 = ((bf16[16,24,1536]{2,1,0:T(8,128)(2,1)}), bf16[16,24,1536]{2,1,0:T(8,128)(2,1)}, u32[]{:S(2)}, u32[]{:S(2)}) async-start(bf16[16,24,1536]{2,1,0:T(8,128)(2,1)} %bitcast.17), calls=%async_computation.2 | async-start | bytes 2359296 | tf_op jit(solution)/shard_map/all_to_all | solution.py:298
  89.6 23.2 %collective-permute-start.3 = (bf16[384,768]{1,0:T(8,128)(2,1)S(1)}, bf16[384,768]{1,0:T(8,128)(2,1)S(1)}, u32[]{:S(2)}, u32[]{:S(2)}) collective-permute-start(bf16[384,768]{1,0:T(8,128)(2,1)S(1)} %drop.7), channel_id=1, source_target_pairs={{0,1},{1,0},{2,3},{3,2},{4,5},{5,4},{6,7},{7,6},{8,9},{9,8},{10,11... | collective-permute-start | bytes 1769480 | tf_op jit(solution)/shard_map/ppermute | solution.py:391
  89.9 3.8 %copy-start.3 = (s32[128,2]{0,1:T(2,128)S(1)}, s32[128,2]{0,1:T(2,128)}, u32[]{:S(2)}) copy-start(s32[128,2]{0,1:T(2,128)} %param.7) | copy-start | bytes 3076
  89.9 3.8 %copy-start.4 = (f32[128,2]{0,1:T(2,128)S(1)}, f32[128,2]{0,1:T(2,128)}, u32[]{:S(2)}) copy-start(f32[128,2]{0,1:T(2,128)} %param.8) | copy-start | bytes 3076
  92.3 20.4 %collective-permute-start.2 = (bf16[384,512]{1,0:T(8,128)(2,1)S(1)}, bf16[384,512]{1,0:T(8,128)(2,1)S(1)}, u32[]{:S(2)}, u32[]{:S(2)}) collective-permute-start(bf16[384,512]{1,0:T(8,128)(2,1)S(1)} %drop.5), channel_id=1, source_target_pairs={{0,1},{1,0},{2,3},{3,2},{4,5},{5,4},{6,7},{7,6},{8,9},{9,8},{10,11... | collective-permute-start | bytes 1179656 | tf_op jit(solution)/shard_map/ppermute | solution.py:391
  114.2 29.9 %all-to-all-start.3 = ((bf16[16,24,1280]{2,1,0:T(8,128)(2,1)}), bf16[16,24,1280]{2,1,0:T(8,128)(2,1)S(1)}, u32[]{:S(2)}, u32[]{:S(2)}) async-start(bf16[16,24,1280]{2,1,0:T(8,128)(2,1)} %bitcast.23), calls=%async_computation.3 | async-start | bytes 1966080 | tf_op jit(solution)/shard_map/all_to_all | solution.py:298
  126.0 10.4 %collective-permute-start.4 = (f32[128,768]{1,0:T(8,128)S(1)}, f32[128,768]{1,0:T(8,128)S(1)}, u32[]{:S(2)}, u32[]{:S(2)}) collective-permute-start(f32[128,768]{1,0:T(8,128)S(1)} %get-tuple-element.17), channel_id=1, source_target_pairs={{0,1},{1,0},{2,3},{3,2},{4,5},{5,4},{6,7},{7,6},{8,9},{9,8},{10,11... | collective-permute-start | bytes 1179656 | tf_op jit(solution)/shard_map/ppermute | solution.py:391

commit v14 on v13

--- a/solution.py
+++ b/solution.py
@@ -408,7 +408,7 @@
     for piece, at in others[:-1]:
         (sums,) = lift([piece], [at], w_gate, w_up, sums)
 
-    early = round(share * 3 / 8 / 128) * 128
+    early = round(share * 7 / 16 / 128) * 128
     columns = [jnp.int32(rank * share) for rank in range(ranks)]
     last, last_at = others[-1]
     hidden, partial = lift(

time: 146 us -> 147 us (level)
    all_to_all x4, waiting for transfers between devices: 33.2 us -> 35.8 us  [swap(): lax.all_to_all(value.reshape(experts, slots // experts, width), 'expert',...]
  transfers between devices with their start and end apart: 9 -> 9, of which waited for: 7 -> 7; matrix products, arithmetic and copies ran while one was open for 6% -> 7% of each run, Pallas kernels for 19% -> 18%
where the time goes in v14:
time: 147 us; the launch traced here: 146 us
  waiting for transfers between devices  63.9 us (43%)
  Pallas kernels  45 us (31%)
  starting transfers between devices  25.5 us (17%)
  matrix products  7.97 us (5%)
  local copies, waits for them, and re-layouts  3.71 us (3%)
    all_to_all x4, waiting for transfers between devices, swap(): lax.all_to_all(value.reshape(experts, slots // experts, width), 'expert',...  35.8 us
    pallas_call x3, Pallas kernels, lift(): pl.pallas_call(kernel, out_shape=out_shape, in_specs=[pl.BlockSpec(memory...  30.3 us
    ppermute x5, waiting for transfers between devices, send_up(): lax.ppermute(value, 'tensor', [(i, (i + step) % ranks) for i in range(ran...  28.1 us
    all_to_all x4, starting transfers between devices, swap(): lax.all_to_all(value.reshape(experts, slots // experts, width), 'expert',...  22.1 us
    pallas_call x4, Pallas kernels, drop(): pl.pallas_call(kernel, out_shape=jax.ShapeDtypeStruct((rows, width), dtyp...  10.6 us
    dot_general x3, matrix products, mix(): lax.dot_general(w, returned, (((0,), (0,)), ((), ())), preferred_element_...  5.31 us
    ppermute x5, starting transfers between devices, send_up(): lax.ppermute(value, 'tensor', [(i, (i + step) % ranks) for i in range(ran...  3.4 us
  transfers between devices with their start and end apart: 9, of which 7 were waited for; matrix products, arithmetic and copies ran while one was open for 7% of the time, Pallas kernels for 18%

profile of v14, /device:TPU:11, one launch (start us, length us, event | category | flops | bytes accessed | tf_op | source)
XLA Modules:
  0.0 146.4 jit_solution(13975603945078557137)
XLA Ops:
  1.9 1.6 %place.1 = (bf16[384,128]{1,0:T(8,128)(2,1)S(1)}, bf16[384,1280]{1,0:T(8,128)(2,1)}) custom-call(s32[1]{0:T(128)} %bitcast.8.at, s32[2,128]{1,0:T(2,128)S(1)} %bitcast.57, bf16[128,4096]{1,0:T(8,128)(2,1)S(1)} %copy-done), custom_call_target="tpu_custom_call" | custom-call | flops 125829120 | bytes 327680 | tf_op jit(solution)/shard_map/place/pallas_call | solution.py:273
  3.5 6.6 %all-to-all-start = ((bf16[16,24,1280]{2,1,0:T(8,128)(2,1)}), bf16[16,24,1280]{2,1,0:T(8,128)(2,1)S(1)}, u32[]{:S(2)}, u32[]{:S(2)}) async-start(bf16[16,24,1280]{2,1,0:T(8,128)(2,1)} %bitcast.9), calls=%async_computation | async-start | bytes 1966080 | tf_op jit(solution)/shard_map/all_to_all | solution.py:298
  10.1 2.5 %convolution_convert_fusion = bf16[384,1536]{1,0:T(8,128)(2,1)} fusion(bf16[384,128]{1,0:T(8,128)(2,1)S(1)} %get-tuple-element.12, bf16[128,4096]{1,0:T(8,128)(2,1)} %tokens.1), kind=kOutput, calls=%fused_computation | convolution fusion | flops 151584768 | bytes 1671168 | tf_op jit(solution)/shard_map/dot_general | solution.py:405
  12.6 21.1 %all-to-all-done = bf16[16,24,1280]{2,1,0:T(8,128)(2,1)S(1)} async-done(((bf16[16,24,1280]{2,1,0:T(8,128)(2,1)}), bf16[16,24,1280]{2,1,0:T(8,128)(2,1)S(1)}, u32[]{:S(2)}, u32[]{:S(2)}) %all-to-all-start) | async-done | bytes 983072 | tf_op jit(solution)/shard_map/all_to_all | solution.py:298
  33.6 4.9 %all-to-all-start.1 = ((bf16[16,24,1536]{2,1,0:T(8,128)(2,1)}), bf16[16,24,1536]{2,1,0:T(8,128)(2,1)S(1)}, u32[]{:S(2)}, u32[]{:S(2)}) async-start(bf16[16,24,1536]{2,1,0:T(8,128)(2,1)} %bitcast.71), calls=%async_computation.1 | async-start | bytes 2359296 | tf_op jit(solution)/shard_map/all_to_all | solution.py:298
  41.7 7.5 %lift.3.refs_3_ = f32[7,384,512]{2,1,0:T(8,128)} custom-call(s32[1]{0:T(128)} %bitcast.8.at, bf16[384,1280]{1,0:T(8,128)(2,1)S(1)} %bitcast.54, bf16[4096,1792]{1,0:T(8,128)(2,1)} %bitcast.65, bf16[4096,1792]{1,0:T(8,128)(2,1)} %bitcast.68), custom_call_target="tpu_custom_call" | custom-call | flops 3523215360 | bytes 20185088 | tf_op jit(solution)/shard_map/lift/pallas_call | solution.py:175
  49.1 5.0 %collective-permute-done.1.refs_0_ = bf16[384,768]{1,0:T(8,128)(2,1)S(1)} collective-permute-done((bf16[384,768]{1,0:T(8,128)(2,1)}, bf16[384,768]{1,0:T(8,128)(2,1)S(1)}, u32[]{:S(2)}, u32[]{:S(2)}) %collective-permute-start.1) | collective-permute-done | bytes 589856 | tf_op jit(solution)/shard_map/ppermute | solution.py:391
  54.1 7.7 %lift.4.refs_4_ = f32[7,384,512]{2,1,0:T(8,128)} custom-call(s32[1]{0:T(128)} %bitcast.15.at, bf16[384,768]{1,0:T(8,128)(2,1)S(1)} %collective-permute-done.1.refs_0_, bf16[4096,1792]{1,0:T(8,128)(2,1)} %bitcast.66, bf16[4096,1792]{1,0:T(8,128)(2,1)} %bitcast.69, f32[7,384,512]{2,1,0:T(8,128)} %lift.3.refs_3_), custom_call_target="tpu_custom_call" | custom-call | flops 2113929216 | bytes 16515072 | tf_op jit(solution)/shard_map/lift/pallas_call | solution.py:175
  61.8 4.2 %all-to-all-done.1 = bf16[16,24,1536]{2,1,0:T(8,128)(2,1)S(1)} async-done(((bf16[16,24,1536]{2,1,0:T(8,128)(2,1)}), bf16[16,24,1536]{2,1,0:T(8,128)(2,1)S(1)}, u32[]{:S(2)}, u32[]{:S(2)}) %all-to-all-start.1) | async-done | bytes 1179680 | tf_op jit(solution)/shard_map/all_to_all | solution.py:298
  66.1 15.1 %lift.5 = (bf16[384,1792]{1,0:T(8,128)(2,1)S(1)}, bf16[384,1792]{1,0:T(8,128)(2,1)}) custom-call(s32[4]{0:T(128)S(1)} %pad_add_fusion.at, bf16[384,512]{1,0:T(8,128)(2,1)S(1)} %collective-permute-done.refs_0_, bf16[384,1536]{1,0:T(8,128)(2,1)S(1)} %bitcast.55, bf16[4096,1792]{1,0:T(8,128)(2,1)} %bitcast.67, bf16[4096,1792]{1,0:T(8,128)(2,1)} %bitcast.70, ...), custom_call_target="tpu_custom_call" | custom-call | flops 8103395328 | bytes 32112640 | tf_op jit(solution)/shard_map/lift/pallas_call | solution.py:175
  81.2 5.3 %all-to-all-start.2 = ((bf16[16,24,1792]{2,1,0:T(8,128)(2,1)}), bf16[16,24,1792]{2,1,0:T(8,128)(2,1)}, u32[]{:S(2)}, u32[]{:S(2)}) async-start(bf16[16,24,1792]{2,1,0:T(8,128)(2,1)} %bitcast.72), calls=%async_computation.2 | async-start | bytes 2752512 | tf_op jit(solution)/shard_map/all_to_all | solution.py:298
  86.5 2.9 %drop.7 = bf16[384,640]{1,0:T(8,128)(2,1)S(1)} custom-call(s32[1]{0:T(128)} %bitcast.22.at, bf16[384,1792]{1,0:T(8,128)(2,1)S(1)} %get-tuple-element.14.hidden, bf16[1792,4096]{1,0:T(8,128)(2,1)} %bitcast.61), custom_call_target="tpu_custom_call" | custom-call | flops 880803840 | bytes 2293760 | tf_op jit(solution)/shard_map/drop/pallas_call | solution.py:203
  89.8 2.4 %drop.5 = bf16[384,512]{1,0:T(8,128)(2,1)S(1)} custom-call(s32[1]{0:T(128)} %bitcast.20.at, bf16[384,1792]{1,0:T(8,128)(2,1)S(1)} %get-tuple-element.14.hidden, bf16[1792,4096]{1,0:T(8,128)(2,1)} %bitcast.62), custom_call_target="tpu_custom_call" | custom-call | flops 704643072 | bytes 1835008 | tf_op jit(solution)/shard_map/drop/pallas_call | solution.py:203
  93.5 2.4 %drop.4.refs_0_ = f32[384,512]{1,0:T(8,128)S(1)} custom-call(s32[1]{0:T(128)} %bitcast.19.at, bf16[384,1792]{1,0:T(8,128)(2,1)S(1)} %get-tuple-element.14.hidden, bf16[1792,4096]{1,0:T(8,128)(2,1)} %bitcast.63), custom_call_target="tpu_custom_call" | custom-call | flops 704643072 | bytes 1835008 | tf_op jit(solution)/shard_map/drop/pallas_call | solution.py:203
  95.9 2.9 %drop.6.refs_2_ = f32[384,640]{1,0:T(8,128)S(1)} custom-call(s32[1]{0:T(128)} %bitcast.21.at, bf16[384,1792]{1,0:T(8,128)(2,1)S(1)} %get-tuple-element.14.hidden, bf16[1792,4096]{1,0:T(8,128)(2,1)} %bitcast.64), custom_call_target="tpu_custom_call" | custom-call | flops 880803840 | bytes 2293760 | tf_op jit(solution)/shard_map/drop/pallas_call | solution.py:203
  98.8 11.6 %collective-permute-done.2.refs_1_ = bf16[384,512]{1,0:T(8,128)(2,1)S(1)} collective-permute-done((bf16[384,512]{1,0:T(8,128)(2,1)S(1)}, bf16[384,512]{1,0:T(8,128)(2,1)S(1)}, u32[]{:S(2)}, u32[]{:S(2)}) %collective-permute-start.2) | collective-permute-done | bytes 393248 | tf_op jit(solution)/shard_map/ppermute | solution.py:391
  111.5 6.6 %all-to-all-done.2 = bf16[16,24,1792]{2,1,0:T(8,128)(2,1)} async-done(((bf16[16,24,1792]{2,1,0:T(8,128)(2,1)}), bf16[16,24,1792]{2,1,0:T(8,128)(2,1)}, u32[]{:S(2)}, u32[]{:S(2)}) %all-to-all-start.2) | async-done | bytes 1376288 | tf_op jit(solution)/shard_map/all_to_all | solution.py:298
  118.1 5.3 %all-to-all-start.3 = ((bf16[16,24,1152]{2,1,0:T(8,128)(2,1)}), bf16[16,24,1152]{2,1,0:T(8,128)(2,1)S(1)}, u32[]{:S(2)}, u32[]{:S(2)}) async-start(bf16[16,24,1152]{2,1,0:T(8,128)(2,1)} %bitcast.23), calls=%async_computation.3 | async-start | bytes 1769472 | tf_op jit(solution)/shard_map/all_to_all | solution.py:298
  123.8 1.8 %fusion.13 = f32[128,1792]{1,0:T(8,128)S(1)} fusion(bf16[384,128]{1,0:T(8,128)(2,1)S(1)} %get-tuple-element.20.refs_1_, bf16[384,1792]{1,0:T(8,128)(2,1)} %bitcast.18), kind=kOutput, calls=%fused_computation.30 | convolution fusion | flops 176160768 | bytes 2392064 | tf_op jit(solution)/shard_map/dot_general | solution.py:309
  125.5 1.8 %convolution_add_fusion.1 = f32[128,1792]{1,0:T(8,128)S(1)} fusion(f32[128,1792]{1,0:T(8,128)S(1)} %fusion.13, bf16[384,128]{1,0:T(8,128)(2,1)S(1)} %get-tuple-element.21.refs_0_, bf16[384,1792]{1,0:T(8,128)(2,1)} %bitcast.18), kind=kOutput, calls=%fused_computation.2 | convolution fusion | flops 176390144 | bytes 3309568 | tf_op jit(solution)/shard_map/dot_general | solution.py:309
  127.3 1.8 %convolution_add_fusion = f32[128,1792]{1,0:T(8,128)S(1)} fusion(f32[128,1792]{1,0:T(8,128)S(1)} %convolution_add_fusion.1, bf16[384,128]{1,0:T(8,128)(2,1)S(1)} %get-tuple-element.19.refs_2_, bf16[384,1792]{1,0:T(8,128)(2,1)} %bitcast.18), kind=kOutput, calls=%fused_computation.1 | convolution fusion | flops 176390144 | bytes 3309568 | tf_op jit(solution)/shard_map/dot_general | solution.py:309
  129.5 11.5 %collective-permute-done.4.refs_5_ = f32[128,896]{1,0:T(8,128)S(1)} collective-permute-done((f32[128,896]{1,0:T(8,128)S(1)}, f32[128,896]{1,0:T(8,128)S(1)}, u32[]{:S(2)}, u32[]{:S(2)}) %collective-permute-start.4) | collective-permute-done | bytes 458784 | tf_op jit(solution)/shard_map/ppermute | solution.py:391
  141.0 4.0 %all-to-all-done.3 = bf16[16,24,1152]{2,1,0:T(8,128)(2,1)S(1)} async-done(((bf16[16,24,1152]{2,1,0:T(8,128)(2,1)}), bf16[16,24,1152]{2,1,0:T(8,128)(2,1)S(1)}, u32[]{:S(2)}, u32[]{:S(2)}) %all-to-all-start.3) | async-done | bytes 884768 | tf_op jit(solution)/shard_map/all_to_all | solution.py:298
  145.0 1.5 %mix_last.1 = bf16[128,2048]{1,0:T(8,128)(2,1)} custom-call(bf16[384,128]{1,0:T(8,128)(2,1)S(1)} %get-tuple-element.21.refs_0_, bf16[384,128]{1,0:T(8,128)(2,1)S(1)} %get-tuple-element.20.refs_1_, bf16[384,128]{1,0:T(8,128)(2,1)S(1)} %get-tuple-element.19.refs_2_, bf16[384,1152]{1,0:T(8,128)(2,1)S(1)} %bitcast.56, f32[128,896]{1,0:T(8,128)S(1)} %get-tuple-element.18.refs_4_, ...), custom_call_target="tpu_custom_call" | custom-call | flops 339738624 | bytes 524288 | tf_op jit(solution)/shard_map/mix_last/pallas_call | solution.py:362
  (28 shorter events, 8.6 us)
Async XLA Ops:
  0.0 1.2 copy-start
  1.2 0.7 copy-start.1
  3.5 30.1 %all-to-all-start = ((bf16[16,24,1280]{2,1,0:T(8,128)(2,1)}), bf16[16,24,1280]{2,1,0:T(8,128)(2,1)S(1)}, u32[]{:S(2)}, u32[]{:S(2)}) async-start(bf16[16,24,1280]{2,1,0:T(8,128)(2,1)} %bitcast.9), calls=%async_computation | async-start | bytes 1966080 | tf_op jit(solution)/shard_map/all_to_all | solution.py:298
  33.6 32.4 %all-to-all-start.1 = ((bf16[16,24,1536]{2,1,0:T(8,128)(2,1)}), bf16[16,24,1536]{2,1,0:T(8,128)(2,1)S(1)}, u32[]{:S(2)}, u32[]{:S(2)}) async-start(bf16[16,24,1536]{2,1,0:T(8,128)(2,1)} %bitcast.71), calls=%async_computation.1 | async-start | bytes 2359296 | tf_op jit(solution)/shard_map/all_to_all | solution.py:298
  39.4 14.8 %collective-permute-start.1 = (bf16[384,768]{1,0:T(8,128)(2,1)}, bf16[384,768]{1,0:T(8,128)(2,1)S(1)}, u32[]{:S(2)}, u32[]{:S(2)}) collective-permute-start(bf16[384,768]{1,0:T(8,128)(2,1)} %slice.13), channel_id=1, source_target_pairs={{0,1},{1,0},{2,3},{3,2},{4,5},{5,4},{6,7},{7,6},{8,9},{9,8},{10,11... | collective-permute-start | bytes 1769480 | tf_op jit(solution)/shard_map/ppermute | solution.py:391
  40.5 25.6 %collective-permute-start = (bf16[384,512]{1,0:T(8,128)(2,1)}, bf16[384,512]{1,0:T(8,128)(2,1)S(1)}, u32[]{:S(2)}, u32[]{:S(2)}) collective-permute-start(bf16[384,512]{1,0:T(8,128)(2,1)} %slice.12), channel_id=1, source_target_pairs={{0,1},{1,0},{2,3},{3,2},{4,5},{5,4},{6,7},{7,6},{8,9},{9,8},{10,11... | collective-permute-start | bytes 1179656 | tf_op jit(solution)/shard_map/ppermute | solution.py:391
  81.2 5.3 %copy-start.2 = (s32[128,2]{0,1:T(2,128)S(1)}, s32[128,2]{0,1:T(2,128)}, u32[]{:S(2)}) copy-start(s32[128,2]{0,1:T(2,128)} %param.7) | copy-start | bytes 3076
  81.2 5.3 %copy-start.3 = (f32[128,2]{0,1:T(2,128)S(1)}, f32[128,2]{0,1:T(2,128)}, u32[]{:S(2)}) copy-start(f32[128,2]{0,1:T(2,128)} %param.8) | copy-start | bytes 3076
  81.2 36.9 %all-to-all-start.2 = ((bf16[16,24,1792]{2,1,0:T(8,128)(2,1)}), bf16[16,24,1792]{2,1,0:T(8,128)(2,1)}, u32[]{:S(2)}, u32[]{:S(2)}) async-start(bf16[16,24,1792]{2,1,0:T(8,128)(2,1)} %bitcast.72), calls=%async_computation.2 | async-start | bytes 2752512 | tf_op jit(solution)/shard_map/all_to_all | solution.py:298
  89.4 21.0 %collective-permute-start.3 = (bf16[384,640]{1,0:T(8,128)(2,1)S(1)}, bf16[384,640]{1,0:T(8,128)(2,1)S(1)}, u32[]{:S(2)}, u32[]{:S(2)}) collective-permute-start(bf16[384,640]{1,0:T(8,128)(2,1)S(1)} %drop.7), channel_id=1, source_target_pairs={{0,1},{1,0},{2,3},{3,2},{4,5},{5,4},{6,7},{7,6},{8,9},{9,8},{10,11... | collective-permute-start | bytes 1474568 | tf_op jit(solution)/shard_map/ppermute | solution.py:391
  92.1 18.3 %collective-permute-start.2 = (bf16[384,512]{1,0:T(8,128)(2,1)S(1)}, bf16[384,512]{1,0:T(8,128)(2,1)S(1)}, u32[]{:S(2)}, u32[]{:S(2)}) collective-permute-start(bf16[384,512]{1,0:T(8,128)(2,1)S(1)} %drop.5), channel_id=1, source_target_pairs={{0,1},{1,0},{2,3},{3,2},{4,5},{5,4},{6,7},{7,6},{8,9},{9,8},{10,11... | collective-permute-start | bytes 1179656 | tf_op jit(solution)/shard_map/ppermute | solution.py:391
  118.1 26.9 %all-to-all-start.3 = ((bf16[16,24,1152]{2,1,0:T(8,128)(2,1)}), bf16[16,24,1152]{2,1,0:T(8,128)(2,1)S(1)}, u32[]{:S(2)}, u32[]{:S(2)}) async-start(bf16[16,24,1152]{2,1,0:T(8,128)(2,1)} %bitcast.23), calls=%async_computation.3 | async-start | bytes 1769472 | tf_op jit(solution)/shard_map/all_to_all | solution.py:298
  129.2 11.8 %collective-permute-start.4 = (f32[128,896]{1,0:T(8,128)S(1)}, f32[128,896]{1,0:T(8,128)S(1)}, u32[]{:S(2)}, u32[]{:S(2)}) collective-permute-start(f32[128,896]{1,0:T(8,128)S(1)} %get-tuple-element.17), channel_id=1, source_target_pairs={{0,1},{1,0},{2,3},{3,2},{4,5},{5,4},{6,7},{7,6},{8,9},{9,8},{10,11... | collective-permute-start | bytes 1376264 | tf_op jit(solution)/shard_map/ppermute | solution.py:391

commit v15 on v13

--- a/solution.py
+++ b/solution.py
@@ -136,7 +136,7 @@
         if back is not None:
             ranges = [at[count + i] for i in range(len(columns))]
             groups += column_groups(down_from[0], ranges, width, refs[-2], refs[-1])
-        wait = in_turn(groups, 2)
+        wait = in_turn(groups, 3)
         row = 0
         for part, size in zip(parts, depths):
             whole[:, row : row + size] = part[...]

time: 146 us -> 147 us (level)
  transfers between devices with their start and end apart: 9 -> 9, of which waited for: 7 -> 7; matrix products, arithmetic and copies ran while one was open for 6% -> 6% of each run, Pallas kernels for 19% -> 18%
where the time goes in v15:
time: 147 us; the launch traced here: 146 us
  waiting for transfers between devices  62.9 us (43%)
  Pallas kernels  45.7 us (31%)
  starting transfers between devices  26.6 us (18%)
  matrix products  7.65 us (5%)
  local copies, waits for them, and re-layouts  2.96 us (2%)
    all_to_all x4, waiting for transfers between devices, swap(): lax.all_to_all(value.reshape(experts, slots // experts, width), 'expert',...  33.5 us
    pallas_call x3, Pallas kernels, lift(): pl.pallas_call(kernel, out_shape=out_shape, in_specs=[pl.BlockSpec(memory...  30.6 us
    ppermute x5, waiting for transfers between devices, send_up(): lax.ppermute(value, 'tensor', [(i, (i + step) % ranks) for i in range(ran...  29.3 us
    all_to_all x4, starting transfers between devices, swap(): lax.all_to_all(value.reshape(experts, slots // experts, width), 'expert',...  23.2 us
    pallas_call x4, Pallas kernels, drop(): pl.pallas_call(kernel, out_shape=jax.ShapeDtypeStruct((rows, width), dtyp...  10.8 us
    dot_general x3, matrix products, mix(): lax.dot_general(w, returned, (((0,), (0,)), ((), ())), preferred_element_...  4.99 us
    ppermute x5, starting transfers between devices, send_up(): lax.ppermute(value, 'tensor', [(i, (i + step) % ranks) for i in range(ran...  3.44 us
  transfers between devices with their start and end apart: 9, of which 7 were waited for; matrix products, arithmetic and copies ran while one was open for 6% of the time, Pallas kernels for 18%

profile of v15, /device:TPU:11, one launch (start us, length us, event | category | flops | bytes accessed | tf_op | source)
XLA Modules:
  0.0 146.2 jit_solution(8673522562804561290)
XLA Ops:
  1.9 1.6 %place.1 = (bf16[384,128]{1,0:T(8,128)(2,1)S(1)}, bf16[384,1280]{1,0:T(8,128)(2,1)}) custom-call(s32[1]{0:T(128)} %bitcast.8.at, s32[2,128]{1,0:T(2,128)S(1)} %bitcast.57, bf16[128,4096]{1,0:T(8,128)(2,1)S(1)} %copy-done.1), custom_call_target="tpu_custom_call" | custom-call | flops 125829120 | bytes 327680 | tf_op jit(solution)/shard_map/place/pallas_call | solution.py:273
  3.5 6.6 %all-to-all-start = ((bf16[16,24,1280]{2,1,0:T(8,128)(2,1)}), bf16[16,24,1280]{2,1,0:T(8,128)(2,1)S(1)}, u32[]{:S(2)}, u32[]{:S(2)}) async-start(bf16[16,24,1280]{2,1,0:T(8,128)(2,1)} %bitcast.9), calls=%async_computation | async-start | bytes 1966080 | tf_op jit(solution)/shard_map/all_to_all | solution.py:298
  10.1 2.5 %convolution_convert_fusion = bf16[384,1536]{1,0:T(8,128)(2,1)} fusion(bf16[384,128]{1,0:T(8,128)(2,1)S(1)} %get-tuple-element.12, bf16[128,4096]{1,0:T(8,128)(2,1)} %tokens.1), kind=kOutput, calls=%fused_computation | convolution fusion | flops 151584768 | bytes 1671168 | tf_op jit(solution)/shard_map/dot_general | solution.py:405
  12.6 21.1 %all-to-all-done = bf16[16,24,1280]{2,1,0:T(8,128)(2,1)S(1)} async-done(((bf16[16,24,1280]{2,1,0:T(8,128)(2,1)}), bf16[16,24,1280]{2,1,0:T(8,128)(2,1)S(1)}, u32[]{:S(2)}, u32[]{:S(2)}) %all-to-all-start) | async-done | bytes 983072 | tf_op jit(solution)/shard_map/all_to_all | solution.py:298
  33.6 4.9 %all-to-all-start.1 = ((bf16[16,24,1536]{2,1,0:T(8,128)(2,1)}), bf16[16,24,1536]{2,1,0:T(8,128)(2,1)S(1)}, u32[]{:S(2)}, u32[]{:S(2)}) async-start(bf16[16,24,1536]{2,1,0:T(8,128)(2,1)} %bitcast.11), calls=%async_computation.1 | async-start | bytes 2359296 | tf_op jit(solution)/shard_map/all_to_all | solution.py:298
  41.0 7.4 %lift.3.refs_3_ = f32[7,384,512]{2,1,0:T(8,128)} custom-call(s32[1]{0:T(128)} %bitcast.8.at, bf16[384,1280]{1,0:T(8,128)(2,1)S(1)} %bitcast.54, bf16[4096,1792]{1,0:T(8,128)(2,1)} %bitcast.65, bf16[4096,1792]{1,0:T(8,128)(2,1)} %bitcast.68), custom_call_target="tpu_custom_call" | custom-call | flops 3523215360 | bytes 20185088 | tf_op jit(solution)/shard_map/lift/pallas_call | solution.py:175
  48.5 5.7 %collective-permute-done.1.refs_0_ = bf16[384,768]{1,0:T(8,128)(2,1)S(1)} collective-permute-done((bf16[384,768]{1,0:T(8,128)(2,1)}, bf16[384,768]{1,0:T(8,128)(2,1)S(1)}, u32[]{:S(2)}, u32[]{:S(2)}) %collective-permute-start.1) | collective-permute-done | bytes 589856 | tf_op jit(solution)/shard_map/ppermute | solution.py:391
  54.1 7.4 %lift.4.refs_4_ = f32[7,384,512]{2,1,0:T(8,128)} custom-call(s32[1]{0:T(128)} %bitcast.15.at, bf16[384,768]{1,0:T(8,128)(2,1)S(1)} %collective-permute-done.1.refs_0_, bf16[4096,1792]{1,0:T(8,128)(2,1)} %bitcast.66, bf16[4096,1792]{1,0:T(8,128)(2,1)} %bitcast.69, f32[7,384,512]{2,1,0:T(8,128)} %lift.3.refs_3_), custom_call_target="tpu_custom_call" | custom-call | flops 2113929216 | bytes 16515072 | tf_op jit(solution)/shard_map/lift/pallas_call | solution.py:175
  61.6 4.5 %all-to-all-done.1 = bf16[16,24,1536]{2,1,0:T(8,128)(2,1)S(1)} async-done(((bf16[16,24,1536]{2,1,0:T(8,128)(2,1)}), bf16[16,24,1536]{2,1,0:T(8,128)(2,1)S(1)}, u32[]{:S(2)}, u32[]{:S(2)}) %all-to-all-start.1) | async-done | bytes 1179680 | tf_op jit(solution)/shard_map/all_to_all | solution.py:298
  66.1 15.8 %lift.5 = (bf16[384,1792]{1,0:T(8,128)(2,1)}, bf16[384,1536]{1,0:T(8,128)(2,1)}) custom-call(s32[4]{0:T(128)S(1)} %pad_add_fusion.at, bf16[384,512]{1,0:T(8,128)(2,1)S(1)} %collective-permute-done.refs_0_, bf16[384,1536]{1,0:T(8,128)(2,1)S(1)} %bitcast.55, bf16[4096,1792]{1,0:T(8,128)(2,1)} %bitcast.67, bf16[4096,1792]{1,0:T(8,128)(2,1)} %bitcast.70, ...), custom_call_target="tpu_custom_call" | custom-call | flops 7751073792 | bytes 31195136 | tf_op jit(solution)/shard_map/lift/pallas_call | solution.py:175
  81.9 5.2 %all-to-all-start.2 = ((bf16[16,24,1536]{2,1,0:T(8,128)(2,1)}), bf16[16,24,1536]{2,1,0:T(8,128)(2,1)}, u32[]{:S(2)}, u32[]{:S(2)}) async-start(bf16[16,24,1536]{2,1,0:T(8,128)(2,1)} %bitcast.17), calls=%async_computation.2 | async-start | bytes 2359296 | tf_op jit(solution)/shard_map/all_to_all | solution.py:298
  87.1 3.0 %drop.7 = bf16[384,768]{1,0:T(8,128)(2,1)S(1)} custom-call(s32[1]{0:T(128)} %bitcast.22.at, bf16[384,1792]{1,0:T(8,128)(2,1)S(1)} %copy-done, bf16[1792,4096]{1,0:T(8,128)(2,1)} %bitcast.61), custom_call_target="tpu_custom_call" | custom-call | flops 1056964608 | bytes 2752512 | tf_op jit(solution)/shard_map/drop/pallas_call | solution.py:203
  90.4 2.4 %drop.5 = bf16[384,512]{1,0:T(8,128)(2,1)S(1)} custom-call(s32[1]{0:T(128)} %bitcast.20.at, bf16[384,1792]{1,0:T(8,128)(2,1)S(1)} %copy-done, bf16[1792,4096]{1,0:T(8,128)(2,1)} %bitcast.62), custom_call_target="tpu_custom_call" | custom-call | flops 704643072 | bytes 1835008 | tf_op jit(solution)/shard_map/drop/pallas_call | solution.py:203
  92.9 1.3 collective-permute-start.2
  94.3 2.4 %drop.4.refs_0_ = f32[384,512]{1,0:T(8,128)S(1)} custom-call(s32[1]{0:T(128)} %bitcast.19.at, bf16[384,1792]{1,0:T(8,128)(2,1)S(1)} %copy-done, bf16[1792,4096]{1,0:T(8,128)(2,1)} %bitcast.63), custom_call_target="tpu_custom_call" | custom-call | flops 704643072 | bytes 1835008 | tf_op jit(solution)/shard_map/drop/pallas_call | solution.py:203
  96.7 3.0 %drop.6.refs_2_ = f32[384,768]{1,0:T(8,128)S(1)} custom-call(s32[1]{0:T(128)} %bitcast.21.at, bf16[384,1792]{1,0:T(8,128)(2,1)S(1)} %copy-done, bf16[1792,4096]{1,0:T(8,128)(2,1)} %bitcast.64), custom_call_target="tpu_custom_call" | custom-call | flops 1056964608 | bytes 2752512 | tf_op jit(solution)/shard_map/drop/pallas_call | solution.py:203
  99.7 13.6 %collective-permute-done.2.refs_1_ = bf16[384,512]{1,0:T(8,128)(2,1)S(1)} collective-permute-done((bf16[384,512]{1,0:T(8,128)(2,1)S(1)}, bf16[384,512]{1,0:T(8,128)(2,1)S(1)}, u32[]{:S(2)}, u32[]{:S(2)}) %collective-permute-start.2) | collective-permute-done | bytes 393248 | tf_op jit(solution)/shard_map/ppermute | solution.py:391
  114.7 6.4 %all-to-all-start.3 = ((bf16[16,24,1280]{2,1,0:T(8,128)(2,1)}), bf16[16,24,1280]{2,1,0:T(8,128)(2,1)S(1)}, u32[]{:S(2)}, u32[]{:S(2)}) async-start(bf16[16,24,1280]{2,1,0:T(8,128)(2,1)} %bitcast.23), calls=%async_computation.3 | async-start | bytes 1966080 | tf_op jit(solution)/shard_map/all_to_all | solution.py:298
  121.5 1.7 %fusion.13 = f32[128,1536]{1,0:T(8,128)S(1)} fusion(bf16[384,128]{1,0:T(8,128)(2,1)S(1)} %get-tuple-element.20.refs_1_, bf16[384,1536]{1,0:T(8,128)(2,1)} %bitcast.18), kind=kOutput, calls=%fused_computation.30 | convolution fusion | flops 150994944 | bytes 2064384 | tf_op jit(solution)/shard_map/dot_general | solution.py:309
  123.2 1.7 %convolution_add_fusion.1 = f32[128,1536]{1,0:T(8,128)S(1)} fusion(f32[128,1536]{1,0:T(8,128)S(1)} %fusion.13, bf16[384,128]{1,0:T(8,128)(2,1)S(1)} %get-tuple-element.21.refs_0_, bf16[384,1536]{1,0:T(8,128)(2,1)} %bitcast.18), kind=kOutput, calls=%fused_computation.2 | convolution fusion | flops 151191552 | bytes 2850816 | tf_op jit(solution)/shard_map/dot_general | solution.py:309
  124.9 1.7 %convolution_add_fusion = f32[128,1536]{1,0:T(8,128)S(1)} fusion(f32[128,1536]{1,0:T(8,128)S(1)} %convolution_add_fusion.1, bf16[384,128]{1,0:T(8,128)(2,1)S(1)} %get-tuple-element.19.refs_2_, bf16[384,1536]{1,0:T(8,128)(2,1)} %bitcast.18), kind=kOutput, calls=%fused_computation.1 | convolution fusion | flops 151191552 | bytes 2850816 | tf_op jit(solution)/shard_map/dot_general | solution.py:309
  126.9 10.1 %collective-permute-done.4.refs_5_ = f32[128,768]{1,0:T(8,128)S(1)} collective-permute-done((f32[128,768]{1,0:T(8,128)S(1)}, f32[128,768]{1,0:T(8,128)S(1)}, u32[]{:S(2)}, u32[]{:S(2)}) %collective-permute-start.4) | collective-permute-done | bytes 393248 | tf_op jit(solution)/shard_map/ppermute | solution.py:391
  137.0 7.6 %all-to-all-done.3 = bf16[16,24,1280]{2,1,0:T(8,128)(2,1)S(1)} async-done(((bf16[16,24,1280]{2,1,0:T(8,128)(2,1)}), bf16[16,24,1280]{2,1,0:T(8,128)(2,1)S(1)}, u32[]{:S(2)}, u32[]{:S(2)}) %all-to-all-start.3) | async-done | bytes 983072 | tf_op jit(solution)/shard_map/all_to_all | solution.py:298
  144.7 1.5 %mix_last.1 = bf16[128,2048]{1,0:T(8,128)(2,1)} custom-call(bf16[384,128]{1,0:T(8,128)(2,1)S(1)} %get-tuple-element.21.refs_0_, bf16[384,128]{1,0:T(8,128)(2,1)S(1)} %get-tuple-element.20.refs_1_, bf16[384,128]{1,0:T(8,128)(2,1)S(1)} %get-tuple-element.19.refs_2_, bf16[384,1280]{1,0:T(8,128)(2,1)S(1)} %bitcast.56, f32[128,768]{1,0:T(8,128)S(1)} %get-tuple-element.18.refs_4_, ...), custom_call_target="tpu_custom_call" | custom-call | flops 377487360 | bytes 524288 | tf_op jit(solution)/shard_map/mix_last/pallas_call | solution.py:362
  (30 shorter events, 7.0 us)
Async XLA Ops:
  0.0 1.2 copy-start.1
  1.2 0.7 copy-start.2
  3.5 30.1 %all-to-all-start = ((bf16[16,24,1280]{2,1,0:T(8,128)(2,1)}), bf16[16,24,1280]{2,1,0:T(8,128)(2,1)S(1)}, u32[]{:S(2)}, u32[]{:S(2)}) async-start(bf16[16,24,1280]{2,1,0:T(8,128)(2,1)} %bitcast.9), calls=%async_computation | async-start | bytes 1966080 | tf_op jit(solution)/shard_map/all_to_all | solution.py:298
  33.6 32.4 %all-to-all-start.1 = ((bf16[16,24,1536]{2,1,0:T(8,128)(2,1)}), bf16[16,24,1536]{2,1,0:T(8,128)(2,1)S(1)}, u32[]{:S(2)}, u32[]{:S(2)}) async-start(bf16[16,24,1536]{2,1,0:T(8,128)(2,1)} %bitcast.11), calls=%async_computation.1 | async-start | bytes 2359296 | tf_op jit(solution)/shard_map/all_to_all | solution.py:298
  39.4 14.8 %collective-permute-start.1 = (bf16[384,768]{1,0:T(8,128)(2,1)}, bf16[384,768]{1,0:T(8,128)(2,1)S(1)}, u32[]{:S(2)}, u32[]{:S(2)}) collective-permute-start(bf16[384,768]{1,0:T(8,128)(2,1)} %slice.13), channel_id=1, source_target_pairs={{0,1},{1,0},{2,3},{3,2},{4,5},{5,4},{6,7},{7,6},{8,9},{9,8},{10,11... | collective-permute-start | bytes 1769480 | tf_op jit(solution)/shard_map/ppermute | solution.py:391
  39.7 26.3 %collective-permute-start = (bf16[384,512]{1,0:T(8,128)(2,1)S(1)}, bf16[384,512]{1,0:T(8,128)(2,1)S(1)}, u32[]{:S(2)}, u32[]{:S(2)}) collective-permute-start(bf16[384,512]{1,0:T(8,128)(2,1)S(1)} %slice.12), channel_id=1, source_target_pairs={{0,1},{1,0},{2,3},{3,2},{4,5},{5,4},{6,7},{7,6},{8,9},{9,8},{10,11... | collective-permute-start | bytes 1179656 | tf_op jit(solution)/shard_map/ppermute | solution.py:391
  81.9 5.2 %copy-start = (bf16[384,1792]{1,0:T(8,128)(2,1)S(1)}, bf16[384,1792]{1,0:T(8,128)(2,1)}, u32[]{:S(2)}) copy-start(bf16[384,1792]{1,0:T(8,128)(2,1)} %get-tuple-element.14.hidden) | copy-start | bytes 4128772
  81.9 32.9 %all-to-all-start.2 = ((bf16[16,24,1536]{2,1,0:T(8,128)(2,1)}), bf16[16,24,1536]{2,1,0:T(8,128)(2,1)}, u32[]{:S(2)}, u32[]{:S(2)}) async-start(bf16[16,24,1536]{2,1,0:T(8,128)(2,1)} %bitcast.17), calls=%async_computation.2 | async-start | bytes 2359296 | tf_op jit(solution)/shard_map/all_to_all | solution.py:298
  90.1 23.2 %collective-permute-start.3 = (bf16[384,768]{1,0:T(8,128)(2,1)S(1)}, bf16[384,768]{1,0:T(8,128)(2,1)S(1)}, u32[]{:S(2)}, u32[]{:S(2)}) collective-permute-start(bf16[384,768]{1,0:T(8,128)(2,1)S(1)} %drop.7), channel_id=1, source_target_pairs={{0,1},{1,0},{2,3},{3,2},{4,5},{5,4},{6,7},{7,6},{8,9},{9,8},{10,11... | collective-permute-start | bytes 1769480 | tf_op jit(solution)/shard_map/ppermute | solution.py:391
  90.4 3.8 %copy-start.3 = (s32[128,2]{0,1:T(2,128)S(1)}, s32[128,2]{0,1:T(2,128)}, u32[]{:S(2)}) copy-start(s32[128,2]{0,1:T(2,128)} %param.7) | copy-start | bytes 3076
  90.4 3.8 %copy-start.4 = (f32[128,2]{0,1:T(2,128)S(1)}, f32[128,2]{0,1:T(2,128)}, u32[]{:S(2)}) copy-start(f32[128,2]{0,1:T(2,128)} %param.8) | copy-start | bytes 3076
  92.9 20.4 %collective-permute-start.2 = (bf16[384,512]{1,0:T(8,128)(2,1)S(1)}, bf16[384,512]{1,0:T(8,128)(2,1)S(1)}, u32[]{:S(2)}, u32[]{:S(2)}) collective-permute-start(bf16[384,512]{1,0:T(8,128)(2,1)S(1)} %drop.5), channel_id=1, source_target_pairs={{0,1},{1,0},{2,3},{3,2},{4,5},{5,4},{6,7},{7,6},{8,9},{9,8},{10,11... | collective-permute-start | bytes 1179656 | tf_op jit(solution)/shard_map/ppermute | solution.py:391
  114.7 29.9 %all-to-all-start.3 = ((bf16[16,24,1280]{2,1,0:T(8,128)(2,1)}), bf16[16,24,1280]{2,1,0:T(8,128)(2,1)S(1)}, u32[]{:S(2)}, u32[]{:S(2)}) async-start(bf16[16,24,1280]{2,1,0:T(8,128)(2,1)} %bitcast.23), calls=%async_computation.3 | async-start | bytes 1966080 | tf_op jit(solution)/shard_map/all_to_all | solution.py:298
  126.6 10.4 %collective-permute-start.4 = (f32[128,768]{1,0:T(8,128)S(1)}, f32[128,768]{1,0:T(8,128)S(1)}, u32[]{:S(2)}, u32[]{:S(2)}) collective-permute-start(f32[128,768]{1,0:T(8,128)S(1)} %get-tuple-element.17), channel_id=1, source_target_pairs={{0,1},{1,0},{2,3},{3,2},{4,5},{5,4},{6,7},{7,6},{8,9},{9,8},{10,11... | collective-permute-start | bytes 1179656 | tf_op jit(solution)/shard_map/ppermute | solution.py:391
